TPU v7x, 128 devices: a whole 4x4x4 slice. The times are simulated.
128 devices in a mesh: dp: 8 (over y_lo, z), fsdp: 16 (over y_hi, x, core).
Axes of the slice: x: 4, y: 4 (y_hi: 2, y_lo: 2; y = y_hi * 2 + y_lo), z: 4, core: 2. Of those that a mesh axis runs over, the one named last changes fastest.
Arguments:
- img_emb: bfloat16 [16, 2560, 1152], P('fsdp', 'dp'), may hold values from -0.5 to 0.5
- txt_feat: bfloat16 [16, 2560, 1152], P('fsdp', 'dp'), may hold values from -0.405 to 0.405
- w_txt: float32 [1152, 1152], P('fsdp'), may hold values from -0.125 to 1.125
- t_log: float32 [1], replicated, may hold values from 1.6 to 2.4
- bias: float32 [1], replicated, may hold values from -4 to -2.5
Outputs:
- d_img_emb: bfloat16 [16, 2560, 1152], P('fsdp', 'dp')
- d_txt_feat: bfloat16 [16, 2560, 1152], P('fsdp', 'dp')
- d_w_txt: float32 [1152, 1152], P('fsdp')
All inputs are finite; a program needn't handle non-finite values.
Results may differ from a plain program's by a relative error of at most 0.015.
Values may be sent and summed in bfloat16 or wider, within the bound.
No kernel may reach another device: no remote copies, remote signals or barrier semaphores. Data moves between devices by JAX's collectives and lax.ppermute only.
A program may use at most 128 MiB of HBM per device.

v0:
```python
import jax
import jax.numpy as jnp
from jax import lax
from jax.sharding import PartitionSpec as P


def normalize(latent):
    length = jnp.sqrt(jnp.sum(latent * latent, axis=-1, keepdims=True) + 1e-06)
    unit_rows = latent / length
    return (unit_rows, length, unit_rows.astype(jnp.bfloat16))


def project_back(grad_unit, unit_rows, length):
    inner = jnp.sum(unit_rows * grad_unit, axis=-1, keepdims=True)
    return ((grad_unit - unit_rows * inner) / length).astype(jnp.bfloat16)


def scores(img_a, txt_b, logit_scale, logit_bias, on_diagonal):
    logits = (
        logit_scale
        * lax.dot_general(
            img_a, txt_b, (((1,), (1,)), ((), ())), preferred_element_type=jnp.float32
        )
        + logit_bias
    )
    row_ids = lax.broadcasted_iota(jnp.int32, logits.shape, 0)
    col_ids = lax.broadcasted_iota(jnp.int32, logits.shape, 1)
    identity = jnp.where(row_ids == col_ids, on_diagonal, 0.0)
    return (jax.nn.sigmoid(logits) - identity).astype(jnp.bfloat16)


def image_side(grad_logit, txt_b, logit_scale):
    return (logit_scale * jnp.dot(grad_logit, txt_b, preferred_element_type=jnp.float32)).astype(
        jnp.bfloat16
    )


def text_side(grad_logit, img_a, logit_scale):
    product = lax.dot_general(
        grad_logit, img_a, (((0,), (0,)), ((), ())), preferred_element_type=jnp.float32
    )
    return (logit_scale * product).astype(jnp.bfloat16)


def on_device(img_emb, txt_feat, w_txt, t_log, bias):
    img_own = img_emb[0]
    txt_rows = txt_feat[0]
    block_rows = img_own.shape[0]
    embed_width = w_txt.shape[1]
    part_rows = w_txt.shape[0]
    logit_scale = jnp.exp(t_log[0])
    logit_bias = bias[0]
    w_half = w_txt.astype(jnp.bfloat16)
    zero_rows = jnp.zeros((block_rows, embed_width), jnp.float32)
    z_txt = jnp.dot(
        txt_rows,
        lax.all_gather(w_half, "fsdp", axis=0, tiled=True),
        preferred_element_type=jnp.float32,
    )
    u_img, s_img, n_img = normalize(img_own.astype(jnp.float32))
    u_txt, s_txt, n_txt = normalize(z_txt)
    own_start = lax.axis_index("dp") * block_rows
    offset = jnp.int32(0)
    acc_img = zero_rows
    acc_txt = zero_rows
    other_img = lax.all_gather(n_img, "dp", axis=0, tiled=True)
    other_txt = lax.all_gather(n_txt, "dp", axis=0, tiled=True)
    for block_id in range(other_img.shape[0] // block_rows):
        blk_img = other_img[block_id * block_rows : (block_id + 1) * block_rows]
        blk_txt = other_txt[block_id * block_rows : (block_id + 1) * block_rows]
        on_diagonal = (offset + block_id * block_rows == own_start).astype(jnp.float32)
        grad_row = scores(n_img, blk_txt, logit_scale, logit_bias, on_diagonal)
        acc_img = acc_img + image_side(grad_row, blk_txt, logit_scale).astype(jnp.float32)
        grad_col = scores(blk_img, n_txt, logit_scale, logit_bias, on_diagonal)
        acc_txt = acc_txt + text_side(grad_col, blk_img, logit_scale).astype(jnp.float32)
    d_img = project_back(acc_img, u_img, s_img)
    dz_txt = project_back(acc_txt, u_txt, s_txt)
    d_feat = lax.dot_general(
        dz_txt,
        lax.all_gather(w_half, "fsdp", axis=0, tiled=True),
        (((1,), (1,)), ((), ())),
        preferred_element_type=jnp.float32,
    ).astype(jnp.bfloat16)
    weight_term = lax.dot_general(
        txt_rows, dz_txt, (((0,), (0,)), ((), ())), preferred_element_type=jnp.float32
    )
    summed = lax.psum(weight_term, ("dp", "fsdp"))
    d_weight = lax.dynamic_slice_in_dim(summed, lax.axis_index("fsdp") * part_rows, part_rows, 0)
    return (d_img[None], d_feat[None], d_weight)


def solution(mesh):
    placed = (P("fsdp", "dp", None), P("fsdp", "dp", None), P("fsdp", None), P(), P())
    return jax.shard_map(
        on_device,
        mesh=mesh,
        in_specs=placed,
        out_specs=(P("fsdp", "dp", None), P("fsdp", "dp", None), P("fsdp", None)),
        check_vma=False,
    )
```

profile of v0, /device:TPU:0, one launch (start us, length us, event | category | flops | bytes accessed | tf_op | source)
XLA Modules:
  0.0 441.3 jit_solution(8491979354116647337)
XLA Ops:
  7.2 0.0 copy-start
  7.2 0.0 copy-start.1
  7.2 0.0 all-gather.4.cloned.1.call-start
  7.2 1.8 convert_element_type.195
  9.0 0.0 all-gather.4.cloned.1.call-update
  9.0 0.0 all-gather.8.cloned.1.call-start
  9.1 1.4 fusion.47
  10.4 0.0 copy-done.1
  10.4 1.2 fusion.324
  11.6 0.0 all-gather.8.cloned.1.call-update
  11.6 0.0 all-reduce.2.cloned.1.call-start
  13.1 51.0 %all-gather.4.cloned.1.call-done = bf16[1152,1152]{1,0:T(8,128)(2,1)} async-done(((bf16[72,1152]{1,0:T(8,128)(2,1)}), bf16[1152,1152]{1,0:T(8,128)(2,1)}) %all-gather.4.cloned.1.call-update) | async-done | bytes 2654224 | tf_op jit(solution)/shard_map/all_gather | solution.py:57
  64.1 0.0 copy-done
  64.1 3.1 multiply_reduce_fusion.2
  67.1 1.1 fusion.325
  68.2 65.7 %all-gather.8.cloned.1.call-done = bf16[2560,1152]{1,0:T(8,128)(2,1)} async-done(((bf16[320,1152]{1,0:T(8,128)(2,1)}), bf16[2560,1152]{1,0:T(8,128)(2,1)}) %all-gather.8.cloned.1.call-update) | async-done | bytes 5898256 | tf_op jit(solution)/shard_map/all_gather | solution.py:66
  133.9 4.0 fusion.33
  137.9 4.1 fusion.35
  142.0 4.1 fusion.37
  146.0 4.0 fusion.39
  150.0 4.1 fusion.41
  154.1 4.0 fusion.43
  158.1 4.0 fusion.45
  162.1 7.3 %multiply_reduce_fusion = (f32[320]{0:T(512)S(1)}, f32[320,1152]{1,0:T(8,128)}) fusion(f32[320,1152]{1,0:T(8,128)S(1)} %get-tuple-element.7, f32[320]{0:T(512)S(1)} %add_sqrt_fusion, f32[320,1152]{1,0:T(8,128)} %fusion.45, f32[320,1152]{1,0:T(8,128)} %fusion.43, f32[320,1152]{1,0:T(8,128)} %fusion.41, f32[320,1152]{1,0:T(8,128)} %fusion.39, ...), kind=kOutput, calls=%fused_computation.69 | convolution fusion | flops 477572800 | bytes 15486980 | tf_op jit(solution)/shard_map/dot_general | solution.py:39
  169.4 1.7 divide_convert_fusion
  171.1 0.0 copy-start.2
  171.1 0.9 copy-done.2
  172.0 4.0 convolution_bitcast_fusion
  176.0 0.0 copy-start.3
  176.0 0.0 all-reduce.2.cloned.1.call-update
  176.0 0.2 all-gather.6.cloned.1.call-start
  176.2 0.3 all-gather.6.cloned.1.call-update
  176.6 0.5 copy-done.3
  177.1 3.9 fusion.46
  180.9 150.5 %all-reduce.2.cloned.1.call-done = f32[1152,1152]{0,1:T(8,128)} async-done(((f32[1152,1152]{0,1:T(8,128)}), f32[1152,1152]{0,1:T(8,128)}) %all-reduce.2.cloned.1.call-update) | async-done | bytes 5308432 | tf_op jit(solution)/shard_map/psum | solution.py:87
  331.4 1.5 constant_dynamic-slice_fusion
  332.9 1.0 copy.8
  333.8 65.9 %all-gather.6.cloned.1.call-done = bf16[2560,1152]{1,0:T(8,128)(2,1)} async-done(((bf16[320,1152]{1,0:T(8,128)(2,1)}), bf16[2560,1152]{1,0:T(8,128)(2,1)}) %all-gather.6.cloned.1.call-update) | async-done | bytes 5898256 | tf_op jit(solution)/shard_map/all_gather | solution.py:67
  399.7 0.0 copy-done.4
  399.7 3.6 fusion.10
  403.4 3.7 fusion.12
  407.0 3.6 fusion.14
  410.7 3.6 fusion.16
  414.3 3.7 fusion.18
  418.0 3.6 fusion.20
  421.6 3.6 fusion.22
  425.2 7.0 %multiply_reduce_fusion.1 = (f32[320]{0:T(512)S(1)}, f32[320,1152]{1,0:T(8,128)}) fusion(f32[320]{0:T(512)S(1)} %add_sqrt_fusion.1, bf16[1,320,1152]{2,1,0:T(8,128)(2,1)S(1)} %copy-done.1, f32[320,1152]{1,0:T(8,128)} %fusion.22, f32[320,1152]{1,0:T(8,128)} %fusion.20, f32[320,1152]{1,0:T(8,128)} %fusion.18, f32[320,1152]{1,0:T(8,128)} %fusion.16, ...), kind=kOutput, calls=%fused_computation.71 | convolution fusion | flops 477941440 | bytes 14749700 | tf_op jit(solution)/shard_map/dot_general | solution.py:33
  432.2 2.6 fusion.195
  (3 shorter events, 0.0 us)
Async XLA Ops:
  7.2 56.9 %copy-start = (bf16[1,320,1152]{2,1,0:T(8,128)(2,1)S(1)}, bf16[1,320,1152]{2,1,0:T(8,128)(2,1)}, u32[]{:S(2)}) copy-start(bf16[1,320,1152]{2,1,0:T(8,128)(2,1)} %param.6) | copy-start | bytes 2211844
  7.2 3.3 copy-start.1
  7.2 56.9 %all-gather.4.cloned.1.call-start = ((), (), s32[]{:S(2)}) async-start(), calls=%async_computation | async-start | bytes 2820096 | tf_op jit(solution)/shard_map/all_gather | solution.py:57
  9.0 124.9 %all-gather.8.cloned.1.call-start = ((), (), s32[]{:S(2)}) async-start(), calls=%async_computation.2 | async-start | bytes 6635520 | tf_op jit(solution)/shard_map/all_gather | solution.py:66
  11.6 319.8 %all-reduce.2.cloned.1.call-start = ((), (), s32[]{:S(2)}) async-start(), calls=%async_computation.3 | async-start | bytes 10616832 | tf_op jit(solution)/shard_map/psum | solution.py:87
  171.1 0.9 copy-start.2
  176.0 1.1 copy-start.3
  176.0 223.8 %all-gather.6.cloned.1.call-start = ((), (), s32[]{:S(2)}) async-start(), calls=%async_computation.1 | async-start | bytes 6635520 | tf_op jit(solution)/shard_map/all_gather | solution.py:67
  180.9 218.8 %copy-start.4 = (bf16[320,1152]{1,0:T(8,128)(2,1)S(1)}, bf16[320,1152]{1,0:T(8,128)(2,1)}, u32[]{:S(2)}) copy-start(bf16[320,1152]{1,0:T(8,128)(2,1)} %fusion.324) | copy-start | bytes 2211844
Sparse Core Ops, SparseCore 0:
  11.1 52.9 all-gather.3
  66.3 67.5 all-gather.7
  176.1 155.2 all-reduce.1
  332.9 66.8 all-gather.5
where the time goes:
time: 443 us; the launch traced here: 441 us
  waiting for transfers between devices  333 us (75%)
  matrix products  78.9 us (18%)
  between operations  15.2 us (3%)
  other arithmetic  9.61 us (2%)
    psum x1, waiting for transfers between devices, on_device(): summed = lax.psum(weight_term, ('dp', 'fsdp'))  150 us
    all_gather x1, waiting for transfers between devices, on_device(): other_txt = lax.all_gather(n_txt, 'dp', axis=0, tiled=True)  65.9 us
    all_gather x1, waiting for transfers between devices, on_device(): other_img = lax.all_gather(n_img, 'dp', axis=0, tiled=True)  65.7 us
    all_gather x1, waiting for transfers between devices, on_device(): lax.all_gather(w_half, 'fsdp', axis=0, tiled=True)  51 us
    dot_general x8, matrix products, text_side(): lax.dot_general(grad_logit, img_a, (((0,), (0,)), ((), ())), preferred_el...  35.5 us
    dot_general x8, matrix products, image_side(): jnp.dot(grad_logit, txt_b, preferred_element_type=jnp.float32)  32.4 us
  transfers between devices with their start and end apart: 4, of which 4 were waited for; matrix products, arithmetic and copies ran while one was open for 3% of the time, Pallas kernels for 0%

commit v1 on v0

v1 whole, which is shorter than its diff:
```python
import jax
import jax.numpy as jnp
from jax import lax
from jax.experimental import pallas as pl
from jax.experimental.pallas import tpu as pltpu
from jax.sharding import Mesh, PartitionSpec as P

BF = jnp.bfloat16
F32 = jnp.float32
MIB = 1024 * 1024
AXES = {"ylo": 2, "z": 4, "yhi": 2, "x": 4, "core": 2}

VM = pl.BlockSpec(memory_space=pltpu.VMEM)
SM = pl.BlockSpec(memory_space=pltpu.SMEM)


def shift(value, axis, step):
    n = AXES[axis]
    return lax.ppermute(value, axis, [(i, (i + step) % n) for i in range(n)])


def swap_far(value):
    pairs = [(a * 2 + b, (1 - a) * 2 + 1 - b) for a in range(2) for b in range(2)]
    return lax.ppermute(value, ("ylo", "yhi"), pairs)


def shaped(shape, dtype):
    return jax.ShapeDtypeStruct(shape, dtype)


def call(kernel, outs, specs, flops, nbytes, scratch=(), vmem=48):
    return pl.pallas_call(
        kernel,
        out_shape=outs,
        in_specs=specs,
        out_specs=[VM] * len(outs),
        scratch_shapes=list(scratch),
        compiler_params=pltpu.CompilerParams(vmem_limit_bytes=vmem * MIB),
        cost_estimate=pl.CostEstimate(flops=flops, bytes_accessed=nbytes, transcendentals=0),
    )


def row_length(rows):
    return jnp.sqrt(jnp.sum(rows * rows, axis=-1, keepdims=True) + 1e-06)


def project(grad, unit, length):
    inner = jnp.sum(unit * grad, axis=-1, keepdims=True)
    return (grad - unit * inner) / length


def prepare_kernel(img, w, n_img, w_half):
    w_half[...] = w[...].astype(BF)
    rows = img[...].astype(F32)
    n_img[...] = (rows / row_length(rows)).astype(BF)


def text_kernel(at, txt, txt_far, *refs):
    pieces, (w_full, z, n_txt, wide) = refs[:16], refs[16:]
    yhi, x, core = at[0], at[1], at[2]
    for flip_core in range(2):
        for flip_y in range(2):
            for back in range(4):
                y_of = yhi if flip_y == 0 else 1 - yhi
                c_of = core if flip_core == 0 else 1 - core
                owner = y_of * 8 + ((x + 4 - back) % 4) * 2 + c_of
                piece = pieces[flip_core * 8 + flip_y * 4 + back]
                start = pl.multiple_of(owner * 72, 8)
                wide[pl.ds(start, 72), :] = piece[...].astype(F32)
    w_full[...] = wide[...].astype(BF)
    head = w_full[...]
    for half, rows in enumerate((txt, txt_far)):
        out = jnp.dot(rows[...], head, preferred_element_type=F32)
        z[half] = out
        n_txt[half] = (out / row_length(out)).astype(BF)


def tile(scal, img_blk, txt_blk, diagonal):
    logits = scal[0] * lax.dot_general(
        img_blk, txt_blk, (((1,), (1,)), ((), ())), preferred_element_type=F32
    ) + scal[1]
    grad = jax.nn.sigmoid(logits)
    if diagonal:
        row_ids = lax.broadcasted_iota(jnp.int32, logits.shape, 0)
        col_ids = lax.broadcasted_iota(jnp.int32, logits.shape, 1)
        grad = grad - jnp.where(row_ids == col_ids, 1.0, 0.0)
    grad = grad.astype(BF)
    part = scal[0] * jnp.dot(grad, txt_blk, preferred_element_type=F32)
    back = lax.dot_general(
        grad, img_blk, (((0,), (0,)), ((), ())), preferred_element_type=F32
    )
    return part, back


def near_kernel(scal, n_own, n_a, n_b, n_txt, part_own, part_a, part_b, acc):
    txt_blk = n_txt[...].reshape(640, 1152)
    for step, (img_blk, part_ref) in enumerate(
        ((n_own, part_own), (n_a, part_a), (n_b, part_b))
    ):
        part, back = tile(scal, img_blk[...], txt_blk, step == 0)
        part_ref[...] = part.astype(BF)
        if step == 0:
            acc[...] = back
        else:
            acc[...] += back


def far_kernel(scal, n_c, n_txt, acc, z, part_c, g_own, g_far, dz):
    txt_blk = n_txt[...].reshape(640, 1152)
    part, back = tile(scal, n_c[...], txt_blk, False)
    part_c[...] = part.astype(BF)
    for half, out in enumerate((g_own, g_far)):
        rows = pl.ds(half * 320, 320)
        grad = scal[0] * (acc[rows, :] + back[half * 320 : half * 320 + 320])
        out[...] = grad.astype(BF)
        z_rows = z[half]
        length = row_length(z_rows)
        dz[rows, :] = project(grad, z_rows / length, length).astype(BF)


def weight_kernel(at, txt, txt_far, dz, mine, other, wide):
    core = at[2]
    for k in range(3):
        cols = pl.ds(k * 384, 384)
        total = None
        for half, rows in enumerate((txt, txt_far)):
            term = lax.dot_general(
                rows[:, cols],
                dz[pl.ds(half * 320, 320), :],
                (((0,), (0,)), ((), ())),
                preferred_element_type=F32,
            )
            total = term if total is None else total + term
        wide[cols, :] = total
    for j in range(8):
        a = pl.multiple_of((2 * j + core) * 72, 8)
        b = pl.multiple_of((2 * j + 1 - core) * 72, 8)
        mine[j] = wide[pl.ds(a, 72), :].astype(BF)
        other[j] = wide[pl.ds(b, 72), :].astype(BF)


def core_sum_kernel(at, mine, got, *outs):
    x = at[1]
    for r in range(4):
        owner = (x + r) % 4
        for h in range(2):
            j = h * 4 + owner
            outs[r][h] = (mine[j].astype(F32) + got[j].astype(F32)).astype(BF)


def x_sum_kernel(at, a, b, c, d, keep, send):
    yhi = at[0]
    for out, h in ((keep, yhi), (send, 1 - yhi)):
        total = (a[h].astype(F32) + b[h].astype(F32)) + (c[h].astype(F32) + d[h].astype(F32))
        out[...] = total.astype(BF)


def pair_sum_kernel(a, b, out):
    out[...] = (a[...].astype(F32) + b[...].astype(F32)).astype(BF)


def z_sum_kernel(a, b, c, d, out):
    out[...] = (a[...].astype(F32) + b[...].astype(F32)) + (c[...].astype(F32) + d[...].astype(F32))


def image_out_kernel(img, a, b, c, d, out):
    rows = img[...].astype(F32)
    length = row_length(rows)
    grad = (a[...].astype(F32) + b[...].astype(F32)) + (c[...].astype(F32) + d[...].astype(F32))
    out[...] = project(grad, rows / length, length).astype(BF)


def text_out_kernel(z, a, b, w_full, out):
    rows = z[0]
    length = row_length(rows)
    grad = a[...].astype(F32) + b[...].astype(F32)
    dz = project(grad, rows / length, length).astype(BF)
    out[...] = lax.dot_general(
        dz, w_full[...], (((1,), (1,)), ((), ())), preferred_element_type=F32
    ).astype(BF)


def on_device(img_emb, txt_feat, w_txt, t_log, bias):
    img, txt = img_emb[0], txt_feat[0]
    at = jnp.stack([lax.axis_index("yhi"), lax.axis_index("x"), lax.axis_index("core")]).astype(jnp.int32)
    scal = jnp.concatenate([jnp.exp(t_log), bias])
    block = shaped((320, 1152), BF)
    mac = 2 * 320 * 1152

    txt_far = shift(txt, "ylo", 1)
    n_img, w_half = call(
        prepare_kernel, [block, shaped((72, 1152), BF)], [VM] * 2, mac, 2 * MIB
    )(img, w_txt)

    w_y = swap_far(w_half)
    own = [w_half] + [shift(w_half, "x", s) for s in (1, 2, 3)]
    own += [w_y] + [shift(w_y, "x", s) for s in (1, 2, 3)]
    cross = [shift(p, "core", 1) for p in own]
    n_a = shift(n_img, "z", 1)
    n_b = shift(n_img, "z", -1)
    n_c = shift(n_img, "z", 2)

    w_full, z, n_txt = call(
        text_kernel,
        [shaped((1152, 1152), BF), shaped((2, 320, 1152), F32), shaped((2, 320, 1152), BF)],
        [SM] + [VM] * 18,
        640 * 1152 * 1152 * 2,
        10 * MIB,
        [pltpu.VMEM((1152, 1152), F32)],
    )(at, txt, txt_far, *own, *cross)

    part_own, part_a, part_b, acc = call(
        near_kernel,
        [block, block, block, shaped((640, 1152), F32)],
        [SM] + [VM] * 4,
        3 * 3 * 640 * mac,
        10 * MIB,
    )(scal, n_img, n_a, n_b, n_txt)
    got_a = shift(part_a, "z", -1)
    got_b = shift(part_b, "z", 1)

    part_c, g_own, g_far, dz = call(
        far_kernel,
        [block, block, block, shaped((640, 1152), BF)],
        [SM] + [VM] * 4,
        3 * 640 * mac,
        10 * MIB,
    )(scal, n_c, n_txt, acc, z)
    got_c = shift(part_c, "z", 2)
    g_got = shift(g_far, "ylo", 1)

    eight = shaped((8, 72, 1152), BF)
    mine, other = call(
        weight_kernel,
        [eight, eight],
        [SM] + [VM] * 3,
        640 * 1152 * 1152 * 2,
        6 * MIB,
        [pltpu.VMEM((1152, 1152), F32)],
    )(at, txt, txt_far, dz)
    got_core = shift(other, "core", 1)
    two = shaped((2, 72, 1152), BF)
    rel = call(core_sum_kernel, [two] * 4, [SM, VM, VM], MIB, 4 * MIB)(at, mine, got_core)
    x_got = [shift(rel[s], "x", s) for s in (1, 2, 3)]
    one = shaped((72, 1152), BF)
    keep, send = call(x_sum_kernel, [one, one], [SM] + [VM] * 4, MIB, 2 * MIB)(at, rel[0], *x_got)
    (pair,) = call(pair_sum_kernel, [one], [VM] * 2, MIB, MIB)(keep, swap_far(send))
    (quad,) = call(pair_sum_kernel, [one], [VM] * 2, MIB, MIB)(pair, shift(pair, "ylo", 1))
    (d_weight,) = call(z_sum_kernel, [shaped((72, 1152), F32)], [VM] * 4, MIB, MIB)(
        quad, shift(quad, "z", 2), shift(quad, "z", 1), shift(quad, "z", -1)
    )

    (d_img,) = call(image_out_kernel, [block], [VM] * 5, 10 * mac, 4 * MIB)(
        img, part_own, got_c, got_a, got_b
    )
    (d_feat,) = call(text_out_kernel, [block], [VM] * 4, 1152 * mac, 6 * MIB)(
        z, g_own, g_got, w_full
    )
    return (d_img[None], d_feat[None], d_weight)


def solution(mesh):
    fine = Mesh(mesh.devices.reshape(2, 4, 2, 4, 2), tuple(AXES))
    dp, fsdp = ("ylo", "z"), ("yhi", "x", "core")
    placed = (P(fsdp, dp, None), P(fsdp, dp, None), P(fsdp, None), P(), P())
    return jax.shard_map(
        on_device,
        mesh=fine,
        in_specs=placed,
        out_specs=(P(fsdp, dp, None), P(fsdp, dp, None), P(fsdp, None)),
        check_vma=False,
    )
```

time: 443 us -> 139 us (0.31)
  waiting for transfers between devices: 333 us -> 45.4 us
  matrix products: 78.9 us -> 0 us
  starting transfers between devices: 0.34 us -> 36.4 us
  Pallas kernels: 0 us -> 33.6 us
  local copies, waits for them, and re-layouts: 3.82 us -> 20.6 us
  between operations: 15.2 us -> 2.14 us
  other arithmetic: 9.61 us -> 0.15 us
    all_gather x3 -> x0, waiting for transfers between devices: 183 us -> none  [the longest x1 65.9 us: on_device(): other_txt = lax.all_gather(n_txt, 'dp', axis=0, tiled=True)]
    psum x1 -> x0, waiting for transfers between devices: 150 us -> none  [on_device(): summed = lax.psum(weight_term, ('dp', 'fsdp'))]
    dot_general x19 -> x0, matrix products: 78.9 us -> none  [the longest x8 35.5 us: text_side(): lax.dot_general(grad_logit, img_a, (((0,), (0,)), ((), ())), preferred_el...]
    ppermute x0 -> x32, waiting for transfers between devices: none -> 45.4 us  [the longest x30 38.9 us: shift(): return lax.ppermute(value, axis, [(i, (i + step) % n) for i in range(n)])]
    ppermute x0 -> x32, starting transfers between devices: none -> 36.4 us  [the longest x30 33.1 us: shift(): return lax.ppermute(value, axis, [(i, (i + step) % n) for i in range(n)])]
    pallas_call x0 -> x12, Pallas kernels: none -> 33.6 us  [the longest x1 9.37 us: on_device(): call(near_kernel, [block, block, block, shaped((640, 1152), F32)], [SM] +...]
    unnamed x11 -> x56, local copies, waits for them, and re-layouts: 2.33 us -> 20.6 us
    convert_element_type x4 -> x0, other arithmetic: 5.65 us -> none  [the longest x2 2.22 us: normalize(): return (unit_rows, length, unit_rows.astype(jnp.bfloat16))]
  transfers between devices with their start and end apart: 4 -> 32, of which waited for: 4 -> 12; matrix products, arithmetic and copies ran while one was open for 3% -> 0% of each run, Pallas kernels for 0% -> 16%
where the time goes in v1:
time: 139 us; the launch traced here: 138 us
  waiting for transfers between devices  45.4 us (33%)
  starting transfers between devices  36.4 us (26%)
  Pallas kernels  33.6 us (24%)
  local copies, waits for them, and re-layouts  20.6 us (15%)
  between operations  2.14 us (2%)
    ppermute x30, waiting for transfers between devices, shift(): return lax.ppermute(value, axis, [(i, (i + step) % n) for i in range(n)])  38.9 us
    ppermute x30, starting transfers between devices, shift(): return lax.ppermute(value, axis, [(i, (i + step) % n) for i in range(n)])  33.1 us
    unnamed x56, local copies, waits for them, and re-layouts  20.6 us
    pallas_call x1, Pallas kernels, on_device(): call(near_kernel, [block, block, block, shaped((640, 1152), F32)], [SM] +...  9.37 us
    ppermute x2, waiting for transfers between devices, swap_far(): return lax.ppermute(value, ('ylo', 'yhi'), pairs)  6.54 us
    pallas_call x1, Pallas kernels, on_device(): call(far_kernel, [block, block, block, shaped((640, 1152), BF)], [SM] + [...  5.79 us
    pallas_call x1, Pallas kernels, on_device(): call(text_kernel, [shaped((1152, 1152), BF), shaped((2, 320, 1152), F32),...  5.35 us
    pallas_call x1, Pallas kernels, on_device(): call(text_out_kernel, [block], [VM] * 4, 1152 * mac, 6 * MIB)  4.41 us
  transfers between devices with their start and end apart: 32, of which 12 were waited for; matrix products, arithmetic and copies ran while one was open for 0% of the time, Pallas kernels for 16%

profile of v1, /device:TPU:0, one launch (start us, length us, event | category | flops | bytes accessed | tf_op | source)
XLA Modules:
  0.0 138.3 jit_solution(12061225101060292582)
XLA Ops:
  0.6 1.1 copy-done
  1.8 1.0 copy-done.3
  3.0 3.2 %collective-permute-start.6 = (bf16[72,1152]{1,0:T(8,128)(2,1)S(1)}, bf16[72,1152]{1,0:T(8,128)(2,1)S(1)}, u32[]{:S(2)}, u32[]{:S(2)}) collective-permute-start(bf16[72,1152]{1,0:T(8,128)(2,1)S(1)} %get-tuple-element.25.refs_0_), channel_id=1, source_target_pairs={{0,72},{8,64},{64,8},{72,0},{1,73},{9,65},{65,9},{73,1},{2,74},{10... | collective-permute-start | bytes 497672 | tf_op jit(solution)/shard_map/ppermute | solution.py:24
  6.2 2.8 %collective-permute-start.5 = (bf16[72,1152]{1,0:T(8,128)(2,1)S(1)}, bf16[72,1152]{1,0:T(8,128)(2,1)S(1)}, u32[]{:S(2)}, u32[]{:S(2)}) collective-permute-start(bf16[72,1152]{1,0:T(8,128)(2,1)S(1)} %get-tuple-element.25.refs_0_), channel_id=1, source_target_pairs={{0,6},{2,0},{4,2},{6,4},{1,7},{3,1},{5,3},{7,5},{8,14},{10,8},{12,... | collective-permute-start | bytes 497672 | tf_op jit(solution)/shard_map/ppermute | solution.py:19
  9.0 0.8 collective-permute-start.4
  9.8 0.9 collective-permute-start.3
  10.7 2.5 %collective-permute-start.9 = (bf16[72,1152]{1,0:T(8,128)(2,1)S(1)}, bf16[72,1152]{1,0:T(8,128)(2,1)S(1)}, u32[]{:S(2)}, u32[]{:S(2)}) collective-permute-start(bf16[72,1152]{1,0:T(8,128)(2,1)S(1)} %collective-permute-done.6.refs_4_), channel_id=1, source_target_pairs={{0,6},{2,0},{4,2},{6,4},{1,7},{3,1},{5,3},{7,5},{8,14},{10,8},{12,... | collective-permute-start | bytes 497672 | tf_op jit(solution)/shard_map/ppermute | solution.py:19
  13.2 3.7 %collective-permute-done.5.refs_3_ = bf16[72,1152]{1,0:T(8,128)(2,1)S(1)} collective-permute-done((bf16[72,1152]{1,0:T(8,128)(2,1)S(1)}, bf16[72,1152]{1,0:T(8,128)(2,1)S(1)}, u32[]{:S(2)}, u32[]{:S(2)}) %collective-permute-start.5) | collective-permute-done | bytes 165920 | tf_op jit(solution)/shard_map/ppermute | solution.py:19
  17.7 2.7 %collective-permute-done.3.refs_1_ = bf16[72,1152]{1,0:T(8,128)(2,1)S(1)} collective-permute-done((bf16[72,1152]{1,0:T(8,128)(2,1)S(1)}, bf16[72,1152]{1,0:T(8,128)(2,1)S(1)}, u32[]{:S(2)}, u32[]{:S(2)}) %collective-permute-start.3) | collective-permute-done | bytes 165920 | tf_op jit(solution)/shard_map/ppermute | solution.py:19
  20.4 1.4 collective-permute-start.7
  21.8 0.7 copy-done.12
  23.1 4.0 %collective-permute-start.1 = (bf16[320,1152]{1,0:T(8,128)(2,1)S(1)}, bf16[320,1152]{1,0:T(8,128)(2,1)S(1)}, u32[]{:S(2)}, u32[]{:S(2)}) collective-permute-start(bf16[320,1152]{1,0:T(8,128)(2,1)S(1)} %get-tuple-element.24.n_own), channel_id=1, source_target_pairs={{0,48},{16,0},{32,16},{48,32},{1,49},{17,1},{33,17},{49,33},{2,50}... | collective-permute-start | bytes 2211848 | tf_op jit(solution)/shard_map/ppermute | solution.py:19
  27.5 1.1 collective-permute-done.7.refs_5_
  36.2 3.9 %collective-permute-start.18 = (bf16[320,1152]{1,0:T(8,128)(2,1)S(1)}, bf16[320,1152]{1,0:T(8,128)(2,1)S(1)}, u32[]{:S(2)}, u32[]{:S(2)}) collective-permute-start(bf16[320,1152]{1,0:T(8,128)(2,1)S(1)} %get-tuple-element.24.n_own), channel_id=1, source_target_pairs={{0,32},{16,48},{32,0},{48,16},{1,33},{17,49},{33,1},{49,17},{2,34}... | collective-permute-start | bytes 2211848 | tf_op jit(solution)/shard_map/ppermute | solution.py:19
  40.9 1.6 %collective-permute-done.15.refs_13_ = bf16[72,1152]{1,0:T(8,128)(2,1)} collective-permute-done((bf16[72,1152]{1,0:T(8,128)(2,1)}, bf16[72,1152]{1,0:T(8,128)(2,1)}, u32[]{:S(2)}, u32[]{:S(2)}) %collective-permute-start.15) | collective-permute-done | bytes 165920 | tf_op jit(solution)/shard_map/ppermute | solution.py:19
  42.5 1.1 copy-done.4
  43.6 0.9 copy-done.7
  44.6 0.9 copy-done.9
  45.5 0.9 copy-done.11
  46.4 0.9 copy-done.13
  47.3 0.9 copy-done.15
  48.2 0.9 copy-done.17
  49.1 0.9 copy-done.19
  50.1 0.9 copy-done.21
  51.0 0.9 copy-done.23
  51.9 0.9 copy-done.25
  52.8 0.9 copy-done.27
  53.7 5.3 %shard_map.77 = (bf16[1152,1152]{1,0:T(8,128)(2,1)}, f32[2,320,1152]{2,1,0:T(8,128)}, bf16[2,320,1152]{2,1,0:T(8,128)(2,1)S(1)}) custom-call(s32[3]{0:T(128)S(1)} %pad_add_fusion.at, bf16[320,1152]{1,0:T(8,128)(2,1)S(1)} %bitcast.10, bf16[320,1152]{1,0:T(8,128)(2,1)S(1)} %collective-permute-done.2.txt_far, bf16[72,1152]{1,0:T(8,128)(2,1)S(1)} %get-tuple-element.25.refs_0_, ...), custom_call_target="tpu_custom_call" | custom-call | flops 1698693120 | bytes 10485760 | tf_op jit(solution)/shard_map/pallas_call | solution.py:203
  59.4 3.5 %collective-permute-done.n_a = bf16[320,1152]{1,0:T(8,128)(2,1)} collective-permute-done((bf16[320,1152]{1,0:T(8,128)(2,1)S(1)}, bf16[320,1152]{1,0:T(8,128)(2,1)}, u32[]{:S(2)}, u32[]{:S(2)}) %collective-permute-start) | collective-permute-done | bytes 737312 | tf_op jit(solution)/shard_map/ppermute | solution.py:19
  62.9 9.4 %shard_map.78 = (bf16[320,1152]{1,0:T(8,128)(2,1)S(1)}, bf16[320,1152]{1,0:T(8,128)(2,1)}, bf16[320,1152]{1,0:T(8,128)(2,1)S(1)}, f32[640,1152]{1,0:T(8,128)}) custom-call(f32[2]{0:T(128)S(1)} %pad_maximum_fusion.scal, bf16[320,1152]{1,0:T(8,128)(2,1)S(1)} %get-tuple-element.24.n_own, bf16[320,1152]{1,0:T(8,128)(2,1)} %collective-permute-done.n_a, ...), custom_call_target="tpu_custom_call" | custom-call | flops 4246732800 | bytes 10485760 | tf_op jit(solution)/shard_map/pallas_call | solution.py:212
  72.3 5.8 %shard_map.79 = (bf16[320,1152]{1,0:T(8,128)(2,1)S(1)}, bf16[320,1152]{1,0:T(8,128)(2,1)S(1)}, bf16[320,1152]{1,0:T(8,128)(2,1)S(1)}, bf16[640,1152]{1,0:T(8,128)(2,1)S(1)}) custom-call(f32[2]{0:T(128)S(1)} %pad_maximum_fusion.scal, bf16[320,1152]{1,0:T(8,128)(2,1)S(1)} %collective-permute-done.18.n_c, bf16[2,320,1152]{2,1,0:T(8,128)(2,1)S(1)} %get-tuple-element.26.n_txt, ...), custom_call_target="tpu_custom_call" | custom-call | flops 1415577600 | bytes 10485760 | tf_op jit(solution)/shard_map/pallas_call | solution.py:222
  78.1 4.1 %shard_map.82 = (bf16[8,72,1152]{2,1,0:T(8,128)(2,1)S(1)}, bf16[8,72,1152]{2,1,0:T(8,128)(2,1)S(1)}) custom-call(s32[3]{0:T(128)S(1)} %pad_add_fusion.at, bf16[320,1152]{1,0:T(8,128)(2,1)S(1)} %bitcast.11, bf16[320,1152]{1,0:T(8,128)(2,1)S(1)} %collective-permute-done.2.txt_far, bf16[640,1152]{1,0:T(8,128)(2,1)S(1)} %get-tuple-element.36.dz), custom_call_target="tpu_custom_call" | custom-call | flops 1698693120 | bytes 6291456 | tf_op jit(solution)/shard_map/pallas_call | solution.py:233
  82.3 3.0 %collective-permute-done.23.got = bf16[8,72,1152]{2,1,0:T(8,128)(2,1)S(1)} collective-permute-done((bf16[8,72,1152]{2,1,0:T(8,128)(2,1)S(1)}, bf16[8,72,1152]{2,1,0:T(8,128)(2,1)S(1)}, u32[]{:S(2)}, u32[]{:S(2)}) %collective-permute-start.23) | collective-permute-done | bytes 1327136 | tf_op jit(solution)/shard_map/ppermute | solution.py:19
  85.4 0.9 shard_map.83
  86.3 3.3 %collective-permute-start.25 = (bf16[2,72,1152]{2,1,0:T(8,128)(2,1)S(1)}, bf16[2,72,1152]{2,1,0:T(8,128)(2,1)S(1)}, u32[]{:S(2)}, u32[]{:S(2)}) collective-permute-start(bf16[2,72,1152]{2,1,0:T(8,128)(2,1)S(1)} %get-tuple-element.41), channel_id=1, source_target_pairs={{0,4},{2,6},{4,0},{6,2},{1,5},{3,7},{5,1},{7,3},{8,12},{10,14},{12... | collective-permute-start | bytes 995336 | tf_op jit(solution)/shard_map/ppermute | solution.py:19
  89.8 1.9 %collective-permute-start.21 = (bf16[320,1152]{1,0:T(8,128)(2,1)S(1)}, bf16[320,1152]{1,0:T(8,128)(2,1)S(1)}, u32[]{:S(2)}, u32[]{:S(2)}) collective-permute-start(bf16[320,1152]{1,0:T(8,128)(2,1)S(1)} %get-tuple-element.32), channel_id=1, source_target_pairs={{0,16},{16,32},{32,48},{48,0},{1,17},{17,33},{33,49},{49,1},{2,18}... | collective-permute-start | bytes 2211848 | tf_op jit(solution)/shard_map/ppermute | solution.py:19
  91.7 6.4 %collective-permute-done.24.b = bf16[2,72,1152]{2,1,0:T(8,128)(2,1)S(1)} collective-permute-done((bf16[2,72,1152]{2,1,0:T(8,128)(2,1)S(1)}, bf16[2,72,1152]{2,1,0:T(8,128)(2,1)S(1)}, u32[]{:S(2)}, u32[]{:S(2)}) %collective-permute-start.24) | collective-permute-done | bytes 331808 | tf_op jit(solution)/shard_map/ppermute | solution.py:19
  98.1 2.6 %collective-permute-start.19 = (bf16[320,1152]{1,0:T(8,128)(2,1)S(1)}, bf16[320,1152]{1,0:T(8,128)(2,1)S(1)}, u32[]{:S(2)}, u32[]{:S(2)}) collective-permute-start(bf16[320,1152]{1,0:T(8,128)(2,1)S(1)} %get-tuple-element.30), channel_id=1, source_target_pairs={{0,32},{16,48},{32,0},{48,16},{1,33},{17,49},{33,1},{49,17},{2,34}... | collective-permute-start | bytes 2211848 | tf_op jit(solution)/shard_map/ppermute | solution.py:19
  100.7 3.9 %collective-permute-done.25.c = bf16[2,72,1152]{2,1,0:T(8,128)(2,1)S(1)} collective-permute-done((bf16[2,72,1152]{2,1,0:T(8,128)(2,1)S(1)}, bf16[2,72,1152]{2,1,0:T(8,128)(2,1)S(1)}, u32[]{:S(2)}, u32[]{:S(2)}) %collective-permute-start.25) | collective-permute-done | bytes 331808 | tf_op jit(solution)/shard_map/ppermute | solution.py:19
  104.6 1.8 %collective-permute-start.22 = (bf16[320,1152]{1,0:T(8,128)(2,1)S(1)}, bf16[320,1152]{1,0:T(8,128)(2,1)S(1)}, u32[]{:S(2)}, u32[]{:S(2)}) collective-permute-start(bf16[320,1152]{1,0:T(8,128)(2,1)S(1)} %get-tuple-element.34), channel_id=1, source_target_pairs={{0,64},{64,0},{1,65},{65,1},{2,66},{66,2},{3,67},{67,3},{4,68},{68... | collective-permute-start | bytes 2211848 | tf_op jit(solution)/shard_map/ppermute | solution.py:19
  106.4 0.7 shard_map.84
  107.2 6.5 %collective-permute-done.27.b = bf16[72,1152]{1,0:T(8,128)(2,1)S(1)} collective-permute-done((bf16[72,1152]{1,0:T(8,128)(2,1)S(1)}, bf16[72,1152]{1,0:T(8,128)(2,1)S(1)}, u32[]{:S(2)}, u32[]{:S(2)}) %collective-permute-start.27) | collective-permute-done | bytes 165920 | tf_op jit(solution)/shard_map/ppermute | solution.py:24
  113.9 12.0 %collective-permute-done.28.b = bf16[72,1152]{1,0:T(8,128)(2,1)S(1)} collective-permute-done((bf16[72,1152]{1,0:T(8,128)(2,1)S(1)}, bf16[72,1152]{1,0:T(8,128)(2,1)S(1)}, u32[]{:S(2)}, u32[]{:S(2)}) %collective-permute-start.28) | collective-permute-done | bytes 165920 | tf_op jit(solution)/shard_map/ppermute | solution.py:19
  126.2 1.9 %collective-permute-start.30 = (bf16[72,1152]{1,0:T(8,128)(2,1)S(1)}, bf16[72,1152]{1,0:T(8,128)(2,1)S(1)}, u32[]{:S(2)}, u32[]{:S(2)}) collective-permute-start(bf16[72,1152]{1,0:T(8,128)(2,1)S(1)} %shard_map.86.a), channel_id=1, source_target_pairs={{0,16},{16,32},{32,48},{48,0},{1,17},{17,33},{33,49},{49,1},{2,18}... | collective-permute-start | bytes 497672 | tf_op jit(solution)/shard_map/ppermute | solution.py:19
  128.0 3.2 %collective-permute-start.29 = (bf16[72,1152]{1,0:T(8,128)(2,1)S(1)}, bf16[72,1152]{1,0:T(8,128)(2,1)S(1)}, u32[]{:S(2)}, u32[]{:S(2)}) collective-permute-start(bf16[72,1152]{1,0:T(8,128)(2,1)S(1)} %shard_map.86.a), channel_id=1, source_target_pairs={{0,32},{16,48},{32,0},{48,16},{1,33},{17,49},{33,1},{49,17},{2,34}... | collective-permute-start | bytes 497672 | tf_op jit(solution)/shard_map/ppermute | solution.py:19
  131.3 1.8 %shard_map.80 = bf16[320,1152]{1,0:T(8,128)(2,1)} custom-call(bf16[320,1152]{1,0:T(8,128)(2,1)S(1)} %bitcast.8, bf16[320,1152]{1,0:T(8,128)(2,1)S(1)} %get-tuple-element.27.a, bf16[320,1152]{1,0:T(8,128)(2,1)S(1)} %collective-permute-done.19.b, bf16[320,1152]{1,0:T(8,128)(2,1)S(1)} %collective-permute-done.20.c, bf16[320,1152]{1,0:T(8,128)(2,1)S(1)} %collective-permute-done.21.d), custom_call_target="tpu_custom_call" | custom-call | flops 7372800 | bytes 4194304 | tf_op jit(solution)/shard_map/pallas_call | solution.py:253
  133.1 4.4 %shard_map.81 = bf16[320,1152]{1,0:T(8,128)(2,1)} custom-call(f32[2,320,1152]{2,1,0:T(8,128)} %get-tuple-element.29.z, bf16[320,1152]{1,0:T(8,128)(2,1)S(1)} %get-tuple-element.33.a, bf16[320,1152]{1,0:T(8,128)(2,1)S(1)} %collective-permute-done.22.b, bf16[1152,1152]{1,0:T(8,128)(2,1)S(1)} %copy-done.2), custom_call_target="tpu_custom_call" | custom-call | flops 849346560 | bytes 6291456 | tf_op jit(solution)/shard_map/pallas_call | solution.py:256
  137.5 0.8 shard_map.87
  (86 shorter events, 10.4 us)
Async XLA Ops:
  0.6 1.1 copy-start
  1.7 1.0 copy-start.3
  3.0 7.6 %collective-permute-start.6 = (bf16[72,1152]{1,0:T(8,128)(2,1)S(1)}, bf16[72,1152]{1,0:T(8,128)(2,1)S(1)}, u32[]{:S(2)}, u32[]{:S(2)}) collective-permute-start(bf16[72,1152]{1,0:T(8,128)(2,1)S(1)} %get-tuple-element.25.refs_0_), channel_id=1, source_target_pairs={{0,72},{8,64},{64,8},{72,0},{1,73},{9,65},{65,9},{73,1},{2,74},{10... | collective-permute-start | bytes 497672 | tf_op jit(solution)/shard_map/ppermute | solution.py:24
  6.2 4.5 %collective-permute-start.10 = (bf16[72,1152]{1,0:T(8,128)(2,1)S(1)}, bf16[72,1152]{1,0:T(8,128)(2,1)S(1)}, u32[]{:S(2)}, u32[]{:S(2)}) collective-permute-start(bf16[72,1152]{1,0:T(8,128)(2,1)S(1)} %get-tuple-element.25.refs_0_), channel_id=1, source_target_pairs={{0,1},{1,0},{2,3},{3,2},{4,5},{5,4},{6,7},{7,6},{8,9},{9,8},{10,11... | collective-permute-start | bytes 497672 | tf_op jit(solution)/shard_map/ppermute | solution.py:19
  6.2 10.7 %collective-permute-start.5 = (bf16[72,1152]{1,0:T(8,128)(2,1)S(1)}, bf16[72,1152]{1,0:T(8,128)(2,1)S(1)}, u32[]{:S(2)}, u32[]{:S(2)}) collective-permute-start(bf16[72,1152]{1,0:T(8,128)(2,1)S(1)} %get-tuple-element.25.refs_0_), channel_id=1, source_target_pairs={{0,6},{2,0},{4,2},{6,4},{1,7},{3,1},{5,3},{7,5},{8,14},{10,8},{12,... | collective-permute-start | bytes 497672 | tf_op jit(solution)/shard_map/ppermute | solution.py:19
  9.0 8.6 %collective-permute-start.4 = (bf16[72,1152]{1,0:T(8,128)(2,1)S(1)}, bf16[72,1152]{1,0:T(8,128)(2,1)S(1)}, u32[]{:S(2)}, u32[]{:S(2)}) collective-permute-start(bf16[72,1152]{1,0:T(8,128)(2,1)S(1)} %get-tuple-element.25.refs_0_), channel_id=1, source_target_pairs={{0,4},{2,6},{4,0},{6,2},{1,5},{3,7},{5,1},{7,3},{8,12},{10,14},{12... | collective-permute-start | bytes 497672 | tf_op jit(solution)/shard_map/ppermute | solution.py:19
  9.8 10.6 %collective-permute-start.3 = (bf16[72,1152]{1,0:T(8,128)(2,1)S(1)}, bf16[72,1152]{1,0:T(8,128)(2,1)S(1)}, u32[]{:S(2)}, u32[]{:S(2)}) collective-permute-start(bf16[72,1152]{1,0:T(8,128)(2,1)S(1)} %get-tuple-element.25.refs_0_), channel_id=1, source_target_pairs={{0,2},{2,4},{4,6},{6,0},{1,3},{3,5},{5,7},{7,1},{8,10},{10,12},{12... | collective-permute-start | bytes 497672 | tf_op jit(solution)/shard_map/ppermute | solution.py:19
  10.6 11.1 %collective-permute-start.14 = (bf16[72,1152]{1,0:T(8,128)(2,1)S(1)}, bf16[72,1152]{1,0:T(8,128)(2,1)S(1)}, u32[]{:S(2)}, u32[]{:S(2)}) collective-permute-start(bf16[72,1152]{1,0:T(8,128)(2,1)S(1)} %collective-permute-done.6.refs_4_), channel_id=1, source_target_pairs={{0,1},{1,0},{2,3},{3,2},{4,5},{5,4},{6,7},{7,6},{8,9},{9,8},{10,11... | collective-permute-start | bytes 497672 | tf_op jit(solution)/shard_map/ppermute | solution.py:19
  10.7 12.5 %collective-permute-start.9 = (bf16[72,1152]{1,0:T(8,128)(2,1)S(1)}, bf16[72,1152]{1,0:T(8,128)(2,1)S(1)}, u32[]{:S(2)}, u32[]{:S(2)}) collective-permute-start(bf16[72,1152]{1,0:T(8,128)(2,1)S(1)} %collective-permute-done.6.refs_4_), channel_id=1, source_target_pairs={{0,6},{2,0},{4,2},{6,4},{1,7},{3,1},{5,3},{7,5},{8,14},{10,8},{12,... | collective-permute-start | bytes 497672 | tf_op jit(solution)/shard_map/ppermute | solution.py:19
  16.9 10.2 %collective-permute-start.8 = (bf16[72,1152]{1,0:T(8,128)(2,1)S(1)}, bf16[72,1152]{1,0:T(8,128)(2,1)S(1)}, u32[]{:S(2)}, u32[]{:S(2)}) collective-permute-start(bf16[72,1152]{1,0:T(8,128)(2,1)S(1)} %collective-permute-done.6.refs_4_), channel_id=1, source_target_pairs={{0,4},{2,6},{4,0},{6,2},{1,5},{3,7},{5,1},{7,3},{8,12},{10,14},{12... | collective-permute-start | bytes 497672 | tf_op jit(solution)/shard_map/ppermute | solution.py:19
  17.6 24.9 %collective-permute-start.2 = (bf16[320,1152]{1,0:T(8,128)(2,1)}, bf16[320,1152]{1,0:T(8,128)(2,1)S(1)}, u32[]{:S(2)}, u32[]{:S(2)}) collective-permute-start(bf16[320,1152]{1,0:T(8,128)(2,1)} %bitcast.9), channel_id=1, source_target_pairs={{0,64},{64,0},{1,65},{65,1},{2,66},{66,2},{3,67},{67,3},{4,68},{68... | collective-permute-start | bytes 2211848 | tf_op jit(solution)/shard_map/ppermute | solution.py:19
  20.4 8.1 %collective-permute-start.7 = (bf16[72,1152]{1,0:T(8,128)(2,1)S(1)}, bf16[72,1152]{1,0:T(8,128)(2,1)}, u32[]{:S(2)}, u32[]{:S(2)}) collective-permute-start(bf16[72,1152]{1,0:T(8,128)(2,1)S(1)} %collective-permute-done.6.refs_4_), channel_id=1, source_target_pairs={{0,2},{2,4},{4,6},{6,0},{1,3},{3,5},{5,7},{7,1},{8,10},{10,12},{12... | collective-permute-start | bytes 497672 | tf_op jit(solution)/shard_map/ppermute | solution.py:19
  22.4 6.8 %collective-permute-start.13 = (bf16[72,1152]{1,0:T(8,128)(2,1)S(1)}, bf16[72,1152]{1,0:T(8,128)(2,1)S(1)}, u32[]{:S(2)}, u32[]{:S(2)}) collective-permute-start(bf16[72,1152]{1,0:T(8,128)(2,1)S(1)} %collective-permute-done.5.refs_3_), channel_id=1, source_target_pairs={{0,1},{1,0},{2,3},{3,2},{4,5},{5,4},{6,7},{7,6},{8,9},{9,8},{10,11... | collective-permute-start | bytes 497672 | tf_op jit(solution)/shard_map/ppermute | solution.py:19
  23.1 36.3 %collective-permute-start.1 = (bf16[320,1152]{1,0:T(8,128)(2,1)S(1)}, bf16[320,1152]{1,0:T(8,128)(2,1)S(1)}, u32[]{:S(2)}, u32[]{:S(2)}) collective-permute-start(bf16[320,1152]{1,0:T(8,128)(2,1)S(1)} %get-tuple-element.24.n_own), channel_id=1, source_target_pairs={{0,48},{16,0},{32,16},{48,32},{1,49},{17,1},{33,17},{49,33},{2,50}... | collective-permute-start | bytes 2211848 | tf_op jit(solution)/shard_map/ppermute | solution.py:19
  27.2 35.7 %collective-permute-start = (bf16[320,1152]{1,0:T(8,128)(2,1)S(1)}, bf16[320,1152]{1,0:T(8,128)(2,1)}, u32[]{:S(2)}, u32[]{:S(2)}) collective-permute-start(bf16[320,1152]{1,0:T(8,128)(2,1)S(1)} %get-tuple-element.24.n_own), channel_id=1, source_target_pairs={{0,16},{16,32},{32,48},{48,0},{1,17},{17,33},{33,49},{49,1},{2,18}... | collective-permute-start | bytes 2211848 | tf_op jit(solution)/shard_map/ppermute | solution.py:19
  28.5 2.5 %collective-permute-start.12 = (bf16[72,1152]{1,0:T(8,128)(2,1)S(1)}, bf16[72,1152]{1,0:T(8,128)(2,1)S(1)}, u32[]{:S(2)}, u32[]{:S(2)}) collective-permute-start(bf16[72,1152]{1,0:T(8,128)(2,1)S(1)} %collective-permute-done.4.refs_2_), channel_id=1, source_target_pairs={{0,1},{1,0},{2,3},{3,2},{4,5},{5,4},{6,7},{7,6},{8,9},{9,8},{10,11... | collective-permute-start | bytes 497672 | tf_op jit(solution)/shard_map/ppermute | solution.py:19
  29.9 2.5 %collective-permute-start.11 = (bf16[72,1152]{1,0:T(8,128)(2,1)S(1)}, bf16[72,1152]{1,0:T(8,128)(2,1)S(1)}, u32[]{:S(2)}, u32[]{:S(2)}) collective-permute-start(bf16[72,1152]{1,0:T(8,128)(2,1)S(1)} %collective-permute-done.3.refs_1_), channel_id=1, source_target_pairs={{0,1},{1,0},{2,3},{3,2},{4,5},{5,4},{6,7},{7,6},{8,9},{9,8},{10,11... | collective-permute-start | bytes 497672 | tf_op jit(solution)/shard_map/ppermute | solution.py:19
  31.7 3.8 %collective-permute-start.17 = (bf16[72,1152]{1,0:T(8,128)(2,1)S(1)}, bf16[72,1152]{1,0:T(8,128)(2,1)S(1)}, u32[]{:S(2)}, u32[]{:S(2)}) collective-permute-start(bf16[72,1152]{1,0:T(8,128)(2,1)S(1)} %collective-permute-done.9.refs_7_), channel_id=1, source_target_pairs={{0,1},{1,0},{2,3},{3,2},{4,5},{5,4},{6,7},{7,6},{8,9},{9,8},{10,11... | collective-permute-start | bytes 497672 | tf_op jit(solution)/shard_map/ppermute | solution.py:19
  33.1 7.1 %collective-permute-start.16 = (bf16[72,1152]{1,0:T(8,128)(2,1)S(1)}, bf16[72,1152]{1,0:T(8,128)(2,1)S(1)}, u32[]{:S(2)}, u32[]{:S(2)}) collective-permute-start(bf16[72,1152]{1,0:T(8,128)(2,1)S(1)} %collective-permute-done.8.refs_6_), channel_id=1, source_target_pairs={{0,1},{1,0},{2,3},{3,2},{4,5},{5,4},{6,7},{7,6},{8,9},{9,8},{10,11... | collective-permute-start | bytes 497672 | tf_op jit(solution)/shard_map/ppermute | solution.py:19
  36.2 36.0 %collective-permute-start.18 = (bf16[320,1152]{1,0:T(8,128)(2,1)S(1)}, bf16[320,1152]{1,0:T(8,128)(2,1)S(1)}, u32[]{:S(2)}, u32[]{:S(2)}) collective-permute-start(bf16[320,1152]{1,0:T(8,128)(2,1)S(1)} %get-tuple-element.24.n_own), channel_id=1, source_target_pairs={{0,32},{16,48},{32,0},{48,16},{1,33},{17,49},{33,1},{49,17},{2,34}... | collective-permute-start | bytes 2211848 | tf_op jit(solution)/shard_map/ppermute | solution.py:19
  40.8 1.7 %collective-permute-start.15 = (bf16[72,1152]{1,0:T(8,128)(2,1)}, bf16[72,1152]{1,0:T(8,128)(2,1)}, u32[]{:S(2)}, u32[]{:S(2)}) collective-permute-start(bf16[72,1152]{1,0:T(8,128)(2,1)} %collective-permute-done.7.refs_5_), channel_id=1, source_target_pairs={{0,1},{1,0},{2,3},{3,2},{4,5},{5,4},{6,7},{7,6},{8,9},{9,8},{10,11... | collective-permute-start | bytes 497672 | tf_op jit(solution)/shard_map/ppermute | solution.py:19
  42.5 1.1 copy-start.4
  43.6 0.9 copy-start.7
  44.6 0.9 copy-start.9
  45.5 0.9 copy-start.11
  46.4 0.9 copy-start.13
  47.3 0.9 copy-start.15
  48.2 0.9 copy-start.17
  49.1 0.9 copy-start.19
  51.0 0.9 copy-start.23
  51.9 0.9 copy-start.25
  52.8 0.9 copy-start.27
  72.3 5.8 %copy-start.5 = (bf16[1,320,1152]{2,1,0:T(8,128)(2,1)S(1)}, bf16[1,320,1152]{2,1,0:T(8,128)(2,1)}, u32[]{:S(2)}) copy-start(bf16[1,320,1152]{2,1,0:T(8,128)(2,1)} %param.6) | copy-start | bytes 2211844
  82.2 3.1 %collective-permute-start.23 = (bf16[8,72,1152]{2,1,0:T(8,128)(2,1)S(1)}, bf16[8,72,1152]{2,1,0:T(8,128)(2,1)S(1)}, u32[]{:S(2)}, u32[]{:S(2)}) collective-permute-start(bf16[8,72,1152]{2,1,0:T(8,128)(2,1)S(1)} %get-tuple-element.38), channel_id=1, source_target_pairs={{0,1},{1,0},{2,3},{3,2},{4,5},{5,4},{6,7},{7,6},{8,9},{9,8},{10,11... | collective-permute-start | bytes 3981320 | tf_op jit(solution)/shard_map/ppermute | solution.py:19
  86.2 45.1 %copy-start.1 = (bf16[1,320,1152]{2,1,0:T(8,128)(2,1)S(1)}, bf16[1,320,1152]{2,1,0:T(8,128)(2,1)}, u32[]{:S(2)}) copy-start(bf16[1,320,1152]{2,1,0:T(8,128)(2,1)} %param.5) | copy-start | bytes 2211844
  86.2 11.8 %collective-permute-start.24 = (bf16[2,72,1152]{2,1,0:T(8,128)(2,1)S(1)}, bf16[2,72,1152]{2,1,0:T(8,128)(2,1)S(1)}, u32[]{:S(2)}, u32[]{:S(2)}) collective-permute-start(bf16[2,72,1152]{2,1,0:T(8,128)(2,1)S(1)} %get-tuple-element.40), channel_id=1, source_target_pairs={{0,2},{2,4},{4,6},{6,0},{1,3},{3,5},{5,7},{7,1},{8,10},{10,12},{12... | collective-permute-start | bytes 995336 | tf_op jit(solution)/shard_map/ppermute | solution.py:19
  86.3 18.2 %collective-permute-start.25 = (bf16[2,72,1152]{2,1,0:T(8,128)(2,1)S(1)}, bf16[2,72,1152]{2,1,0:T(8,128)(2,1)S(1)}, u32[]{:S(2)}, u32[]{:S(2)}) collective-permute-start(bf16[2,72,1152]{2,1,0:T(8,128)(2,1)S(1)} %get-tuple-element.41), channel_id=1, source_target_pairs={{0,4},{2,6},{4,0},{6,2},{1,5},{3,7},{5,1},{7,3},{8,12},{10,14},{12... | collective-permute-start | bytes 995336 | tf_op jit(solution)/shard_map/ppermute | solution.py:19
  89.6 36.5 %collective-permute-start.20 = (bf16[320,1152]{1,0:T(8,128)(2,1)}, bf16[320,1152]{1,0:T(8,128)(2,1)S(1)}, u32[]{:S(2)}, u32[]{:S(2)}) collective-permute-start(bf16[320,1152]{1,0:T(8,128)(2,1)} %get-tuple-element.31), channel_id=1, source_target_pairs={{0,48},{16,0},{32,16},{48,32},{1,49},{17,1},{33,17},{49,33},{2,50}... | collective-permute-start | bytes 2211848 | tf_op jit(solution)/shard_map/ppermute | solution.py:19
  89.8 38.2 %collective-permute-start.21 = (bf16[320,1152]{1,0:T(8,128)(2,1)S(1)}, bf16[320,1152]{1,0:T(8,128)(2,1)S(1)}, u32[]{:S(2)}, u32[]{:S(2)}) collective-permute-start(bf16[320,1152]{1,0:T(8,128)(2,1)S(1)} %get-tuple-element.32), channel_id=1, source_target_pairs={{0,16},{16,32},{32,48},{48,0},{1,17},{17,33},{33,49},{49,1},{2,18}... | collective-permute-start | bytes 2211848 | tf_op jit(solution)/shard_map/ppermute | solution.py:19
  91.7 14.7 %collective-permute-start.26 = (bf16[2,72,1152]{2,1,0:T(8,128)(2,1)S(1)}, bf16[2,72,1152]{2,1,0:T(8,128)(2,1)S(1)}, u32[]{:S(2)}, u32[]{:S(2)}) collective-permute-start(bf16[2,72,1152]{2,1,0:T(8,128)(2,1)S(1)} %get-tuple-element.42), channel_id=1, source_target_pairs={{0,6},{2,0},{4,2},{6,4},{1,7},{3,1},{5,3},{7,5},{8,14},{10,8},{12,... | collective-permute-start | bytes 995336 | tf_op jit(solution)/shard_map/ppermute | solution.py:19
  98.1 33.2 %collective-permute-start.19 = (bf16[320,1152]{1,0:T(8,128)(2,1)S(1)}, bf16[320,1152]{1,0:T(8,128)(2,1)S(1)}, u32[]{:S(2)}, u32[]{:S(2)}) collective-permute-start(bf16[320,1152]{1,0:T(8,128)(2,1)S(1)} %get-tuple-element.30), channel_id=1, source_target_pairs={{0,32},{16,48},{32,0},{48,16},{1,33},{17,49},{33,1},{49,17},{2,34}... | collective-permute-start | bytes 2211848 | tf_op jit(solution)/shard_map/ppermute | solution.py:19
  104.6 28.5 %collective-permute-start.22 = (bf16[320,1152]{1,0:T(8,128)(2,1)S(1)}, bf16[320,1152]{1,0:T(8,128)(2,1)S(1)}, u32[]{:S(2)}, u32[]{:S(2)}) collective-permute-start(bf16[320,1152]{1,0:T(8,128)(2,1)S(1)} %get-tuple-element.34), channel_id=1, source_target_pairs={{0,64},{64,0},{1,65},{65,1},{2,66},{66,2},{3,67},{67,3},{4,68},{68... | collective-permute-start | bytes 2211848 | tf_op jit(solution)/shard_map/ppermute | solution.py:19
  107.1 6.6 %collective-permute-start.27 = (bf16[72,1152]{1,0:T(8,128)(2,1)S(1)}, bf16[72,1152]{1,0:T(8,128)(2,1)S(1)}, u32[]{:S(2)}, u32[]{:S(2)}) collective-permute-start(bf16[72,1152]{1,0:T(8,128)(2,1)S(1)} %get-tuple-element.44), channel_id=1, source_target_pairs={{0,72},{8,64},{64,8},{72,0},{1,73},{9,65},{65,9},{73,1},{2,74},{10... | collective-permute-start | bytes 497672 | tf_op jit(solution)/shard_map/ppermute | solution.py:24
  113.8 12.1 %collective-permute-start.28 = (bf16[72,1152]{1,0:T(8,128)(2,1)S(1)}, bf16[72,1152]{1,0:T(8,128)(2,1)S(1)}, u32[]{:S(2)}, u32[]{:S(2)}) collective-permute-start(bf16[72,1152]{1,0:T(8,128)(2,1)S(1)} %shard_map.85.a), channel_id=1, source_target_pairs={{0,64},{64,0},{1,65},{65,1},{2,66},{66,2},{3,67},{67,3},{4,68},{68... | collective-permute-start | bytes 497672 | tf_op jit(solution)/shard_map/ppermute | solution.py:19
  125.9 11.5 %collective-permute-start.31 = (bf16[72,1152]{1,0:T(8,128)(2,1)S(1)}, bf16[72,1152]{1,0:T(8,128)(2,1)S(1)}, u32[]{:S(2)}, u32[]{:S(2)}) collective-permute-start(bf16[72,1152]{1,0:T(8,128)(2,1)S(1)} %shard_map.86.a), channel_id=1, source_target_pairs={{0,48},{16,0},{32,16},{48,32},{1,49},{17,1},{33,17},{49,33},{2,50}... | collective-permute-start | bytes 497672 | tf_op jit(solution)/shard_map/ppermute | solution.py:19
  126.2 11.3 %collective-permute-start.30 = (bf16[72,1152]{1,0:T(8,128)(2,1)S(1)}, bf16[72,1152]{1,0:T(8,128)(2,1)S(1)}, u32[]{:S(2)}, u32[]{:S(2)}) collective-permute-start(bf16[72,1152]{1,0:T(8,128)(2,1)S(1)} %shard_map.86.a), channel_id=1, source_target_pairs={{0,16},{16,32},{32,48},{48,0},{1,17},{17,33},{33,49},{49,1},{2,18}... | collective-permute-start | bytes 497672 | tf_op jit(solution)/shard_map/ppermute | solution.py:19
  128.0 9.4 %collective-permute-start.29 = (bf16[72,1152]{1,0:T(8,128)(2,1)S(1)}, bf16[72,1152]{1,0:T(8,128)(2,1)S(1)}, u32[]{:S(2)}, u32[]{:S(2)}) collective-permute-start(bf16[72,1152]{1,0:T(8,128)(2,1)S(1)} %shard_map.86.a), channel_id=1, source_target_pairs={{0,32},{16,48},{32,0},{48,16},{1,33},{17,49},{33,1},{49,17},{2,34}... | collective-permute-start | bytes 497672 | tf_op jit(solution)/shard_map/ppermute | solution.py:19
  131.3 1.8 %copy-start.2 = (bf16[1152,1152]{1,0:T(8,128)(2,1)S(1)}, bf16[1152,1152]{1,0:T(8,128)(2,1)}, u32[]{:S(2)}) copy-start(bf16[1152,1152]{1,0:T(8,128)(2,1)} %get-tuple-element.35.w_full) | copy-start | bytes 7962628
  (12 other events, 8.2 us)

commit v2 on v0

v2 whole, which is shorter than its diff:
```python
import jax
import jax.numpy as jnp
from jax import lax
from jax.experimental import pallas as pl
from jax.experimental.pallas import tpu as pltpu
from jax.sharding import Mesh, PartitionSpec as P

BF = jnp.bfloat16
F32 = jnp.float32
MIB = 1024 * 1024
AXES = {"ylo": 2, "z": 4, "yhi": 2, "x": 4, "core": 2}

VM = pl.BlockSpec(memory_space=pltpu.VMEM)
SM = pl.BlockSpec(memory_space=pltpu.SMEM)
ANY = pl.BlockSpec(memory_space=pl.ANY)


def shift(value, axis, step):
    n = AXES[axis]
    return lax.ppermute(value, axis, [(i, (i + step) % n) for i in range(n)])


def swap_far(value):
    pairs = [(a * 2 + b, (1 - a) * 2 + 1 - b) for a in range(2) for b in range(2)]
    return lax.ppermute(value, ("ylo", "yhi"), pairs)


def shaped(shape, dtype):
    return jax.ShapeDtypeStruct(shape, dtype)


def call(kernel, outs, specs, scratch=(), vmem=48, out_specs=None, flops=1024):
    return pl.pallas_call(
        kernel,
        out_shape=outs,
        in_specs=specs,
        out_specs=out_specs or [VM] * len(outs),
        scratch_shapes=list(scratch),
        compiler_params=pltpu.CompilerParams(vmem_limit_bytes=vmem * MIB),
        cost_estimate=pl.CostEstimate(flops=flops, bytes_accessed=1024, transcendentals=0),
    )


def inverse_length(rows):
    return 1.0 / jnp.sqrt(jnp.sum(rows * rows, axis=-1, keepdims=True) + 1e-06)


def project(grad, rows):
    inv = inverse_length(rows)
    unit = rows * inv
    inner = jnp.sum(unit * grad, axis=-1, keepdims=True)
    return (grad - unit * inner) * inv


def prepare_kernel(w, img, w_half, n_img):
    w_half[...] = w[...].astype(BF)
    rows = img[...].astype(F32)
    n_img[...] = (rows * inverse_length(rows)).astype(BF)


def pack_kernel(*refs):
    pieces, out, sems = refs[:7], refs[7], refs[8]
    copies = [pltpu.make_async_copy(p, out.at[k], sems.at[k]) for k, p in enumerate(pieces)]
    for c in copies:
        c.start()
    for c in copies:
        c.wait()


def text_kernel(at, near_core, far_core, near_last, far_last, txt, txt_far, w_full, z, n_txt, mine, other, rows, sems):
    copies = [
        pltpu.make_async_copy(near_core, mine.at[pl.ds(0, 7)], sems.at[0]),
        pltpu.make_async_copy(far_core, other.at[pl.ds(0, 7)], sems.at[1]),
        pltpu.make_async_copy(near_last, mine.at[7], sems.at[2]),
        pltpu.make_async_copy(far_last, other.at[7], sems.at[3]),
        pltpu.make_async_copy(txt, rows.at[pl.ds(0, 320)], sems.at[4]),
        pltpu.make_async_copy(txt_far, rows.at[pl.ds(320, 320)], sems.at[5]),
    ]
    for c in copies:
        c.start()
    for c in copies[:4]:
        c.wait()
    yhi, x, core = at[0], at[1], at[2]
    for k in range(8):
        y_of = yhi if k < 4 else 1 - yhi
        owner = y_of * 4 + (x + 4 - (0, 1, 3, 2)[k % 4]) % 4
        a, b = mine[k].astype(F32), other[k].astype(F32)
        first = jnp.where(core == 0, a, b)
        second = jnp.where(core == 0, b, a)
        pair = jnp.concatenate([first, second], axis=0).astype(BF)
        w_full[pl.ds(pl.multiple_of(owner * 144, 16), 144), :] = pair
    for c in copies[4:]:
        c.wait()
    out = jnp.dot(rows[...], w_full[...], preferred_element_type=F32)
    z[...] = out
    n_txt[...] = (out * inverse_length(out)).astype(BF)


def logit_gradient(scal, img_rows, txt_rows):
    logits = scal[0] * lax.dot_general(
        img_rows, txt_rows, (((1,), (1,)), ((), ())), preferred_element_type=F32
    ) + scal[1]
    return 1.0 / (1.0 + jnp.exp(-logits))


def near_kernel(scal, n_own, n_a, n_b, n_txt, grad, acc, rows):
    rows[pl.ds(0, 320), :] = n_own[...]
    rows[pl.ds(320, 320), :] = n_a[...]
    rows[pl.ds(640, 320), :] = n_b[...]
    g = logit_gradient(scal, rows[...], n_txt[...])
    row_ids = lax.broadcasted_iota(jnp.int32, g.shape, 0)
    col_ids = lax.broadcasted_iota(jnp.int32, g.shape, 1)
    g = g - jnp.where((row_ids == col_ids) & (row_ids < 320), 1.0, 0.0)
    grad[...] = g.astype(BF)
    acc[...] = lax.dot_general(
        grad[...], rows[...], (((0,), (0,)), ((), ())), preferred_element_type=F32
    )


def far_kernel(at, scal, n_c0, n_c1, n_txt, acc, z, txt, txt_far, grad, g_own, g_far, mine, other, rows, feat, wide):
    rows[pl.ds(0, 160), :] = n_c0[...]
    rows[pl.ds(160, 160), :] = n_c1[...]
    feat[pl.ds(0, 320), :] = txt[...]
    feat[pl.ds(320, 320), :] = txt_far[...]
    grad[...] = logit_gradient(scal, rows[...], n_txt[...]).astype(BF)
    total = scal[0] * (
        acc[...]
        + lax.dot_general(grad[...], rows[...], (((0,), (0,)), ((), ())), preferred_element_type=F32)
    )
    g_own[...] = total[:320].astype(BF)
    g_far[...] = total[320:].astype(BF)
    dz = project(total, z[...]).astype(BF)
    wide[...] = lax.dot_general(
        feat[...], dz, (((0,), (0,)), ((), ())), preferred_element_type=F32
    )
    core = at[2]
    for j in range(8):
        a = pl.multiple_of((2 * j + core) * 72, 8)
        b = pl.multiple_of((2 * j + 1 - core) * 72, 8)
        mine[j] = wide[pl.ds(a, 72), :].astype(BF)
        other[j] = wide[pl.ds(b, 72), :].astype(BF)


def part_kernel(scal, grad, grad_c, n_txt, part_a, part_b, part_c):
    out = scal[0] * jnp.dot(grad[pl.ds(320, 640), :], n_txt[...], preferred_element_type=F32)
    part_a[...] = out[:320].astype(BF)
    part_b[...] = out[320:].astype(BF)
    part_c[...] = (scal[0] * jnp.dot(grad_c[...], n_txt[...], preferred_element_type=F32)).astype(BF)


def part_own_kernel(scal, grad, n_txt, part_own):
    part_own[...] = (
        scal[0] * jnp.dot(grad[pl.ds(0, 320), :], n_txt[...], preferred_element_type=F32)
    ).astype(BF)


def core_sum_kernel(at, mine, got, own, up, far_h, far_y, down):
    x = at[1]
    for r, outs in enumerate(
        ((own.at[0], own.at[1]), (up.at[0], up.at[1]), (far_h, far_y), (down.at[0], down.at[1]))
    ):
        for h in range(2):
            j = h * 4 + (x + r) % 4
            outs[h][...] = (mine[j].astype(F32) + got[j].astype(F32)).astype(BF)


def pass_kernel(up, got_h, down, got_y, up_out, down_out):
    up_out[0] = (up[0].astype(F32) + got_h[...].astype(F32)).astype(BF)
    up_out[1] = up[1]
    down_out[0] = down[0]
    down_out[1] = (down[1].astype(F32) + got_y[...].astype(F32)).astype(BF)


def x_sum_kernel(at, a, b, c, keep, send):
    yhi = at[0]
    for out, h in ((keep, yhi), (send, 1 - yhi)):
        out[...] = (a[h].astype(F32) + (b[h].astype(F32) + c[h].astype(F32))).astype(BF)


def quad_sum_kernel(a, b, c, d, out):
    total = (a[...].astype(F32) + b[...].astype(F32)) + (c[...].astype(F32) + d[...].astype(F32))
    out[...] = total.astype(out.dtype)


def image_out_kernel(img, a, b, c, d, out):
    grad = (a[...].astype(F32) + b[...].astype(F32)) + (c[...].astype(F32) + d[...].astype(F32))
    out[...] = project(grad, img[...].astype(F32)).astype(BF)


def text_out_kernel(z, a, b, w_full, out):
    grad = a[...].astype(F32) + b[...].astype(F32)
    dz = project(grad, z[pl.ds(0, 320), :]).astype(BF)
    out[...] = lax.dot_general(
        dz, w_full[...], (((1,), (1,)), ((), ())), preferred_element_type=F32
    ).astype(BF)


def apart(step, *args):
    outs = jax.eval_shape(step, *args)
    return lax.cond(
        lax.axis_index("z") < AXES["z"],
        step,
        lambda *_: tuple(jnp.zeros(o.shape, o.dtype) for o in outs),
        *args,
    )


BLOCK = shaped((320, 1152), BF)


def stack_of(*lead):
    return shaped((*lead, 72, 1152), BF)


def gather_head(w_h):
    hold = lax.optimization_barrier
    w_y, h_a = swap_far(w_h), shift(w_h, "x", 1)
    w_h, w_y, h_a = hold((w_h, w_y, h_a))
    h_b, y_a = shift(w_h, "x", -1), shift(w_y, "x", 1)
    w_y, h_a, h_b, y_a = hold((w_y, h_a, h_b, y_a))
    y_b, h_c = shift(w_y, "x", -1), shift(h_a, "x", 1)
    y_b, h_c = hold((y_b, h_c))
    y_c = shift(y_b, "x", -1)
    (near_core,) = call(
        pack_kernel, [stack_of(7)], [ANY] * 7, [pltpu.SemaphoreType.DMA((7,))], out_specs=[ANY]
    )(w_h, h_a, h_b, h_c, w_y, y_a, y_b)
    return near_core, shift(near_core, "core", 1), y_c, shift(y_c, "core", 1)


def reduce_x(at, mine, got_core, scal, grad, n_txt):
    rel = call(core_sum_kernel, [stack_of(2), stack_of(2), stack_of(), stack_of(), stack_of(2)], [SM, VM, VM])(
        at, mine, got_core
    )
    own, up, far_h, far_y, down = rel
    up, down = call(pass_kernel, [stack_of(2)] * 2, [VM] * 4)(
        up, shift(far_h, "x", 1), down, shift(far_y, "x", -1)
    )
    keep, send = call(x_sum_kernel, [stack_of()] * 2, [SM] + [VM] * 3)(
        at, own, shift(up, "x", 1), shift(down, "x", -1)
    )
    (part_own,) = call(part_own_kernel, [BLOCK], [SM] + [VM] * 2, flops=1 << 30)(scal, grad, n_txt)
    return keep, send, part_own


def reduce_yz(keep, send, z, g_own, g_got, w_full):
    (quad,) = call(quad_sum_kernel, [stack_of()], [VM] * 4)(
        keep, shift(keep, "ylo", 1), swap_far(send), shift(send, "yhi", 1)
    )
    (d_weight,) = call(quad_sum_kernel, [shaped((72, 1152), F32)], [VM] * 4)(
        quad, shift(quad, "z", 2), shift(quad, "z", 1), shift(quad, "z", -1)
    )
    (d_feat,) = call(text_out_kernel, [BLOCK], [VM] * 4, flops=1 << 31)(z, g_own, g_got, w_full)
    return d_weight, d_feat


def on_device(img_emb, txt_feat, w_txt, t_log, bias):
    img, txt = img_emb[0], txt_feat[0]
    at = jnp.stack([lax.axis_index("yhi"), lax.axis_index("x"), lax.axis_index("core")]).astype(jnp.int32)
    scal = jnp.concatenate([jnp.exp(t_log), bias])
    block = BLOCK

    txt_far = shift(txt, "ylo", 1)
    w_h, n_img = call(prepare_kernel, [stack_of(), block], [VM] * 2)(w_txt, img)
    n_a, n_b = shift(n_img, "z", 1), shift(n_img, "z", -1)
    head = apart(gather_head, w_h)
    head, n_a, n_b, txt_far = lax.optimization_barrier((head, n_a, n_b, txt_far))
    n_c0, n_c1 = shift(n_a[:160], "z", 1), shift(n_b[160:], "z", -1)

    w_full, z, n_txt = call(
        text_kernel,
        [shaped((1152, 1152), BF), shaped((640, 1152), F32), shaped((640, 1152), BF)],
        [SM] + [ANY] * 6,
        [
            pltpu.VMEM((8, 72, 1152), BF),
            pltpu.VMEM((8, 72, 1152), BF),
            pltpu.VMEM((640, 1152), BF),
            pltpu.SemaphoreType.DMA((6,)),
        ],
    )(at, *head, txt, txt_far)

    grad, acc = call(
        near_kernel,
        [shaped((960, 640), BF), shaped((640, 1152), F32)],
        [SM] + [VM] * 4,
        [pltpu.VMEM((960, 1152), BF)],
    )(scal, n_img, n_a, n_b, n_txt)
    grad_c, g_own, g_far, mine, other = call(
        far_kernel,
        [shaped((320, 640), BF), block, block, stack_of(8), stack_of(8)],
        [SM, SM] + [VM] * 7,
        [pltpu.VMEM((320, 1152), BF), pltpu.VMEM((640, 1152), BF), pltpu.VMEM((1152, 1152), F32)],
    )(at, scal, n_c0, n_c1, n_txt, acc, z, txt, txt_far)

    got_core = shift(other, "core", 1)
    g_got = shift(g_far, "ylo", 1)
    part_a, part_b, part_c = call(part_kernel, [block] * 3, [SM] + [VM] * 3)(
        scal, grad, grad_c, n_txt
    )
    got_a, got_b = shift(part_a, "z", -1), shift(part_b, "z", 1)
    keep, send, part_own = apart(reduce_x, at, mine, got_core, scal, grad, n_txt)
    keep, send, g_got, got_a, got_b, part_c = lax.optimization_barrier(
        (keep, send, g_got, got_a, got_b, part_c)
    )
    got_c = shift(part_c, "z", 2)
    d_weight, d_feat = apart(reduce_yz, keep, send, z, g_own, g_got, w_full)
    d_weight, got_c = lax.optimization_barrier((d_weight, got_c))

    (d_img,) = call(image_out_kernel, [block], [VM] * 5)(img, part_own, got_c, got_a, got_b)
    return (d_img[None], d_feat[None], d_weight)


def solution(mesh):
    fine = Mesh(mesh.devices.reshape(2, 4, 2, 4, 2), tuple(AXES))
    dp, fsdp = ("ylo", "z"), ("yhi", "x", "core")
    placed = (P(fsdp, dp, None), P(fsdp, dp, None), P(fsdp, None), P(), P())
    return jax.shard_map(
        on_device,
        mesh=fine,
        in_specs=placed,
        out_specs=(P(fsdp, dp, None), P(fsdp, dp, None), P(fsdp, None)),
        check_vma=False,
    )
```

time: 443 us -> 128 us (0.29)
  waiting for transfers between devices: 333 us -> 41.3 us
  matrix products: 78.9 us -> 0 us
  starting transfers between devices: 0.34 us -> 42.2 us
  Pallas kernels: 0 us -> 36 us
  between operations: 15.2 us -> 2.11 us
  other arithmetic: 9.61 us -> 0.15 us
    all_gather x3 -> x0, waiting for transfers between devices: 183 us -> none  [the longest x1 65.9 us: on_device(): other_txt = lax.all_gather(n_txt, 'dp', axis=0, tiled=True)]
    psum x1 -> x0, waiting for transfers between devices: 150 us -> none  [on_device(): summed = lax.psum(weight_term, ('dp', 'fsdp'))]
    dot_general x19 -> x0, matrix products: 78.9 us -> none  [the longest x8 35.5 us: text_side(): lax.dot_general(grad_logit, img_a, (((0,), (0,)), ((), ())), preferred_el...]
    ppermute x0 -> x29, starting transfers between devices: none -> 42.2 us  [the longest x27 38.9 us: shift(): return lax.ppermute(value, axis, [(i, (i + step) % n) for i in range(n)])]
    ppermute x0 -> x29, waiting for transfers between devices: none -> 41.3 us  [the longest x27 38.1 us: shift(): return lax.ppermute(value, axis, [(i, (i + step) % n) for i in range(n)])]
    pallas_call x0 -> x14, Pallas kernels: none -> 36 us  [the longest x1 7.88 us: on_device(): call(far_kernel, [shaped((320, 640), BF), block, block, stack_of(8), stac...]
    convert_element_type x4 -> x0, other arithmetic: 5.65 us -> none  [the longest x2 2.22 us: normalize(): return (unit_rows, length, unit_rows.astype(jnp.bfloat16))]
  transfers between devices with their start and end apart: 4 -> 29, of which waited for: 4 -> 15; matrix products, arithmetic and copies ran while one was open for 3% -> 0% of each run, Pallas kernels for 0% -> 20%
where the time goes in v2:
time: 128 us; the launch traced here: 127 us
  starting transfers between devices  42.2 us (33%)
  waiting for transfers between devices  41.3 us (32%)
  Pallas kernels  36 us (28%)
  local copies, waits for them, and re-layouts  5.26 us (4%)
  between operations  2.11 us (2%)
    ppermute x27, starting transfers between devices, shift(): return lax.ppermute(value, axis, [(i, (i + step) % n) for i in range(n)])  38.9 us
    ppermute x27, waiting for transfers between devices, shift(): return lax.ppermute(value, axis, [(i, (i + step) % n) for i in range(n)])  38.1 us
    pallas_call x1, Pallas kernels, on_device(): call(far_kernel, [shaped((320, 640), BF), block, block, stack_of(8), stac...  7.88 us
    pallas_call x1, Pallas kernels, on_device(): call(near_kernel, [shaped((960, 640), BF), shaped((640, 1152), F32)], [SM...  5.94 us
    pallas_call x1, Pallas kernels, on_device(): call(text_kernel, [shaped((1152, 1152), BF), shaped((640, 1152), F32), sh...  5.35 us
    pallas_call x1, Pallas kernels, reduce_yz(): call(text_out_kernel, [BLOCK], [VM] * 4, flops=1 << 31)  4.8 us
    unnamed x18, local copies, waits for them, and re-layouts  3.73 us
    pallas_call x1, Pallas kernels, on_device(): call(part_kernel, [block] * 3, [SM] + [VM] * 3)(scal, grad, grad_c, n_txt)  3.49 us
  transfers between devices with their start and end apart: 29, of which 15 were waited for; matrix products, arithmetic and copies ran while one was open for 0% of the time, Pallas kernels for 20%

profile of v2, /device:TPU:0, one launch (start us, length us, event | category | flops | bytes accessed | tf_op | source)
XLA Modules:
  0.0 127.1 jit_solution(8382622214535801861)
XLA Ops:
  0.6 1.7 %collective-permute-start.21 = (bf16[320,1152]{1,0:T(8,128)(2,1)}, bf16[320,1152]{1,0:T(8,128)(2,1)S(1)}, u32[]{:S(2)}, u32[]{:S(2)}) collective-permute-start(bf16[320,1152]{1,0:T(8,128)(2,1)} %bitcast.7), channel_id=1, source_target_pairs={{0,64},{64,0},{1,65},{65,1},{2,66},{66,2},{3,67},{67,3},{4,68},{68... | collective-permute-start | bytes 2211848 | tf_op jit(solution)/shard_map/ppermute | solution.py:20
  2.4 1.1 copy-done.2
  3.5 1.0 copy-done.4
  4.5 1.1 shard_map.76
  5.6 4.0 %collective-permute-start.20 = (bf16[320,1152]{1,0:T(8,128)(2,1)}, bf16[320,1152]{1,0:T(8,128)(2,1)S(1)}, u32[]{:S(2)}, u32[]{:S(2)}) collective-permute-start(bf16[320,1152]{1,0:T(8,128)(2,1)} %get-tuple-element.103.n_own), channel_id=1, source_target_pairs={{0,48},{16,0},{32,16},{48,32},{1,49},{17,1},{33,17},{49,33},{2,50}... | collective-permute-start | bytes 2211848 | tf_op jit(solution)/shard_map/ppermute | solution.py:20
  9.7 33.3 %conditional.3 = (bf16[7,72,1152]{2,1,0:T(8,128)(2,1)}, bf16[7,72,1152]{2,1,0:T(8,128)(2,1)}, bf16[72,1152]{1,0:T(8,128)(2,1)}, bf16[72,1152]{1,0:T(8,128)(2,1)}) conditional(s32[]{:T(128)} %convert_element_type.2, () %tuple.41, bf16[72,1152]{1,0:T(8,128)(2,1)S(1)} %get-tuple-element.98), branch_computations={%region_0.0_spmd, %region_1.0_spmd} | conditional | flops 1024 | bytes 9954696 | solution.py:200
  9.7 1.5 %collective-permute-start.1 = (bf16[72,1152]{1,0:T(8,128)(2,1)S(1)}, bf16[72,1152]{1,0:T(8,128)(2,1)S(1)}, u32[]{:S(2)}, u32[]{:S(2)}) collective-permute-start(bf16[72,1152]{1,0:T(8,128)(2,1)S(1)} %refs_0_), channel_id=1, source_target_pairs={{0,2},{2,4},{4,6},{6,0},{1,3},{3,5},{5,7},{7,1},{8,10},{10,12},{12... | collective-permute-start | bytes 497672 | tf_op jit(solution)/shard_map/cond/branch_1_fun/ppermute | solution.py:20
  11.1 2.2 %collective-permute-start = (bf16[72,1152]{1,0:T(8,128)(2,1)S(1)}, bf16[72,1152]{1,0:T(8,128)(2,1)S(1)}, u32[]{:S(2)}, u32[]{:S(2)}) collective-permute-start(bf16[72,1152]{1,0:T(8,128)(2,1)S(1)} %refs_0_), channel_id=1, source_target_pairs={{0,72},{8,64},{64,8},{72,0},{1,73},{9,65},{65,9},{73,1},{2,74},{10... | collective-permute-start | bytes 497672 | tf_op jit(solution)/shard_map/cond/branch_1_fun/ppermute | solution.py:25
  13.3 3.0 %collective-permute-done.1.refs_1_ = bf16[72,1152]{1,0:T(8,128)(2,1)S(1)} collective-permute-done((bf16[72,1152]{1,0:T(8,128)(2,1)S(1)}, bf16[72,1152]{1,0:T(8,128)(2,1)S(1)}, u32[]{:S(2)}, u32[]{:S(2)}) %collective-permute-start.1) | collective-permute-done | bytes 165920 | tf_op jit(solution)/shard_map/cond/branch_1_fun/ppermute | solution.py:20
  16.3 1.4 %collective-permute-done.refs_4_ = bf16[72,1152]{1,0:T(8,128)(2,1)S(1)} collective-permute-done((bf16[72,1152]{1,0:T(8,128)(2,1)S(1)}, bf16[72,1152]{1,0:T(8,128)(2,1)S(1)}, u32[]{:S(2)}, u32[]{:S(2)}) %collective-permute-start) | collective-permute-done | bytes 165920 | tf_op jit(solution)/shard_map/cond/branch_1_fun/ppermute | solution.py:25
  17.7 1.7 %collective-permute-start.2 = (bf16[72,1152]{1,0:T(8,128)(2,1)S(1)}, bf16[72,1152]{1,0:T(8,128)(2,1)S(1)}, u32[]{:S(2)}, u32[]{:S(2)}) collective-permute-start(bf16[72,1152]{1,0:T(8,128)(2,1)S(1)} %refs_0_), channel_id=1, source_target_pairs={{0,6},{2,0},{4,2},{6,4},{1,7},{3,1},{5,3},{7,5},{8,14},{10,8},{12,... | collective-permute-start | bytes 497672 | tf_op jit(solution)/shard_map/cond/branch_1_fun/ppermute | solution.py:20
  19.7 3.3 %collective-permute-done.2.refs_2_ = bf16[72,1152]{1,0:T(8,128)(2,1)S(1)} collective-permute-done((bf16[72,1152]{1,0:T(8,128)(2,1)S(1)}, bf16[72,1152]{1,0:T(8,128)(2,1)S(1)}, u32[]{:S(2)}, u32[]{:S(2)}) %collective-permute-start.2) | collective-permute-done | bytes 165920 | tf_op jit(solution)/shard_map/cond/branch_1_fun/ppermute | solution.py:20
  23.0 3.0 %collective-permute-done.3.refs_5_ = bf16[72,1152]{1,0:T(8,128)(2,1)S(1)} collective-permute-done((bf16[72,1152]{1,0:T(8,128)(2,1)S(1)}, bf16[72,1152]{1,0:T(8,128)(2,1)S(1)}, u32[]{:S(2)}, u32[]{:S(2)}) %collective-permute-start.3) | collective-permute-done | bytes 165920 | tf_op jit(solution)/shard_map/cond/branch_1_fun/ppermute | solution.py:20
  26.0 3.2 %collective-permute-start.4 = (bf16[72,1152]{1,0:T(8,128)(2,1)S(1)}, bf16[72,1152]{1,0:T(8,128)(2,1)S(1)}, u32[]{:S(2)}, u32[]{:S(2)}) collective-permute-start(bf16[72,1152]{1,0:T(8,128)(2,1)S(1)} %collective-permute-done.refs_4_), channel_id=1, source_target_pairs={{0,6},{2,0},{4,2},{6,4},{1,7},{3,1},{5,3},{7,5},{8,14},{10,8},{12,... | collective-permute-start | bytes 497672 | tf_op jit(solution)/shard_map/cond/branch_1_fun/ppermute | solution.py:20
  29.2 3.3 %collective-permute-done.5.refs_3_ = bf16[72,1152]{1,0:T(8,128)(2,1)S(1)} collective-permute-done((bf16[72,1152]{1,0:T(8,128)(2,1)S(1)}, bf16[72,1152]{1,0:T(8,128)(2,1)S(1)}, u32[]{:S(2)}, u32[]{:S(2)}) %collective-permute-start.5) | collective-permute-done | bytes 165920 | tf_op jit(solution)/shard_map/cond/branch_1_fun/ppermute | solution.py:20
  32.5 1.1 branch_1_fun.8
  33.7 3.3 %collective-permute-start.7 = (bf16[72,1152]{1,0:T(8,128)(2,1)S(1)}, bf16[72,1152]{1,0:T(8,128)(2,1)}, u32[]{:S(2)}, u32[]{:S(2)}) collective-permute-start(bf16[72,1152]{1,0:T(8,128)(2,1)S(1)} %collective-permute-done.4.refs_6_), channel_id=1, source_target_pairs={{0,6},{2,0},{4,2},{6,4},{1,7},{3,1},{5,3},{7,5},{8,14},{10,8},{12,... | collective-permute-start | bytes 497672 | tf_op jit(solution)/shard_map/cond/branch_1_fun/ppermute | solution.py:20
  37.0 4.1 %collective-permute-done.7 = bf16[72,1152]{1,0:T(8,128)(2,1)} collective-permute-done((bf16[72,1152]{1,0:T(8,128)(2,1)S(1)}, bf16[72,1152]{1,0:T(8,128)(2,1)}, u32[]{:S(2)}, u32[]{:S(2)}) %collective-permute-start.7) | collective-permute-done | bytes 165920 | tf_op jit(solution)/shard_map/cond/branch_1_fun/ppermute | solution.py:20
  41.2 1.7 %collective-permute-done.8 = bf16[72,1152]{1,0:T(8,128)(2,1)} collective-permute-done((bf16[72,1152]{1,0:T(8,128)(2,1)}, bf16[72,1152]{1,0:T(8,128)(2,1)}, u32[]{:S(2)}, u32[]{:S(2)}) %collective-permute-start.8) | collective-permute-done | bytes 165920 | tf_op jit(solution)/shard_map/cond/branch_1_fun/ppermute | solution.py:20
  44.5 3.2 %collective-permute-start.23 = (bf16[160,1152]{1,0:T(8,128)(2,1)}, bf16[160,1152]{1,0:T(8,128)(2,1)S(1)}, u32[]{:S(2)}, u32[]{:S(2)}) collective-permute-start(bf16[160,1152]{1,0:T(8,128)(2,1)} %slice.7), channel_id=1, source_target_pairs={{0,48},{16,0},{32,16},{48,32},{1,49},{17,1},{33,17},{49,33},{2,50}... | collective-permute-start | bytes 1105928 | tf_op jit(solution)/shard_map/ppermute | solution.py:20
  49.2 5.3 %shard_map.77 = (bf16[1152,1152]{1,0:T(8,128)(2,1)}, f32[640,1152]{1,0:T(8,128)S(1)}, bf16[640,1152]{1,0:T(8,128)(2,1)S(1)}) custom-call(s32[3]{0:T(128)S(1)} %pad_add_fusion.at, bf16[7,72,1152]{2,1,0:T(8,128)(2,1)} %get-tuple-element.106.near_core, bf16[7,72,1152]{2,1,0:T(8,128)(2,1)} %get-tuple-element.107.far_core, ...), custom_call_target="tpu_custom_call" | custom-call | flops 1024 | bytes 1024 | tf_op jit(solution)/shard_map/pallas_call | solution.py:269
  54.6 5.9 %shard_map.78 = (bf16[960,640]{1,0:T(8,128)(2,1)S(1)}, f32[640,1152]{1,0:T(8,128)S(1)}) custom-call(f32[2]{0:T(128)S(1)} %pad_maximum_fusion.scal, bf16[320,1152]{1,0:T(8,128)(2,1)} %get-tuple-element.103.n_own, bf16[320,1152]{1,0:T(8,128)(2,1)S(1)} %collective-permute-done.19.n_a, bf16[320,1152]{1,0:T(8,128)(2,1)S(1)} %collective-permute-done.20.n_b, ...), custom_call_target="tpu_custom_call" | custom-call | flops 1024 | bytes 1024 | tf_op jit(solution)/shard_map/pallas_call | solution.py:281
  60.5 1.6 %copy-done = f32[640,1152]{1,0:T(8,128)} copy-done((f32[640,1152]{1,0:T(8,128)}, f32[640,1152]{1,0:T(8,128)S(1)}, u32[]{:S(2)}) %copy-start) | copy-done | bytes 2949144
  62.1 7.9 %shard_map.79 = (bf16[320,640]{1,0:T(8,128)(2,1)S(1)}, bf16[320,1152]{1,0:T(8,128)(2,1)}, bf16[320,1152]{1,0:T(8,128)(2,1)S(1)}, bf16[8,72,1152]{2,1,0:T(8,128)(2,1)S(1)}, bf16[8,72,1152]{2,1,0:T(8,128)(2,1)S(1)}) custom-call(s32[3]{0:T(128)S(1)} %pad_add_fusion.at, f32[2]{0:T(128)S(1)} %pad_maximum_fusion.scal, ...), custom_call_target="tpu_custom_call" | custom-call | flops 1024 | bytes 1024 | tf_op jit(solution)/shard_map/pallas_call | solution.py:287
  70.0 3.5 %shard_map.80 = (bf16[320,1152]{1,0:T(8,128)(2,1)}, bf16[320,1152]{1,0:T(8,128)(2,1)S(1)}, bf16[320,1152]{1,0:T(8,128)(2,1)}) custom-call(f32[2]{0:T(128)S(1)} %pad_maximum_fusion.scal, bf16[960,640]{1,0:T(8,128)(2,1)S(1)} %get-tuple-element.116.grad, bf16[320,640]{1,0:T(8,128)(2,1)S(1)} %get-tuple-element.121.grad_c, ...), custom_call_target="tpu_custom_call" | custom-call | flops 1024 | bytes 1024 | tf_op jit(solution)/shard_map/pallas_call | solution.py:296
  73.5 3.2 %collective-permute-start.26 = (bf16[320,1152]{1,0:T(8,128)(2,1)}, bf16[320,1152]{1,0:T(8,128)(2,1)S(1)}, u32[]{:S(2)}, u32[]{:S(2)}) collective-permute-start(bf16[320,1152]{1,0:T(8,128)(2,1)} %get-tuple-element.122), channel_id=1, source_target_pairs={{0,48},{16,0},{32,16},{48,32},{1,49},{17,1},{33,17},{49,33},{2,50}... | collective-permute-start | bytes 2211848 | tf_op jit(solution)/shard_map/ppermute | solution.py:20
  76.7 20.9 %conditional.4 = (bf16[72,1152]{1,0:T(8,128)(2,1)S(1)}, bf16[72,1152]{1,0:T(8,128)(2,1)S(1)}, bf16[320,1152]{1,0:T(8,128)(2,1)S(1)}) conditional(s32[]{:T(128)} %convert_element_type.2, () %tuple.40, (s32[3]{0:T(128)S(1)}, bf16[8,72,1152]{2,1,0:T(8,128)(2,1)S(1)}, bf16[8,72,1152]{2,1,0:T(8,128)(2,1)S(1)}, f32[2]{0:T(128)S(1)}, ...), branch_computations={%region_2.0_spmd, %region_3.0_spmd} | conditional | flops 1073744896 | bytes 3985592 | solution.py:200
  76.7 0.9 branch_1_fun.9
  77.7 3.9 %collective-permute-start.10 = (bf16[72,1152]{1,0:T(8,128)(2,1)S(1)}, bf16[72,1152]{1,0:T(8,128)(2,1)S(1)}, u32[]{:S(2)}, u32[]{:S(2)}) collective-permute-start(bf16[72,1152]{1,0:T(8,128)(2,1)S(1)} %get-tuple-element.42), channel_id=1, source_target_pairs={{0,6},{2,0},{4,2},{6,4},{1,7},{3,1},{5,3},{7,5},{8,14},{10,8},{12,... | collective-permute-start | bytes 497672 | tf_op jit(solution)/shard_map/cond/branch_1_fun/ppermute | solution.py:20
  81.6 4.5 %collective-permute-done.9.got_h = bf16[72,1152]{1,0:T(8,128)(2,1)S(1)} collective-permute-done((bf16[72,1152]{1,0:T(8,128)(2,1)S(1)}, bf16[72,1152]{1,0:T(8,128)(2,1)S(1)}, u32[]{:S(2)}, u32[]{:S(2)}) %collective-permute-start.9) | collective-permute-done | bytes 165920 | tf_op jit(solution)/shard_map/cond/branch_1_fun/ppermute | solution.py:20
  86.2 1.2 collective-permute-start.11
  87.4 2.1 %collective-permute-start.12 = (bf16[2,72,1152]{2,1,0:T(8,128)(2,1)S(1)}, bf16[2,72,1152]{2,1,0:T(8,128)(2,1)S(1)}, u32[]{:S(2)}, u32[]{:S(2)}) collective-permute-start(bf16[2,72,1152]{2,1,0:T(8,128)(2,1)S(1)} %get-tuple-element.44), channel_id=1, source_target_pairs={{0,6},{2,0},{4,2},{6,4},{1,7},{3,1},{5,3},{7,5},{8,14},{10,8},{12,... | collective-permute-start | bytes 995336 | tf_op jit(solution)/shard_map/cond/branch_1_fun/ppermute | solution.py:20
  89.5 1.3 %branch_1_fun.12 = bf16[320,1152]{1,0:T(8,128)(2,1)S(1)} custom-call(f32[2]{0:T(128)S(1)} %get-tuple-element.47.scal, bf16[960,640]{1,0:T(8,128)(2,1)S(1)} %get-tuple-element.48.grad, bf16[640,1152]{1,0:T(8,128)(2,1)S(1)} %get-tuple-element.49.n_txt), custom_call_target="tpu_custom_call" | custom-call | flops 1073741824 | bytes 1024 | tf_op jit(solution)/shard_map/cond/branch_1_fun/pallas_call | solution.py:241
  90.9 6.1 %collective-permute-done.11.b = bf16[2,72,1152]{2,1,0:T(8,128)(2,1)S(1)} collective-permute-done((bf16[2,72,1152]{2,1,0:T(8,128)(2,1)S(1)}, bf16[2,72,1152]{2,1,0:T(8,128)(2,1)S(1)}, u32[]{:S(2)}, u32[]{:S(2)}) %collective-permute-start.11) | collective-permute-done | bytes 331808 | tf_op jit(solution)/shard_map/cond/branch_1_fun/ppermute | solution.py:20
  97.6 1.5 %collective-permute-start.28 = (bf16[320,1152]{1,0:T(8,128)(2,1)}, bf16[320,1152]{1,0:T(8,128)(2,1)S(1)}, u32[]{:S(2)}, u32[]{:S(2)}) collective-permute-start(bf16[320,1152]{1,0:T(8,128)(2,1)} %get-tuple-element.131), channel_id=1, source_target_pairs={{0,32},{16,48},{32,0},{48,16},{1,33},{17,49},{33,1},{49,17},{2,34}... | collective-permute-start | bytes 2211848 | tf_op jit(solution)/shard_map/ppermute | solution.py:20
  99.2 24.7 %conditional.5 = (f32[72,1152]{1,0:T(8,128)S(1)}, bf16[1,320,1152]{2,1,0:T(8,128)(2,1)S(1)}) conditional(s32[]{:T(128)} %convert_element_type.2, () %tuple.44, (bf16[72,1152]{1,0:T(8,128)(2,1)S(1)}, bf16[72,1152]{1,0:T(8,128)(2,1)S(1)}, f32[640,1152]{1,0:T(8,128)}, bf16[320,1152]{1,0:T(8,128)(2,1)}, bf16[320,1152]{1,0:T(8,128)(2,1)}, ...), branch_computations={%region_4.0_spmd, %region_5.0_spmd} | conditional | flops 2147485696 | bytes 3984640 | solution.py:200
  99.2 1.4 %collective-permute-start.13 = (bf16[72,1152]{1,0:T(8,128)(2,1)S(1)}, bf16[72,1152]{1,0:T(8,128)(2,1)S(1)}, u32[]{:S(2)}, u32[]{:S(2)}) collective-permute-start(bf16[72,1152]{1,0:T(8,128)(2,1)S(1)} %get-tuple-element.50.a), channel_id=1, source_target_pairs={{0,64},{64,0},{1,65},{65,1},{2,66},{66,2},{3,67},{67,3},{4,68},{68... | collective-permute-start | bytes 497672 | tf_op jit(solution)/shard_map/cond/branch_1_fun/ppermute | solution.py:20
  100.6 2.1 %collective-permute-start.15 = (bf16[72,1152]{1,0:T(8,128)(2,1)S(1)}, bf16[72,1152]{1,0:T(8,128)(2,1)S(1)}, u32[]{:S(2)}, u32[]{:S(2)}) collective-permute-start(bf16[72,1152]{1,0:T(8,128)(2,1)S(1)} %get-tuple-element.51), channel_id=1, source_target_pairs={{0,8},{8,0},{1,9},{9,1},{2,10},{10,2},{3,11},{11,3},{4,12},{12,4},... | collective-permute-start | bytes 497672 | tf_op jit(solution)/shard_map/cond/branch_1_fun/ppermute | solution.py:20
  102.8 1.1 collective-permute-start.14
  103.9 1.8 %collective-permute-done.13.b = bf16[72,1152]{1,0:T(8,128)(2,1)S(1)} collective-permute-done((bf16[72,1152]{1,0:T(8,128)(2,1)S(1)}, bf16[72,1152]{1,0:T(8,128)(2,1)S(1)}, u32[]{:S(2)}, u32[]{:S(2)}) %collective-permute-start.13) | collective-permute-done | bytes 165920 | tf_op jit(solution)/shard_map/cond/branch_1_fun/ppermute | solution.py:20
  105.7 3.3 %collective-permute-done.15.d = bf16[72,1152]{1,0:T(8,128)(2,1)S(1)} collective-permute-done((bf16[72,1152]{1,0:T(8,128)(2,1)S(1)}, bf16[72,1152]{1,0:T(8,128)(2,1)S(1)}, u32[]{:S(2)}, u32[]{:S(2)}) %collective-permute-start.15) | collective-permute-done | bytes 165920 | tf_op jit(solution)/shard_map/cond/branch_1_fun/ppermute | solution.py:20
  109.0 1.7 %collective-permute-done.14.c = bf16[72,1152]{1,0:T(8,128)(2,1)S(1)} collective-permute-done((bf16[72,1152]{1,0:T(8,128)(2,1)S(1)}, bf16[72,1152]{1,0:T(8,128)(2,1)S(1)}, u32[]{:S(2)}, u32[]{:S(2)}) %collective-permute-start.14) | collective-permute-done | bytes 165920 | tf_op jit(solution)/shard_map/cond/branch_1_fun/ppermute | solution.py:25
  110.8 1.9 %collective-permute-start.18 = (bf16[72,1152]{1,0:T(8,128)(2,1)S(1)}, bf16[72,1152]{1,0:T(8,128)(2,1)S(1)}, u32[]{:S(2)}, u32[]{:S(2)}) collective-permute-start(bf16[72,1152]{1,0:T(8,128)(2,1)S(1)} %branch_1_fun.13.a), channel_id=1, source_target_pairs={{0,48},{16,0},{32,16},{48,32},{1,49},{17,1},{33,17},{49,33},{2,50}... | collective-permute-start | bytes 497672 | tf_op jit(solution)/shard_map/cond/branch_1_fun/ppermute | solution.py:20
  112.9 2.1 %collective-permute-start.16 = (bf16[72,1152]{1,0:T(8,128)(2,1)S(1)}, bf16[72,1152]{1,0:T(8,128)(2,1)S(1)}, u32[]{:S(2)}, u32[]{:S(2)}) collective-permute-start(bf16[72,1152]{1,0:T(8,128)(2,1)S(1)} %branch_1_fun.13.a), channel_id=1, source_target_pairs={{0,32},{16,48},{32,0},{48,16},{1,33},{17,49},{33,1},{49,17},{2,34}... | collective-permute-start | bytes 497672 | tf_op jit(solution)/shard_map/cond/branch_1_fun/ppermute | solution.py:20
  115.0 4.8 %branch_1_fun.15 = bf16[320,1152]{1,0:T(8,128)(2,1)S(1)} custom-call(f32[640,1152]{1,0:T(8,128)} %get-tuple-element.52.z, bf16[320,1152]{1,0:T(8,128)(2,1)} %get-tuple-element.53.a, bf16[320,1152]{1,0:T(8,128)(2,1)} %get-tuple-element.54.b, bf16[1152,1152]{1,0:T(8,128)(2,1)} %get-tuple-element.55.w_full), custom_call_target="tpu_custom_call" | custom-call | flops 2147483648 | bytes 1024 | tf_op jit(solution)/shard_map/cond/branch_1_fun/pallas_call | solution.py:252
  119.8 1.9 %collective-permute-done.18.d = bf16[72,1152]{1,0:T(8,128)(2,1)S(1)} collective-permute-done((bf16[72,1152]{1,0:T(8,128)(2,1)S(1)}, bf16[72,1152]{1,0:T(8,128)(2,1)S(1)}, u32[]{:S(2)}, u32[]{:S(2)}) %collective-permute-start.18) | collective-permute-done | bytes 165920 | tf_op jit(solution)/shard_map/cond/branch_1_fun/ppermute | solution.py:20
  122.0 1.8 %collective-permute-done.16.b = bf16[72,1152]{1,0:T(8,128)(2,1)S(1)} collective-permute-done((bf16[72,1152]{1,0:T(8,128)(2,1)S(1)}, bf16[72,1152]{1,0:T(8,128)(2,1)S(1)}, u32[]{:S(2)}, u32[]{:S(2)}) %collective-permute-start.16) | collective-permute-done | bytes 165920 | tf_op jit(solution)/shard_map/cond/branch_1_fun/ppermute | solution.py:20
  123.9 3.2 %shard_map.81 = bf16[320,1152]{1,0:T(8,128)(2,1)} custom-call(bf16[320,1152]{1,0:T(8,128)(2,1)S(1)} %bitcast.11, bf16[320,1152]{1,0:T(8,128)(2,1)} %copy-done.6, bf16[320,1152]{1,0:T(8,128)(2,1)S(1)} %collective-permute-done.28.b, bf16[320,1152]{1,0:T(8,128)(2,1)S(1)} %collective-permute-done.26.c, bf16[320,1152]{1,0:T(8,128)(2,1)S(1)} %collective-permute-done.27.d), custom_call_target="tpu_custom_call" | custom-call | flops 1024 | bytes 1024 | tf_op jit(solution)/shard_map/pallas_call | solution.py:308
  (49 shorter events, 3.7 us)
Async XLA Ops:
  0.6 42.3 %collective-permute-start.21 = (bf16[320,1152]{1,0:T(8,128)(2,1)}, bf16[320,1152]{1,0:T(8,128)(2,1)S(1)}, u32[]{:S(2)}, u32[]{:S(2)}) collective-permute-start(bf16[320,1152]{1,0:T(8,128)(2,1)} %bitcast.7), channel_id=1, source_target_pairs={{0,64},{64,0},{1,65},{65,1},{2,66},{66,2},{3,67},{67,3},{4,68},{68... | collective-permute-start | bytes 2211848 | tf_op jit(solution)/shard_map/ppermute | solution.py:20
  2.4 1.1 copy-start.2
  3.5 1.0 copy-start.4
  5.6 37.3 %collective-permute-start.20 = (bf16[320,1152]{1,0:T(8,128)(2,1)}, bf16[320,1152]{1,0:T(8,128)(2,1)S(1)}, u32[]{:S(2)}, u32[]{:S(2)}) collective-permute-start(bf16[320,1152]{1,0:T(8,128)(2,1)} %get-tuple-element.103.n_own), channel_id=1, source_target_pairs={{0,48},{16,0},{32,16},{48,32},{1,49},{17,1},{33,17},{49,33},{2,50}... | collective-permute-start | bytes 2211848 | tf_op jit(solution)/shard_map/ppermute | solution.py:20
  9.6 33.3 %collective-permute-start.19 = (bf16[320,1152]{1,0:T(8,128)(2,1)}, bf16[320,1152]{1,0:T(8,128)(2,1)S(1)}, u32[]{:S(2)}, u32[]{:S(2)}) collective-permute-start(bf16[320,1152]{1,0:T(8,128)(2,1)} %get-tuple-element.103.n_own), channel_id=1, source_target_pairs={{0,16},{16,32},{32,48},{48,0},{1,17},{17,33},{33,49},{49,1},{2,18}... | collective-permute-start | bytes 2211848 | tf_op jit(solution)/shard_map/ppermute | solution.py:20
  9.7 6.6 %collective-permute-start.1 = (bf16[72,1152]{1,0:T(8,128)(2,1)S(1)}, bf16[72,1152]{1,0:T(8,128)(2,1)S(1)}, u32[]{:S(2)}, u32[]{:S(2)}) collective-permute-start(bf16[72,1152]{1,0:T(8,128)(2,1)S(1)} %refs_0_), channel_id=1, source_target_pairs={{0,2},{2,4},{4,6},{6,0},{1,3},{3,5},{5,7},{7,1},{8,10},{10,12},{12... | collective-permute-start | bytes 497672 | tf_op jit(solution)/shard_map/cond/branch_1_fun/ppermute | solution.py:20
  11.1 6.6 %collective-permute-start = (bf16[72,1152]{1,0:T(8,128)(2,1)S(1)}, bf16[72,1152]{1,0:T(8,128)(2,1)S(1)}, u32[]{:S(2)}, u32[]{:S(2)}) collective-permute-start(bf16[72,1152]{1,0:T(8,128)(2,1)S(1)} %refs_0_), channel_id=1, source_target_pairs={{0,72},{8,64},{64,8},{72,0},{1,73},{9,65},{65,9},{73,1},{2,74},{10... | collective-permute-start | bytes 497672 | tf_op jit(solution)/shard_map/cond/branch_1_fun/ppermute | solution.py:25
  17.7 5.3 %collective-permute-start.2 = (bf16[72,1152]{1,0:T(8,128)(2,1)S(1)}, bf16[72,1152]{1,0:T(8,128)(2,1)S(1)}, u32[]{:S(2)}, u32[]{:S(2)}) collective-permute-start(bf16[72,1152]{1,0:T(8,128)(2,1)S(1)} %refs_0_), channel_id=1, source_target_pairs={{0,6},{2,0},{4,2},{6,4},{1,7},{3,1},{5,3},{7,5},{8,14},{10,8},{12,... | collective-permute-start | bytes 497672 | tf_op jit(solution)/shard_map/cond/branch_1_fun/ppermute | solution.py:20
  19.4 6.6 %collective-permute-start.3 = (bf16[72,1152]{1,0:T(8,128)(2,1)S(1)}, bf16[72,1152]{1,0:T(8,128)(2,1)S(1)}, u32[]{:S(2)}, u32[]{:S(2)}) collective-permute-start(bf16[72,1152]{1,0:T(8,128)(2,1)S(1)} %collective-permute-done.refs_4_), channel_id=1, source_target_pairs={{0,2},{2,4},{4,6},{6,0},{1,3},{3,5},{5,7},{7,1},{8,10},{10,12},{12... | collective-permute-start | bytes 497672 | tf_op jit(solution)/shard_map/cond/branch_1_fun/ppermute | solution.py:20
  26.0 6.6 %collective-permute-start.5 = (bf16[72,1152]{1,0:T(8,128)(2,1)S(1)}, bf16[72,1152]{1,0:T(8,128)(2,1)S(1)}, u32[]{:S(2)}, u32[]{:S(2)}) collective-permute-start(bf16[72,1152]{1,0:T(8,128)(2,1)S(1)} %collective-permute-done.1.refs_1_), channel_id=1, source_target_pairs={{0,2},{2,4},{4,6},{6,0},{1,3},{3,5},{5,7},{7,1},{8,10},{10,12},{12... | collective-permute-start | bytes 497672 | tf_op jit(solution)/shard_map/cond/branch_1_fun/ppermute | solution.py:20
  26.0 6.6 %collective-permute-start.4 = (bf16[72,1152]{1,0:T(8,128)(2,1)S(1)}, bf16[72,1152]{1,0:T(8,128)(2,1)S(1)}, u32[]{:S(2)}, u32[]{:S(2)}) collective-permute-start(bf16[72,1152]{1,0:T(8,128)(2,1)S(1)} %collective-permute-done.refs_4_), channel_id=1, source_target_pairs={{0,6},{2,0},{4,2},{6,4},{1,7},{3,1},{5,3},{7,5},{8,14},{10,8},{12,... | collective-permute-start | bytes 497672 | tf_op jit(solution)/shard_map/cond/branch_1_fun/ppermute | solution.py:20
  33.7 9.2 %collective-permute-start.6 = (bf16[7,72,1152]{2,1,0:T(8,128)(2,1)}, bf16[7,72,1152]{2,1,0:T(8,128)(2,1)}, u32[]{:S(2)}, u32[]{:S(2)}) collective-permute-start(bf16[7,72,1152]{2,1,0:T(8,128)(2,1)} %branch_1_fun.8), channel_id=1, source_target_pairs={{0,1},{1,0},{2,3},{3,2},{4,5},{5,4},{6,7},{7,6},{8,9},{9,8},{10,11... | collective-permute-start | bytes 3483656 | tf_op jit(solution)/shard_map/cond/branch_1_fun/ppermute | solution.py:20
  33.7 7.4 %collective-permute-start.7 = (bf16[72,1152]{1,0:T(8,128)(2,1)S(1)}, bf16[72,1152]{1,0:T(8,128)(2,1)}, u32[]{:S(2)}, u32[]{:S(2)}) collective-permute-start(bf16[72,1152]{1,0:T(8,128)(2,1)S(1)} %collective-permute-done.4.refs_6_), channel_id=1, source_target_pairs={{0,6},{2,0},{4,2},{6,4},{1,7},{3,1},{5,3},{7,5},{8,14},{10,8},{12,... | collective-permute-start | bytes 497672 | tf_op jit(solution)/shard_map/cond/branch_1_fun/ppermute | solution.py:20
  41.2 1.7 %collective-permute-start.8 = (bf16[72,1152]{1,0:T(8,128)(2,1)}, bf16[72,1152]{1,0:T(8,128)(2,1)}, u32[]{:S(2)}, u32[]{:S(2)}) collective-permute-start(bf16[72,1152]{1,0:T(8,128)(2,1)} %collective-permute-done.7), channel_id=1, source_target_pairs={{0,1},{1,0},{2,3},{3,2},{4,5},{5,4},{6,7},{7,6},{8,9},{9,8},{10,11... | collective-permute-start | bytes 497672 | tf_op jit(solution)/shard_map/cond/branch_1_fun/ppermute | solution.py:20
  42.9 6.3 %copy-start.1 = (bf16[1,320,1152]{2,1,0:T(8,128)(2,1)S(1)}, bf16[1,320,1152]{2,1,0:T(8,128)(2,1)}, u32[]{:S(2)}) copy-start(bf16[1,320,1152]{2,1,0:T(8,128)(2,1)} %param.12) | copy-start | bytes 2211844
  44.5 17.7 %collective-permute-start.23 = (bf16[160,1152]{1,0:T(8,128)(2,1)}, bf16[160,1152]{1,0:T(8,128)(2,1)S(1)}, u32[]{:S(2)}, u32[]{:S(2)}) collective-permute-start(bf16[160,1152]{1,0:T(8,128)(2,1)} %slice.7), channel_id=1, source_target_pairs={{0,48},{16,0},{32,16},{48,32},{1,49},{17,1},{33,17},{49,33},{2,50}... | collective-permute-start | bytes 1105928 | tf_op jit(solution)/shard_map/ppermute | solution.py:20
  47.7 14.4 %collective-permute-start.22 = (bf16[160,1152]{1,0:T(8,128)(2,1)}, bf16[160,1152]{1,0:T(8,128)(2,1)}, u32[]{:S(2)}, u32[]{:S(2)}) collective-permute-start(bf16[160,1152]{1,0:T(8,128)(2,1)} %slice.6), channel_id=1, source_target_pairs={{0,16},{16,32},{32,48},{48,0},{1,17},{17,33},{33,49},{49,1},{2,18}... | collective-permute-start | bytes 1105928 | tf_op jit(solution)/shard_map/ppermute | solution.py:20
  54.6 7.6 %copy-start.5 = (f32[640,1152]{1,0:T(8,128)}, f32[640,1152]{1,0:T(8,128)S(1)}, u32[]{:S(2)}) copy-start(f32[640,1152]{1,0:T(8,128)S(1)} %get-tuple-element.113.z) | copy-start | bytes 8847364
  60.5 1.6 %copy-start = (f32[640,1152]{1,0:T(8,128)}, f32[640,1152]{1,0:T(8,128)S(1)}, u32[]{:S(2)}) copy-start(f32[640,1152]{1,0:T(8,128)S(1)} %get-tuple-element.112.acc) | copy-start | bytes 8847364
  70.0 6.7 %collective-permute-start.24 = (bf16[8,72,1152]{2,1,0:T(8,128)(2,1)S(1)}, bf16[8,72,1152]{2,1,0:T(8,128)(2,1)S(1)}, u32[]{:S(2)}, u32[]{:S(2)}) collective-permute-start(bf16[8,72,1152]{2,1,0:T(8,128)(2,1)S(1)} %get-tuple-element.115), channel_id=1, source_target_pairs={{0,1},{1,0},{2,3},{3,2},{4,5},{5,4},{6,7},{7,6},{8,9},{9,8},{10,11... | collective-permute-start | bytes 3981320 | tf_op jit(solution)/shard_map/ppermute | solution.py:20
  70.0 27.6 %collective-permute-start.25 = (bf16[320,1152]{1,0:T(8,128)(2,1)S(1)}, bf16[320,1152]{1,0:T(8,128)(2,1)}, u32[]{:S(2)}, u32[]{:S(2)}) collective-permute-start(bf16[320,1152]{1,0:T(8,128)(2,1)S(1)} %get-tuple-element.120), channel_id=1, source_target_pairs={{0,64},{64,0},{1,65},{65,1},{2,66},{66,2},{3,67},{67,3},{4,68},{68... | collective-permute-start | bytes 2211848 | tf_op jit(solution)/shard_map/ppermute | solution.py:20
  73.5 24.1 %collective-permute-start.26 = (bf16[320,1152]{1,0:T(8,128)(2,1)}, bf16[320,1152]{1,0:T(8,128)(2,1)S(1)}, u32[]{:S(2)}, u32[]{:S(2)}) collective-permute-start(bf16[320,1152]{1,0:T(8,128)(2,1)} %get-tuple-element.122), channel_id=1, source_target_pairs={{0,48},{16,0},{32,16},{48,32},{1,49},{17,1},{33,17},{49,33},{2,50}... | collective-permute-start | bytes 2211848 | tf_op jit(solution)/shard_map/ppermute | solution.py:20
  76.7 20.9 %collective-permute-start.27 = (bf16[320,1152]{1,0:T(8,128)(2,1)S(1)}, bf16[320,1152]{1,0:T(8,128)(2,1)S(1)}, u32[]{:S(2)}, u32[]{:S(2)}) collective-permute-start(bf16[320,1152]{1,0:T(8,128)(2,1)S(1)} %get-tuple-element.123), channel_id=1, source_target_pairs={{0,16},{16,32},{32,48},{48,0},{1,17},{17,33},{33,49},{49,1},{2,18}... | collective-permute-start | bytes 2211848 | tf_op jit(solution)/shard_map/ppermute | solution.py:20
  77.6 8.5 %collective-permute-start.9 = (bf16[72,1152]{1,0:T(8,128)(2,1)S(1)}, bf16[72,1152]{1,0:T(8,128)(2,1)S(1)}, u32[]{:S(2)}, u32[]{:S(2)}) collective-permute-start(bf16[72,1152]{1,0:T(8,128)(2,1)S(1)} %get-tuple-element.40), channel_id=1, source_target_pairs={{0,2},{2,4},{4,6},{6,0},{1,3},{3,5},{5,7},{7,1},{8,10},{10,12},{12... | collective-permute-start | bytes 497672 | tf_op jit(solution)/shard_map/cond/branch_1_fun/ppermute | solution.py:20
  77.7 8.4 %collective-permute-start.10 = (bf16[72,1152]{1,0:T(8,128)(2,1)S(1)}, bf16[72,1152]{1,0:T(8,128)(2,1)S(1)}, u32[]{:S(2)}, u32[]{:S(2)}) collective-permute-start(bf16[72,1152]{1,0:T(8,128)(2,1)S(1)} %get-tuple-element.42), channel_id=1, source_target_pairs={{0,6},{2,0},{4,2},{6,4},{1,7},{3,1},{5,3},{7,5},{8,14},{10,8},{12,... | collective-permute-start | bytes 497672 | tf_op jit(solution)/shard_map/cond/branch_1_fun/ppermute | solution.py:20
  86.2 10.7 %collective-permute-start.11 = (bf16[2,72,1152]{2,1,0:T(8,128)(2,1)S(1)}, bf16[2,72,1152]{2,1,0:T(8,128)(2,1)S(1)}, u32[]{:S(2)}, u32[]{:S(2)}) collective-permute-start(bf16[2,72,1152]{2,1,0:T(8,128)(2,1)S(1)} %get-tuple-element.43), channel_id=1, source_target_pairs={{0,2},{2,4},{4,6},{6,0},{1,3},{3,5},{5,7},{7,1},{8,10},{10,12},{12... | collective-permute-start | bytes 995336 | tf_op jit(solution)/shard_map/cond/branch_1_fun/ppermute | solution.py:20
  87.4 9.5 %collective-permute-start.12 = (bf16[2,72,1152]{2,1,0:T(8,128)(2,1)S(1)}, bf16[2,72,1152]{2,1,0:T(8,128)(2,1)S(1)}, u32[]{:S(2)}, u32[]{:S(2)}) collective-permute-start(bf16[2,72,1152]{2,1,0:T(8,128)(2,1)S(1)} %get-tuple-element.44), channel_id=1, source_target_pairs={{0,6},{2,0},{4,2},{6,4},{1,7},{3,1},{5,3},{7,5},{8,14},{10,8},{12,... | collective-permute-start | bytes 995336 | tf_op jit(solution)/shard_map/cond/branch_1_fun/ppermute | solution.py:20
  97.6 1.6 %copy-start.6 = (bf16[320,1152]{1,0:T(8,128)(2,1)}, bf16[320,1152]{1,0:T(8,128)(2,1)S(1)}, u32[]{:S(2)}) copy-start(bf16[320,1152]{1,0:T(8,128)(2,1)S(1)} %get-tuple-element.117.a) | copy-start | bytes 2211844
  97.6 26.3 %collective-permute-start.28 = (bf16[320,1152]{1,0:T(8,128)(2,1)}, bf16[320,1152]{1,0:T(8,128)(2,1)S(1)}, u32[]{:S(2)}, u32[]{:S(2)}) collective-permute-start(bf16[320,1152]{1,0:T(8,128)(2,1)} %get-tuple-element.131), channel_id=1, source_target_pairs={{0,32},{16,48},{32,0},{48,16},{1,33},{17,49},{33,1},{49,17},{2,34}... | collective-permute-start | bytes 2211848 | tf_op jit(solution)/shard_map/ppermute | solution.py:20
  99.2 24.7 %copy-start.3 = (bf16[1,320,1152]{2,1,0:T(8,128)(2,1)S(1)}, bf16[1,320,1152]{2,1,0:T(8,128)(2,1)}, u32[]{:S(2)}) copy-start(bf16[1,320,1152]{2,1,0:T(8,128)(2,1)} %param.11) | copy-start | bytes 2211844
  99.2 6.5 %collective-permute-start.13 = (bf16[72,1152]{1,0:T(8,128)(2,1)S(1)}, bf16[72,1152]{1,0:T(8,128)(2,1)S(1)}, u32[]{:S(2)}, u32[]{:S(2)}) collective-permute-start(bf16[72,1152]{1,0:T(8,128)(2,1)S(1)} %get-tuple-element.50.a), channel_id=1, source_target_pairs={{0,64},{64,0},{1,65},{65,1},{2,66},{66,2},{3,67},{67,3},{4,68},{68... | collective-permute-start | bytes 497672 | tf_op jit(solution)/shard_map/cond/branch_1_fun/ppermute | solution.py:20
  100.6 8.4 %collective-permute-start.15 = (bf16[72,1152]{1,0:T(8,128)(2,1)S(1)}, bf16[72,1152]{1,0:T(8,128)(2,1)S(1)}, u32[]{:S(2)}, u32[]{:S(2)}) collective-permute-start(bf16[72,1152]{1,0:T(8,128)(2,1)S(1)} %get-tuple-element.51), channel_id=1, source_target_pairs={{0,8},{8,0},{1,9},{9,1},{2,10},{10,2},{3,11},{11,3},{4,12},{12,4},... | collective-permute-start | bytes 497672 | tf_op jit(solution)/shard_map/cond/branch_1_fun/ppermute | solution.py:20
  102.8 8.0 %collective-permute-start.14 = (bf16[72,1152]{1,0:T(8,128)(2,1)S(1)}, bf16[72,1152]{1,0:T(8,128)(2,1)S(1)}, u32[]{:S(2)}, u32[]{:S(2)}) collective-permute-start(bf16[72,1152]{1,0:T(8,128)(2,1)S(1)} %get-tuple-element.51), channel_id=1, source_target_pairs={{0,72},{8,64},{64,8},{72,0},{1,73},{9,65},{65,9},{73,1},{2,74},{10... | collective-permute-start | bytes 497672 | tf_op jit(solution)/shard_map/cond/branch_1_fun/ppermute | solution.py:25
  110.8 10.8 %collective-permute-start.18 = (bf16[72,1152]{1,0:T(8,128)(2,1)S(1)}, bf16[72,1152]{1,0:T(8,128)(2,1)S(1)}, u32[]{:S(2)}, u32[]{:S(2)}) collective-permute-start(bf16[72,1152]{1,0:T(8,128)(2,1)S(1)} %branch_1_fun.13.a), channel_id=1, source_target_pairs={{0,48},{16,0},{32,16},{48,32},{1,49},{17,1},{33,17},{49,33},{2,50}... | collective-permute-start | bytes 497672 | tf_op jit(solution)/shard_map/cond/branch_1_fun/ppermute | solution.py:20
  112.7 9.3 %collective-permute-start.17 = (bf16[72,1152]{1,0:T(8,128)(2,1)S(1)}, bf16[72,1152]{1,0:T(8,128)(2,1)S(1)}, u32[]{:S(2)}, u32[]{:S(2)}) collective-permute-start(bf16[72,1152]{1,0:T(8,128)(2,1)S(1)} %branch_1_fun.13.a), channel_id=1, source_target_pairs={{0,16},{16,32},{32,48},{48,0},{1,17},{17,33},{33,49},{49,1},{2,18}... | collective-permute-start | bytes 497672 | tf_op jit(solution)/shard_map/cond/branch_1_fun/ppermute | solution.py:20
  112.9 10.9 %collective-permute-start.16 = (bf16[72,1152]{1,0:T(8,128)(2,1)S(1)}, bf16[72,1152]{1,0:T(8,128)(2,1)S(1)}, u32[]{:S(2)}, u32[]{:S(2)}) collective-permute-start(bf16[72,1152]{1,0:T(8,128)(2,1)S(1)} %branch_1_fun.13.a), channel_id=1, source_target_pairs={{0,32},{16,48},{32,0},{48,16},{1,33},{17,49},{33,1},{49,17},{2,34}... | collective-permute-start | bytes 497672 | tf_op jit(solution)/shard_map/cond/branch_1_fun/ppermute | solution.py:20
  123.9 3.2 %copy-start.7 = (bf16[1,320,1152]{2,1,0:T(8,128)(2,1)}, bf16[1,320,1152]{2,1,0:T(8,128)(2,1)S(1)}, u32[]{:S(2)}) copy-start(bf16[1,320,1152]{2,1,0:T(8,128)(2,1)S(1)} %get-tuple-element.96) | copy-start | bytes 2211844
  123.9 3.2 %copy-start.8 = (f32[72,1152]{1,0:T(8,128)}, f32[72,1152]{1,0:T(8,128)S(1)}, u32[]{:S(2)}) copy-start(f32[72,1152]{1,0:T(8,128)S(1)} %get-tuple-element.97) | copy-start | bytes 995332

commit v3 on v2

v3 whole, which is shorter than its diff:
```python
import jax
import jax.numpy as jnp
from jax import lax
from jax.experimental import pallas as pl
from jax.experimental.pallas import tpu as pltpu
from jax.sharding import Mesh, PartitionSpec as P

BF = jnp.bfloat16
F32 = jnp.float32
MIB = 1024 * 1024
AXES = {"ylo": 2, "z": 4, "yhi": 2, "x": 4, "core": 2}

VM = pl.BlockSpec(memory_space=pltpu.VMEM)
SM = pl.BlockSpec(memory_space=pltpu.SMEM)
ANY = pl.BlockSpec(memory_space=pl.ANY)


def shift(value, axis, step):
    n = AXES[axis]
    return lax.ppermute(value, axis, [(i, (i + step) % n) for i in range(n)])


def swap_far(value):
    pairs = [(a * 2 + b, (1 - a) * 2 + 1 - b) for a in range(2) for b in range(2)]
    return lax.ppermute(value, ("ylo", "yhi"), pairs)


def shaped(shape, dtype):
    return jax.ShapeDtypeStruct(shape, dtype)


def call(kernel, outs, specs, scratch=(), vmem=48, out_specs=None, flops=1024):
    return pl.pallas_call(
        kernel,
        out_shape=outs,
        in_specs=specs,
        out_specs=out_specs or [VM] * len(outs),
        scratch_shapes=list(scratch),
        compiler_params=pltpu.CompilerParams(vmem_limit_bytes=vmem * MIB),
        cost_estimate=pl.CostEstimate(flops=flops, bytes_accessed=1024, transcendentals=0),
    )


def inverse_length(rows):
    return 1.0 / jnp.sqrt(jnp.sum(rows * rows, axis=-1, keepdims=True) + 1e-06)


def project(grad, rows):
    inv = inverse_length(rows)
    unit = rows * inv
    inner = jnp.sum(unit * grad, axis=-1, keepdims=True)
    return (grad - unit * inner) * inv


def half_kernel(w, out):
    half = w[...].astype(BF)
    for k in range(8):
        out[k] = half


def unit_kernel(img, first, second):
    for at, out in ((0, first), (160, second)):
        rows = img[pl.ds(at, 160), :].astype(F32)
        out[...] = (rows * inverse_length(rows)).astype(BF)


def text_kernel(at, near_core, far_core, txt, txt_far, w_full, z, n_txt, mine, other, rows, sems):
    copies = [
        pltpu.make_async_copy(near_core, mine, sems.at[0]),
        pltpu.make_async_copy(far_core, other, sems.at[1]),
        pltpu.make_async_copy(txt, rows.at[pl.ds(0, 320)], sems.at[2]),
        pltpu.make_async_copy(txt_far, rows.at[pl.ds(320, 320)], sems.at[3]),
    ]
    for c in copies:
        c.start()
    for c in copies[:2]:
        c.wait()
    core = at[1]
    for k in range(8):
        a, b = mine[k].astype(F32), other[k].astype(F32)
        first = jnp.where(core == 0, a, b)
        second = jnp.where(core == 0, b, a)
        w_full[pl.ds(k * 144, 144), :] = jnp.concatenate([first, second], axis=0).astype(BF)
    for c in copies[2:]:
        c.wait()
    out = jnp.dot(rows[...], w_full[...], preferred_element_type=F32)
    z[...] = out
    n_txt[...] = (out * inverse_length(out)).astype(BF)


def logit_gradient(scal, img_rows, txt_rows):
    logits = scal[0] * lax.dot_general(
        img_rows, txt_rows, (((1,), (1,)), ((), ())), preferred_element_type=F32
    ) + scal[1]
    return 1.0 / (1.0 + jnp.exp(-logits))


def near_kernel(scal, n_own0, n_own1, n_a0, n_a1, n_b0, n_b1, n_txt, grad, acc, rows):
    for k, part in enumerate((n_own0, n_own1, n_a0, n_a1, n_b0, n_b1)):
        rows[pl.ds(k * 160, 160), :] = part[...]
    g = logit_gradient(scal, rows[...], n_txt[...])
    row_ids = lax.broadcasted_iota(jnp.int32, g.shape, 0)
    col_ids = lax.broadcasted_iota(jnp.int32, g.shape, 1)
    g = g - jnp.where((row_ids == col_ids) & (row_ids < 320), 1.0, 0.0)
    grad[...] = g.astype(BF)
    acc[...] = lax.dot_general(
        grad[...], rows[...], (((0,), (0,)), ((), ())), preferred_element_type=F32
    )


def far_kernel(at, scal, n_c0, n_c1, n_txt, acc, z, txt, txt_far, grad, g_own, g_far, mine, other, rows, feat, wide):
    rows[pl.ds(0, 160), :] = n_c0[...]
    rows[pl.ds(160, 160), :] = n_c1[...]
    feat[pl.ds(0, 320), :] = txt[...]
    feat[pl.ds(320, 320), :] = txt_far[...]
    grad[...] = logit_gradient(scal, rows[...], n_txt[...]).astype(BF)
    total = scal[0] * (
        acc[...]
        + lax.dot_general(grad[...], rows[...], (((0,), (0,)), ((), ())), preferred_element_type=F32)
    )
    g_own[...] = total[:320].astype(BF)
    g_far[...] = total[320:].astype(BF)
    dz = project(total, z[...]).astype(BF)
    wide[...] = lax.dot_general(
        feat[...], dz, (((0,), (0,)), ((), ())), preferred_element_type=F32
    )
    core = at[1]
    for j in range(8):
        a = pl.multiple_of((2 * j + core) * 72, 8)
        b = pl.multiple_of((2 * j + 1 - core) * 72, 8)
        mine[j] = wide[pl.ds(a, 72), :].astype(BF)
        other[j] = wide[pl.ds(b, 72), :].astype(BF)


def part_kernel(scal, grad, grad_c, n_txt, part_a, part_b, part_c):
    out = scal[0] * jnp.dot(grad[pl.ds(320, 640), :], n_txt[...], preferred_element_type=F32)
    part_a[...] = out[:320].astype(BF)
    part_b[...] = out[320:].astype(BF)
    part_c[...] = (scal[0] * jnp.dot(grad_c[...], n_txt[...], preferred_element_type=F32)).astype(BF)


def part_own_kernel(scal, grad, n_txt, part_own):
    part_own[...] = (
        scal[0] * jnp.dot(grad[pl.ds(0, 320), :], n_txt[...], preferred_element_type=F32)
    ).astype(BF)


def core_sum_kernel(a, b, out):
    out[...] = (a[...].astype(F32) + b[...].astype(F32)).astype(BF)


def plane_sum_kernel(got, out):
    out[...] = jnp.sum(got[...].astype(F32), axis=0).astype(BF)


def quad_sum_kernel(a, b, c, d, out):
    total = (a[...].astype(F32) + b[...].astype(F32)) + (c[...].astype(F32) + d[...].astype(F32))
    out[...] = total.astype(out.dtype)


def image_out_kernel(img, a, b, c, d, out):
    grad = (a[...].astype(F32) + b[...].astype(F32)) + (c[...].astype(F32) + d[...].astype(F32))
    out[...] = project(grad, img[...].astype(F32)).astype(BF)


def text_out_kernel(z, a, b, w_full, out):
    grad = a[...].astype(F32) + b[...].astype(F32)
    dz = project(grad, z[pl.ds(0, 320), :]).astype(BF)
    out[...] = lax.dot_general(
        dz, w_full[...], (((1,), (1,)), ((), ())), preferred_element_type=F32
    ).astype(BF)


def exchange_plane(value):
    groups = [
        [(ylo ^ yhi) * 8 + yhi * 4 + x for yhi in range(2) for x in range(4)] for ylo in range(2)
    ]
    return lax.all_to_all(
        value, ("ylo", "yhi", "x"), split_axis=0, concat_axis=0, axis_index_groups=groups, tiled=True
    )


BLOCK = shaped((320, 1152), BF)


def stack_of(*lead):
    return shaped((*lead, 72, 1152), BF)


def on_device(img_emb, txt_feat, w_txt, t_log, bias):
    img, txt = img_emb[0], txt_feat[0]
    at = jnp.stack([lax.axis_index("yhi"), lax.axis_index("core")]).astype(jnp.int32)
    scal = jnp.concatenate([jnp.exp(t_log), bias])
    block = BLOCK

    txt_far = shift(txt, "ylo", 1)
    (pieces,) = call(half_kernel, [stack_of(8)], [VM])(w_txt)
    img_a, img_b = shift(img, "z", 1), shift(img, "z", -1)
    near_core, img_a, img_b, txt_far = lax.optimization_barrier(
        (exchange_plane(pieces), img_a, img_b, txt_far)
    )
    far_core = shift(near_core, "core", 1)
    half = shaped((160, 1152), BF)
    n_a = call(unit_kernel, [half, half], [VM])(img_a)
    n_b = call(unit_kernel, [half, half], [VM])(img_b)
    n_c = shift(n_a[0], "z", 1), shift(n_b[1], "z", -1)
    n_own = call(unit_kernel, [half, half], [VM])(img)

    w_full, z, n_txt = call(
        text_kernel,
        [shaped((1152, 1152), BF), shaped((640, 1152), F32), shaped((640, 1152), BF)],
        [SM] + [ANY] * 4,
        [
            pltpu.VMEM((8, 72, 1152), BF),
            pltpu.VMEM((8, 72, 1152), BF),
            pltpu.VMEM((640, 1152), BF),
            pltpu.SemaphoreType.DMA((4,)),
        ],
    )(at, near_core, far_core, txt, txt_far)

    grad, acc = call(
        near_kernel,
        [shaped((960, 640), BF), shaped((640, 1152), F32)],
        [SM] + [VM] * 7,
        [pltpu.VMEM((960, 1152), BF)],
    )(scal, *n_own, *n_a, *n_b, n_txt)
    grad_c, g_own, g_far, mine, other = call(
        far_kernel,
        [shaped((320, 640), BF), block, block, stack_of(8), stack_of(8)],
        [SM, SM] + [VM] * 7,
        [pltpu.VMEM((320, 1152), BF), pltpu.VMEM((640, 1152), BF), pltpu.VMEM((1152, 1152), F32)],
    )(at, scal, *n_c, n_txt, acc, z, txt, txt_far)

    got_core = shift(other, "core", 1)
    g_got = shift(g_far, "ylo", 1)
    part_a, part_b, part_c = call(part_kernel, [block] * 3, [SM] + [VM] * 3)(
        scal, grad, grad_c, n_txt
    )
    got_a, got_b = shift(part_a, "z", -1), shift(part_b, "z", 1)
    got_c = shift(part_c, "z", 2)
    (both,) = call(core_sum_kernel, [stack_of(8)], [VM] * 2)(mine, got_core)
    (one,) = call(plane_sum_kernel, [stack_of()], [VM])(exchange_plane(both))
    (pair,) = call(core_sum_kernel, [stack_of()], [VM] * 2)(one, shift(one, "ylo", 1))
    got_a, got_b, got_c, g_got, pair = lax.optimization_barrier((got_a, got_b, got_c, g_got, pair))
    (part_own,) = call(part_own_kernel, [block], [SM] + [VM] * 2, flops=1 << 30)(scal, grad, n_txt)
    (d_feat,) = call(text_out_kernel, [block], [VM] * 4, flops=1 << 31)(z, g_own, g_got, w_full)
    (d_img,) = call(image_out_kernel, [block], [VM] * 5, flops=1 << 30)(img, part_own, got_c, got_a, got_b)
    (d_weight,) = call(quad_sum_kernel, [shaped((72, 1152), F32)], [VM] * 4)(
        pair, shift(pair, "z", 2), shift(pair, "z", 1), shift(pair, "z", -1)
    )
    return (d_img[None], d_feat[None], d_weight)


def solution(mesh):
    fine = Mesh(mesh.devices.reshape(2, 4, 2, 4, 2), tuple(AXES))
    dp, fsdp = ("ylo", "z"), ("yhi", "x", "core")
    placed = (P(fsdp, dp, None), P(fsdp, dp, None), P(fsdp, None), P(), P())
    return jax.shard_map(
        on_device,
        mesh=fine,
        in_specs=placed,
        out_specs=(P(fsdp, dp, None), P(fsdp, dp, None), P(fsdp, None)),
        check_vma=False,
    )
```

time: 128 us -> 138 us (1.078)
  starting transfers between devices: 42.2 us -> 27.3 us
  waiting for transfers between devices: 41.3 us -> 52 us
  local copies, waits for them, and re-layouts: 5.26 us -> 13.9 us
  Pallas kernels: 36 us -> 41.3 us
    ppermute x27 -> x15, starting transfers between devices: 38.9 us -> 13.7 us  [shift(): return lax.ppermute(value, axis, [(i, (i + step) % n) for i in range(n)])]
    all_to_all x0 -> x2, starting transfers between devices: none -> 13.7 us  [exchange_plane(): lax.all_to_all(value, ('ylo', 'yhi', 'x'), split_axis=0, concat_axis=0, a...]
    all_to_all x0 -> x2, waiting for transfers between devices: none -> 12.4 us  [exchange_plane(): lax.all_to_all(value, ('ylo', 'yhi', 'x'), split_axis=0, concat_axis=0, a...]
    unnamed x18 -> x52, local copies, waits for them, and re-layouts: 3.73 us -> 13.9 us
    ppermute x2 -> x0, starting transfers between devices: 3.32 us -> none  [swap_far(): return lax.ppermute(value, ('ylo', 'yhi'), pairs)]
    ppermute x2 -> x0, waiting for transfers between devices: 3.14 us -> none  [swap_far(): return lax.ppermute(value, ('ylo', 'yhi'), pairs)]
    pallas_call x1, Pallas kernels: 7.88 us -> 9.93 us  [on_device(): call(far_kernel, [shaped((320, 640), BF), block, block, stack_of(8), stac...]
    pallas_call x1, Pallas kernels: 5.94 us -> 7.5 us  [on_device(): call(near_kernel, [shaped((960, 640), BF), shaped((640, 1152), F32)], [SM...]
  transfers between devices with their start and end apart: 29 -> 17, of which waited for: 15 -> 6; matrix products, arithmetic and copies ran while one was open for 0% -> 0% of each run, Pallas kernels for 20% -> 21%
where the time goes in v3:
time: 138 us; the launch traced here: 137 us
  waiting for transfers between devices  52 us (38%)
  Pallas kernels  41.3 us (30%)
  starting transfers between devices  27.3 us (20%)
  local copies, waits for them, and re-layouts  13.9 us (10%)
  between operations  2.19 us (2%)
    ppermute x15, waiting for transfers between devices, shift(): return lax.ppermute(value, axis, [(i, (i + step) % n) for i in range(n)])  39.6 us
    unnamed x52, local copies, waits for them, and re-layouts  13.9 us
    ppermute x15, starting transfers between devices, shift(): return lax.ppermute(value, axis, [(i, (i + step) % n) for i in range(n)])  13.7 us
    all_to_all x2, starting transfers between devices, exchange_plane(): lax.all_to_all(value, ('ylo', 'yhi', 'x'), split_axis=0, concat_axis=0, a...  13.7 us
    all_to_all x2, waiting for transfers between devices, exchange_plane(): lax.all_to_all(value, ('ylo', 'yhi', 'x'), split_axis=0, concat_axis=0, a...  12.4 us
    pallas_call x1, Pallas kernels, on_device(): call(far_kernel, [shaped((320, 640), BF), block, block, stack_of(8), stac...  9.93 us
    pallas_call x1, Pallas kernels, on_device(): call(near_kernel, [shaped((960, 640), BF), shaped((640, 1152), F32)], [SM...  7.5 us
    pallas_call x1, Pallas kernels, on_device(): call(text_kernel, [shaped((1152, 1152), BF), shaped((640, 1152), F32), sh...  6.39 us
  transfers between devices with their start and end apart: 17, of which 6 were waited for; matrix products, arithmetic and copies ran while one was open for 0% of the time, Pallas kernels for 21%

profile of v3, /device:TPU:0, one launch (start us, length us, event | category | flops | bytes accessed | tf_op | source)
XLA Modules:
  0.0 136.9 jit_solution(13398153608047921750)
XLA Ops:
  0.6 1.0 copy-done.22
  1.6 1.2 shard_map.77
  2.8 7.0 %all-to-all-start = ((bf16[8,72,1152]{2,1,0:T(8,128)(2,1)}), bf16[8,72,1152]{2,1,0:T(8,128)(2,1)S(1)}, u32[]{:S(2)}, u32[]{:S(2)}) async-start(bf16[8,72,1152]{2,1,0:T(8,128)(2,1)} %shard_map.77), calls=%async_computation | async-start | bytes 2654208 | tf_op jit(solution)/shard_map/all_to_all | solution.py:178
  9.8 4.1 %collective-permute-start.1 = (bf16[320,1152]{1,0:T(8,128)(2,1)S(1)}, bf16[320,1152]{1,0:T(8,128)(2,1)S(1)}, u32[]{:S(2)}, u32[]{:S(2)}) collective-permute-start(bf16[320,1152]{1,0:T(8,128)(2,1)S(1)} %bitcast.9), channel_id=1, source_target_pairs={{0,48},{16,0},{32,16},{48,32},{1,49},{17,1},{33,17},{49,33},{2,50}... | collective-permute-start | bytes 2211848 | tf_op jit(solution)/shard_map/ppermute | solution.py:20
  13.9 0.1 collective-permute-start.2
  14.0 15.3 %collective-permute-done.1.img = bf16[320,1152]{1,0:T(8,128)(2,1)S(1)} collective-permute-done((bf16[320,1152]{1,0:T(8,128)(2,1)S(1)}, bf16[320,1152]{1,0:T(8,128)(2,1)S(1)}, u32[]{:S(2)}, u32[]{:S(2)}) %collective-permute-start.1) | collective-permute-done | bytes 737312 | tf_op jit(solution)/shard_map/ppermute | solution.py:20
  29.3 0.9 copy-done.8
  30.2 2.5 %collective-permute-done.img = bf16[320,1152]{1,0:T(8,128)(2,1)S(1)} collective-permute-done((bf16[320,1152]{1,0:T(8,128)(2,1)S(1)}, bf16[320,1152]{1,0:T(8,128)(2,1)S(1)}, u32[]{:S(2)}, u32[]{:S(2)}) %collective-permute-start) | collective-permute-done | bytes 737312 | tf_op jit(solution)/shard_map/ppermute | solution.py:20
  32.8 0.9 copy-done.10
  33.7 1.1 copy-done.11
  34.8 1.0 shard_map.78
  35.7 0.7 copy-done.14
  36.5 1.1 copy-done.9
  37.6 1.0 shard_map.79
  38.6 0.8 copy-done.16
  39.3 3.2 %collective-permute-start.5 = (bf16[160,1152]{1,0:T(8,128)(2,1)}, bf16[160,1152]{1,0:T(8,128)(2,1)}, u32[]{:S(2)}, u32[]{:S(2)}) collective-permute-start(bf16[160,1152]{1,0:T(8,128)(2,1)} %get-tuple-element.38.n_b1), channel_id=1, source_target_pairs={{0,48},{16,0},{32,16},{48,32},{1,49},{17,1},{33,17},{49,33},{2,50}... | collective-permute-start | bytes 1105928 | tf_op jit(solution)/shard_map/ppermute | solution.py:20
  42.5 0.3 shard_map.76
  42.8 0.0 copy-start.18
  42.8 0.7 copy-done.18
  43.6 0.7 copy-done.20
  45.6 0.1 pad_maximum_fusion.scal
  45.7 0.1 pad_add_fusion.at
  45.8 6.4 %shard_map.80 = (bf16[1152,1152]{1,0:T(8,128)(2,1)}, f32[640,1152]{1,0:T(8,128)}, bf16[640,1152]{1,0:T(8,128)(2,1)S(1)}) custom-call(s32[2]{0:T(128)S(1)} %pad_add_fusion.at, bf16[8,72,1152]{2,1,0:T(8,128)(2,1)S(1)} %all-to-all-done.near_core, bf16[8,72,1152]{2,1,0:T(8,128)(2,1)} %collective-permute-done.3.far_core, bf16[320,1152]{1,0:T(8,128)(2,1)S(1)} %bitcast.7, ...), custom_call_target="tpu_custom_call" | custom-call | flops 1024 | bytes 1024 | tf_op jit(solution)/shard_map/pallas_call | solution.py:209
  52.3 7.5 %shard_map.81 = (bf16[960,640]{1,0:T(8,128)(2,1)S(1)}, f32[640,1152]{1,0:T(8,128)}) custom-call(f32[2]{0:T(128)S(1)} %pad_maximum_fusion.scal, bf16[160,1152]{1,0:T(8,128)(2,1)S(1)} %copy-done.19, bf16[160,1152]{1,0:T(8,128)(2,1)S(1)} %copy-done.21, bf16[160,1152]{1,0:T(8,128)(2,1)} %get-tuple-element.34.n_a0, bf16[160,1152]{1,0:T(8,128)(2,1)S(1)} %copy-done.15, ...), custom_call_target="tpu_custom_call" | custom-call | flops 1024 | bytes 1024 | tf_op jit(solution)/shard_map/pallas_call | solution.py:221
  59.8 9.9 %shard_map.83 = (bf16[320,640]{1,0:T(8,128)(2,1)S(1)}, bf16[320,1152]{1,0:T(8,128)(2,1)S(1)}, bf16[320,1152]{1,0:T(8,128)(2,1)}, bf16[8,72,1152]{2,1,0:T(8,128)(2,1)S(1)}, bf16[8,72,1152]{2,1,0:T(8,128)(2,1)}) custom-call(s32[2]{0:T(128)S(1)} %pad_add_fusion.at, f32[2]{0:T(128)S(1)} %pad_maximum_fusion.scal, bf16[160,1152]{1,0:T(8,128)(2,1)} %collective-permute-done.4.n_c0, ...), custom_call_target="tpu_custom_call" | custom-call | flops 1024 | bytes 1024 | tf_op jit(solution)/shard_map/pallas_call | solution.py:227
  69.7 0.7 copy-done.12
  70.5 0.9 copy-done.24
  71.4 3.3 %collective-permute-done.10.b = bf16[8,72,1152]{2,1,0:T(8,128)(2,1)S(1)} collective-permute-done((bf16[8,72,1152]{2,1,0:T(8,128)(2,1)}, bf16[8,72,1152]{2,1,0:T(8,128)(2,1)S(1)}, u32[]{:S(2)}, u32[]{:S(2)}) %collective-permute-start.10) | collective-permute-done | bytes 1327136 | tf_op jit(solution)/shard_map/ppermute | solution.py:20
  74.6 0.3 shard_map.85
  74.9 1.1 copy-done.2
  76.0 6.7 %all-to-all-start.1 = ((bf16[8,72,1152]{2,1,0:T(8,128)(2,1)}), bf16[8,72,1152]{2,1,0:T(8,128)(2,1)S(1)}, u32[]{:S(2)}, u32[]{:S(2)}) async-start(bf16[8,72,1152]{2,1,0:T(8,128)(2,1)} %copy-done.2), calls=%async_computation.1 | async-start | bytes 2654208 | tf_op jit(solution)/shard_map/all_to_all | solution.py:178
  82.7 1.3 copy-done.6
  84.0 1.0 copy-done.13
  85.0 3.5 %shard_map.84 = (bf16[320,1152]{1,0:T(8,128)(2,1)}, bf16[320,1152]{1,0:T(8,128)(2,1)}, bf16[320,1152]{1,0:T(8,128)(2,1)}) custom-call(f32[2]{0:T(128)S(1)} %pad_maximum_fusion.scal, bf16[960,640]{1,0:T(8,128)(2,1)S(1)} %copy-done.6, bf16[320,640]{1,0:T(8,128)(2,1)S(1)} %copy-done.13, bf16[640,1152]{1,0:T(8,128)(2,1)S(1)} %copy-done.1), custom_call_target="tpu_custom_call" | custom-call | flops 1024 | bytes 1024 | tf_op jit(solution)/shard_map/pallas_call | solution.py:236
  88.5 2.0 %collective-permute-start.7 = (bf16[320,1152]{1,0:T(8,128)(2,1)}, bf16[320,1152]{1,0:T(8,128)(2,1)}, u32[]{:S(2)}, u32[]{:S(2)}) collective-permute-start(bf16[320,1152]{1,0:T(8,128)(2,1)} %get-tuple-element.47), channel_id=1, source_target_pairs={{0,16},{16,32},{32,48},{48,0},{1,17},{17,33},{33,49},{49,1},{2,18}... | collective-permute-start | bytes 2211848 | tf_op jit(solution)/shard_map/ppermute | solution.py:20
  90.5 12.4 %all-to-all-done.1.got = bf16[8,72,1152]{2,1,0:T(8,128)(2,1)S(1)} async-done(((bf16[8,72,1152]{2,1,0:T(8,128)(2,1)}), bf16[8,72,1152]{2,1,0:T(8,128)(2,1)S(1)}, u32[]{:S(2)}, u32[]{:S(2)}) %all-to-all-start.1) | async-done | bytes 1327136 | tf_op jit(solution)/shard_map/all_to_all | solution.py:178
  102.9 0.2 shard_map.86.a
  103.1 0.1 collective-permute-start.11
  103.2 1.0 copy-done.7
  104.2 1.3 shard_map.82.a
  105.5 6.4 %collective-permute-done.11.b = bf16[72,1152]{1,0:T(8,128)(2,1)S(1)} collective-permute-done((bf16[72,1152]{1,0:T(8,128)(2,1)S(1)}, bf16[72,1152]{1,0:T(8,128)(2,1)S(1)}, u32[]{:S(2)}, u32[]{:S(2)}) %collective-permute-start.11) | collective-permute-done | bytes 165920 | tf_op jit(solution)/shard_map/ppermute | solution.py:20
  112.1 12.0 %collective-permute-done.7.d = bf16[320,1152]{1,0:T(8,128)(2,1)} collective-permute-done((bf16[320,1152]{1,0:T(8,128)(2,1)}, bf16[320,1152]{1,0:T(8,128)(2,1)}, u32[]{:S(2)}, u32[]{:S(2)}) %collective-permute-start.7) | collective-permute-done | bytes 737312 | tf_op jit(solution)/shard_map/ppermute | solution.py:20
  124.1 1.5 %collective-permute-start.14 = (bf16[72,1152]{1,0:T(8,128)(2,1)S(1)}, bf16[72,1152]{1,0:T(8,128)(2,1)S(1)}, u32[]{:S(2)}, u32[]{:S(2)}) collective-permute-start(bf16[72,1152]{1,0:T(8,128)(2,1)S(1)} %shard_map.87.a), channel_id=1, source_target_pairs={{0,48},{16,0},{32,16},{48,32},{1,49},{17,1},{33,17},{49,33},{2,50}... | collective-permute-start | bytes 497672 | tf_op jit(solution)/shard_map/ppermute | solution.py:20
  125.6 0.6 collective-permute-start.13
  126.1 2.0 %collective-permute-start.12 = (bf16[72,1152]{1,0:T(8,128)(2,1)S(1)}, bf16[72,1152]{1,0:T(8,128)(2,1)S(1)}, u32[]{:S(2)}, u32[]{:S(2)}) collective-permute-start(bf16[72,1152]{1,0:T(8,128)(2,1)S(1)} %shard_map.87.a), channel_id=1, source_target_pairs={{0,32},{16,48},{32,0},{48,16},{1,33},{17,49},{33,1},{49,17},{2,34}... | collective-permute-start | bytes 497672 | tf_op jit(solution)/shard_map/ppermute | solution.py:20
  128.2 3.3 %shard_map.88 = bf16[320,1152]{1,0:T(8,128)(2,1)} custom-call(bf16[320,1152]{1,0:T(8,128)(2,1)S(1)} %bitcast.12, bf16[320,1152]{1,0:T(8,128)(2,1)S(1)} %shard_map.82.a, bf16[320,1152]{1,0:T(8,128)(2,1)} %collective-permute-done.8.b, bf16[320,1152]{1,0:T(8,128)(2,1)} %collective-permute-done.6.c, bf16[320,1152]{1,0:T(8,128)(2,1)} %collective-permute-done.7.d), custom_call_target="tpu_custom_call" | custom-call | flops 1073741824 | bytes 1024 | tf_op jit(solution)/shard_map/pallas_call | solution.py:247
  131.5 4.6 %shard_map.89 = bf16[320,1152]{1,0:T(8,128)(2,1)} custom-call(f32[640,1152]{1,0:T(8,128)} %get-tuple-element.44.z, bf16[320,1152]{1,0:T(8,128)(2,1)S(1)} %copy-done.25, bf16[320,1152]{1,0:T(8,128)(2,1)} %collective-permute-done.9.b, bf16[1152,1152]{1,0:T(8,128)(2,1)S(1)} %copy-done.23), custom_call_target="tpu_custom_call" | custom-call | flops 2147483648 | bytes 1024 | tf_op jit(solution)/shard_map/pallas_call | solution.py:246
  136.1 0.8 shard_map.90
  (55 shorter events, 0.2 us)
Async XLA Ops:
  0.6 1.0 copy-start.22
  2.8 7.0 %copy-start.4 = (bf16[1,320,1152]{2,1,0:T(8,128)(2,1)S(1)}, bf16[1,320,1152]{2,1,0:T(8,128)(2,1)}, u32[]{:S(2)}) copy-start(bf16[1,320,1152]{2,1,0:T(8,128)(2,1)} %param.5) | copy-start | bytes 2211844
  2.8 11.1 %copy-start.3 = (bf16[1,320,1152]{2,1,0:T(8,128)(2,1)S(1)}, bf16[1,320,1152]{2,1,0:T(8,128)(2,1)}, u32[]{:S(2)}) copy-start(bf16[1,320,1152]{2,1,0:T(8,128)(2,1)} %param.6) | copy-start | bytes 2211844
  2.8 30.8 %all-to-all-start = ((bf16[8,72,1152]{2,1,0:T(8,128)(2,1)}), bf16[8,72,1152]{2,1,0:T(8,128)(2,1)S(1)}, u32[]{:S(2)}, u32[]{:S(2)}) async-start(bf16[8,72,1152]{2,1,0:T(8,128)(2,1)} %shard_map.77), calls=%async_computation | async-start | bytes 2654208 | tf_op jit(solution)/shard_map/all_to_all | solution.py:178
  9.8 19.6 %collective-permute-start.1 = (bf16[320,1152]{1,0:T(8,128)(2,1)S(1)}, bf16[320,1152]{1,0:T(8,128)(2,1)S(1)}, u32[]{:S(2)}, u32[]{:S(2)}) collective-permute-start(bf16[320,1152]{1,0:T(8,128)(2,1)S(1)} %bitcast.9), channel_id=1, source_target_pairs={{0,48},{16,0},{32,16},{48,32},{1,49},{17,1},{33,17},{49,33},{2,50}... | collective-permute-start | bytes 2211848 | tf_op jit(solution)/shard_map/ppermute | solution.py:20
  13.9 18.9 %collective-permute-start = (bf16[320,1152]{1,0:T(8,128)(2,1)S(1)}, bf16[320,1152]{1,0:T(8,128)(2,1)S(1)}, u32[]{:S(2)}, u32[]{:S(2)}) collective-permute-start(bf16[320,1152]{1,0:T(8,128)(2,1)S(1)} %bitcast.10), channel_id=1, source_target_pairs={{0,16},{16,32},{32,48},{48,0},{1,17},{17,33},{33,49},{49,1},{2,18}... | collective-permute-start | bytes 2211848 | tf_op jit(solution)/shard_map/ppermute | solution.py:20
  13.9 19.7 %collective-permute-start.2 = (bf16[320,1152]{1,0:T(8,128)(2,1)S(1)}, bf16[320,1152]{1,0:T(8,128)(2,1)S(1)}, u32[]{:S(2)}, u32[]{:S(2)}) collective-permute-start(bf16[320,1152]{1,0:T(8,128)(2,1)S(1)} %bitcast.6), channel_id=1, source_target_pairs={{0,64},{64,0},{1,65},{65,1},{2,66},{66,2},{3,67},{67,3},{4,68},{68... | collective-permute-start | bytes 2211848 | tf_op jit(solution)/shard_map/ppermute | solution.py:20
  29.3 0.9 copy-start.8
  32.8 0.9 copy-start.10
  33.6 12.2 %collective-permute-start.3 = (bf16[8,72,1152]{2,1,0:T(8,128)(2,1)S(1)}, bf16[8,72,1152]{2,1,0:T(8,128)(2,1)}, u32[]{:S(2)}, u32[]{:S(2)}) collective-permute-start(bf16[8,72,1152]{2,1,0:T(8,128)(2,1)S(1)} %all-to-all-done.near_core), channel_id=1, source_target_pairs={{0,1},{1,0},{2,3},{3,2},{4,5},{5,4},{6,7},{7,6},{8,9},{9,8},{10,11... | collective-permute-start | bytes 3981320 | tf_op jit(solution)/shard_map/ppermute | solution.py:20
  33.6 1.1 copy-start.11
  35.7 0.7 copy-start.14
  36.5 23.3 %collective-permute-start.4 = (bf16[160,1152]{1,0:T(8,128)(2,1)}, bf16[160,1152]{1,0:T(8,128)(2,1)}, u32[]{:S(2)}, u32[]{:S(2)}) collective-permute-start(bf16[160,1152]{1,0:T(8,128)(2,1)} %get-tuple-element.34.n_a0), channel_id=1, source_target_pairs={{0,16},{16,32},{32,48},{48,0},{1,17},{17,33},{33,49},{49,1},{2,18}... | collective-permute-start | bytes 1105928 | tf_op jit(solution)/shard_map/ppermute | solution.py:20
  36.5 1.1 copy-start.9
  38.6 0.8 copy-start.16
  39.3 20.5 %collective-permute-start.5 = (bf16[160,1152]{1,0:T(8,128)(2,1)}, bf16[160,1152]{1,0:T(8,128)(2,1)}, u32[]{:S(2)}, u32[]{:S(2)}) collective-permute-start(bf16[160,1152]{1,0:T(8,128)(2,1)} %get-tuple-element.38.n_b1), channel_id=1, source_target_pairs={{0,48},{16,0},{32,16},{48,32},{1,49},{17,1},{33,17},{49,33},{2,50}... | collective-permute-start | bytes 1105928 | tf_op jit(solution)/shard_map/ppermute | solution.py:20
  42.8 0.7 copy-start.18
  43.6 0.7 copy-start.20
  45.8 6.4 %copy-start.15 = (bf16[160,1152]{1,0:T(8,128)(2,1)S(1)}, bf16[160,1152]{1,0:T(8,128)(2,1)}, u32[]{:S(2)}) copy-start(bf16[160,1152]{1,0:T(8,128)(2,1)} %copy-done.14) | copy-start | bytes 1105924
  45.8 6.4 %copy-start.17 = (bf16[160,1152]{1,0:T(8,128)(2,1)S(1)}, bf16[160,1152]{1,0:T(8,128)(2,1)}, u32[]{:S(2)}) copy-start(bf16[160,1152]{1,0:T(8,128)(2,1)} %copy-done.16) | copy-start | bytes 1105924
  45.8 6.5 %copy-start.19 = (bf16[160,1152]{1,0:T(8,128)(2,1)S(1)}, bf16[160,1152]{1,0:T(8,128)(2,1)}, u32[]{:S(2)}) copy-start(bf16[160,1152]{1,0:T(8,128)(2,1)} %copy-done.18) | copy-start | bytes 1105924
  45.8 6.5 %copy-start.21 = (bf16[160,1152]{1,0:T(8,128)(2,1)S(1)}, bf16[160,1152]{1,0:T(8,128)(2,1)}, u32[]{:S(2)}) copy-start(bf16[160,1152]{1,0:T(8,128)(2,1)} %copy-done.20) | copy-start | bytes 1105924
  52.2 7.6 %copy-start = (bf16[640,1152]{1,0:T(8,128)(2,1)}, bf16[640,1152]{1,0:T(8,128)(2,1)S(1)}, u32[]{:S(2)}) copy-start(bf16[640,1152]{1,0:T(8,128)(2,1)S(1)} %get-tuple-element.41.n_txt) | copy-start | bytes 4423684
  59.8 9.9 %copy-start.5 = (bf16[960,640]{1,0:T(8,128)(2,1)}, bf16[960,640]{1,0:T(8,128)(2,1)S(1)}, u32[]{:S(2)}) copy-start(bf16[960,640]{1,0:T(8,128)(2,1)S(1)} %get-tuple-element.42.grad) | copy-start | bytes 3686404
  69.7 0.8 copy-start.12
  70.5 0.9 copy-start.24
  71.3 3.3 %collective-permute-start.10 = (bf16[8,72,1152]{2,1,0:T(8,128)(2,1)}, bf16[8,72,1152]{2,1,0:T(8,128)(2,1)S(1)}, u32[]{:S(2)}, u32[]{:S(2)}) collective-permute-start(bf16[8,72,1152]{2,1,0:T(8,128)(2,1)} %get-tuple-element.51), channel_id=1, source_target_pairs={{0,1},{1,0},{2,3},{3,2},{4,5},{5,4},{6,7},{7,6},{8,9},{9,8},{10,11... | collective-permute-start | bytes 3981320 | tf_op jit(solution)/shard_map/ppermute | solution.py:20
  74.9 1.1 copy-start.2
  76.0 6.7 %copy-start.1 = (bf16[640,1152]{1,0:T(8,128)(2,1)S(1)}, bf16[640,1152]{1,0:T(8,128)(2,1)}, u32[]{:S(2)}) copy-start(bf16[640,1152]{1,0:T(8,128)(2,1)} %copy-done) | copy-start | bytes 4423684
  76.0 26.9 %all-to-all-start.1 = ((bf16[8,72,1152]{2,1,0:T(8,128)(2,1)}), bf16[8,72,1152]{2,1,0:T(8,128)(2,1)S(1)}, u32[]{:S(2)}, u32[]{:S(2)}) async-start(bf16[8,72,1152]{2,1,0:T(8,128)(2,1)} %copy-done.2), calls=%async_computation.1 | async-start | bytes 2654208 | tf_op jit(solution)/shard_map/all_to_all | solution.py:178
  82.7 1.3 copy-start.6
  84.0 1.0 copy-start.13
  88.5 23.6 %collective-permute-start.6 = (bf16[320,1152]{1,0:T(8,128)(2,1)}, bf16[320,1152]{1,0:T(8,128)(2,1)}, u32[]{:S(2)}, u32[]{:S(2)}) collective-permute-start(bf16[320,1152]{1,0:T(8,128)(2,1)} %get-tuple-element.46), channel_id=1, source_target_pairs={{0,48},{16,0},{32,16},{48,32},{1,49},{17,1},{33,17},{49,33},{2,50}... | collective-permute-start | bytes 2211848 | tf_op jit(solution)/shard_map/ppermute | solution.py:20
  88.5 35.6 %collective-permute-start.7 = (bf16[320,1152]{1,0:T(8,128)(2,1)}, bf16[320,1152]{1,0:T(8,128)(2,1)}, u32[]{:S(2)}, u32[]{:S(2)}) collective-permute-start(bf16[320,1152]{1,0:T(8,128)(2,1)} %get-tuple-element.47), channel_id=1, source_target_pairs={{0,16},{16,32},{32,48},{48,0},{1,17},{17,33},{33,49},{49,1},{2,18}... | collective-permute-start | bytes 2211848 | tf_op jit(solution)/shard_map/ppermute | solution.py:20
  90.5 33.6 %collective-permute-start.8 = (bf16[320,1152]{1,0:T(8,128)(2,1)}, bf16[320,1152]{1,0:T(8,128)(2,1)}, u32[]{:S(2)}, u32[]{:S(2)}) collective-permute-start(bf16[320,1152]{1,0:T(8,128)(2,1)} %get-tuple-element.48), channel_id=1, source_target_pairs={{0,32},{16,48},{32,0},{48,16},{1,33},{17,49},{33,1},{49,17},{2,34}... | collective-permute-start | bytes 2211848 | tf_op jit(solution)/shard_map/ppermute | solution.py:20
  90.5 33.6 %collective-permute-start.9 = (bf16[320,1152]{1,0:T(8,128)(2,1)}, bf16[320,1152]{1,0:T(8,128)(2,1)}, u32[]{:S(2)}, u32[]{:S(2)}) collective-permute-start(bf16[320,1152]{1,0:T(8,128)(2,1)} %get-tuple-element.49), channel_id=1, source_target_pairs={{0,64},{64,0},{1,65},{65,1},{2,66},{66,2},{3,67},{67,3},{4,68},{68... | collective-permute-start | bytes 2211848 | tf_op jit(solution)/shard_map/ppermute | solution.py:20
  102.9 1.3 copy-start.7
  103.1 8.9 %collective-permute-start.11 = (bf16[72,1152]{1,0:T(8,128)(2,1)S(1)}, bf16[72,1152]{1,0:T(8,128)(2,1)S(1)}, u32[]{:S(2)}, u32[]{:S(2)}) collective-permute-start(bf16[72,1152]{1,0:T(8,128)(2,1)S(1)} %shard_map.86.a), channel_id=1, source_target_pairs={{0,64},{64,0},{1,65},{65,1},{2,66},{66,2},{3,67},{67,3},{4,68},{68... | collective-permute-start | bytes 497672 | tf_op jit(solution)/shard_map/ppermute | solution.py:20
  112.0 19.4 %copy-start.23 = (bf16[1152,1152]{1,0:T(8,128)(2,1)S(1)}, bf16[1152,1152]{1,0:T(8,128)(2,1)}, u32[]{:S(2)}) copy-start(bf16[1152,1152]{1,0:T(8,128)(2,1)} %get-tuple-element.57.w_full) | copy-start | bytes 7962628
  112.1 19.4 %copy-start.25 = (bf16[320,1152]{1,0:T(8,128)(2,1)S(1)}, bf16[320,1152]{1,0:T(8,128)(2,1)}, u32[]{:S(2)}) copy-start(bf16[320,1152]{1,0:T(8,128)(2,1)} %copy-done.24) | copy-start | bytes 2211844
  124.1 11.9 %collective-permute-start.14 = (bf16[72,1152]{1,0:T(8,128)(2,1)S(1)}, bf16[72,1152]{1,0:T(8,128)(2,1)S(1)}, u32[]{:S(2)}, u32[]{:S(2)}) collective-permute-start(bf16[72,1152]{1,0:T(8,128)(2,1)S(1)} %shard_map.87.a), channel_id=1, source_target_pairs={{0,48},{16,0},{32,16},{48,32},{1,49},{17,1},{33,17},{49,33},{2,50}... | collective-permute-start | bytes 497672 | tf_op jit(solution)/shard_map/ppermute | solution.py:20
  125.6 10.5 %collective-permute-start.13 = (bf16[72,1152]{1,0:T(8,128)(2,1)S(1)}, bf16[72,1152]{1,0:T(8,128)(2,1)S(1)}, u32[]{:S(2)}, u32[]{:S(2)}) collective-permute-start(bf16[72,1152]{1,0:T(8,128)(2,1)S(1)} %shard_map.87.a), channel_id=1, source_target_pairs={{0,16},{16,32},{32,48},{48,0},{1,17},{17,33},{33,49},{49,1},{2,18}... | collective-permute-start | bytes 497672 | tf_op jit(solution)/shard_map/ppermute | solution.py:20
  126.1 9.9 %collective-permute-start.12 = (bf16[72,1152]{1,0:T(8,128)(2,1)S(1)}, bf16[72,1152]{1,0:T(8,128)(2,1)S(1)}, u32[]{:S(2)}, u32[]{:S(2)}) collective-permute-start(bf16[72,1152]{1,0:T(8,128)(2,1)S(1)} %shard_map.87.a), channel_id=1, source_target_pairs={{0,32},{16,48},{32,0},{48,16},{1,33},{17,49},{33,1},{49,17},{2,34}... | collective-permute-start | bytes 497672 | tf_op jit(solution)/shard_map/ppermute | solution.py:20

commit v4 on v2

v4 whole, which is shorter than its diff:
```python
import jax
import jax.numpy as jnp
from jax import lax
from jax.experimental import pallas as pl
from jax.experimental.pallas import tpu as pltpu
from jax.sharding import Mesh, PartitionSpec as P

BF = jnp.bfloat16
F32 = jnp.float32
MIB = 1024 * 1024
AXES = {"ylo": 2, "z": 4, "yhi": 2, "x": 4, "core": 2}

VM = pl.BlockSpec(memory_space=pltpu.VMEM)
SM = pl.BlockSpec(memory_space=pltpu.SMEM)
ANY = pl.BlockSpec(memory_space=pl.ANY)


def shift(value, axis, step):
    n = AXES[axis]
    return lax.ppermute(value, axis, [(i, (i + step) % n) for i in range(n)])


def swap_far(value):
    pairs = [(a * 2 + b, (1 - a) * 2 + 1 - b) for a in range(2) for b in range(2)]
    return lax.ppermute(value, ("ylo", "yhi"), pairs)


def shaped(shape, dtype):
    return jax.ShapeDtypeStruct(shape, dtype)


def call(kernel, outs, specs, scratch=(), vmem=48, out_specs=None, flops=1024):
    return pl.pallas_call(
        kernel,
        out_shape=outs,
        in_specs=specs,
        out_specs=out_specs or [VM] * len(outs),
        scratch_shapes=list(scratch),
        compiler_params=pltpu.CompilerParams(vmem_limit_bytes=vmem * MIB),
        cost_estimate=pl.CostEstimate(flops=flops, bytes_accessed=1024, transcendentals=0),
    )


def inverse_length(rows):
    return 1.0 / jnp.sqrt(jnp.sum(rows * rows, axis=-1, keepdims=True) + 1e-06)


def project(grad, rows):
    inv = inverse_length(rows)
    unit = rows * inv
    inner = jnp.sum(unit * grad, axis=-1, keepdims=True)
    return (grad - unit * inner) * inv


def prepare_kernel(w, img, w_half, n_img):
    w_half[...] = w[...].astype(BF)
    rows = img[...].astype(F32)
    n_img[...] = (rows * inverse_length(rows)).astype(BF)


def pack_kernel(*refs):
    pieces, out, sems = refs[:-2], refs[-2], refs[-1]
    copies = [pltpu.make_async_copy(p, out.at[k], sems.at[k]) for k, p in enumerate(pieces)]
    for c in copies:
        c.start()
    for c in copies:
        c.wait()


def pack(*pieces):
    n = len(pieces)
    (out,) = call(
        pack_kernel, [stack_of(n)], [ANY] * n, [pltpu.SemaphoreType.DMA((n,))], out_specs=[ANY]
    )(*pieces)
    return out


def text_kernel(at, near5, far5, near3, far3, txt, txt_far, w_full, z, n_txt, mine, other, rows, sems):
    copies = [
        pltpu.make_async_copy(near5, mine.at[pl.ds(0, 5)], sems.at[0]),
        pltpu.make_async_copy(far5, other.at[pl.ds(0, 5)], sems.at[1]),
        pltpu.make_async_copy(near3, mine.at[pl.ds(5, 3)], sems.at[2]),
        pltpu.make_async_copy(far3, other.at[pl.ds(5, 3)], sems.at[3]),
        pltpu.make_async_copy(txt, rows.at[pl.ds(0, 320)], sems.at[4]),
        pltpu.make_async_copy(txt_far, rows.at[pl.ds(320, 320)], sems.at[5]),
    ]
    for c in copies:
        c.start()
    for c in copies[:4]:
        c.wait()
    yhi, x, core = at[0], at[1], at[2]
    for k in range(8):
        y_of = yhi if k < 4 else 1 - yhi
        owner = y_of * 4 + (x + 4 - (0, 1, 3, 2)[k % 4]) % 4
        a, b = mine[k].astype(F32), other[k].astype(F32)
        first = jnp.where(core == 0, a, b)
        second = jnp.where(core == 0, b, a)
        pair = jnp.concatenate([first, second], axis=0).astype(BF)
        w_full[pl.ds(pl.multiple_of(owner * 144, 16), 144), :] = pair
    for c in copies[4:]:
        c.wait()
    out = jnp.dot(rows[...], w_full[...], preferred_element_type=F32)
    z[...] = out
    n_txt[...] = (out * inverse_length(out)).astype(BF)


def logit_gradient(scal, img_rows, txt_rows):
    logits = scal[0] * lax.dot_general(
        img_rows, txt_rows, (((1,), (1,)), ((), ())), preferred_element_type=F32
    ) + scal[1]
    return 1.0 / (1.0 + jnp.exp(-logits))


def own_kernel(scal, n_img, n_txt, grad, acc):
    g = logit_gradient(scal, n_img[...], n_txt[...])
    row_ids = lax.broadcasted_iota(jnp.int32, g.shape, 0)
    col_ids = lax.broadcasted_iota(jnp.int32, g.shape, 1)
    grad[...] = (g - jnp.where(row_ids == col_ids, 1.0, 0.0)).astype(BF)
    acc[...] = lax.dot_general(
        grad[...], n_img[...], (((0,), (0,)), ((), ())), preferred_element_type=F32
    )


def rest_kernel(at, scal, n_all, n_txt, acc, z, txt, txt_far, grad, g_own, g_far, mine, other, rows, feat, wide, sems):
    copies = [
        pltpu.make_async_copy(
            n_all.at[pl.ds(pl.multiple_of((at[3] + k) % 4 * 320, 320), 320)],
            rows.at[pl.ds((k - 1) * 320, 320)],
            sems.at[k - 1],
        )
        for k in (1, 2, 3)
    ]
    copies += [
        pltpu.make_async_copy(txt, feat.at[pl.ds(0, 320)], sems.at[3]),
        pltpu.make_async_copy(txt_far, feat.at[pl.ds(320, 320)], sems.at[4]),
    ]
    for c in copies:
        c.start()
    for c in copies:
        c.wait()
    grad[...] = logit_gradient(scal, rows[...], n_txt[...]).astype(BF)
    total = scal[0] * (
        acc[...]
        + lax.dot_general(grad[...], rows[...], (((0,), (0,)), ((), ())), preferred_element_type=F32)
    )
    g_own[...] = total[:320].astype(BF)
    g_far[...] = total[320:].astype(BF)
    dz = project(total, z[...]).astype(BF)
    wide[...] = lax.dot_general(
        feat[...], dz, (((0,), (0,)), ((), ())), preferred_element_type=F32
    )
    core = at[2]
    for j in range(8):
        a = pl.multiple_of((2 * j + core) * 72, 8)
        b = pl.multiple_of((2 * j + 1 - core) * 72, 8)
        mine[j] = wide[pl.ds(a, 72), :].astype(BF)
        other[j] = wide[pl.ds(b, 72), :].astype(BF)


def part_kernel(at, scal, grad_own, grad, n_txt, parts):
    for k in range(4):
        g = grad_own[...] if k == 0 else grad[pl.ds((k - 1) * 320, 320), :]
        out = scal[0] * jnp.dot(g, n_txt[...], preferred_element_type=F32)
        parts[pl.ds(pl.multiple_of((at[3] + k) % 4 * 320, 320), 320), :] = out.astype(BF)


def core_sum_kernel(at, mine, got, *outs):
    for r, out in enumerate(outs):
        for h in range(2):
            j = h * 4 + (at[1] + r) % 4
            out[h] = (mine[j].astype(F32) + got[j].astype(F32)).astype(BF)


def x_sum_kernel(at, a, b, c, d, keep, send):
    for out, h in ((keep, at[0]), (send, 1 - at[0])):
        total = (a[h].astype(F32) + b[h].astype(F32)) + (c[h].astype(F32) + d[h].astype(F32))
        out[...] = total.astype(BF)


def pair_sum_kernel(a, b, out):
    out[...] = (a[...].astype(F32) + b[...].astype(F32)).astype(BF)


def quad_sum_kernel(a, b, c, d, out):
    total = (a[...].astype(F32) + b[...].astype(F32)) + (c[...].astype(F32) + d[...].astype(F32))
    out[...] = total.astype(out.dtype)


def image_out_kernel(img, grad, out):
    out[...] = project(grad[...].astype(F32), img[...].astype(F32)).astype(BF)


def text_out_kernel(z, a, b, w_full, out):
    grad = a[...].astype(F32) + b[...].astype(F32)
    dz = project(grad, z[pl.ds(0, 320), :]).astype(BF)
    out[...] = lax.dot_general(
        dz, w_full[...], (((1,), (1,)), ((), ())), preferred_element_type=F32
    ).astype(BF)


def apart(step, *args):
    outs = jax.eval_shape(step, *args)
    return lax.cond(
        lax.axis_index("z") < AXES["z"],
        step,
        lambda *_: tuple(jnp.zeros(o.shape, o.dtype) for o in outs),
        *args,
    )


BLOCK = shaped((320, 1152), BF)


def stack_of(*lead):
    return shaped((*lead, 72, 1152), BF)


def gather_head(w_h):
    w_y = swap_far(w_h)
    h = [shift(w_h, "x", s) for s in (1, 3, 2)]
    y = [shift(w_y, "x", s) for s in (1, 3, 2)]
    near5, near3 = pack(w_h, *h, w_y), pack(*y)
    return near5, shift(near5, "core", 1), near3, shift(near3, "core", 1)


def swap_and_parts(other, at, scal, grad_own, grad, n_txt):
    (parts,) = call(
        part_kernel, [shaped((1280, 1152), BF)], [SM, SM] + [VM] * 3, flops=1 << 31
    )(at, scal, grad_own, grad, n_txt)
    return shift(other, "core", 1), parts


def on_device(img_emb, txt_feat, w_txt, t_log, bias):
    img, txt = img_emb[0], txt_feat[0]
    at = jnp.stack([lax.axis_index(a) for a in ("yhi", "x", "core", "z")]).astype(jnp.int32)
    scal = jnp.concatenate([jnp.exp(t_log), bias])

    txt_far = shift(txt, "ylo", 1)
    w_h, n_img = call(prepare_kernel, [stack_of(), BLOCK], [VM] * 2)(w_txt, img)
    n_all = lax.all_gather(n_img, "z", axis=0, tiled=True)
    head = apart(gather_head, w_h)
    head, txt_far = lax.optimization_barrier((head, txt_far))

    w_full, z, n_txt = call(
        text_kernel,
        [shaped((1152, 1152), BF), shaped((640, 1152), F32), shaped((640, 1152), BF)],
        [SM] + [ANY] * 6,
        [
            pltpu.VMEM((8, 72, 1152), BF),
            pltpu.VMEM((8, 72, 1152), BF),
            pltpu.VMEM((640, 1152), BF),
            pltpu.SemaphoreType.DMA((6,)),
        ],
    )(at, *head, txt, txt_far)
    grad_own, acc = call(
        own_kernel, [shaped((320, 640), BF), shaped((640, 1152), F32)], [SM] + [VM] * 2
    )(scal, n_img, n_txt)
    n_all, acc = lax.optimization_barrier((n_all, acc))
    grad, g_own, g_far, mine, other = call(
        rest_kernel,
        [shaped((960, 640), BF), BLOCK, BLOCK, stack_of(8), stack_of(8)],
        [SM, SM, ANY, VM, VM, VM, ANY, ANY],
        [
            pltpu.VMEM((960, 1152), BF),
            pltpu.VMEM((640, 1152), BF),
            pltpu.VMEM((1152, 1152), F32),
            pltpu.SemaphoreType.DMA((5,)),
        ],
    )(at, scal, n_all, n_txt, acc, z, txt, txt_far)

    got_core, parts = apart(swap_and_parts, other, at, scal, grad_own, grad, n_txt)
    g_img = lax.psum_scatter(parts, "z", scatter_dimension=0, tiled=True)
    rel = call(core_sum_kernel, [stack_of(2)] * 4, [SM, VM, VM])(at, mine, got_core)
    g_got = shift(g_far, "ylo", 1)
    keep, send = call(x_sum_kernel, [stack_of()] * 2, [SM] + [VM] * 4)(
        at, rel[0], *[shift(rel[s], "x", s) for s in (1, 2, 3)]
    )
    (pair,) = call(pair_sum_kernel, [stack_of()], [VM] * 2)(keep, swap_far(send))
    (quad,) = call(pair_sum_kernel, [stack_of()], [VM] * 2)(pair, shift(pair, "ylo", 1))
    (d_feat,) = call(text_out_kernel, [BLOCK], [VM] * 4, flops=1 << 31)(z, g_own, g_got, w_full)
    (d_img,) = call(image_out_kernel, [BLOCK], [VM] * 2, flops=1 << 30)(img, g_img)
    (d_weight,) = call(quad_sum_kernel, [shaped((72, 1152), F32)], [VM] * 4)(
        quad, shift(quad, "z", 2), shift(quad, "z", 1), shift(quad, "z", -1)
    )
    return (d_img[None], d_feat[None], d_weight)


def solution(mesh):
    fine = Mesh(mesh.devices.reshape(2, 4, 2, 4, 2), tuple(AXES))
    dp, fsdp = ("ylo", "z"), ("yhi", "x", "core")
    placed = (P(fsdp, dp, None), P(fsdp, dp, None), P(fsdp, None), P(), P())
    return jax.shard_map(
        on_device,
        mesh=fine,
        in_specs=placed,
        out_specs=(P(fsdp, dp, None), P(fsdp, dp, None), P(fsdp, None)),
        check_vma=False,
    )
```

time: 128 us -> 136 us (1.062); the launches traced: 127 us -> 133 us
  starting transfers between devices: 42.2 us -> 26.9 us
  between operations: 2.11 us -> 15.5 us
  local copies, waits for them, and re-layouts: 5.26 us -> 9.43 us
  Pallas kernels: 36 us -> 39.1 us
    ppermute x27 -> x18, starting transfers between devices: 38.9 us -> 23.6 us  [shift(): return lax.ppermute(value, axis, [(i, (i + step) % n) for i in range(n)])]
    unnamed x18 -> x26, local copies, waits for them, and re-layouts: 3.73 us -> 9.43 us
    ppermute x2, waiting for transfers between devices: 3.14 us -> 5.62 us  [swap_far(): return lax.ppermute(value, ('ylo', 'yhi'), pairs)]
    pallas_call x13, Pallas kernels: 30.7 us -> 32.3 us  [the longest x1 12.4 us: on_device(): call(rest_kernel, [shaped((960, 640), BF), BLOCK, BLOCK, stack_of(8), sta...]
    ppermute x27 -> x18, waiting for transfers between devices: 38.1 us -> 36.6 us  [shift(): return lax.ppermute(value, axis, [(i, (i + step) % n) for i in range(n)])]
    slice x2 -> x0, local copies, waits for them, and re-layouts: 1.53 us -> none  [on_device(): n_c0, n_c1 = (shift(n_a[:160], 'z', 1), shift(n_b[160:], 'z', -1))]
    pallas_call x1, Pallas kernels: 5.35 us -> 6.81 us  [on_device(): call(text_kernel, [shaped((1152, 1152), BF), shaped((640, 1152), F32), sh...]
  transfers between devices with their start and end apart: 29 -> 22, of which waited for: 15 -> 13; matrix products, arithmetic and copies ran while one was open for 0% -> 0% of each run, Pallas kernels for 20% -> 18%
where the time goes in v4:
time: 136 us; the launch traced here: 133 us
  waiting for transfers between devices  42.2 us (31%)
  Pallas kernels  39.1 us (29%)
  starting transfers between devices  26.9 us (20%)
  between operations  15.5 us (11%)
  local copies, waits for them, and re-layouts  9.43 us (7%)
    ppermute x18, waiting for transfers between devices, shift(): return lax.ppermute(value, axis, [(i, (i + step) % n) for i in range(n)])  36.6 us
    ppermute x18, starting transfers between devices, shift(): return lax.ppermute(value, axis, [(i, (i + step) % n) for i in range(n)])  23.6 us
    pallas_call x1, Pallas kernels, on_device(): call(rest_kernel, [shaped((960, 640), BF), BLOCK, BLOCK, stack_of(8), sta...  12.4 us
    unnamed x26, local copies, waits for them, and re-layouts  9.43 us
    pallas_call x1, Pallas kernels, on_device(): call(text_kernel, [shaped((1152, 1152), BF), shaped((640, 1152), F32), sh...  6.81 us
    ppermute x2, waiting for transfers between devices, swap_far(): return lax.ppermute(value, ('ylo', 'yhi'), pairs)  5.62 us
    pallas_call x1, Pallas kernels, swap_and_parts(): call(part_kernel, [shaped((1280, 1152), BF)], [SM, SM] + [VM] * 3, flops=...  4.75 us
    pallas_call x1, Pallas kernels, on_device(): call(text_out_kernel, [BLOCK], [VM] * 4, flops=1 << 31)  4.47 us
  transfers between devices with their start and end apart: 22, of which 13 were waited for; matrix products, arithmetic and copies ran while one was open for 0% of the time, Pallas kernels for 18%

profile of v4, /device:TPU:0, one launch (start us, length us, event | category | flops | bytes accessed | tf_op | source)
XLA Modules:
  0.0 133.5 jit_solution(12714461333529634220)
XLA Ops:
  7.2 1.1 copy-done.2
  8.3 1.0 copy-done.4
  9.3 1.1 shard_map.76
  10.5 1.7 %collective-permute-start.10 = (bf16[320,1152]{1,0:T(8,128)(2,1)}, bf16[320,1152]{1,0:T(8,128)(2,1)S(1)}, u32[]{:S(2)}, u32[]{:S(2)}) collective-permute-start(bf16[320,1152]{1,0:T(8,128)(2,1)} %bitcast.8), channel_id=1, source_target_pairs={{0,64},{64,0},{1,65},{65,1},{2,66},{66,2},{3,67},{67,3},{4,68},{68... | collective-permute-start | bytes 2211848 | tf_op jit(solution)/shard_map/ppermute | solution.py:20
  13.6 29.5 %conditional.2 = (bf16[5,72,1152]{2,1,0:T(8,128)(2,1)}, bf16[5,72,1152]{2,1,0:T(8,128)(2,1)}, bf16[3,72,1152]{2,1,0:T(8,128)(2,1)}, bf16[3,72,1152]{2,1,0:T(8,128)(2,1)}) conditional(s32[]{:T(128)} %convert_element_type.4, () %tuple.27, bf16[72,1152]{1,0:T(8,128)(2,1)S(1)} %get-tuple-element.54), branch_computations={%region_0.0_spmd, %region_1.0_spmd} | conditional | flops 2048 | bytes 9955720 | solution.py:203
  13.6 2.3 %collective-permute-start.3 = (bf16[72,1152]{1,0:T(8,128)(2,1)S(1)}, bf16[72,1152]{1,0:T(8,128)(2,1)S(1)}, u32[]{:S(2)}, u32[]{:S(2)}) collective-permute-start(bf16[72,1152]{1,0:T(8,128)(2,1)S(1)} %refs_0_), channel_id=1, source_target_pairs={{0,72},{8,64},{64,8},{72,0},{1,73},{9,65},{65,9},{73,1},{2,74},{10... | collective-permute-start | bytes 497672 | tf_op jit(solution)/shard_map/cond/branch_1_fun/ppermute | solution.py:25
  15.9 3.0 %collective-permute-start.2 = (bf16[72,1152]{1,0:T(8,128)(2,1)S(1)}, bf16[72,1152]{1,0:T(8,128)(2,1)S(1)}, u32[]{:S(2)}, u32[]{:S(2)}) collective-permute-start(bf16[72,1152]{1,0:T(8,128)(2,1)S(1)} %refs_0_), channel_id=1, source_target_pairs={{0,4},{2,6},{4,0},{6,2},{1,5},{3,7},{5,1},{7,3},{8,12},{10,14},{12... | collective-permute-start | bytes 497672 | tf_op jit(solution)/shard_map/cond/branch_1_fun/ppermute | solution.py:20
  18.9 1.1 collective-permute-start.1
  20.0 0.9 collective-permute-start
  20.9 3.5 %collective-permute-done.2.refs_3_ = bf16[72,1152]{1,0:T(8,128)(2,1)S(1)} collective-permute-done((bf16[72,1152]{1,0:T(8,128)(2,1)S(1)}, bf16[72,1152]{1,0:T(8,128)(2,1)S(1)}, u32[]{:S(2)}, u32[]{:S(2)}) %collective-permute-start.2) | collective-permute-done | bytes 165920 | tf_op jit(solution)/shard_map/cond/branch_1_fun/ppermute | solution.py:20
  24.5 2.0 %collective-permute-done.1.refs_2_ = bf16[72,1152]{1,0:T(8,128)(2,1)S(1)} collective-permute-done((bf16[72,1152]{1,0:T(8,128)(2,1)S(1)}, bf16[72,1152]{1,0:T(8,128)(2,1)S(1)}, u32[]{:S(2)}, u32[]{:S(2)}) %collective-permute-start.1) | collective-permute-done | bytes 165920 | tf_op jit(solution)/shard_map/cond/branch_1_fun/ppermute | solution.py:20
  26.5 0.6 collective-permute-done.refs_1_
  27.1 1.0 branch_1_fun.3
  28.2 2.4 %collective-permute-start.7 = (bf16[72,1152]{1,0:T(8,128)(2,1)S(1)}, bf16[72,1152]{1,0:T(8,128)(2,1)S(1)}, u32[]{:S(2)}, u32[]{:S(2)}) collective-permute-start(bf16[72,1152]{1,0:T(8,128)(2,1)S(1)} %collective-permute-done.3.refs_4_), channel_id=1, source_target_pairs={{0,4},{2,6},{4,0},{6,2},{1,5},{3,7},{5,1},{7,3},{8,12},{10,14},{12... | collective-permute-start | bytes 497672 | tf_op jit(solution)/shard_map/cond/branch_1_fun/ppermute | solution.py:20
  30.5 1.2 collective-permute-start.6
  31.7 0.9 collective-permute-start.5
  32.6 4.2 %collective-permute-done.7.refs_2_ = bf16[72,1152]{1,0:T(8,128)(2,1)S(1)} collective-permute-done((bf16[72,1152]{1,0:T(8,128)(2,1)S(1)}, bf16[72,1152]{1,0:T(8,128)(2,1)S(1)}, u32[]{:S(2)}, u32[]{:S(2)}) %collective-permute-start.7) | collective-permute-done | bytes 165920 | tf_op jit(solution)/shard_map/cond/branch_1_fun/ppermute | solution.py:20
  36.8 2.5 %collective-permute-done.6.refs_1_ = bf16[72,1152]{1,0:T(8,128)(2,1)S(1)} collective-permute-done((bf16[72,1152]{1,0:T(8,128)(2,1)S(1)}, bf16[72,1152]{1,0:T(8,128)(2,1)S(1)}, u32[]{:S(2)}, u32[]{:S(2)}) %collective-permute-start.6) | collective-permute-done | bytes 165920 | tf_op jit(solution)/shard_map/cond/branch_1_fun/ppermute | solution.py:20
  39.9 0.8 branch_1_fun.4
  41.0 2.2 %collective-permute-done.8 = bf16[3,72,1152]{2,1,0:T(8,128)(2,1)} collective-permute-done((bf16[3,72,1152]{2,1,0:T(8,128)(2,1)}, bf16[3,72,1152]{2,1,0:T(8,128)(2,1)}, u32[]{:S(2)}, u32[]{:S(2)}) %collective-permute-start.8) | collective-permute-done | bytes 497696 | tf_op jit(solution)/shard_map/cond/branch_1_fun/ppermute | solution.py:20
  43.3 6.8 %shard_map.77 = (bf16[1152,1152]{1,0:T(8,128)(2,1)S(1)}, f32[640,1152]{1,0:T(8,128)}, bf16[640,1152]{1,0:T(8,128)(2,1)S(1)}) custom-call(s32[4]{0:T(128)S(1)} %pad_add_fusion.at, bf16[5,72,1152]{2,1,0:T(8,128)(2,1)} %get-tuple-element.59.near5, bf16[5,72,1152]{2,1,0:T(8,128)(2,1)} %get-tuple-element.60.far5, bf16[3,72,1152]{2,1,0:T(8,128)(2,1)} %get-tuple-element.61.near3, ...), custom_call_target="tpu_custom_call" | custom-call | flops 1024 | bytes 1024 | tf_op jit(solution)/shard_map/pallas_call | solution.py:244
  50.1 1.5 %copy-done.5 = bf16[1152,1152]{1,0:T(8,128)(2,1)} copy-done((bf16[1152,1152]{1,0:T(8,128)(2,1)}, bf16[1152,1152]{1,0:T(8,128)(2,1)S(1)}, u32[]{:S(2)}) %copy-start.5) | copy-done | bytes 2654232
  51.6 1.2 copy-done.10
  52.8 3.0 %shard_map.78 = (bf16[320,640]{1,0:T(8,128)(2,1)}, f32[640,1152]{1,0:T(8,128)S(1)}) custom-call(f32[2]{0:T(128)S(1)} %pad_maximum_fusion.scal, bf16[320,1152]{1,0:T(8,128)(2,1)} %get-tuple-element.53.n_img, bf16[640,1152]{1,0:T(8,128)(2,1)S(1)} %get-tuple-element.64.n_txt), custom_call_target="tpu_custom_call" | custom-call | flops 1024 | bytes 1024 | tf_op jit(solution)/shard_map/pallas_call | solution.py:255
  55.8 1.6 %copy-done = f32[640,1152]{1,0:T(8,128)} copy-done((f32[640,1152]{1,0:T(8,128)}, f32[640,1152]{1,0:T(8,128)S(1)}, u32[]{:S(2)}) %copy-start) | copy-done | bytes 2949144
  57.5 12.4 %shard_map.79 = (bf16[960,640]{1,0:T(8,128)(2,1)S(1)}, bf16[320,1152]{1,0:T(8,128)(2,1)S(1)}, bf16[320,1152]{1,0:T(8,128)(2,1)S(1)}, bf16[8,72,1152]{2,1,0:T(8,128)(2,1)S(1)}, bf16[8,72,1152]{2,1,0:T(8,128)(2,1)S(1)}) custom-call(s32[4]{0:T(128)S(1)} %pad_add_fusion.at, f32[2]{0:T(128)S(1)} %pad_maximum_fusion.scal, ...), custom_call_target="tpu_custom_call" | custom-call | flops 1024 | bytes 1024 | tf_op jit(solution)/shard_map/pallas_call | solution.py:259
  70.0 0.8 copy-done.7
  70.8 4.9 %conditional.3 = (bf16[8,72,1152]{2,1,0:T(8,128)(2,1)}, bf16[1280,1152]{1,0:T(8,128)(2,1)}) conditional(s32[]{:T(128)} %convert_element_type.4, () %tuple.26, (bf16[8,72,1152]{2,1,0:T(8,128)(2,1)S(1)}, s32[4]{0:T(128)S(1)}, f32[2]{0:T(128)S(1)}, bf16[320,640]{1,0:T(8,128)(2,1)S(1)}, bf16[960,640]{1,0:T(8,128)(2,1)S(1)}, ...), branch_computations={%region_2.0_spmd, %region_3.0_spmd} | conditional | flops 2147483648 | bytes 5309496 | solution.py:203
  70.9 4.7 %branch_1_fun.5 = bf16[1280,1152]{1,0:T(8,128)(2,1)} custom-call(s32[4]{0:T(128)S(1)} %get-tuple-element.14.at, f32[2]{0:T(128)S(1)} %get-tuple-element.15.scal, bf16[320,640]{1,0:T(8,128)(2,1)S(1)} %get-tuple-element.16.grad_own, bf16[960,640]{1,0:T(8,128)(2,1)S(1)} %get-tuple-element.17.grad, bf16[640,1152]{1,0:T(8,128)(2,1)S(1)} %get-tuple-element.18.n_txt), custom_call_target="tpu_custom_call" | custom-call | flops 2147483648 | bytes 1024 | tf_op jit(solution)/shard_map/cond/branch_1_fun/pallas_call | solution.py:227
  75.7 1.1 copy-done.8
  76.8 0.7 collective-permute-start.11
  77.5 1.6 %shard_map.82 = (bf16[2,72,1152]{2,1,0:T(8,128)(2,1)S(1)}, bf16[2,72,1152]{2,1,0:T(8,128)(2,1)S(1)}, bf16[2,72,1152]{2,1,0:T(8,128)(2,1)S(1)}, bf16[2,72,1152]{2,1,0:T(8,128)(2,1)S(1)}) custom-call(s32[4]{0:T(128)S(1)} %pad_add_fusion.at, bf16[8,72,1152]{2,1,0:T(8,128)(2,1)S(1)} %get-tuple-element.76.mine, bf16[8,72,1152]{2,1,0:T(8,128)(2,1)} %get-tuple-element.77.got), custom_call_target="tpu_custom_call" | custom-call | flops 1024 | bytes 1024 | tf_op jit(solution)/shard_map/pallas_call | solution.py:273
  79.1 0.9 collective-permute-start.12
  80.0 2.7 %collective-permute-start.13 = (bf16[2,72,1152]{2,1,0:T(8,128)(2,1)S(1)}, bf16[2,72,1152]{2,1,0:T(8,128)(2,1)S(1)}, u32[]{:S(2)}, u32[]{:S(2)}) collective-permute-start(bf16[2,72,1152]{2,1,0:T(8,128)(2,1)S(1)} %get-tuple-element.80), channel_id=1, source_target_pairs={{0,4},{2,6},{4,0},{6,2},{1,5},{3,7},{5,1},{7,3},{8,12},{10,14},{12... | collective-permute-start | bytes 995336 | tf_op jit(solution)/shard_map/ppermute | solution.py:20
  82.7 1.4 %collective-permute-start.14 = (bf16[2,72,1152]{2,1,0:T(8,128)(2,1)S(1)}, bf16[2,72,1152]{2,1,0:T(8,128)(2,1)S(1)}, u32[]{:S(2)}, u32[]{:S(2)}) collective-permute-start(bf16[2,72,1152]{2,1,0:T(8,128)(2,1)S(1)} %get-tuple-element.81), channel_id=1, source_target_pairs={{0,6},{2,0},{4,2},{6,4},{1,7},{3,1},{5,3},{7,5},{8,14},{10,8},{12,... | collective-permute-start | bytes 995336 | tf_op jit(solution)/shard_map/ppermute | solution.py:20
  84.1 6.7 %collective-permute-done.12.b = bf16[2,72,1152]{2,1,0:T(8,128)(2,1)S(1)} collective-permute-done((bf16[2,72,1152]{2,1,0:T(8,128)(2,1)S(1)}, bf16[2,72,1152]{2,1,0:T(8,128)(2,1)S(1)}, u32[]{:S(2)}, u32[]{:S(2)}) %collective-permute-start.12) | collective-permute-done | bytes 331808 | tf_op jit(solution)/shard_map/ppermute | solution.py:20
  90.8 6.8 %collective-permute-done.13.c = bf16[2,72,1152]{2,1,0:T(8,128)(2,1)S(1)} collective-permute-done((bf16[2,72,1152]{2,1,0:T(8,128)(2,1)S(1)}, bf16[2,72,1152]{2,1,0:T(8,128)(2,1)S(1)}, u32[]{:S(2)}, u32[]{:S(2)}) %collective-permute-start.13) | collective-permute-done | bytes 331808 | tf_op jit(solution)/shard_map/ppermute | solution.py:20
  97.9 0.7 shard_map.83
  98.6 1.0 collective-permute-start.15
  99.6 5.6 %collective-permute-done.15.b = bf16[72,1152]{1,0:T(8,128)(2,1)S(1)} collective-permute-done((bf16[72,1152]{1,0:T(8,128)(2,1)S(1)}, bf16[72,1152]{1,0:T(8,128)(2,1)S(1)}, u32[]{:S(2)}, u32[]{:S(2)}) %collective-permute-start.15) | collective-permute-done | bytes 165920 | tf_op jit(solution)/shard_map/ppermute | solution.py:25
  105.6 5.2 %collective-permute-done.16.b = bf16[72,1152]{1,0:T(8,128)(2,1)S(1)} collective-permute-done((bf16[72,1152]{1,0:T(8,128)(2,1)S(1)}, bf16[72,1152]{1,0:T(8,128)(2,1)S(1)}, u32[]{:S(2)}, u32[]{:S(2)}) %collective-permute-start.16) | collective-permute-done | bytes 165920 | tf_op jit(solution)/shard_map/ppermute | solution.py:20
  110.8 4.1 %collective-permute-start.19 = (bf16[72,1152]{1,0:T(8,128)(2,1)S(1)}, bf16[72,1152]{1,0:T(8,128)(2,1)S(1)}, u32[]{:S(2)}, u32[]{:S(2)}) collective-permute-start(bf16[72,1152]{1,0:T(8,128)(2,1)S(1)} %shard_map.85.a), channel_id=1, source_target_pairs={{0,48},{16,0},{32,16},{48,32},{1,49},{17,1},{33,17},{49,33},{2,50}... | collective-permute-start | bytes 497672 | tf_op jit(solution)/shard_map/ppermute | solution.py:20
  114.9 1.9 %collective-permute-start.17 = (bf16[72,1152]{1,0:T(8,128)(2,1)S(1)}, bf16[72,1152]{1,0:T(8,128)(2,1)S(1)}, u32[]{:S(2)}, u32[]{:S(2)}) collective-permute-start(bf16[72,1152]{1,0:T(8,128)(2,1)S(1)} %shard_map.85.a), channel_id=1, source_target_pairs={{0,32},{16,48},{32,0},{48,16},{1,33},{17,49},{33,1},{49,17},{2,34}... | collective-permute-start | bytes 497672 | tf_op jit(solution)/shard_map/ppermute | solution.py:20
  116.8 4.5 %shard_map.81 = bf16[320,1152]{1,0:T(8,128)(2,1)} custom-call(f32[640,1152]{1,0:T(8,128)} %get-tuple-element.68.z, bf16[320,1152]{1,0:T(8,128)(2,1)S(1)} %get-tuple-element.73.a, bf16[320,1152]{1,0:T(8,128)(2,1)S(1)} %collective-permute-done.11.b, bf16[1152,1152]{1,0:T(8,128)(2,1)S(1)} %copy-done.6), custom_call_target="tpu_custom_call" | custom-call | flops 2147483648 | bytes 1024 | tf_op jit(solution)/shard_map/pallas_call | solution.py:280
  121.2 2.0 %collective-permute-done.18.c = bf16[72,1152]{1,0:T(8,128)(2,1)S(1)} collective-permute-done((bf16[72,1152]{1,0:T(8,128)(2,1)S(1)}, bf16[72,1152]{1,0:T(8,128)(2,1)S(1)}, u32[]{:S(2)}, u32[]{:S(2)}) %collective-permute-start.18) | collective-permute-done | bytes 165920 | tf_op jit(solution)/shard_map/ppermute | solution.py:20
  123.2 0.8 shard_map.86
  124.0 1.1 copy-done.9
  125.1 1.5 %shard_map.80 = bf16[320,1152]{1,0:T(8,128)(2,1)} custom-call(bf16[320,1152]{1,0:T(8,128)(2,1)S(1)} %bitcast.12, bf16[320,1152]{1,0:T(8,128)(2,1)S(1)} %copy-done.9), custom_call_target="tpu_custom_call" | custom-call | flops 1073741824 | bytes 1024 | tf_op jit(solution)/shard_map/pallas_call | solution.py:281
  (42 shorter events, 2.1 us)
Async XLA Ops:
  7.2 50.3 %all-gather.2.cloned.1.call-start = ((), (), s32[]{:S(2)}) async-start(), calls=%async_computation.1 | async-start | bytes 3686400 | tf_op jit(solution)/shard_map/all_gather | solution.py:240
  7.2 1.1 copy-start.2
  8.3 1.0 copy-start.4
  10.5 113.5 %reduce-scatter.2.cloned.1.call-start = ((), (), s32[]{:S(2)}) async-start(), calls=%async_computation.2 | async-start | bytes 3686400 | tf_op jit(solution)/shard_map/reduce_scatter | solution.py:272
  10.5 32.8 %collective-permute-start.10 = (bf16[320,1152]{1,0:T(8,128)(2,1)}, bf16[320,1152]{1,0:T(8,128)(2,1)S(1)}, u32[]{:S(2)}, u32[]{:S(2)}) collective-permute-start(bf16[320,1152]{1,0:T(8,128)(2,1)} %bitcast.8), channel_id=1, source_target_pairs={{0,64},{64,0},{1,65},{65,1},{2,66},{66,2},{3,67},{67,3},{4,68},{68... | collective-permute-start | bytes 2211848 | tf_op jit(solution)/shard_map/ppermute | solution.py:20
  13.6 29.7 %copy-start.1 = (bf16[1,320,1152]{2,1,0:T(8,128)(2,1)S(1)}, bf16[1,320,1152]{2,1,0:T(8,128)(2,1)}, u32[]{:S(2)}) copy-start(bf16[1,320,1152]{2,1,0:T(8,128)(2,1)} %param.10) | copy-start | bytes 2211844
  13.6 7.3 %collective-permute-start.3 = (bf16[72,1152]{1,0:T(8,128)(2,1)S(1)}, bf16[72,1152]{1,0:T(8,128)(2,1)S(1)}, u32[]{:S(2)}, u32[]{:S(2)}) collective-permute-start(bf16[72,1152]{1,0:T(8,128)(2,1)S(1)} %refs_0_), channel_id=1, source_target_pairs={{0,72},{8,64},{64,8},{72,0},{1,73},{9,65},{65,9},{73,1},{2,74},{10... | collective-permute-start | bytes 497672 | tf_op jit(solution)/shard_map/cond/branch_1_fun/ppermute | solution.py:25
  15.9 8.6 %collective-permute-start.2 = (bf16[72,1152]{1,0:T(8,128)(2,1)S(1)}, bf16[72,1152]{1,0:T(8,128)(2,1)S(1)}, u32[]{:S(2)}, u32[]{:S(2)}) collective-permute-start(bf16[72,1152]{1,0:T(8,128)(2,1)S(1)} %refs_0_), channel_id=1, source_target_pairs={{0,4},{2,6},{4,0},{6,2},{1,5},{3,7},{5,1},{7,3},{8,12},{10,14},{12... | collective-permute-start | bytes 497672 | tf_op jit(solution)/shard_map/cond/branch_1_fun/ppermute | solution.py:20
  18.9 7.5 %collective-permute-start.1 = (bf16[72,1152]{1,0:T(8,128)(2,1)S(1)}, bf16[72,1152]{1,0:T(8,128)(2,1)S(1)}, u32[]{:S(2)}, u32[]{:S(2)}) collective-permute-start(bf16[72,1152]{1,0:T(8,128)(2,1)S(1)} %refs_0_), channel_id=1, source_target_pairs={{0,6},{2,0},{4,2},{6,4},{1,7},{3,1},{5,3},{7,5},{8,14},{10,8},{12,... | collective-permute-start | bytes 497672 | tf_op jit(solution)/shard_map/cond/branch_1_fun/ppermute | solution.py:20
  20.0 7.0 %collective-permute-start = (bf16[72,1152]{1,0:T(8,128)(2,1)S(1)}, bf16[72,1152]{1,0:T(8,128)(2,1)S(1)}, u32[]{:S(2)}, u32[]{:S(2)}) collective-permute-start(bf16[72,1152]{1,0:T(8,128)(2,1)S(1)} %refs_0_), channel_id=1, source_target_pairs={{0,2},{2,4},{4,6},{6,0},{1,3},{3,5},{5,7},{7,1},{8,10},{10,12},{12... | collective-permute-start | bytes 497672 | tf_op jit(solution)/shard_map/cond/branch_1_fun/ppermute | solution.py:20
  28.1 15.1 %collective-permute-start.4 = (bf16[5,72,1152]{2,1,0:T(8,128)(2,1)}, bf16[5,72,1152]{2,1,0:T(8,128)(2,1)}, u32[]{:S(2)}, u32[]{:S(2)}) collective-permute-start(bf16[5,72,1152]{2,1,0:T(8,128)(2,1)} %branch_1_fun.3), channel_id=1, source_target_pairs={{0,1},{1,0},{2,3},{3,2},{4,5},{5,4},{6,7},{7,6},{8,9},{9,8},{10,11... | collective-permute-start | bytes 2488328 | tf_op jit(solution)/shard_map/cond/branch_1_fun/ppermute | solution.py:20
  28.2 8.6 %collective-permute-start.7 = (bf16[72,1152]{1,0:T(8,128)(2,1)S(1)}, bf16[72,1152]{1,0:T(8,128)(2,1)S(1)}, u32[]{:S(2)}, u32[]{:S(2)}) collective-permute-start(bf16[72,1152]{1,0:T(8,128)(2,1)S(1)} %collective-permute-done.3.refs_4_), channel_id=1, source_target_pairs={{0,4},{2,6},{4,0},{6,2},{1,5},{3,7},{5,1},{7,3},{8,12},{10,14},{12... | collective-permute-start | bytes 497672 | tf_op jit(solution)/shard_map/cond/branch_1_fun/ppermute | solution.py:20
  30.5 8.7 %collective-permute-start.6 = (bf16[72,1152]{1,0:T(8,128)(2,1)S(1)}, bf16[72,1152]{1,0:T(8,128)(2,1)S(1)}, u32[]{:S(2)}, u32[]{:S(2)}) collective-permute-start(bf16[72,1152]{1,0:T(8,128)(2,1)S(1)} %collective-permute-done.3.refs_4_), channel_id=1, source_target_pairs={{0,6},{2,0},{4,2},{6,4},{1,7},{3,1},{5,3},{7,5},{8,14},{10,8},{12,... | collective-permute-start | bytes 497672 | tf_op jit(solution)/shard_map/cond/branch_1_fun/ppermute | solution.py:20
  31.7 8.2 %collective-permute-start.5 = (bf16[72,1152]{1,0:T(8,128)(2,1)S(1)}, bf16[72,1152]{1,0:T(8,128)(2,1)S(1)}, u32[]{:S(2)}, u32[]{:S(2)}) collective-permute-start(bf16[72,1152]{1,0:T(8,128)(2,1)S(1)} %collective-permute-done.3.refs_4_), channel_id=1, source_target_pairs={{0,2},{2,4},{4,6},{6,0},{1,3},{3,5},{5,7},{7,1},{8,10},{10,12},{12... | collective-permute-start | bytes 497672 | tf_op jit(solution)/shard_map/cond/branch_1_fun/ppermute | solution.py:20
  40.7 2.5 %collective-permute-start.8 = (bf16[3,72,1152]{2,1,0:T(8,128)(2,1)}, bf16[3,72,1152]{2,1,0:T(8,128)(2,1)}, u32[]{:S(2)}, u32[]{:S(2)}) collective-permute-start(bf16[3,72,1152]{2,1,0:T(8,128)(2,1)} %branch_1_fun.4), channel_id=1, source_target_pairs={{0,1},{1,0},{2,3},{3,2},{4,5},{5,4},{6,7},{7,6},{8,9},{9,8},{10,11... | collective-permute-start | bytes 1493000 | tf_op jit(solution)/shard_map/cond/branch_1_fun/ppermute | solution.py:20
  50.1 1.5 %copy-start.5 = (bf16[1152,1152]{1,0:T(8,128)(2,1)}, bf16[1152,1152]{1,0:T(8,128)(2,1)S(1)}, u32[]{:S(2)}) copy-start(bf16[1152,1152]{1,0:T(8,128)(2,1)S(1)} %get-tuple-element.75.w_full) | copy-start | bytes 7962628
  51.6 1.2 copy-start.10
  55.8 1.6 %copy-start = (f32[640,1152]{1,0:T(8,128)}, f32[640,1152]{1,0:T(8,128)S(1)}, u32[]{:S(2)}) copy-start(f32[640,1152]{1,0:T(8,128)S(1)} %get-tuple-element.67.acc) | copy-start | bytes 8847364
  57.5 12.5 %copy-start.11 = (bf16[640,1152]{1,0:T(8,128)(2,1)S(1)}, bf16[640,1152]{1,0:T(8,128)(2,1)}, u32[]{:S(2)}) copy-start(bf16[640,1152]{1,0:T(8,128)(2,1)} %copy-done.10) | copy-start | bytes 4423684
  57.5 12.5 %copy-start.12 = (bf16[320,640]{1,0:T(8,128)(2,1)S(1)}, bf16[320,640]{1,0:T(8,128)(2,1)}, u32[]{:S(2)}) copy-start(bf16[320,640]{1,0:T(8,128)(2,1)} %get-tuple-element.70) | copy-start | bytes 1228804
  69.9 0.9 copy-start.7
  70.8 4.9 %collective-permute-start.9 = (bf16[8,72,1152]{2,1,0:T(8,128)(2,1)S(1)}, bf16[8,72,1152]{2,1,0:T(8,128)(2,1)}, u32[]{:S(2)}, u32[]{:S(2)}) collective-permute-start(bf16[8,72,1152]{2,1,0:T(8,128)(2,1)S(1)} %get-tuple-element.13), channel_id=1, source_target_pairs={{0,1},{1,0},{2,3},{3,2},{4,5},{5,4},{6,7},{7,6},{8,9},{9,8},{10,11... | collective-permute-start | bytes 3981320 | tf_op jit(solution)/shard_map/cond/branch_1_fun/ppermute | solution.py:20
  75.7 1.1 copy-start.8
  75.7 41.1 %copy-start.6 = (bf16[1152,1152]{1,0:T(8,128)(2,1)S(1)}, bf16[1152,1152]{1,0:T(8,128)(2,1)}, u32[]{:S(2)}) copy-start(bf16[1152,1152]{1,0:T(8,128)(2,1)} %copy-done.5) | copy-start | bytes 7962628
  76.8 40.0 %collective-permute-start.11 = (bf16[320,1152]{1,0:T(8,128)(2,1)S(1)}, bf16[320,1152]{1,0:T(8,128)(2,1)S(1)}, u32[]{:S(2)}, u32[]{:S(2)}) collective-permute-start(bf16[320,1152]{1,0:T(8,128)(2,1)S(1)} %copy-done.8), channel_id=1, source_target_pairs={{0,64},{64,0},{1,65},{65,1},{2,66},{66,2},{3,67},{67,3},{4,68},{68... | collective-permute-start | bytes 2211848 | tf_op jit(solution)/shard_map/ppermute | solution.py:20
  79.1 11.6 %collective-permute-start.12 = (bf16[2,72,1152]{2,1,0:T(8,128)(2,1)S(1)}, bf16[2,72,1152]{2,1,0:T(8,128)(2,1)S(1)}, u32[]{:S(2)}, u32[]{:S(2)}) collective-permute-start(bf16[2,72,1152]{2,1,0:T(8,128)(2,1)S(1)} %get-tuple-element.79), channel_id=1, source_target_pairs={{0,2},{2,4},{4,6},{6,0},{1,3},{3,5},{5,7},{7,1},{8,10},{10,12},{12... | collective-permute-start | bytes 995336 | tf_op jit(solution)/shard_map/ppermute | solution.py:20
  80.0 17.5 %collective-permute-start.13 = (bf16[2,72,1152]{2,1,0:T(8,128)(2,1)S(1)}, bf16[2,72,1152]{2,1,0:T(8,128)(2,1)S(1)}, u32[]{:S(2)}, u32[]{:S(2)}) collective-permute-start(bf16[2,72,1152]{2,1,0:T(8,128)(2,1)S(1)} %get-tuple-element.80), channel_id=1, source_target_pairs={{0,4},{2,6},{4,0},{6,2},{1,5},{3,7},{5,1},{7,3},{8,12},{10,14},{12... | collective-permute-start | bytes 995336 | tf_op jit(solution)/shard_map/ppermute | solution.py:20
  82.7 15.2 %collective-permute-start.14 = (bf16[2,72,1152]{2,1,0:T(8,128)(2,1)S(1)}, bf16[2,72,1152]{2,1,0:T(8,128)(2,1)S(1)}, u32[]{:S(2)}, u32[]{:S(2)}) collective-permute-start(bf16[2,72,1152]{2,1,0:T(8,128)(2,1)S(1)} %get-tuple-element.81), channel_id=1, source_target_pairs={{0,6},{2,0},{4,2},{6,4},{1,7},{3,1},{5,3},{7,5},{8,14},{10,8},{12,... | collective-permute-start | bytes 995336 | tf_op jit(solution)/shard_map/ppermute | solution.py:20
  98.6 6.6 %collective-permute-start.15 = (bf16[72,1152]{1,0:T(8,128)(2,1)S(1)}, bf16[72,1152]{1,0:T(8,128)(2,1)S(1)}, u32[]{:S(2)}, u32[]{:S(2)}) collective-permute-start(bf16[72,1152]{1,0:T(8,128)(2,1)S(1)} %get-tuple-element.83), channel_id=1, source_target_pairs={{0,72},{8,64},{64,8},{72,0},{1,73},{9,65},{65,9},{73,1},{2,74},{10... | collective-permute-start | bytes 497672 | tf_op jit(solution)/shard_map/ppermute | solution.py:25
  105.3 5.4 %collective-permute-start.16 = (bf16[72,1152]{1,0:T(8,128)(2,1)S(1)}, bf16[72,1152]{1,0:T(8,128)(2,1)S(1)}, u32[]{:S(2)}, u32[]{:S(2)}) collective-permute-start(bf16[72,1152]{1,0:T(8,128)(2,1)S(1)} %shard_map.84.a), channel_id=1, source_target_pairs={{0,64},{64,0},{1,65},{65,1},{2,66},{66,2},{3,67},{67,3},{4,68},{68... | collective-permute-start | bytes 497672 | tf_op jit(solution)/shard_map/ppermute | solution.py:20
  110.8 10.4 %collective-permute-start.19 = (bf16[72,1152]{1,0:T(8,128)(2,1)S(1)}, bf16[72,1152]{1,0:T(8,128)(2,1)S(1)}, u32[]{:S(2)}, u32[]{:S(2)}) collective-permute-start(bf16[72,1152]{1,0:T(8,128)(2,1)S(1)} %shard_map.85.a), channel_id=1, source_target_pairs={{0,48},{16,0},{32,16},{48,32},{1,49},{17,1},{33,17},{49,33},{2,50}... | collective-permute-start | bytes 497672 | tf_op jit(solution)/shard_map/ppermute | solution.py:20
  114.9 8.3 %collective-permute-start.18 = (bf16[72,1152]{1,0:T(8,128)(2,1)S(1)}, bf16[72,1152]{1,0:T(8,128)(2,1)S(1)}, u32[]{:S(2)}, u32[]{:S(2)}) collective-permute-start(bf16[72,1152]{1,0:T(8,128)(2,1)S(1)} %shard_map.85.a), channel_id=1, source_target_pairs={{0,16},{16,32},{32,48},{48,0},{1,17},{17,33},{33,49},{49,1},{2,18}... | collective-permute-start | bytes 497672 | tf_op jit(solution)/shard_map/ppermute | solution.py:20
  114.9 8.3 %collective-permute-start.17 = (bf16[72,1152]{1,0:T(8,128)(2,1)S(1)}, bf16[72,1152]{1,0:T(8,128)(2,1)S(1)}, u32[]{:S(2)}, u32[]{:S(2)}) collective-permute-start(bf16[72,1152]{1,0:T(8,128)(2,1)S(1)} %shard_map.85.a), channel_id=1, source_target_pairs={{0,32},{16,48},{32,0},{48,16},{1,33},{17,49},{33,1},{49,17},{2,34}... | collective-permute-start | bytes 497672 | tf_op jit(solution)/shard_map/ppermute | solution.py:20
  116.8 7.3 %copy-start.3 = (bf16[1,320,1152]{2,1,0:T(8,128)(2,1)S(1)}, bf16[1,320,1152]{2,1,0:T(8,128)(2,1)}, u32[]{:S(2)}) copy-start(bf16[1,320,1152]{2,1,0:T(8,128)(2,1)} %param.9) | copy-start | bytes 2211844
  124.0 1.1 copy-start.9
Sparse Core Ops, SparseCore 0:
  10.6 40.5 all-gather.1
  75.8 36.4 reduce-scatter.1

commit v5 on v3

v5 whole, which is shorter than its diff:
```python
import functools

import jax
import jax.numpy as jnp
from jax import lax
from jax.experimental import pallas as pl
from jax.experimental.pallas import tpu as pltpu
from jax.sharding import Mesh, PartitionSpec as P

BF = jnp.bfloat16
F32 = jnp.float32
MIB = 1024 * 1024
EARLY = 768
TEXT_MIB = 16
MAIN_MIB = 26
AXES = {"ylo": 2, "z": 4, "yhi": 2, "x": 4, "core": 2}

VM = pl.BlockSpec(memory_space=pltpu.VMEM)
SM = pl.BlockSpec(memory_space=pltpu.SMEM)
ANY = pl.BlockSpec(memory_space=pl.ANY)


def shift(value, axis, step):
    n = AXES[axis]
    return lax.ppermute(value, axis, [(i, (i + step) % n) for i in range(n)])


def swap_far(value):
    pairs = [(a * 2 + b, (1 - a) * 2 + 1 - b) for a in range(2) for b in range(2)]
    return lax.ppermute(value, ("ylo", "yhi"), pairs)


def shaped(shape, dtype):
    return jax.ShapeDtypeStruct(shape, dtype)


def call(kernel, outs, specs, scratch=(), vmem=10, out_specs=None, flops=1024):
    return pl.pallas_call(
        kernel,
        out_shape=outs,
        in_specs=specs,
        out_specs=out_specs or [VM] * len(outs),
        scratch_shapes=list(scratch),
        compiler_params=pltpu.CompilerParams(vmem_limit_bytes=vmem * MIB),
        cost_estimate=pl.CostEstimate(flops=flops, bytes_accessed=1024, transcendentals=0),
    )


def inverse_length(rows):
    return 1.0 / jnp.sqrt(jnp.sum(rows * rows, axis=-1, keepdims=True) + 1e-06)


def project(grad, rows):
    inv = inverse_length(rows)
    unit = rows * inv
    inner = jnp.sum(unit * grad, axis=-1, keepdims=True)
    return (grad - unit * inner) * inv


def half_kernel(w, w_half):
    w_half[...] = w[...].astype(BF)


def repeat_kernel(at, w_h, w_y, out):
    for k in range(4):
        out[k, at[0]] = w_h[...]
        out[k, 1 - at[0]] = w_y[...]


def unit_kernel(img, _, n_img):
    rows = img[...].astype(F32)
    n_img[...] = (rows * inverse_length(rows)).astype(BF)


def text_kernel(at, near, far, txt, txt_far, w_full, z, n_txt, mine, other, rows, sems):
    copies = [
        pltpu.make_async_copy(near, mine, sems.at[0]),
        pltpu.make_async_copy(far, other, sems.at[1]),
        pltpu.make_async_copy(txt, rows.at[pl.ds(0, 320)], sems.at[2]),
        pltpu.make_async_copy(txt_far, rows.at[pl.ds(320, 320)], sems.at[3]),
    ]
    for c in copies:
        c.start()
    for c in copies[:2]:
        c.wait()
    core = at[2]
    for x in range(4):
        for h in range(2):
            a, b = mine[x, h].astype(F32), other[x, h].astype(F32)
            first = jnp.where(core == 0, a, b)
            second = jnp.where(core == 0, b, a)
            w_full[pl.ds((h * 4 + x) * 144, 144), :] = jnp.concatenate([first, second], axis=0).astype(BF)
    for c in copies[2:]:
        c.wait()
    out = jnp.dot(rows[...], w_full[...], preferred_element_type=F32)
    z[...] = out
    n_txt[...] = (out * inverse_length(out)).astype(BF)


def logit_gradient(scal, img_rows, txt_rows):
    logits = scal[0] * lax.dot_general(
        img_rows, txt_rows, (((1,), (1,)), ((), ())), preferred_element_type=F32
    ) + scal[1]
    return 1.0 / (1.0 + jnp.exp(-logits))


def main_kernel(at, scal, n_txt, n_own, n_a, n_b, n_c, z, txt, txt_far, grad, g_own, g_far, mine, other, rows, feat, wide, sems):
    moves = [(block, rows.at[pl.ds(k * 320, 320)]) for k, block in enumerate((n_own, n_a, n_b, n_c))]
    moves += [(txt, feat.at[pl.ds(0, 320)]), (txt_far, feat.at[pl.ds(320, 320)])]
    copies = [pltpu.make_async_copy(a, b, sems.at[k]) for k, (a, b) in enumerate(moves)]
    for c in copies:
        c.start()
    for c in copies[:4]:
        c.wait()
    g = logit_gradient(scal, n_txt[...], rows[...])
    row_ids = lax.broadcasted_iota(jnp.int32, g.shape, 0)
    col_ids = lax.broadcasted_iota(jnp.int32, g.shape, 1)
    grad[...] = (g - jnp.where((row_ids == col_ids) & (row_ids < 320), 1.0, 0.0)).astype(BF)
    total = scal[0] * jnp.dot(grad[...], rows[...], preferred_element_type=F32)
    g_own[...] = total[:320].astype(BF)
    g_far[...] = total[320:].astype(BF)
    for c in copies[4:]:
        c.wait()
    dz = project(total, z[...]).astype(BF)
    wide[...] = lax.dot_general(
        feat[...], dz, (((0,), (0,)), ((), ())), preferred_element_type=F32
    )
    core = at[2]
    for j in range(8):
        a = pl.multiple_of((2 * j + core) * 72, 8)
        b = pl.multiple_of((2 * j + 1 - core) * 72, 8)
        mine[j % 4, j // 4] = wide[pl.ds(a, 72), :].astype(BF)
        other[j % 4, j // 4] = wide[pl.ds(b, 72), :].astype(BF)


def part_kernel(first, scal, grad, n_txt, *outs):
    start = first * 320
    rows = sum(ref.shape[0] for ref in outs)
    out = scal[0] * lax.dot_general(
        grad[:, start : start + rows], n_txt[...], (((0,), (0,)), ((), ())), preferred_element_type=F32
    )
    at = 0
    for ref in outs:
        ref[...] = out[at : at + ref.shape[0]].astype(BF)
        at += ref.shape[0]


def pass_on_kernel(part_a, part_b, got_b, got_a, out_a, out_b):
    out_a[pl.ds(0, 160), :] = part_a[pl.ds(0, 160), :]
    out_a[pl.ds(160, 160), :] = (part_a[pl.ds(160, 160), :].astype(F32) + got_a[...].astype(F32)).astype(BF)
    out_b[pl.ds(0, 160), :] = (part_b[pl.ds(0, 160), :].astype(F32) + got_b[...].astype(F32)).astype(BF)
    out_b[pl.ds(160, 160), :] = part_b[pl.ds(160, 160), :]


def core_sum_kernel(at, mine, got, early, keep, send):
    early[0] = (mine[0, :, :, :EARLY].astype(F32) + got[0, :, :, :EARLY].astype(F32)).astype(BF)
    for out, h in ((keep, at[0]), (send, 1 - at[0])):
        out[0] = (mine[0, h, :, EARLY:].astype(F32) + got[0, h, :, EARLY:].astype(F32)).astype(BF)


def core_sum(at, mine, got):
    late = 1152 - EARLY
    shapes = (2, 72, EARLY), (72, late), (72, late)
    whole = pl.BlockSpec((1, 2, 72, 1152), lambda x: (x, 0, 0, 0))
    return pl.pallas_call(
        core_sum_kernel,
        grid=(4,),
        out_shape=[shaped((4, *s), BF) for s in shapes],
        in_specs=[SM, whole, whole],
        out_specs=[
            pl.BlockSpec((1, *s), lambda x, n=len(s): (x,) + (0,) * n) for s in shapes
        ],
        compiler_params=pltpu.CompilerParams(vmem_limit_bytes=16 * MIB),
        cost_estimate=pl.CostEstimate(flops=1024, bytes_accessed=1024, transcendentals=0),
    )(at, mine, got)


def x_sum_kernel(at, got, keep, send):
    for out, h in ((keep, at[0]), (send, 1 - at[0])):
        a, b, c, d = (got[x, h].astype(F32) for x in range(4))
        out[...] = ((a + b) + (c + d)).astype(BF)


def join_kernel(keep, got, along, out):
    out[:, :EARLY] = (keep[...].astype(F32) + got[...].astype(F32)).astype(BF)
    a, b, c, d = (along[x].astype(F32) for x in range(4))
    out[:, EARLY:] = ((a + b) + (c + d)).astype(BF)


def pair_sum_kernel(a, b, out):
    out[...] = (a[...].astype(F32) + b[...].astype(F32)).astype(BF)


def quad_sum_kernel(a, b, c, d, out):
    total = (a[...].astype(F32) + b[...].astype(F32)) + (c[...].astype(F32) + d[...].astype(F32))
    out[...] = total.astype(out.dtype)


def image_out_kernel(img, a, b, c, out):
    grad = a[...].astype(F32) + (b[...].astype(F32) + c[...].astype(F32))
    out[...] = project(grad, img[...].astype(F32)).astype(BF)


def text_out_kernel(z, a, b, w_full, out, rows, head, sems):
    copies = [
        pltpu.make_async_copy(z.at[pl.ds(0, 320)], rows, sems.at[0]),
        pltpu.make_async_copy(w_full, head, sems.at[1]),
    ]
    for c in copies:
        c.start()
    grad = a[...].astype(F32) + b[...].astype(F32)
    copies[0].wait()
    dz = project(grad, rows[...]).astype(BF)
    copies[1].wait()
    out[...] = lax.dot_general(
        dz, head[...], (((1,), (1,)), ((), ())), preferred_element_type=F32
    ).astype(BF)


def apart(step, *args):
    outs = jax.eval_shape(step, *args)
    return lax.cond(
        lax.axis_index("z") < AXES["z"],
        step,
        lambda *_: tuple(jnp.zeros(o.shape, o.dtype) for o in outs),
        *args,
    )


hold = lax.optimization_barrier
BLOCK = shaped((320, 1152), BF)


def stack_of(*lead):
    return shaped((*lead, 72, 1152), BF)


def along_x(value):
    return lax.all_to_all(value, "x", split_axis=0, concat_axis=0, tiled=True)


def gather_head(at, w_h, w_y):
    (pieces,) = call(repeat_kernel, [stack_of(4, 2)], [SM, VM, VM])(at, w_h, w_y)
    near = along_x(pieces)
    return near, shift(near, "core", 1)


def parts_of(first, shapes, *args):
    kernel = functools.partial(part_kernel, first)
    return call(kernel, shapes, [SM] + [VM] * 2, flops=1 << 31)(*args)


def sum_plane(at, scal, mine, got_core, part_c, grad, n_txt, z, g_own, g_far, w_full):
    early, keep_q, send_q = core_sum(at, mine, got_core)
    early, send_q, part_c = hold((early, send_q, part_c))
    got_x = along_x(early)
    (both_q,) = call(pair_sum_kernel, [shaped(keep_q.shape, BF)], [VM] * 2)(keep_q, swap_far(send_q))
    both_q, grad = hold((both_q, grad))
    along_q = along_x(both_q)
    got_b, got_a = shift(part_c[0], "z", 1), shift(part_c[1], "z", -1)
    part_own, part_a, part_b = parts_of(0, [BLOCK] * 3, scal, grad, n_txt)
    part_a, part_b = call(pass_on_kernel, [BLOCK] * 2, [VM] * 4)(part_a, part_b, got_b, got_a)
    got_a, got_b = shift(part_a, "z", -1), shift(part_b, "z", 1)
    g_got = shift(g_far, "ylo", 1)
    keep, send = call(x_sum_kernel, [shaped((72, EARLY), BF)] * 2, [SM, VM])(at, got_x)
    (one,) = call(join_kernel, [stack_of()], [VM] * 3)(keep, swap_far(send), along_q)
    one, g_got = hold((one, g_got))
    (pair,) = call(pair_sum_kernel, [stack_of()], [VM] * 2)(one, shift(one, "ylo", 1))
    (d_feat,) = call(
        text_out_kernel,
        [BLOCK],
        [ANY, VM, VM, ANY],
        [pltpu.VMEM((320, 1152), F32), pltpu.VMEM((1152, 1152), BF), pltpu.SemaphoreType.DMA((2,))],
        flops=1 << 31,
    )(z, g_own, g_got, w_full)
    pair, d_feat, got_a, got_b = hold((pair, d_feat, got_a, got_b))
    return pair, d_feat, part_own, got_a, got_b


def on_device(img_emb, txt_feat, w_txt, t_log, bias):
    img, txt = img_emb[0], txt_feat[0]
    at = jnp.stack([lax.axis_index(a) for a in ("yhi", "x", "core", "z")]).astype(jnp.int32)
    scal = jnp.concatenate([jnp.exp(t_log), bias])

    txt_far = shift(txt, "ylo", 1)
    (w_h,) = call(half_kernel, [stack_of()], [VM])(w_txt)
    w_y = swap_far(w_h)
    (n_img,) = call(unit_kernel, [BLOCK], [VM, ANY])(img, w_h)
    n_c, n_b, n_a = (shift(n_img, "z", s) for s in (2, -1, 1))
    near, far = apart(gather_head, at, w_h, w_y)
    near, far, txt_far = hold((near, far, txt_far))

    w_full, z, n_txt = call(
        text_kernel,
        [shaped((1152, 1152), BF), shaped((640, 1152), F32), shaped((640, 1152), BF)],
        [SM] + [ANY] * 4,
        [
            pltpu.VMEM((4, 2, 72, 1152), BF),
            pltpu.VMEM((4, 2, 72, 1152), BF),
            pltpu.VMEM((640, 1152), BF),
            pltpu.SemaphoreType.DMA((4,)),
        ],
        vmem=TEXT_MIB,
        flops=1 << 34,
    )(at, near, far, txt, txt_far)
    n_txt, n_a, n_b, n_c = hold((n_txt, n_a, n_b, n_c))
    grad, g_own, g_far, mine, other = call(
        main_kernel,
        [shaped((640, 1280), BF), BLOCK, BLOCK, stack_of(4, 2), stack_of(4, 2)],
        [SM, SM, VM] + [ANY] * 4 + [VM, ANY, ANY],
        [
            pltpu.VMEM((1280, 1152), BF),
            pltpu.VMEM((640, 1152), BF),
            pltpu.VMEM((1152, 1152), F32),
            pltpu.SemaphoreType.DMA((6,)),
        ],
        vmem=MAIN_MIB,
    )(at, scal, n_txt, n_img, n_a, n_b, n_c, z, txt, txt_far)

    half = shaped((160, 1152), BF)
    got_core, part_c = hold(
        (shift(other, "core", 1), parts_of(3, [half] * 2, scal, grad, n_txt))
    )
    quad, d_feat, part_own, got_a, got_b = sum_plane(
        at, scal, mine, got_core, part_c, grad, n_txt, z, g_own, g_far, w_full
    )
    (d_img,) = call(image_out_kernel, [BLOCK], [VM] * 4, flops=1 << 30)(img, part_own, got_a, got_b)
    (d_weight,) = call(quad_sum_kernel, [shaped((72, 1152), F32)], [VM] * 4)(
        quad, shift(quad, "z", 2), shift(quad, "z", 1), shift(quad, "z", -1)
    )
    return (d_img[None], d_feat[None], d_weight)


def solution(mesh):
    fine = Mesh(mesh.devices.reshape(2, 4, 2, 4, 2), tuple(AXES))
    dp, fsdp = ("ylo", "z"), ("yhi", "x", "core")
    placed = (P(fsdp, dp, None), P(fsdp, dp, None), P(fsdp, None), P(), P())
    return jax.shard_map(
        on_device,
        mesh=fine,
        in_specs=placed,
        out_specs=(P(fsdp, dp, None), P(fsdp, dp, None), P(fsdp, None)),
        check_vma=False,
    )
```

time: 138 us -> 115 us (0.83)
  waiting for transfers between devices: 52 us -> 16.3 us
  blocking collectives: 0 us -> 20.9 us
  Pallas kernels: 41.3 us -> 35.4 us
  local copies, waits for them, and re-layouts: 13.9 us -> 10.6 us
    ppermute x15, waiting for transfers between devices: 39.6 us -> 7.95 us  [shift(): return lax.ppermute(value, axis, [(i, (i + step) % n) for i in range(n)])]
    all_to_all x0 -> x1, blocking collectives: none -> 20.9 us  [along_x(): return lax.all_to_all(value, 'x', split_axis=0, concat_axis=0, tiled=True)]
    all_to_all x2, starting transfers between devices: 13.7 us -> 6.88 us  [along_x(): return lax.all_to_all(value, 'x', split_axis=0, concat_axis=0, tiled=True)]
    ppermute x0 -> x3, starting transfers between devices: none -> 5.58 us  [swap_far(): return lax.ppermute(value, ('ylo', 'yhi'), pairs)]
    all_to_all x2, waiting for transfers between devices: 12.4 us -> 7.27 us  [along_x(): return lax.all_to_all(value, 'x', split_axis=0, concat_axis=0, tiled=True)]
    pallas_call x13 -> x14, Pallas kernels: 34.1 us -> 29.2 us  [the longest x1 10.7 us: on_device(): call(main_kernel, [shaped((640, 1280), BF), BLOCK, BLOCK, stack_of(4, 2),...]
    unnamed x52 -> x36, local copies, waits for them, and re-layouts: 13.9 us -> 10.6 us
    ppermute x15, starting transfers between devices: 13.7 us -> 16.1 us  [shift(): return lax.ppermute(value, axis, [(i, (i + step) % n) for i in range(n)])]
  transfers between devices with their start and end apart: 17 -> 20, of which waited for: 6 -> 8; matrix products, arithmetic and copies ran while one was open for 0% -> 0% of each run, Pallas kernels for 21% -> 19%
where the time goes in v5:
time: 115 us; the launch traced here: 114 us
  Pallas kernels  35.4 us (31%)
  starting transfers between devices  28.6 us (25%)
  blocking collectives  20.9 us (18%)
  waiting for transfers between devices  16.3 us (14%)
  local copies, waits for them, and re-layouts  10.6 us (9%)
  between operations  2.22 us (2%)
    all_to_all x1, blocking collectives, along_x(): return lax.all_to_all(value, 'x', split_axis=0, concat_axis=0, tiled=True)  20.9 us
    ppermute x15, starting transfers between devices, shift(): return lax.ppermute(value, axis, [(i, (i + step) % n) for i in range(n)])  16.1 us
    pallas_call x1, Pallas kernels, on_device(): call(main_kernel, [shaped((640, 1280), BF), BLOCK, BLOCK, stack_of(4, 2),...  10.7 us
    unnamed x36, local copies, waits for them, and re-layouts  10.6 us
    ppermute x15, waiting for transfers between devices, shift(): return lax.ppermute(value, axis, [(i, (i + step) % n) for i in range(n)])  7.95 us
    all_to_all x2, waiting for transfers between devices, along_x(): return lax.all_to_all(value, 'x', split_axis=0, concat_axis=0, tiled=True)  7.27 us
    all_to_all x2, starting transfers between devices, along_x(): return lax.all_to_all(value, 'x', split_axis=0, concat_axis=0, tiled=True)  6.88 us
    ppermute x3, starting transfers between devices, swap_far(): return lax.ppermute(value, ('ylo', 'yhi'), pairs)  5.58 us
  transfers between devices with their start and end apart: 20, of which 8 were waited for; matrix products, arithmetic and copies ran while one was open for 0% of the time, Pallas kernels for 19%

profile of v5, /device:TPU:0, one launch (start us, length us, event | category | flops | bytes accessed | tf_op | source)
XLA Modules:
  0.0 114.1 jit_solution(9662949409326679556)
XLA Ops:
  0.6 1.7 %collective-permute-start.2 = (bf16[320,1152]{1,0:T(8,128)(2,1)}, bf16[320,1152]{1,0:T(8,128)(2,1)S(1)}, u32[]{:S(2)}, u32[]{:S(2)}) collective-permute-start(bf16[320,1152]{1,0:T(8,128)(2,1)} %bitcast.8), channel_id=1, source_target_pairs={{0,64},{64,0},{1,65},{65,1},{2,66},{66,2},{3,67},{67,3},{4,68},{68... | collective-permute-start | bytes 2211848 | tf_op jit(solution)/shard_map/ppermute | solution.py:25
  2.4 1.0 copy-done.8
  3.4 2.3 %collective-permute-start.1 = (bf16[72,1152]{1,0:T(8,128)(2,1)S(1)}, bf16[72,1152]{1,0:T(8,128)(2,1)S(1)}, u32[]{:S(2)}, u32[]{:S(2)}) collective-permute-start(bf16[72,1152]{1,0:T(8,128)(2,1)S(1)} %shard_map.76._), channel_id=1, source_target_pairs={{0,72},{8,64},{64,8},{72,0},{1,73},{9,65},{65,9},{73,1},{2,74},{10... | collective-permute-start | bytes 497672 | tf_op jit(solution)/shard_map/ppermute | solution.py:30
  5.6 1.1 copy-done.3
  6.7 0.3 shard_map.78.n_own
  7.0 4.0 %collective-permute-start.5 = (bf16[320,1152]{1,0:T(8,128)(2,1)S(1)}, bf16[320,1152]{1,0:T(8,128)(2,1)}, u32[]{:S(2)}, u32[]{:S(2)}) collective-permute-start(bf16[320,1152]{1,0:T(8,128)(2,1)S(1)} %shard_map.78.n_own), channel_id=1, source_target_pairs={{0,32},{16,48},{32,0},{48,16},{1,33},{17,49},{33,1},{49,17},{2,34}... | collective-permute-start | bytes 2211848 | tf_op jit(solution)/shard_map/ppermute | solution.py:25
  11.0 0.7 collective-permute-start.4
  11.7 1.3 %collective-permute-start.3 = (bf16[320,1152]{1,0:T(8,128)(2,1)S(1)}, bf16[320,1152]{1,0:T(8,128)(2,1)}, u32[]{:S(2)}, u32[]{:S(2)}) collective-permute-start(bf16[320,1152]{1,0:T(8,128)(2,1)S(1)} %shard_map.78.n_own), channel_id=1, source_target_pairs={{0,16},{16,32},{32,48},{48,0},{1,17},{17,33},{33,49},{49,1},{2,18}... | collective-permute-start | bytes 2211848 | tf_op jit(solution)/shard_map/ppermute | solution.py:25
  14.5 24.9 %conditional.1 = (bf16[4,2,72,1152]{3,2,1,0:T(8,128)(2,1)}, bf16[4,2,72,1152]{3,2,1,0:T(8,128)(2,1)}) conditional(s32[]{:T(128)} %convert_element_type.3, () %tuple.23, (s32[4]{0:T(128)S(1)}, bf16[72,1152]{1,0:T(8,128)(2,1)S(1)}, bf16[72,1152]{1,0:T(8,128)(2,1)S(1)}) %tuple.24), branch_computations={%region_0.0_spmd, %region_1.0_spmd} | conditional | flops 1024 | bytes 7963704 | solution.py:222
  14.5 0.7 branch_1_fun.1
  15.2 20.9 %all_to_all.14 = bf16[4,2,72,1152]{3,2,1,0:T(8,128)(2,1)} all-to-all(bf16[4,2,72,1152]{3,2,1,0:T(8,128)(2,1)S(1)} %branch_1_fun.1), channel_id=1, replica_groups=mesh['ylo'=2,'z'=4,'yhi'=2,'x'=4,'core'=2] {'x'}, dimensions={0} | all-to-all | bytes 2654208 | tf_op jit(solution)/shard_map/cond/branch_1_fun/all_to_all | solution.py:239
  36.0 3.4 %collective-permute-done = bf16[4,2,72,1152]{3,2,1,0:T(8,128)(2,1)} collective-permute-done((bf16[4,2,72,1152]{3,2,1,0:T(8,128)(2,1)}, bf16[4,2,72,1152]{3,2,1,0:T(8,128)(2,1)}, u32[]{:S(2)}, u32[]{:S(2)}) %collective-permute-start) | collective-permute-done | bytes 1327136 | tf_op jit(solution)/shard_map/cond/branch_1_fun/ppermute | solution.py:25
  39.5 0.9 copy-done.5
  40.3 1.1 copy-done.6
  41.4 5.5 %shard_map.77 = (bf16[1152,1152]{1,0:T(8,128)(2,1)S(1)}, f32[640,1152]{1,0:T(8,128)S(1)}, bf16[640,1152]{1,0:T(8,128)(2,1)S(1)}) custom-call(s32[4]{0:T(128)S(1)} %pad_add_fusion.at, bf16[4,2,72,1152]{3,2,1,0:T(8,128)(2,1)} %get-tuple-element.58.near, bf16[4,2,72,1152]{3,2,1,0:T(8,128)(2,1)} %get-tuple-element.59.far, bf16[320,1152]{1,0:T(8,128)(2,1)S(1)} %bitcast.9, ...), custom_call_target="tpu_custom_call" | custom-call | flops 17179869184 | bytes 1024 | tf_op jit(solution)/shard_map/pallas_call | solution.py:293
  46.9 1.5 %copy-done.14 = bf16[1152,1152]{1,0:T(8,128)(2,1)} copy-done((bf16[1152,1152]{1,0:T(8,128)(2,1)}, bf16[1152,1152]{1,0:T(8,128)(2,1)S(1)}, u32[]{:S(2)}) %copy-start.14) | copy-done | bytes 2654232
  48.4 10.7 %shard_map.79 = (bf16[640,1280]{1,0:T(8,128)(2,1)S(1)}, bf16[320,1152]{1,0:T(8,128)(2,1)S(1)}, bf16[320,1152]{1,0:T(8,128)(2,1)S(1)}, bf16[4,2,72,1152]{3,2,1,0:T(8,128)(2,1)S(1)}, bf16[4,2,72,1152]{3,2,1,0:T(8,128)(2,1)S(1)}) custom-call(s32[4]{0:T(128)S(1)} %pad_add_fusion.at, f32[2]{0:T(128)S(1)} %pad_maximum_fusion.scal, ...), custom_call_target="tpu_custom_call" | custom-call | flops 1024 | bytes 1024 | tf_op jit(solution)/shard_map/pallas_call | solution.py:307
  59.2 0.2 collective-permute-start.6
  59.4 2.4 %shard_map.80 = (bf16[160,1152]{1,0:T(8,128)(2,1)}, bf16[160,1152]{1,0:T(8,128)(2,1)}) custom-call(f32[2]{0:T(128)S(1)} %pad_maximum_fusion.scal, bf16[640,1280]{1,0:T(8,128)(2,1)S(1)} %get-tuple-element.79.grad, bf16[640,1152]{1,0:T(8,128)(2,1)S(1)} %get-tuple-element.62.n_txt), custom_call_target="tpu_custom_call" | custom-call | flops 2147483648 | bytes 1024 | tf_op jit(solution)/shard_map/pallas_call | solution.py:250
  61.9 0.5 collective-permute-done.6.got
  62.4 2.2 %shard_map.81 = (bf16[4,2,72,768]{3,2,1,0:T(8,128)(2,1)}, bf16[4,72,384]{2,1,0:T(8,128)(2,1)S(1)}, bf16[4,72,384]{2,1,0:T(8,128)(2,1)}) custom-call(s32[4]{0:T(128)S(1)} %pad_add_fusion.at, bf16[4,2,72,1152]{3,2,1,0:T(8,128)(2,1)S(1)} %get-tuple-element.67.mine, bf16[4,2,72,1152]{3,2,1,0:T(8,128)(2,1)S(1)} %collective-permute-done.6.got), custom_call_target="tpu_custom_call" | custom-call | flops 1024 | bytes 1024 | tf_op jit(solution)/shard_map/pallas_call | solution.py:165
  64.6 1.1 collective-permute-start.7
  65.6 1.0 collective-permute-start.11
  66.6 2.2 %collective-permute-start.12 = (bf16[160,1152]{1,0:T(8,128)(2,1)}, bf16[160,1152]{1,0:T(8,128)(2,1)S(1)}, u32[]{:S(2)}, u32[]{:S(2)}) collective-permute-start(bf16[160,1152]{1,0:T(8,128)(2,1)} %get-tuple-element.93), channel_id=1, source_target_pairs={{0,48},{16,0},{32,16},{48,32},{1,49},{17,1},{33,17},{49,33},{2,50}... | collective-permute-start | bytes 1105928 | tf_op jit(solution)/shard_map/ppermute | solution.py:25
  68.9 3.5 %all-to-all-start.1 = ((bf16[4,2,72,768]{3,2,1,0:T(8,128)(2,1)}), bf16[4,2,72,768]{3,2,1,0:T(8,128)(2,1)S(1)}, u32[]{:S(2)}, u32[]{:S(2)}) async-start(bf16[4,2,72,768]{3,2,1,0:T(8,128)(2,1)} %get-tuple-element.81), calls=%async_computation.1 | async-start | bytes 1769472 | tf_op jit(solution)/shard_map/all_to_all | solution.py:239
  72.4 0.3 collective-permute-start.9
  72.7 0.8 collective-permute-done.7.b
  73.5 0.7 shard_map.82
  74.2 1.4 %copy-done.10 = bf16[640,1280]{1,0:T(8,128)(2,1)S(1)} copy-done((bf16[640,1280]{1,0:T(8,128)(2,1)S(1)}, bf16[640,1280]{1,0:T(8,128)(2,1)}, u32[]{:S(2)}) %copy-start.10) | copy-done | bytes 1638424
  75.6 2.6 %shard_map.83 = (bf16[320,1152]{1,0:T(8,128)(2,1)S(1)}, bf16[320,1152]{1,0:T(8,128)(2,1)S(1)}, bf16[320,1152]{1,0:T(8,128)(2,1)S(1)}) custom-call(f32[2]{0:T(128)S(1)} %pad_maximum_fusion.scal, bf16[640,1280]{1,0:T(8,128)(2,1)S(1)} %copy-done.10, bf16[640,1152]{1,0:T(8,128)(2,1)S(1)} %get-tuple-element.62.n_txt), custom_call_target="tpu_custom_call" | custom-call | flops 2147483648 | bytes 1024 | tf_op jit(solution)/shard_map/pallas_call | solution.py:250
  78.3 1.3 %shard_map.88 = (bf16[320,1152]{1,0:T(8,128)(2,1)}, bf16[320,1152]{1,0:T(8,128)(2,1)}) custom-call(bf16[320,1152]{1,0:T(8,128)(2,1)S(1)} %get-tuple-element.90.part_a, bf16[320,1152]{1,0:T(8,128)(2,1)S(1)} %get-tuple-element.91.part_b, bf16[160,1152]{1,0:T(8,128)(2,1)S(1)} %collective-permute-done.11.got_b, bf16[160,1152]{1,0:T(8,128)(2,1)S(1)} %collective-permute-done.12.got_a), custom_call_target="tpu_custom_call" | custom-call | flops 1024 | bytes 1024 | tf_op jit(solution)/shard_map/pallas_call | solution.py:262
  79.6 2.0 %collective-permute-start.13 = (bf16[320,1152]{1,0:T(8,128)(2,1)}, bf16[320,1152]{1,0:T(8,128)(2,1)S(1)}, u32[]{:S(2)}, u32[]{:S(2)}) collective-permute-start(bf16[320,1152]{1,0:T(8,128)(2,1)} %get-tuple-element.94), channel_id=1, source_target_pairs={{0,48},{16,0},{32,16},{48,32},{1,49},{17,1},{33,17},{49,33},{2,50}... | collective-permute-start | bytes 2211848 | tf_op jit(solution)/shard_map/ppermute | solution.py:25
  81.6 3.8 %all-to-all-done.1.got = bf16[4,2,72,768]{3,2,1,0:T(8,128)(2,1)S(1)} async-done(((bf16[4,2,72,768]{3,2,1,0:T(8,128)(2,1)}), bf16[4,2,72,768]{3,2,1,0:T(8,128)(2,1)S(1)}, u32[]{:S(2)}, u32[]{:S(2)}) %all-to-all-start.1) | async-done | bytes 884768 | tf_op jit(solution)/shard_map/all_to_all | solution.py:239
  85.4 3.4 %all-to-all-start.2 = ((bf16[4,72,384]{2,1,0:T(8,128)(2,1)}), bf16[4,72,384]{2,1,0:T(8,128)(2,1)S(1)}, u32[]{:S(2)}, u32[]{:S(2)}) async-start(bf16[4,72,384]{2,1,0:T(8,128)(2,1)} %shard_map.82), calls=%async_computation.2 | async-start | bytes 442368 | tf_op jit(solution)/shard_map/all_to_all | solution.py:239
  88.8 0.7 shard_map.84
  89.5 2.3 %collective-permute-start.8 = (bf16[72,768]{1,0:T(8,128)(2,1)S(1)}, bf16[72,768]{1,0:T(8,128)(2,1)S(1)}, u32[]{:S(2)}, u32[]{:S(2)}) collective-permute-start(bf16[72,768]{1,0:T(8,128)(2,1)S(1)} %get-tuple-element.83), channel_id=1, source_target_pairs={{0,72},{8,64},{64,8},{72,0},{1,73},{9,65},{65,9},{73,1},{2,74},{10... | collective-permute-start | bytes 331784 | tf_op jit(solution)/shard_map/ppermute | solution.py:30
  91.7 3.5 %all-to-all-done.2.along = bf16[4,72,384]{2,1,0:T(8,128)(2,1)S(1)} async-done(((bf16[4,72,384]{2,1,0:T(8,128)(2,1)}), bf16[4,72,384]{2,1,0:T(8,128)(2,1)S(1)}, u32[]{:S(2)}, u32[]{:S(2)}) %all-to-all-start.2) | async-done | bytes 221216 | tf_op jit(solution)/shard_map/all_to_all | solution.py:239
  95.2 0.3 collective-permute-done.8.got
  95.7 1.8 %copy-done.1 = f32[640,1152]{1,0:T(8,128)S(1)} copy-done((f32[640,1152]{1,0:T(8,128)S(1)}, f32[640,1152]{1,0:T(8,128)}, u32[]{:S(2)}) %copy-start.1) | copy-done | bytes 2949144
  97.5 1.7 %copy-done.15 = bf16[1152,1152]{1,0:T(8,128)(2,1)S(1)} copy-done((bf16[1152,1152]{1,0:T(8,128)(2,1)S(1)}, bf16[1152,1152]{1,0:T(8,128)(2,1)}, u32[]{:S(2)}) %copy-start.15) | copy-done | bytes 2654232
  99.3 4.6 %shard_map.87 = bf16[320,1152]{1,0:T(8,128)(2,1)} custom-call(f32[640,1152]{1,0:T(8,128)S(1)} %copy-done.1, bf16[320,1152]{1,0:T(8,128)(2,1)S(1)} %copy-done.12, bf16[320,1152]{1,0:T(8,128)(2,1)} %collective-permute-done.9.b, bf16[1152,1152]{1,0:T(8,128)(2,1)S(1)} %copy-done.15), custom_call_target="tpu_custom_call" | custom-call | flops 2147483648 | bytes 1024 | tf_op jit(solution)/shard_map/pallas_call | solution.py:269
  104.0 0.8 collective-permute-start.17
  104.8 1.3 %collective-permute-start.16 = (bf16[72,1152]{1,0:T(8,128)(2,1)S(1)}, bf16[72,1152]{1,0:T(8,128)(2,1)S(1)}, u32[]{:S(2)}, u32[]{:S(2)}) collective-permute-start(bf16[72,1152]{1,0:T(8,128)(2,1)S(1)} %shard_map.86.a), channel_id=1, source_target_pairs={{0,16},{16,32},{32,48},{48,0},{1,17},{17,33},{33,49},{49,1},{2,18}... | collective-permute-start | bytes 497672 | tf_op jit(solution)/shard_map/ppermute | solution.py:25
  106.1 0.4 collective-permute-start.15
  106.5 2.8 %shard_map.89 = bf16[320,1152]{1,0:T(8,128)(2,1)} custom-call(bf16[320,1152]{1,0:T(8,128)(2,1)S(1)} %bitcast.12, bf16[320,1152]{1,0:T(8,128)(2,1)S(1)} %copy-done.17, bf16[320,1152]{1,0:T(8,128)(2,1)S(1)} %collective-permute-done.13.b, bf16[320,1152]{1,0:T(8,128)(2,1)} %collective-permute-done.14.c), custom_call_target="tpu_custom_call" | custom-call | flops 1073741824 | bytes 1024 | tf_op jit(solution)/shard_map/pallas_call | solution.py:327
  109.3 0.7 collective-permute-done.17.d
  109.9 3.4 %collective-permute-done.16.c = bf16[72,1152]{1,0:T(8,128)(2,1)S(1)} collective-permute-done((bf16[72,1152]{1,0:T(8,128)(2,1)S(1)}, bf16[72,1152]{1,0:T(8,128)(2,1)S(1)}, u32[]{:S(2)}, u32[]{:S(2)}) %collective-permute-start.16) | collective-permute-done | bytes 165920 | tf_op jit(solution)/shard_map/ppermute | solution.py:25
  113.3 0.8 shard_map.90
  (48 shorter events, 0.5 us)
Async XLA Ops:
  0.6 38.8 %collective-permute-start.2 = (bf16[320,1152]{1,0:T(8,128)(2,1)}, bf16[320,1152]{1,0:T(8,128)(2,1)S(1)}, u32[]{:S(2)}, u32[]{:S(2)}) collective-permute-start(bf16[320,1152]{1,0:T(8,128)(2,1)} %bitcast.8), channel_id=1, source_target_pairs={{0,64},{64,0},{1,65},{65,1},{2,66},{66,2},{3,67},{67,3},{4,68},{68... | collective-permute-start | bytes 2211848 | tf_op jit(solution)/shard_map/ppermute | solution.py:25
  2.4 1.0 copy-start.8
  3.4 11.1 %collective-permute-start.1 = (bf16[72,1152]{1,0:T(8,128)(2,1)S(1)}, bf16[72,1152]{1,0:T(8,128)(2,1)S(1)}, u32[]{:S(2)}, u32[]{:S(2)}) collective-permute-start(bf16[72,1152]{1,0:T(8,128)(2,1)S(1)} %shard_map.76._), channel_id=1, source_target_pairs={{0,72},{8,64},{64,8},{72,0},{1,73},{9,65},{65,9},{73,1},{2,74},{10... | collective-permute-start | bytes 497672 | tf_op jit(solution)/shard_map/ppermute | solution.py:30
  5.6 1.1 copy-start.3
  7.0 41.4 %collective-permute-start.5 = (bf16[320,1152]{1,0:T(8,128)(2,1)S(1)}, bf16[320,1152]{1,0:T(8,128)(2,1)}, u32[]{:S(2)}, u32[]{:S(2)}) collective-permute-start(bf16[320,1152]{1,0:T(8,128)(2,1)S(1)} %shard_map.78.n_own), channel_id=1, source_target_pairs={{0,32},{16,48},{32,0},{48,16},{1,33},{17,49},{33,1},{49,17},{2,34}... | collective-permute-start | bytes 2211848 | tf_op jit(solution)/shard_map/ppermute | solution.py:25
  11.0 37.4 %collective-permute-start.4 = (bf16[320,1152]{1,0:T(8,128)(2,1)S(1)}, bf16[320,1152]{1,0:T(8,128)(2,1)}, u32[]{:S(2)}, u32[]{:S(2)}) collective-permute-start(bf16[320,1152]{1,0:T(8,128)(2,1)S(1)} %shard_map.78.n_own), channel_id=1, source_target_pairs={{0,48},{16,0},{32,16},{48,32},{1,49},{17,1},{33,17},{49,33},{2,50}... | collective-permute-start | bytes 2211848 | tf_op jit(solution)/shard_map/ppermute | solution.py:25
  11.7 36.7 %collective-permute-start.3 = (bf16[320,1152]{1,0:T(8,128)(2,1)S(1)}, bf16[320,1152]{1,0:T(8,128)(2,1)}, u32[]{:S(2)}, u32[]{:S(2)}) collective-permute-start(bf16[320,1152]{1,0:T(8,128)(2,1)S(1)} %shard_map.78.n_own), channel_id=1, source_target_pairs={{0,16},{16,32},{32,48},{48,0},{1,17},{17,33},{33,49},{49,1},{2,18}... | collective-permute-start | bytes 2211848 | tf_op jit(solution)/shard_map/ppermute | solution.py:25
  14.5 25.8 %copy-start.2 = (bf16[1,320,1152]{2,1,0:T(8,128)(2,1)S(1)}, bf16[1,320,1152]{2,1,0:T(8,128)(2,1)}, u32[]{:S(2)}) copy-start(bf16[1,320,1152]{2,1,0:T(8,128)(2,1)} %param.8) | copy-start | bytes 2211844
  36.0 3.4 %collective-permute-start = (bf16[4,2,72,1152]{3,2,1,0:T(8,128)(2,1)}, bf16[4,2,72,1152]{3,2,1,0:T(8,128)(2,1)}, u32[]{:S(2)}, u32[]{:S(2)}) collective-permute-start(bf16[4,2,72,1152]{3,2,1,0:T(8,128)(2,1)} %all_to_all.14), channel_id=1, source_target_pairs={{0,1},{1,0},{2,3},{3,2},{4,5},{5,4},{6,7},{7,6},{8,9},{9,8},{10,11... | collective-permute-start | bytes 3981320 | tf_op jit(solution)/shard_map/cond/branch_1_fun/ppermute | solution.py:25
  39.5 0.9 copy-start.5
  40.3 1.1 copy-start.6
  41.4 7.0 %copy-start.7 = (bf16[320,1152]{1,0:T(8,128)(2,1)S(1)}, bf16[320,1152]{1,0:T(8,128)(2,1)}, u32[]{:S(2)}) copy-start(bf16[320,1152]{1,0:T(8,128)(2,1)} %copy-done.5) | copy-start | bytes 2211844
  46.9 1.5 %copy-start.14 = (bf16[1152,1152]{1,0:T(8,128)(2,1)}, bf16[1152,1152]{1,0:T(8,128)(2,1)S(1)}, u32[]{:S(2)}) copy-start(bf16[1152,1152]{1,0:T(8,128)(2,1)S(1)} %get-tuple-element.89.w_full) | copy-start | bytes 7962628
  48.4 10.8 %copy-start = (f32[640,1152]{1,0:T(8,128)}, f32[640,1152]{1,0:T(8,128)S(1)}, u32[]{:S(2)}) copy-start(f32[640,1152]{1,0:T(8,128)S(1)} %get-tuple-element.66.z) | copy-start | bytes 8847364
  59.2 2.7 %copy-start.9 = (bf16[640,1280]{1,0:T(8,128)(2,1)}, bf16[640,1280]{1,0:T(8,128)(2,1)S(1)}, u32[]{:S(2)}) copy-start(bf16[640,1280]{1,0:T(8,128)(2,1)S(1)} %get-tuple-element.79.grad) | copy-start | bytes 4915204
  59.2 2.7 %copy-start.11 = (bf16[320,1152]{1,0:T(8,128)(2,1)}, bf16[320,1152]{1,0:T(8,128)(2,1)S(1)}, u32[]{:S(2)}) copy-start(bf16[320,1152]{1,0:T(8,128)(2,1)S(1)} %get-tuple-element.87.a) | copy-start | bytes 2211844
  59.2 2.7 %copy-start.13 = (bf16[320,1152]{1,0:T(8,128)(2,1)}, bf16[320,1152]{1,0:T(8,128)(2,1)S(1)}, u32[]{:S(2)}) copy-start(bf16[320,1152]{1,0:T(8,128)(2,1)S(1)} %get-tuple-element.85) | copy-start | bytes 2211844
  59.2 3.1 %collective-permute-start.6 = (bf16[4,2,72,1152]{3,2,1,0:T(8,128)(2,1)S(1)}, bf16[4,2,72,1152]{3,2,1,0:T(8,128)(2,1)S(1)}, u32[]{:S(2)}, u32[]{:S(2)}) collective-permute-start(bf16[4,2,72,1152]{3,2,1,0:T(8,128)(2,1)S(1)} %get-tuple-element.68), channel_id=1, source_target_pairs={{0,1},{1,0},{2,3},{3,2},{4,5},{5,4},{6,7},{7,6},{8,9},{9,8},{10,11... | collective-permute-start | bytes 3981320 | tf_op jit(solution)/shard_map/ppermute | solution.py:25
  64.6 8.9 %collective-permute-start.7 = (bf16[4,72,384]{2,1,0:T(8,128)(2,1)}, bf16[4,72,384]{2,1,0:T(8,128)(2,1)S(1)}, u32[]{:S(2)}, u32[]{:S(2)}) collective-permute-start(bf16[4,72,384]{2,1,0:T(8,128)(2,1)} %get-tuple-element.78), channel_id=1, source_target_pairs={{0,72},{8,64},{64,8},{72,0},{1,73},{9,65},{65,9},{73,1},{2,74},{10... | collective-permute-start | bytes 663560 | tf_op jit(solution)/shard_map/ppermute | solution.py:30
  65.6 12.7 %collective-permute-start.11 = (bf16[160,1152]{1,0:T(8,128)(2,1)}, bf16[160,1152]{1,0:T(8,128)(2,1)S(1)}, u32[]{:S(2)}, u32[]{:S(2)}) collective-permute-start(bf16[160,1152]{1,0:T(8,128)(2,1)} %get-tuple-element.92), channel_id=1, source_target_pairs={{0,16},{16,32},{32,48},{48,0},{1,17},{17,33},{33,49},{49,1},{2,18}... | collective-permute-start | bytes 1105928 | tf_op jit(solution)/shard_map/ppermute | solution.py:25
  66.6 11.6 %collective-permute-start.12 = (bf16[160,1152]{1,0:T(8,128)(2,1)}, bf16[160,1152]{1,0:T(8,128)(2,1)S(1)}, u32[]{:S(2)}, u32[]{:S(2)}) collective-permute-start(bf16[160,1152]{1,0:T(8,128)(2,1)} %get-tuple-element.93), channel_id=1, source_target_pairs={{0,48},{16,0},{32,16},{48,32},{1,49},{17,1},{33,17},{49,33},{2,50}... | collective-permute-start | bytes 1105928 | tf_op jit(solution)/shard_map/ppermute | solution.py:25
  68.9 16.6 %all-to-all-start.1 = ((bf16[4,2,72,768]{3,2,1,0:T(8,128)(2,1)}), bf16[4,2,72,768]{3,2,1,0:T(8,128)(2,1)S(1)}, u32[]{:S(2)}, u32[]{:S(2)}) async-start(bf16[4,2,72,768]{3,2,1,0:T(8,128)(2,1)} %get-tuple-element.81), calls=%async_computation.1 | async-start | bytes 1769472 | tf_op jit(solution)/shard_map/all_to_all | solution.py:239
  72.4 23.2 %collective-permute-start.9 = (bf16[320,1152]{1,0:T(8,128)(2,1)}, bf16[320,1152]{1,0:T(8,128)(2,1)}, u32[]{:S(2)}, u32[]{:S(2)}) collective-permute-start(bf16[320,1152]{1,0:T(8,128)(2,1)} %copy-done.13), channel_id=1, source_target_pairs={{0,64},{64,0},{1,65},{65,1},{2,66},{66,2},{3,67},{67,3},{4,68},{68... | collective-permute-start | bytes 2211848 | tf_op jit(solution)/shard_map/ppermute | solution.py:25
  74.2 1.4 %copy-start.10 = (bf16[640,1280]{1,0:T(8,128)(2,1)S(1)}, bf16[640,1280]{1,0:T(8,128)(2,1)}, u32[]{:S(2)}) copy-start(bf16[640,1280]{1,0:T(8,128)(2,1)} %copy-done.9) | copy-start | bytes 4915204
  78.3 3.3 %copy-start.16 = (bf16[320,1152]{1,0:T(8,128)(2,1)}, bf16[320,1152]{1,0:T(8,128)(2,1)S(1)}, u32[]{:S(2)}) copy-start(bf16[320,1152]{1,0:T(8,128)(2,1)S(1)} %get-tuple-element.80.a) | copy-start | bytes 2211844
  79.6 16.1 %copy-start.12 = (bf16[320,1152]{1,0:T(8,128)(2,1)S(1)}, bf16[320,1152]{1,0:T(8,128)(2,1)}, u32[]{:S(2)}) copy-start(bf16[320,1152]{1,0:T(8,128)(2,1)} %copy-done.11) | copy-start | bytes 2211844
  79.6 24.4 %collective-permute-start.13 = (bf16[320,1152]{1,0:T(8,128)(2,1)}, bf16[320,1152]{1,0:T(8,128)(2,1)S(1)}, u32[]{:S(2)}, u32[]{:S(2)}) collective-permute-start(bf16[320,1152]{1,0:T(8,128)(2,1)} %get-tuple-element.94), channel_id=1, source_target_pairs={{0,48},{16,0},{32,16},{48,32},{1,49},{17,1},{33,17},{49,33},{2,50}... | collective-permute-start | bytes 2211848 | tf_op jit(solution)/shard_map/ppermute | solution.py:25
  81.6 22.4 %collective-permute-start.14 = (bf16[320,1152]{1,0:T(8,128)(2,1)}, bf16[320,1152]{1,0:T(8,128)(2,1)}, u32[]{:S(2)}, u32[]{:S(2)}) collective-permute-start(bf16[320,1152]{1,0:T(8,128)(2,1)} %get-tuple-element.95), channel_id=1, source_target_pairs={{0,16},{16,32},{32,48},{48,0},{1,17},{17,33},{33,49},{49,1},{2,18}... | collective-permute-start | bytes 2211848 | tf_op jit(solution)/shard_map/ppermute | solution.py:25
  85.4 9.8 %all-to-all-start.2 = ((bf16[4,72,384]{2,1,0:T(8,128)(2,1)}), bf16[4,72,384]{2,1,0:T(8,128)(2,1)S(1)}, u32[]{:S(2)}, u32[]{:S(2)}) async-start(bf16[4,72,384]{2,1,0:T(8,128)(2,1)} %shard_map.82), calls=%async_computation.2 | async-start | bytes 442368 | tf_op jit(solution)/shard_map/all_to_all | solution.py:239
  89.5 6.0 %collective-permute-start.8 = (bf16[72,768]{1,0:T(8,128)(2,1)S(1)}, bf16[72,768]{1,0:T(8,128)(2,1)S(1)}, u32[]{:S(2)}, u32[]{:S(2)}) collective-permute-start(bf16[72,768]{1,0:T(8,128)(2,1)S(1)} %get-tuple-element.83), channel_id=1, source_target_pairs={{0,72},{8,64},{64,8},{72,0},{1,73},{9,65},{65,9},{73,1},{2,74},{10... | collective-permute-start | bytes 331784 | tf_op jit(solution)/shard_map/ppermute | solution.py:30
  95.6 8.3 %collective-permute-start.10 = (bf16[72,1152]{1,0:T(8,128)(2,1)S(1)}, bf16[72,1152]{1,0:T(8,128)(2,1)S(1)}, u32[]{:S(2)}, u32[]{:S(2)}) collective-permute-start(bf16[72,1152]{1,0:T(8,128)(2,1)S(1)} %shard_map.85.a), channel_id=1, source_target_pairs={{0,64},{64,0},{1,65},{65,1},{2,66},{66,2},{3,67},{67,3},{4,68},{68... | collective-permute-start | bytes 497672 | tf_op jit(solution)/shard_map/ppermute | solution.py:25
  95.7 1.8 %copy-start.1 = (f32[640,1152]{1,0:T(8,128)S(1)}, f32[640,1152]{1,0:T(8,128)}, u32[]{:S(2)}) copy-start(f32[640,1152]{1,0:T(8,128)} %copy-done) | copy-start | bytes 8847364
  97.5 1.7 %copy-start.15 = (bf16[1152,1152]{1,0:T(8,128)(2,1)S(1)}, bf16[1152,1152]{1,0:T(8,128)(2,1)}, u32[]{:S(2)}) copy-start(bf16[1152,1152]{1,0:T(8,128)(2,1)} %copy-done.14) | copy-start | bytes 7962628
  99.3 7.3 %copy-start.4 = (bf16[1,320,1152]{2,1,0:T(8,128)(2,1)S(1)}, bf16[1,320,1152]{2,1,0:T(8,128)(2,1)}, u32[]{:S(2)}) copy-start(bf16[1,320,1152]{2,1,0:T(8,128)(2,1)} %param.7) | copy-start | bytes 2211844
  99.3 7.3 %copy-start.17 = (bf16[320,1152]{1,0:T(8,128)(2,1)S(1)}, bf16[320,1152]{1,0:T(8,128)(2,1)}, u32[]{:S(2)}) copy-start(bf16[320,1152]{1,0:T(8,128)(2,1)} %copy-done.16) | copy-start | bytes 2211844
  104.0 5.9 %collective-permute-start.17 = (bf16[72,1152]{1,0:T(8,128)(2,1)S(1)}, bf16[72,1152]{1,0:T(8,128)(2,1)S(1)}, u32[]{:S(2)}, u32[]{:S(2)}) collective-permute-start(bf16[72,1152]{1,0:T(8,128)(2,1)S(1)} %shard_map.86.a), channel_id=1, source_target_pairs={{0,48},{16,0},{32,16},{48,32},{1,49},{17,1},{33,17},{49,33},{2,50}... | collective-permute-start | bytes 497672 | tf_op jit(solution)/shard_map/ppermute | solution.py:25
  104.8 8.6 %collective-permute-start.16 = (bf16[72,1152]{1,0:T(8,128)(2,1)S(1)}, bf16[72,1152]{1,0:T(8,128)(2,1)S(1)}, u32[]{:S(2)}, u32[]{:S(2)}) collective-permute-start(bf16[72,1152]{1,0:T(8,128)(2,1)S(1)} %shard_map.86.a), channel_id=1, source_target_pairs={{0,16},{16,32},{32,48},{48,0},{1,17},{17,33},{33,49},{49,1},{2,18}... | collective-permute-start | bytes 497672 | tf_op jit(solution)/shard_map/ppermute | solution.py:25
  106.1 7.2 %collective-permute-start.15 = (bf16[72,1152]{1,0:T(8,128)(2,1)S(1)}, bf16[72,1152]{1,0:T(8,128)(2,1)S(1)}, u32[]{:S(2)}, u32[]{:S(2)}) collective-permute-start(bf16[72,1152]{1,0:T(8,128)(2,1)S(1)} %shard_map.86.a), channel_id=1, source_target_pairs={{0,32},{16,48},{32,0},{48,16},{1,33},{17,49},{33,1},{49,17},{2,34}... | collective-permute-start | bytes 497672 | tf_op jit(solution)/shard_map/ppermute | solution.py:25

commit v6 on v5

v6 whole, which is shorter than its diff:
```python
import functools

import jax
import jax.numpy as jnp
from jax import lax
from jax.experimental import pallas as pl
from jax.experimental.pallas import tpu as pltpu
from jax.sharding import Mesh, PartitionSpec as P

BF = jnp.bfloat16
F32 = jnp.float32
MIB = 1024 * 1024
TEXT_MIB = 14
MAIN_MIB = 24
AXES = {"ylo": 2, "z": 4, "yhi": 2, "x": 4, "core": 2}

VM = pl.BlockSpec(memory_space=pltpu.VMEM)
SM = pl.BlockSpec(memory_space=pltpu.SMEM)
ANY = pl.BlockSpec(memory_space=pl.ANY)


def shift(value, axis, step):
    n = AXES[axis]
    return lax.ppermute(value, axis, [(i, (i + step) % n) for i in range(n)])


def apart_by_core(value):
    pairs = [(z * 2 + c, (z + 1 - 2 * c) % 4 * 2 + c) for z in range(4) for c in range(2)]
    return lax.ppermute(value, ("z", "core"), pairs)


def swap_far(value):
    pairs = [(a * 2 + b, (1 - a) * 2 + 1 - b) for a in range(2) for b in range(2)]
    return lax.ppermute(value, ("ylo", "yhi"), pairs)


def shaped(shape, dtype):
    return jax.ShapeDtypeStruct(shape, dtype)


def call(kernel, outs, specs, scratch=(), vmem=10, out_specs=None, flops=1024):
    return pl.pallas_call(
        kernel,
        out_shape=outs,
        in_specs=specs,
        out_specs=out_specs or [VM] * len(outs),
        scratch_shapes=list(scratch),
        compiler_params=pltpu.CompilerParams(vmem_limit_bytes=vmem * MIB),
        cost_estimate=pl.CostEstimate(flops=flops, bytes_accessed=1024, transcendentals=0),
    )


def inverse_length(rows):
    return 1.0 / jnp.sqrt(jnp.sum(rows * rows, axis=-1, keepdims=True) + 1e-06)


def project(grad, rows):
    inv = inverse_length(rows)
    unit = rows * inv
    inner = jnp.sum(unit * grad, axis=-1, keepdims=True)
    return (grad - unit * inner) * inv


def half_kernel(w, w_half):
    w_half[...] = w[...].astype(BF)


def repeat_kernel(w_h, w_y, out):
    yhi = lax.axis_index("yhi")
    for k in range(4):
        out[k, yhi] = w_h[...]
        out[k, 1 - yhi] = w_y[...]


def unit_kernel(img, _, n_img):
    rows = img[...].astype(F32)
    n_img[...] = (rows * inverse_length(rows)).astype(BF)


def assemble(mine, other, head):
    core = lax.axis_index("core")
    for x in range(4):
        for h in range(2):
            a, b = mine[x, h].astype(F32), other[x, h].astype(F32)
            first = jnp.where(core == 0, a, b)
            second = jnp.where(core == 0, b, a)
            head[pl.ds((h * 4 + x) * 144, 144), :] = jnp.concatenate([first, second], axis=0).astype(BF)


def text_kernel(near, far, txt, txt_far, z, n_txt, mine, other, rows, w_full, sems):
    copies = [
        pltpu.make_async_copy(near, mine, sems.at[0]),
        pltpu.make_async_copy(far, other, sems.at[1]),
        pltpu.make_async_copy(txt, rows.at[pl.ds(0, 320)], sems.at[2]),
        pltpu.make_async_copy(txt_far, rows.at[pl.ds(320, 320)], sems.at[3]),
    ]
    for c in copies:
        c.start()
    for c in copies[:2]:
        c.wait()
    assemble(mine, other, w_full)
    for c in copies[2:]:
        c.wait()
    out = jnp.dot(rows[...], w_full[...], preferred_element_type=F32)
    z[...] = out
    n_txt[...] = (out * inverse_length(out)).astype(BF)


def scale_of(t_log):
    return jnp.exp(jnp.full((1, 1), t_log[0], F32))


def logit_gradient(scale, bias, left, right):
    logits = scale * lax.dot_general(
        left, right, (((1,), (1,)), ((), ())), preferred_element_type=F32
    ) + bias[0]
    return 1.0 / (1.0 + jnp.exp(-logits))


def main_kernel(t_log, bias, n_txt, n_own, n_a, n_b, n_c, z, txt, txt_far, grad, g_own, g_far, mine, other, rows, feat, wide, sems):
    moves = [(block, rows.at[pl.ds(k * 320, 320)]) for k, block in enumerate((n_own, n_a, n_b, n_c))]
    moves += [(txt, feat.at[pl.ds(0, 320)]), (txt_far, feat.at[pl.ds(320, 320)])]
    copies = [pltpu.make_async_copy(a, b, sems.at[k]) for k, (a, b) in enumerate(moves)]
    for c in copies:
        c.start()
    for c in copies[:4]:
        c.wait()
    scale = scale_of(t_log)
    g = logit_gradient(scale, bias, n_txt[...], rows[...])
    row_ids = lax.broadcasted_iota(jnp.int32, g.shape, 0)
    col_ids = lax.broadcasted_iota(jnp.int32, g.shape, 1)
    grad[...] = (g - jnp.where((row_ids == col_ids) & (row_ids < 320), 1.0, 0.0)).astype(BF)
    total = scale * jnp.dot(grad[...], rows[...], preferred_element_type=F32)
    g_own[...] = total[:320].astype(BF)
    g_far[...] = total[320:].astype(BF)
    for c in copies[4:]:
        c.wait()
    dz = project(total, z[...]).astype(BF)
    wide[...] = lax.dot_general(
        feat[...], dz, (((0,), (0,)), ((), ())), preferred_element_type=F32
    )
    core = lax.axis_index("core")
    for j in range(8):
        a = pl.multiple_of((2 * j + core) * 72, 8)
        b = pl.multiple_of((2 * j + 1 - core) * 72, 8)
        mine[j % 4, j // 4] = wide[pl.ds(a, 72), :].astype(BF)
        other[j % 4, j // 4] = wide[pl.ds(b, 72), :].astype(BF)


def part_kernel(first, t_log, grad, n_txt, *outs):
    start = first * 320
    rows = sum(ref.shape[0] for ref in outs)
    out = scale_of(t_log) * lax.dot_general(
        grad[:, start : start + rows], n_txt[...], (((0,), (0,)), ((), ())), preferred_element_type=F32
    )
    at = 0
    for ref in outs:
        ref[...] = out[at : at + ref.shape[0]].astype(BF)
        at += ref.shape[0]


def pass_on_kernel(part_a, part_b, got, out_a, out_b):
    first = lax.axis_index("core") == 0
    for part, out, take in ((part_a, out_a, jnp.logical_not(first)), (part_b, out_b, first)):
        out[...] = (part[...].astype(F32) + jnp.where(take, got[...].astype(F32), 0.0)).astype(BF)


def core_sum_kernel(mine, got, *outs):
    x = lax.axis_index("x")
    for r, out in enumerate(outs):
        k = (x + r) % 4
        out[...] = (mine[k].astype(F32) + got[k].astype(F32)).astype(BF)


def x_sum_kernel(own, p, q, r, keep, send):
    yhi = lax.axis_index("yhi")
    for out, h in ((keep, yhi), (send, 1 - yhi)):
        a, b, c, d = (part[h].astype(F32) for part in (own, p, q, r))
        out[...] = ((a + b) + (c + d)).astype(BF)


def pair_sum_kernel(a, b, out):
    out[...] = (a[...].astype(F32) + b[...].astype(F32)).astype(BF)


def quad_sum_kernel(a, b, c, d, out):
    total = (a[...].astype(F32) + b[...].astype(F32)) + (c[...].astype(F32) + d[...].astype(F32))
    out[...] = total.astype(out.dtype)


def image_out_kernel(img, a, b, c, out):
    grad = a[...].astype(F32) + (b[...].astype(F32) + c[...].astype(F32))
    out[...] = project(grad, img[...].astype(F32)).astype(BF)


def text_out_kernel(z, a, b, near, far, out, rows, mine, other, head, sems):
    moves = (near, mine), (far, other), (z.at[pl.ds(0, 320)], rows)
    copies = [pltpu.make_async_copy(x, y, sems.at[k]) for k, (x, y) in enumerate(moves)]
    for c in copies:
        c.start()
    for c in copies:
        c.wait()
    assemble(mine, other, head)
    dz = project(a[...].astype(F32) + b[...].astype(F32), rows[...]).astype(BF)
    out[...] = lax.dot_general(
        dz, head[...], (((1,), (1,)), ((), ())), preferred_element_type=F32
    ).astype(BF)


def apart(step, *args):
    outs = jax.eval_shape(step, *args)
    return lax.cond(
        lax.axis_index("z") < AXES["z"],
        step,
        lambda *_: jax.tree.map(lambda o: jnp.zeros(o.shape, o.dtype), outs),
        *args,
    )


hold = lax.optimization_barrier
BLOCK = shaped((320, 1152), BF)


def stack_of(*lead):
    return shaped((*lead, 72, 1152), BF)


def along_x(value):
    return lax.all_to_all(value, "x", split_axis=0, concat_axis=0, tiled=True)


def gather_head(w_h, w_y):
    (pieces,) = call(repeat_kernel, [stack_of(4, 2)], [VM, VM])(w_h, w_y)
    near = along_x(pieces)
    return near, shift(near, "core", 1)


def parts_of(first, shapes, *args):
    kernel = functools.partial(part_kernel, first)
    return call(kernel, shapes, [SM] + [VM] * 2, flops=1 << 31)(*args)


def beside_x(part_c, t_log, grad, n_txt):
    got_c = apart_by_core(part_c)
    part_own, part_a, part_b = parts_of(0, [BLOCK] * 3, t_log, grad, n_txt)
    return part_own, *call(pass_on_kernel, [BLOCK] * 2, [VM] * 3)(part_a, part_b, got_c)


def sum_plane(t_log, mine, got_core, part_c, grad, n_txt, z, g_own, g_far, near, far):
    rel = call(core_sum_kernel, [stack_of(2)] * 4, [VM] * 2)(mine, got_core)
    got_x = [shift(rel[s], "x", s) for s in (1, 3, 2)]
    g_got = shift(g_far, "ylo", 1)
    part_own, part_a, part_b = beside_x(part_c, t_log, grad, n_txt)
    got_x[2], part_a, part_b = hold((got_x[2], part_a, part_b))
    keep, send = call(x_sum_kernel, [stack_of()] * 2, [VM] * 4)(rel[0], *got_x)
    got_a, got_b = shift(part_a, "z", -1), shift(part_b, "z", 1)
    (d_feat,) = call(
        text_out_kernel,
        [BLOCK],
        [ANY, VM, VM, ANY, ANY],
        [
            pltpu.VMEM((320, 1152), F32),
            pltpu.VMEM((4, 2, 72, 1152), BF),
            pltpu.VMEM((4, 2, 72, 1152), BF),
            pltpu.VMEM((1152, 1152), BF),
            pltpu.SemaphoreType.DMA((3,)),
        ],
        vmem=50,
        flops=1 << 31,
    )(z, g_own, g_got, near, far)
    (one,) = call(pair_sum_kernel, [stack_of()], [VM] * 2)(keep, swap_far(send))
    (pair,) = call(pair_sum_kernel, [stack_of()], [VM] * 2)(one, shift(one, "ylo", 1))
    pair, d_feat = hold((pair, d_feat))
    return pair, d_feat, part_own, got_a, got_b


def on_device(img_emb, txt_feat, w_txt, t_log, bias):
    img, txt = img_emb[0], txt_feat[0]

    txt_far = shift(txt, "ylo", 1)
    (w_h,) = call(half_kernel, [stack_of()], [VM])(w_txt)
    w_y = swap_far(w_h)
    (n_img,) = call(unit_kernel, [BLOCK], [VM, ANY])(img, w_h)
    n_c, n_b, n_a = (shift(n_img, "z", s) for s in (2, -1, 1))
    near, far = apart(gather_head, w_h, w_y)
    near, far, txt_far = hold((near, far, txt_far))

    z, n_txt = call(
        text_kernel,
        [shaped((640, 1152), F32), shaped((640, 1152), BF)],
        [ANY] * 4,
        [
            pltpu.VMEM((4, 2, 72, 1152), BF),
            pltpu.VMEM((4, 2, 72, 1152), BF),
            pltpu.VMEM((640, 1152), BF),
            pltpu.VMEM((1152, 1152), BF),
            pltpu.SemaphoreType.DMA((4,)),
        ],
        vmem=TEXT_MIB,
        flops=1 << 34,
    )(near, far, txt, txt_far)
    n_txt, n_a, n_b, n_c = hold((n_txt, n_a, n_b, n_c))
    grad, g_own, g_far, mine, other = call(
        main_kernel,
        [shaped((640, 1280), BF), BLOCK, BLOCK, stack_of(4, 2), stack_of(4, 2)],
        [SM, SM, VM] + [ANY] * 4 + [VM, ANY, ANY],
        [
            pltpu.VMEM((1280, 1152), BF),
            pltpu.VMEM((640, 1152), BF),
            pltpu.VMEM((1152, 1152), F32),
            pltpu.SemaphoreType.DMA((6,)),
        ],
        vmem=MAIN_MIB,
    )(t_log, bias, n_txt, n_img, n_a, n_b, n_c, z, txt, txt_far)

    got_core, (part_c,) = hold(
        (shift(other, "core", 1), parts_of(3, [BLOCK], t_log, grad, n_txt))
    )
    quad, d_feat, part_own, got_a, got_b = sum_plane(
        t_log, mine, got_core, part_c, grad, n_txt, z, g_own, g_far, near, far
    )
    (d_img,) = call(image_out_kernel, [BLOCK], [VM] * 4, flops=1 << 30)(img, part_own, got_a, got_b)
    got_z = [shift(quad, "z", k) for k in (2, 1, -1)]
    got_z, d_img = hold((got_z, d_img))
    (d_weight,) = call(quad_sum_kernel, [shaped((72, 1152), F32)], [VM] * 4)(quad, *got_z)
    return (d_img[None], d_feat[None], d_weight)


def solution(mesh):
    fine = Mesh(mesh.devices.reshape(2, 4, 2, 4, 2), tuple(AXES))
    dp, fsdp = ("ylo", "z"), ("yhi", "x", "core")
    placed = (P(fsdp, dp, None), P(fsdp, dp, None), P(fsdp, None), P(), P())
    return jax.shard_map(
        on_device,
        mesh=fine,
        in_specs=placed,
        out_specs=(P(fsdp, dp, None), P(fsdp, dp, None), P(fsdp, None)),
        check_vma=False,
    )
```

time: 115 us -> 104 us (0.904)
  waiting for transfers between devices: 16.3 us -> 25.5 us
  local copies, waits for them, and re-layouts: 10.6 us -> 2.11 us
  Pallas kernels: 35.4 us -> 28.1 us
  starting transfers between devices: 28.6 us -> 24.3 us
    unnamed x36 -> x10, local copies, waits for them, and re-layouts: 10.6 us -> 2.11 us
    ppermute x15 -> x16, waiting for transfers between devices: 7.95 us -> 16.2 us  [shift(): return lax.ppermute(value, axis, [(i, (i + step) % n) for i in range(n)])]
    all_to_all x2 -> x0, waiting for transfers between devices: 7.27 us -> none  [along_x(): return lax.all_to_all(value, 'x', split_axis=0, concat_axis=0, tiled=True)]
    all_to_all x2 -> x0, starting transfers between devices: 6.88 us -> none  [along_x(): return lax.all_to_all(value, 'x', split_axis=0, concat_axis=0, tiled=True)]
    ppermute x3 -> x2, waiting for transfers between devices: 1.05 us -> 6.42 us  [swap_far(): return lax.ppermute(value, ('ylo', 'yhi'), pairs)]
    pallas_call x9 -> x8, Pallas kernels: 16.5 us -> 11.7 us  [the longest x1 4.94 us: sum_plane(): call(text_out_kernel, [BLOCK], [ANY, VM, VM, ANY, ANY], [pltpu.VMEM((320,...]
    ppermute x15 -> x16, starting transfers between devices: 16.1 us -> 19.9 us  [shift(): return lax.ppermute(value, axis, [(i, (i + step) % n) for i in range(n)])]
    ppermute x0 -> x1, waiting for transfers between devices: none -> 2.93 us  [apart_by_core(): return lax.ppermute(value, ('z', 'core'), pairs)]
  transfers between devices with their start and end apart: 20 -> 19, of which waited for: 8 -> 9; matrix products, arithmetic and copies ran while one was open for 0% -> 0% of each run, Pallas kernels for 19% -> 15%
where the time goes in v6:
time: 104 us; the launch traced here: 103 us
  Pallas kernels  28.1 us (27%)
  waiting for transfers between devices  25.5 us (25%)
  starting transfers between devices  24.3 us (23%)
  blocking collectives  21 us (20%)
  local copies, waits for them, and re-layouts  2.11 us (2%)
  between operations  2.09 us (2%)
    all_to_all x1, blocking collectives, along_x(): return lax.all_to_all(value, 'x', split_axis=0, concat_axis=0, tiled=True)  21 us
    ppermute x16, starting transfers between devices, shift(): return lax.ppermute(value, axis, [(i, (i + step) % n) for i in range(n)])  19.9 us
    ppermute x16, waiting for transfers between devices, shift(): return lax.ppermute(value, axis, [(i, (i + step) % n) for i in range(n)])  16.2 us
    pallas_call x1, Pallas kernels, on_device(): call(main_kernel, [shaped((640, 1280), BF), BLOCK, BLOCK, stack_of(4, 2),...  11.3 us
    ppermute x2, waiting for transfers between devices, swap_far(): return lax.ppermute(value, ('ylo', 'yhi'), pairs)  6.42 us
    pallas_call x1, Pallas kernels, sum_plane(): call(text_out_kernel, [BLOCK], [ANY, VM, VM, ANY, ANY], [pltpu.VMEM((320,...  4.94 us
    pallas_call x1, Pallas kernels, on_device(): call(text_kernel, [shaped((640, 1152), F32), shaped((640, 1152), BF)], [A...  4.84 us
    ppermute x2, starting transfers between devices, swap_far(): return lax.ppermute(value, ('ylo', 'yhi'), pairs)  3.39 us
  transfers between devices with their start and end apart: 19, of which 9 were waited for; matrix products, arithmetic and copies ran while one was open for 0% of the time, Pallas kernels for 15%

profile of v6, /device:TPU:0, one launch (start us, length us, event | category | flops | bytes accessed | tf_op | source)
XLA Modules:
  0.0 103.2 jit_solution(1162127109290897263)
XLA Ops:
  0.6 1.7 %collective-permute-start.2 = (bf16[320,1152]{1,0:T(8,128)(2,1)}, bf16[320,1152]{1,0:T(8,128)(2,1)S(1)}, u32[]{:S(2)}, u32[]{:S(2)}) collective-permute-start(bf16[320,1152]{1,0:T(8,128)(2,1)} %bitcast.4), channel_id=1, source_target_pairs={{0,64},{64,0},{1,65},{65,1},{2,66},{66,2},{3,67},{67,3},{4,68},{68... | collective-permute-start | bytes 2211848 | tf_op jit(solution)/shard_map/ppermute | solution.py:24
  2.4 1.0 copy-done.4
  3.4 2.3 %collective-permute-start.1 = (bf16[72,1152]{1,0:T(8,128)(2,1)S(1)}, bf16[72,1152]{1,0:T(8,128)(2,1)S(1)}, u32[]{:S(2)}, u32[]{:S(2)}) collective-permute-start(bf16[72,1152]{1,0:T(8,128)(2,1)S(1)} %shard_map.76._), channel_id=1, source_target_pairs={{0,72},{8,64},{64,8},{72,0},{1,73},{9,65},{65,9},{73,1},{2,74},{10... | collective-permute-start | bytes 497672 | tf_op jit(solution)/shard_map/ppermute | solution.py:34
  5.6 1.1 %copy-done.2 = bf16[1,320,1152]{2,1,0:T(8,128)(2,1)S(1)} copy-done((bf16[1,320,1152]{2,1,0:T(8,128)(2,1)S(1)}, bf16[1,320,1152]{2,1,0:T(8,128)(2,1)}, u32[]{:S(2)}) %copy-start.2) | copy-done | bytes 737304
  6.7 0.3 shard_map.78.n_own
  7.0 4.0 %collective-permute-start.5 = (bf16[320,1152]{1,0:T(8,128)(2,1)S(1)}, bf16[320,1152]{1,0:T(8,128)(2,1)S(1)}, u32[]{:S(2)}, u32[]{:S(2)}) collective-permute-start(bf16[320,1152]{1,0:T(8,128)(2,1)S(1)} %shard_map.78.n_own), channel_id=1, source_target_pairs={{0,32},{16,48},{32,0},{48,16},{1,33},{17,49},{33,1},{49,17},{2,34}... | collective-permute-start | bytes 2211848 | tf_op jit(solution)/shard_map/ppermute | solution.py:24
  11.0 0.7 collective-permute-start.4
  11.7 1.3 %collective-permute-start.3 = (bf16[320,1152]{1,0:T(8,128)(2,1)S(1)}, bf16[320,1152]{1,0:T(8,128)(2,1)}, u32[]{:S(2)}, u32[]{:S(2)}) collective-permute-start(bf16[320,1152]{1,0:T(8,128)(2,1)S(1)} %shard_map.78.n_own), channel_id=1, source_target_pairs={{0,16},{16,32},{32,48},{48,0},{1,17},{17,33},{33,49},{49,1},{2,18}... | collective-permute-start | bytes 2211848 | tf_op jit(solution)/shard_map/ppermute | solution.py:24
  14.3 0.0 copy-start.1
  14.3 24.5 %conditional.1 = (bf16[4,2,72,1152]{3,2,1,0:T(8,128)(2,1)}, bf16[4,2,72,1152]{3,2,1,0:T(8,128)(2,1)}) conditional(s32[]{:T(128)} %convert_element_type.3, () %tuple.22, (bf16[72,1152]{1,0:T(8,128)(2,1)S(1)}, bf16[72,1152]{1,0:T(8,128)(2,1)S(1)}) %tuple.23), branch_computations={%region_0.0_spmd, %region_1.0_spmd} | conditional | flops 1024 | bytes 7963704 | solution.py:212
  14.3 0.1 branch_1_fun.1
  14.5 21.0 %all_to_all.4 = bf16[4,2,72,1152]{3,2,1,0:T(8,128)(2,1)} all-to-all(bf16[4,2,72,1152]{3,2,1,0:T(8,128)(2,1)S(1)} %branch_1_fun.1), channel_id=1, replica_groups=mesh['ylo'=2,'z'=4,'yhi'=2,'x'=4,'core'=2] {'x'}, dimensions={0} | all-to-all | bytes 2654208 | tf_op jit(solution)/shard_map/cond/branch_1_fun/all_to_all | solution.py:229
  35.5 0.0 collective-permute-start
  35.5 3.4 %collective-permute-done = bf16[4,2,72,1152]{3,2,1,0:T(8,128)(2,1)} collective-permute-done((bf16[4,2,72,1152]{3,2,1,0:T(8,128)(2,1)}, bf16[4,2,72,1152]{3,2,1,0:T(8,128)(2,1)}, u32[]{:S(2)}, u32[]{:S(2)}) %collective-permute-start) | collective-permute-done | bytes 1327136 | tf_op jit(solution)/shard_map/cond/branch_1_fun/ppermute | solution.py:24
  38.9 0.0 collective-permute-done.2.txt_far
  38.9 4.8 %shard_map.77 = (f32[640,1152]{1,0:T(8,128)S(1)}, bf16[640,1152]{1,0:T(8,128)(2,1)S(1)}) custom-call(bf16[4,2,72,1152]{3,2,1,0:T(8,128)(2,1)} %get-tuple-element.49.near, bf16[4,2,72,1152]{3,2,1,0:T(8,128)(2,1)} %get-tuple-element.50.far, bf16[320,1152]{1,0:T(8,128)(2,1)S(1)} %bitcast.5, bf16[320,1152]{1,0:T(8,128)(2,1)S(1)} %collective-permute-done.2.txt_far), custom_call_target="tpu_custom_call" | custom-call | flops 17179869184 | bytes 1024 | tf_op jit(solution)/shard_map/pallas_call | solution.py:288
  43.7 0.0 collective-permute-done.5.n_c
  43.8 0.0 collective-permute-done.4.n_b
  43.8 11.3 %shard_map.79 = (bf16[640,1280]{1,0:T(8,128)(2,1)S(1)}, bf16[320,1152]{1,0:T(8,128)(2,1)S(1)}, bf16[320,1152]{1,0:T(8,128)(2,1)S(1)}, bf16[4,2,72,1152]{3,2,1,0:T(8,128)(2,1)S(1)}, bf16[4,2,72,1152]{3,2,1,0:T(8,128)(2,1)S(1)}) custom-call(f32[1]{0:T(128)S(6)} %copy.12.t_log, f32[1]{0:T(128)S(6)} %copy.13.bias, ...), custom_call_target="tpu_custom_call" | custom-call | flops 1024 | bytes 1024 | tf_op jit(solution)/shard_map/pallas_call | solution.py:303
  55.1 0.4 collective-permute-start.6
  55.5 1.0 shard_map.80
  56.5 1.7 %collective-permute-done.6.got = bf16[4,2,72,1152]{3,2,1,0:T(8,128)(2,1)S(1)} collective-permute-done((bf16[4,2,72,1152]{3,2,1,0:T(8,128)(2,1)S(1)}, bf16[4,2,72,1152]{3,2,1,0:T(8,128)(2,1)S(1)}, u32[]{:S(2)}, u32[]{:S(2)}) %collective-permute-start.6) | collective-permute-done | bytes 1327136 | tf_op jit(solution)/shard_map/ppermute | solution.py:24
  58.3 1.0 collective-permute-start.10
  59.3 0.3 shard_map.81
  59.6 2.4 %collective-permute-start.9 = (bf16[2,72,1152]{2,1,0:T(8,128)(2,1)S(1)}, bf16[2,72,1152]{2,1,0:T(8,128)(2,1)S(1)}, u32[]{:S(2)}, u32[]{:S(2)}) collective-permute-start(bf16[2,72,1152]{2,1,0:T(8,128)(2,1)S(1)} %get-tuple-element.65), channel_id=1, source_target_pairs={{0,4},{2,6},{4,0},{6,2},{1,5},{3,7},{5,1},{7,3},{8,12},{10,14},{12... | collective-permute-start | bytes 995336 | tf_op jit(solution)/shard_map/ppermute | solution.py:24
  62.0 0.7 collective-permute-start.13
  62.7 0.6 collective-permute-start.7
  63.3 2.7 %collective-permute-start.8 = (bf16[2,72,1152]{2,1,0:T(8,128)(2,1)S(1)}, bf16[2,72,1152]{2,1,0:T(8,128)(2,1)S(1)}, u32[]{:S(2)}, u32[]{:S(2)}) collective-permute-start(bf16[2,72,1152]{2,1,0:T(8,128)(2,1)S(1)} %get-tuple-element.64), channel_id=1, source_target_pairs={{0,6},{2,0},{4,2},{6,4},{1,7},{3,1},{5,3},{7,5},{8,14},{10,8},{12,... | collective-permute-start | bytes 995336 | tf_op jit(solution)/shard_map/ppermute | solution.py:24
  66.0 2.1 %shard_map.82 = (bf16[320,1152]{1,0:T(8,128)(2,1)S(1)}, bf16[320,1152]{1,0:T(8,128)(2,1)S(1)}, bf16[320,1152]{1,0:T(8,128)(2,1)S(1)}) custom-call(f32[1]{0:T(128)S(6)} %copy.12.t_log, bf16[640,1280]{1,0:T(8,128)(2,1)S(1)} %get-tuple-element.60.grad, bf16[640,1152]{1,0:T(8,128)(2,1)S(1)} %get-tuple-element.53.n_txt), custom_call_target="tpu_custom_call" | custom-call | flops 2147483648 | bytes 1024 | tf_op jit(solution)/shard_map/pallas_call | solution.py:240
  68.0 2.9 %collective-permute-done.10.got = bf16[320,1152]{1,0:T(8,128)(2,1)S(1)} collective-permute-done((bf16[320,1152]{1,0:T(8,128)(2,1)S(1)}, bf16[320,1152]{1,0:T(8,128)(2,1)S(1)}, u32[]{:S(2)}, u32[]{:S(2)}) %collective-permute-start.10) | collective-permute-done | bytes 737312 | tf_op jit(solution)/shard_map/ppermute | solution.py:29
  70.9 0.4 shard_map.83
  71.4 0.7 collective-permute-done.9.r
  72.1 2.3 %collective-permute-start.17 = (bf16[320,1152]{1,0:T(8,128)(2,1)S(1)}, bf16[320,1152]{1,0:T(8,128)(2,1)S(1)}, u32[]{:S(2)}, u32[]{:S(2)}) collective-permute-start(bf16[320,1152]{1,0:T(8,128)(2,1)S(1)} %get-tuple-element.78), channel_id=1, source_target_pairs={{0,48},{16,0},{32,16},{48,32},{1,49},{17,1},{33,17},{49,33},{2,50}... | collective-permute-start | bytes 2211848 | tf_op jit(solution)/shard_map/ppermute | solution.py:24
  74.4 4.7 %collective-permute-done.7.p = bf16[2,72,1152]{2,1,0:T(8,128)(2,1)S(1)} collective-permute-done((bf16[2,72,1152]{2,1,0:T(8,128)(2,1)S(1)}, bf16[2,72,1152]{2,1,0:T(8,128)(2,1)S(1)}, u32[]{:S(2)}, u32[]{:S(2)}) %collective-permute-start.7) | collective-permute-done | bytes 331808 | tf_op jit(solution)/shard_map/ppermute | solution.py:24
  79.1 0.2 shard_map.84
  79.3 1.1 %collective-permute-start.11 = (bf16[72,1152]{1,0:T(8,128)(2,1)S(1)}, bf16[72,1152]{1,0:T(8,128)(2,1)S(1)}, u32[]{:S(2)}, u32[]{:S(2)}) collective-permute-start(bf16[72,1152]{1,0:T(8,128)(2,1)S(1)} %get-tuple-element.73), channel_id=1, source_target_pairs={{0,72},{8,64},{64,8},{72,0},{1,73},{9,65},{65,9},{73,1},{2,74},{10... | collective-permute-start | bytes 497672 | tf_op jit(solution)/shard_map/ppermute | solution.py:34
  80.4 6.4 %collective-permute-done.11.b = bf16[72,1152]{1,0:T(8,128)(2,1)S(1)} collective-permute-done((bf16[72,1152]{1,0:T(8,128)(2,1)S(1)}, bf16[72,1152]{1,0:T(8,128)(2,1)S(1)}, u32[]{:S(2)}, u32[]{:S(2)}) %collective-permute-start.11) | collective-permute-done | bytes 165920 | tf_op jit(solution)/shard_map/ppermute | solution.py:34
  86.9 0.1 collective-permute-start.12
  87.0 0.0 copy-start.3
  87.0 4.9 %shard_map.87 = bf16[320,1152]{1,0:T(8,128)(2,1)} custom-call(f32[640,1152]{1,0:T(8,128)} %copy-done, bf16[320,1152]{1,0:T(8,128)(2,1)S(1)} %get-tuple-element.74.a, bf16[320,1152]{1,0:T(8,128)(2,1)S(1)} %collective-permute-done.13.b, bf16[4,2,72,1152]{3,2,1,0:T(8,128)(2,1)} %get-tuple-element.49.near, bf16[4,2,72,1152]{3,2,1,0:T(8,128)(2,1)} %get-tuple-element.50.far), custom_call_target="tpu_custom_call" | custom-call | flops 2147483648 | bytes 1024 | tf_op jit(solution)/shard_map/pallas_call | solution.py:257
  91.9 0.4 collective-permute-done.12.b
  92.4 0.2 collective-permute-start.16
  92.6 1.9 %collective-permute-start.15 = (bf16[72,1152]{1,0:T(8,128)(2,1)S(1)}, bf16[72,1152]{1,0:T(8,128)(2,1)S(1)}, u32[]{:S(2)}, u32[]{:S(2)}) collective-permute-start(bf16[72,1152]{1,0:T(8,128)(2,1)S(1)} %shard_map.86.a), channel_id=1, source_target_pairs={{0,16},{16,32},{32,48},{48,0},{1,17},{17,33},{33,49},{49,1},{2,18}... | collective-permute-start | bytes 497672 | tf_op jit(solution)/shard_map/ppermute | solution.py:24
  94.5 1.0 collective-permute-start.14
  95.5 1.7 %shard_map.88 = bf16[320,1152]{1,0:T(8,128)(2,1)} custom-call(bf16[320,1152]{1,0:T(8,128)(2,1)S(1)} %bitcast.8, bf16[320,1152]{1,0:T(8,128)(2,1)S(1)} %get-tuple-element.77.a, bf16[320,1152]{1,0:T(8,128)(2,1)S(1)} %collective-permute-done.17.b, bf16[320,1152]{1,0:T(8,128)(2,1)S(1)} %collective-permute-done.18.c), custom_call_target="tpu_custom_call" | custom-call | flops 1073741824 | bytes 1024 | tf_op jit(solution)/shard_map/pallas_call | solution.py:322
  97.2 2.1 %collective-permute-done.16.d = bf16[72,1152]{1,0:T(8,128)(2,1)S(1)} collective-permute-done((bf16[72,1152]{1,0:T(8,128)(2,1)S(1)}, bf16[72,1152]{1,0:T(8,128)(2,1)S(1)}, u32[]{:S(2)}, u32[]{:S(2)}) %collective-permute-start.16) | collective-permute-done | bytes 165920 | tf_op jit(solution)/shard_map/ppermute | solution.py:24
  99.4 3.0 %collective-permute-done.15.c = bf16[72,1152]{1,0:T(8,128)(2,1)S(1)} collective-permute-done((bf16[72,1152]{1,0:T(8,128)(2,1)S(1)}, bf16[72,1152]{1,0:T(8,128)(2,1)S(1)}, u32[]{:S(2)}, u32[]{:S(2)}) %collective-permute-start.15) | collective-permute-done | bytes 165920 | tf_op jit(solution)/shard_map/ppermute | solution.py:24
  102.4 0.8 shard_map.89
  (17 shorter events, 0.1 us)
Async XLA Ops:
  0.6 38.2 %collective-permute-start.2 = (bf16[320,1152]{1,0:T(8,128)(2,1)}, bf16[320,1152]{1,0:T(8,128)(2,1)S(1)}, u32[]{:S(2)}, u32[]{:S(2)}) collective-permute-start(bf16[320,1152]{1,0:T(8,128)(2,1)} %bitcast.4), channel_id=1, source_target_pairs={{0,64},{64,0},{1,65},{65,1},{2,66},{66,2},{3,67},{67,3},{4,68},{68... | collective-permute-start | bytes 2211848 | tf_op jit(solution)/shard_map/ppermute | solution.py:24
  2.4 1.0 copy-start.4
  3.4 10.9 %collective-permute-start.1 = (bf16[72,1152]{1,0:T(8,128)(2,1)S(1)}, bf16[72,1152]{1,0:T(8,128)(2,1)S(1)}, u32[]{:S(2)}, u32[]{:S(2)}) collective-permute-start(bf16[72,1152]{1,0:T(8,128)(2,1)S(1)} %shard_map.76._), channel_id=1, source_target_pairs={{0,72},{8,64},{64,8},{72,0},{1,73},{9,65},{65,9},{73,1},{2,74},{10... | collective-permute-start | bytes 497672 | tf_op jit(solution)/shard_map/ppermute | solution.py:34
  5.6 1.1 %copy-start.2 = (bf16[1,320,1152]{2,1,0:T(8,128)(2,1)S(1)}, bf16[1,320,1152]{2,1,0:T(8,128)(2,1)}, u32[]{:S(2)}) copy-start(bf16[1,320,1152]{2,1,0:T(8,128)(2,1)} %param.7) | copy-start | bytes 2211844
  7.0 36.7 %collective-permute-start.5 = (bf16[320,1152]{1,0:T(8,128)(2,1)S(1)}, bf16[320,1152]{1,0:T(8,128)(2,1)S(1)}, u32[]{:S(2)}, u32[]{:S(2)}) collective-permute-start(bf16[320,1152]{1,0:T(8,128)(2,1)S(1)} %shard_map.78.n_own), channel_id=1, source_target_pairs={{0,32},{16,48},{32,0},{48,16},{1,33},{17,49},{33,1},{49,17},{2,34}... | collective-permute-start | bytes 2211848 | tf_op jit(solution)/shard_map/ppermute | solution.py:24
  11.0 32.8 %collective-permute-start.4 = (bf16[320,1152]{1,0:T(8,128)(2,1)S(1)}, bf16[320,1152]{1,0:T(8,128)(2,1)}, u32[]{:S(2)}, u32[]{:S(2)}) collective-permute-start(bf16[320,1152]{1,0:T(8,128)(2,1)S(1)} %shard_map.78.n_own), channel_id=1, source_target_pairs={{0,48},{16,0},{32,16},{48,32},{1,49},{17,1},{33,17},{49,33},{2,50}... | collective-permute-start | bytes 2211848 | tf_op jit(solution)/shard_map/ppermute | solution.py:24
  11.7 32.1 %collective-permute-start.3 = (bf16[320,1152]{1,0:T(8,128)(2,1)S(1)}, bf16[320,1152]{1,0:T(8,128)(2,1)}, u32[]{:S(2)}, u32[]{:S(2)}) collective-permute-start(bf16[320,1152]{1,0:T(8,128)(2,1)S(1)} %shard_map.78.n_own), channel_id=1, source_target_pairs={{0,16},{16,32},{32,48},{48,0},{1,17},{17,33},{33,49},{49,1},{2,18}... | collective-permute-start | bytes 2211848 | tf_op jit(solution)/shard_map/ppermute | solution.py:24
  14.3 24.6 %copy-start.1 = (bf16[1,320,1152]{2,1,0:T(8,128)(2,1)S(1)}, bf16[1,320,1152]{2,1,0:T(8,128)(2,1)}, u32[]{:S(2)}) copy-start(bf16[1,320,1152]{2,1,0:T(8,128)(2,1)} %param.8) | copy-start | bytes 2211844
  35.5 3.4 %collective-permute-start = (bf16[4,2,72,1152]{3,2,1,0:T(8,128)(2,1)}, bf16[4,2,72,1152]{3,2,1,0:T(8,128)(2,1)}, u32[]{:S(2)}, u32[]{:S(2)}) collective-permute-start(bf16[4,2,72,1152]{3,2,1,0:T(8,128)(2,1)} %all_to_all.4), channel_id=1, source_target_pairs={{0,1},{1,0},{2,3},{3,2},{4,5},{5,4},{6,7},{7,6},{8,9},{9,8},{10,11... | collective-permute-start | bytes 3981320 | tf_op jit(solution)/shard_map/cond/branch_1_fun/ppermute | solution.py:24
  43.7 11.4 %copy-start = (f32[640,1152]{1,0:T(8,128)}, f32[640,1152]{1,0:T(8,128)S(1)}, u32[]{:S(2)}) copy-start(f32[640,1152]{1,0:T(8,128)S(1)} %get-tuple-element.57.z) | copy-start | bytes 8847364
  55.1 3.1 %collective-permute-start.6 = (bf16[4,2,72,1152]{3,2,1,0:T(8,128)(2,1)S(1)}, bf16[4,2,72,1152]{3,2,1,0:T(8,128)(2,1)S(1)}, u32[]{:S(2)}, u32[]{:S(2)}) collective-permute-start(bf16[4,2,72,1152]{3,2,1,0:T(8,128)(2,1)S(1)} %get-tuple-element.59), channel_id=1, source_target_pairs={{0,1},{1,0},{2,3},{3,2},{4,5},{5,4},{6,7},{7,6},{8,9},{9,8},{10,11... | collective-permute-start | bytes 3981320 | tf_op jit(solution)/shard_map/ppermute | solution.py:24
  58.3 12.7 %collective-permute-start.10 = (bf16[320,1152]{1,0:T(8,128)(2,1)S(1)}, bf16[320,1152]{1,0:T(8,128)(2,1)S(1)}, u32[]{:S(2)}, u32[]{:S(2)}) collective-permute-start(bf16[320,1152]{1,0:T(8,128)(2,1)S(1)} %shard_map.80), channel_id=1, source_target_pairs={{0,16},{1,49},{16,32},{17,1},{32,48},{33,17},{48,0},{49,33},{2,18}... | collective-permute-start | bytes 2211848 | tf_op jit(solution)/shard_map/ppermute | solution.py:29
  59.6 12.5 %collective-permute-start.9 = (bf16[2,72,1152]{2,1,0:T(8,128)(2,1)S(1)}, bf16[2,72,1152]{2,1,0:T(8,128)(2,1)S(1)}, u32[]{:S(2)}, u32[]{:S(2)}) collective-permute-start(bf16[2,72,1152]{2,1,0:T(8,128)(2,1)S(1)} %get-tuple-element.65), channel_id=1, source_target_pairs={{0,4},{2,6},{4,0},{6,2},{1,5},{3,7},{5,1},{7,3},{8,12},{10,14},{12... | collective-permute-start | bytes 995336 | tf_op jit(solution)/shard_map/ppermute | solution.py:24
  62.0 24.9 %collective-permute-start.13 = (bf16[320,1152]{1,0:T(8,128)(2,1)S(1)}, bf16[320,1152]{1,0:T(8,128)(2,1)S(1)}, u32[]{:S(2)}, u32[]{:S(2)}) collective-permute-start(bf16[320,1152]{1,0:T(8,128)(2,1)S(1)} %get-tuple-element.75), channel_id=1, source_target_pairs={{0,64},{64,0},{1,65},{65,1},{2,66},{66,2},{3,67},{67,3},{4,68},{68... | collective-permute-start | bytes 2211848 | tf_op jit(solution)/shard_map/ppermute | solution.py:24
  62.7 16.4 %collective-permute-start.7 = (bf16[2,72,1152]{2,1,0:T(8,128)(2,1)S(1)}, bf16[2,72,1152]{2,1,0:T(8,128)(2,1)S(1)}, u32[]{:S(2)}, u32[]{:S(2)}) collective-permute-start(bf16[2,72,1152]{2,1,0:T(8,128)(2,1)S(1)} %get-tuple-element.63), channel_id=1, source_target_pairs={{0,2},{2,4},{4,6},{6,0},{1,3},{3,5},{5,7},{7,1},{8,10},{10,12},{12... | collective-permute-start | bytes 995336 | tf_op jit(solution)/shard_map/ppermute | solution.py:24
  63.3 15.8 %collective-permute-start.8 = (bf16[2,72,1152]{2,1,0:T(8,128)(2,1)S(1)}, bf16[2,72,1152]{2,1,0:T(8,128)(2,1)S(1)}, u32[]{:S(2)}, u32[]{:S(2)}) collective-permute-start(bf16[2,72,1152]{2,1,0:T(8,128)(2,1)S(1)} %get-tuple-element.64), channel_id=1, source_target_pairs={{0,6},{2,0},{4,2},{6,4},{1,7},{3,1},{5,3},{7,5},{8,14},{10,8},{12,... | collective-permute-start | bytes 995336 | tf_op jit(solution)/shard_map/ppermute | solution.py:24
  72.1 23.4 %collective-permute-start.17 = (bf16[320,1152]{1,0:T(8,128)(2,1)S(1)}, bf16[320,1152]{1,0:T(8,128)(2,1)S(1)}, u32[]{:S(2)}, u32[]{:S(2)}) collective-permute-start(bf16[320,1152]{1,0:T(8,128)(2,1)S(1)} %get-tuple-element.78), channel_id=1, source_target_pairs={{0,48},{16,0},{32,16},{48,32},{1,49},{17,1},{33,17},{49,33},{2,50}... | collective-permute-start | bytes 2211848 | tf_op jit(solution)/shard_map/ppermute | solution.py:24
  74.4 21.1 %collective-permute-start.18 = (bf16[320,1152]{1,0:T(8,128)(2,1)S(1)}, bf16[320,1152]{1,0:T(8,128)(2,1)S(1)}, u32[]{:S(2)}, u32[]{:S(2)}) collective-permute-start(bf16[320,1152]{1,0:T(8,128)(2,1)S(1)} %get-tuple-element.79), channel_id=1, source_target_pairs={{0,16},{16,32},{32,48},{48,0},{1,17},{17,33},{33,49},{49,1},{2,18}... | collective-permute-start | bytes 2211848 | tf_op jit(solution)/shard_map/ppermute | solution.py:24
  79.3 7.5 %collective-permute-start.11 = (bf16[72,1152]{1,0:T(8,128)(2,1)S(1)}, bf16[72,1152]{1,0:T(8,128)(2,1)S(1)}, u32[]{:S(2)}, u32[]{:S(2)}) collective-permute-start(bf16[72,1152]{1,0:T(8,128)(2,1)S(1)} %get-tuple-element.73), channel_id=1, source_target_pairs={{0,72},{8,64},{64,8},{72,0},{1,73},{9,65},{65,9},{73,1},{2,74},{10... | collective-permute-start | bytes 497672 | tf_op jit(solution)/shard_map/ppermute | solution.py:34
  86.9 5.5 %collective-permute-start.12 = (bf16[72,1152]{1,0:T(8,128)(2,1)S(1)}, bf16[72,1152]{1,0:T(8,128)(2,1)S(1)}, u32[]{:S(2)}, u32[]{:S(2)}) collective-permute-start(bf16[72,1152]{1,0:T(8,128)(2,1)S(1)} %shard_map.85.a), channel_id=1, source_target_pairs={{0,64},{64,0},{1,65},{65,1},{2,66},{66,2},{3,67},{67,3},{4,68},{68... | collective-permute-start | bytes 497672 | tf_op jit(solution)/shard_map/ppermute | solution.py:24
  87.0 8.6 %copy-start.3 = (bf16[1,320,1152]{2,1,0:T(8,128)(2,1)S(1)}, bf16[1,320,1152]{2,1,0:T(8,128)(2,1)}, u32[]{:S(2)}) copy-start(bf16[1,320,1152]{2,1,0:T(8,128)(2,1)} %param.7) | copy-start | bytes 2211844
  92.4 6.9 %collective-permute-start.16 = (bf16[72,1152]{1,0:T(8,128)(2,1)S(1)}, bf16[72,1152]{1,0:T(8,128)(2,1)S(1)}, u32[]{:S(2)}, u32[]{:S(2)}) collective-permute-start(bf16[72,1152]{1,0:T(8,128)(2,1)S(1)} %shard_map.86.a), channel_id=1, source_target_pairs={{0,48},{16,0},{32,16},{48,32},{1,49},{17,1},{33,17},{49,33},{2,50}... | collective-permute-start | bytes 497672 | tf_op jit(solution)/shard_map/ppermute | solution.py:24
  92.6 9.8 %collective-permute-start.15 = (bf16[72,1152]{1,0:T(8,128)(2,1)S(1)}, bf16[72,1152]{1,0:T(8,128)(2,1)S(1)}, u32[]{:S(2)}, u32[]{:S(2)}) collective-permute-start(bf16[72,1152]{1,0:T(8,128)(2,1)S(1)} %shard_map.86.a), channel_id=1, source_target_pairs={{0,16},{16,32},{32,48},{48,0},{1,17},{17,33},{33,49},{49,1},{2,18}... | collective-permute-start | bytes 497672 | tf_op jit(solution)/shard_map/ppermute | solution.py:24
  94.5 7.9 %collective-permute-start.14 = (bf16[72,1152]{1,0:T(8,128)(2,1)S(1)}, bf16[72,1152]{1,0:T(8,128)(2,1)S(1)}, u32[]{:S(2)}, u32[]{:S(2)}) collective-permute-start(bf16[72,1152]{1,0:T(8,128)(2,1)S(1)} %shard_map.86.a), channel_id=1, source_target_pairs={{0,32},{16,48},{32,0},{48,16},{1,33},{17,49},{33,1},{49,17},{2,34}... | collective-permute-start | bytes 497672 | tf_op jit(solution)/shard_map/ppermute | solution.py:24

commit v7 on v6

--- a/solution.py
+++ b/solution.py
@@ -11,7 +11,7 @@
 F32 = jnp.float32
 MIB = 1024 * 1024
 TEXT_MIB = 14
-MAIN_MIB = 24
+MAIN_MIB = 28
 AXES = {"ylo": 2, "z": 4, "yhi": 2, "x": 4, "core": 2}
 
 VM = pl.BlockSpec(memory_space=pltpu.VMEM)
@@ -72,14 +72,22 @@
         out[k, 1 - yhi] = w_y[...]
 
 
-def unit_kernel(img, _, n_img):
-    rows = img[...].astype(F32)
-    n_img[...] = (rows * inverse_length(rows)).astype(BF)
-
-
-def assemble(mine, other, head):
+def load_head(near, far, mine, other, sems):
+    copies = [
+        pltpu.make_async_copy(src.at[x], dst.at[x], sems.at[2 * x + k])
+        for x in range(4)
+        for k, (src, dst) in enumerate(((near, mine), (far, other)))
+    ]
+    for c in copies:
+        c.start()
+    return copies
+
+
+def assemble(copies, mine, other, head):
     core = lax.axis_index("core")
     for x in range(4):
+        copies[2 * x].wait()
+        copies[2 * x + 1].wait()
         for h in range(2):
             a, b = mine[x, h].astype(F32), other[x, h].astype(F32)
             first = jnp.where(core == 0, a, b)
@@ -88,48 +96,47 @@
 
 
 def text_kernel(near, far, txt, txt_far, z, n_txt, mine, other, rows, w_full, sems):
-    copies = [
-        pltpu.make_async_copy(near, mine, sems.at[0]),
-        pltpu.make_async_copy(far, other, sems.at[1]),
-        pltpu.make_async_copy(txt, rows.at[pl.ds(0, 320)], sems.at[2]),
-        pltpu.make_async_copy(txt_far, rows.at[pl.ds(320, 320)], sems.at[3]),
+    copies = load_head(near, far, mine, other, sems)
+    late = [
+        pltpu.make_async_copy(txt, rows.at[pl.ds(0, 320)], sems.at[8]),
+        pltpu.make_async_copy(txt_far, rows.at[pl.ds(320, 320)], sems.at[9]),
     ]
-    for c in copies:
+    for c in late:
         c.start()
-    for c in copies[:2]:
-        c.wait()
-    assemble(mine, other, w_full)
-    for c in copies[2:]:
+    assemble(copies, mine, other, w_full)
+    for c in late:
         c.wait()
     out = jnp.dot(rows[...], w_full[...], preferred_element_type=F32)
     z[...] = out
     n_txt[...] = (out * inverse_length(out)).astype(BF)
 
 
-def scale_of(t_log):
-    return jnp.exp(jnp.full((1, 1), t_log[0], F32))
-
-
 def logit_gradient(scale, bias, left, right):
     logits = scale * lax.dot_general(
         left, right, (((1,), (1,)), ((), ())), preferred_element_type=F32
-    ) + bias[0]
+    ) + bias
     return 1.0 / (1.0 + jnp.exp(-logits))
 
 
-def main_kernel(t_log, bias, n_txt, n_own, n_a, n_b, n_c, z, txt, txt_far, grad, g_own, g_far, mine, other, rows, feat, wide, sems):
-    moves = [(block, rows.at[pl.ds(k * 320, 320)]) for k, block in enumerate((n_own, n_a, n_b, n_c))]
+def main_kernel(t_log, bias, n_txt, img, img_a, img_b, img_c, z, txt, txt_far, grad, g_own, g_far, mine, other, raw, rows, feat, wide, sems):
+    moves = [(block, raw.at[pl.ds(k * 320, 320)]) for k, block in enumerate((img, img_a, img_b, img_c))]
     moves += [(txt, feat.at[pl.ds(0, 320)]), (txt_far, feat.at[pl.ds(320, 320)])]
     copies = [pltpu.make_async_copy(a, b, sems.at[k]) for k, (a, b) in enumerate(moves)]
     for c in copies:
         c.start()
-    for c in copies[:4]:
-        c.wait()
-    scale = scale_of(t_log)
-    g = logit_gradient(scale, bias, n_txt[...], rows[...])
-    row_ids = lax.broadcasted_iota(jnp.int32, g.shape, 0)
-    col_ids = lax.broadcasted_iota(jnp.int32, g.shape, 1)
-    grad[...] = (g - jnp.where((row_ids == col_ids) & (row_ids < 320), 1.0, 0.0)).astype(BF)
+    scale = jnp.exp(t_log[...])
+    for first, last, ready in ((0, 512, copies[:2]), (512, 1280, copies[2:4])):
+        for c in ready:
+            c.wait()
+        fresh = pl.ds(0 if first == 0 else 640, 640)
+        wide_rows = raw[fresh, :].astype(F32)
+        rows[fresh, :] = (wide_rows * inverse_length(wide_rows)).astype(BF)
+        g = logit_gradient(scale, bias[...], n_txt[...], rows[pl.ds(first, last - first), :])
+        row_ids = lax.broadcasted_iota(jnp.int32, g.shape, 0)
+        col_ids = lax.broadcasted_iota(jnp.int32, g.shape, 1)
+        if first == 0:
+            g = g - jnp.where((row_ids == col_ids) & (row_ids < 320), 1.0, 0.0)
+        grad[:, first:last] = g.astype(BF)
     total = scale * jnp.dot(grad[...], rows[...], preferred_element_type=F32)
     g_own[...] = total[:320].astype(BF)
     g_far[...] = total[320:].astype(BF)
@@ -150,7 +157,7 @@
 def part_kernel(first, t_log, grad, n_txt, *outs):
     start = first * 320
     rows = sum(ref.shape[0] for ref in outs)
-    out = scale_of(t_log) * lax.dot_general(
+    out = jnp.exp(t_log[...]) * lax.dot_general(
         grad[:, start : start + rows], n_txt[...], (((0,), (0,)), ((), ())), preferred_element_type=F32
     )
     at = 0
@@ -193,15 +200,16 @@
     out[...] = project(grad, img[...].astype(F32)).astype(BF)
 
 
-def text_out_kernel(z, a, b, near, far, out, rows, mine, other, head, sems):
-    moves = (near, mine), (far, other), (z.at[pl.ds(0, 320)], rows)
-    copies = [pltpu.make_async_copy(x, y, sems.at[k]) for k, (x, y) in enumerate(moves)]
-    for c in copies:
-        c.start()
-    for c in copies:
-        c.wait()
-    assemble(mine, other, head)
-    dz = project(a[...].astype(F32) + b[...].astype(F32), rows[...]).astype(BF)
+def head_kernel(near, far, head, mine, other, sems):
+    assemble(load_head(near, far, mine, other, sems), mine, other, head)
+
+
+def text_out_kernel(z, a, b, head, out, rows, sems):
+    copy = pltpu.make_async_copy(z.at[pl.ds(0, 320)], rows, sems.at[0])
+    copy.start()
+    grad = a[...].astype(F32) + b[...].astype(F32)
+    copy.wait()
+    dz = project(grad, rows[...]).astype(BF)
     out[...] = lax.dot_general(
         dz, head[...], (((1,), (1,)), ((), ())), preferred_element_type=F32
     ).astype(BF)
@@ -237,7 +245,7 @@
 
 def parts_of(first, shapes, *args):
     kernel = functools.partial(part_kernel, first)
-    return call(kernel, shapes, [SM] + [VM] * 2, flops=1 << 31)(*args)
+    return call(kernel, shapes, [VM] * 3, flops=1 << 31)(*args)
 
 
 def beside_x(part_c, t_log, grad, n_txt):
@@ -251,23 +259,28 @@
     got_x = [shift(rel[s], "x", s) for s in (1, 3, 2)]
     g_got = shift(g_far, "ylo", 1)
     part_own, part_a, part_b = beside_x(part_c, t_log, grad, n_txt)
-    got_x[2], part_a, part_b = hold((got_x[2], part_a, part_b))
+    got_x[2], part_a, part_b, near, far = hold((got_x[2], part_a, part_b, near, far))
+    (head,) = call(
+        head_kernel,
+        [shaped((1152, 1152), BF)],
+        [ANY] * 2,
+        [
+            pltpu.VMEM((4, 2, 72, 1152), BF),
+            pltpu.VMEM((4, 2, 72, 1152), BF),
+            pltpu.SemaphoreType.DMA((8,)),
+        ],
+        flops=1 << 31,
+    )(near, far)
+    got_x[:2], head = hold((got_x[:2], head))
     keep, send = call(x_sum_kernel, [stack_of()] * 2, [VM] * 4)(rel[0], *got_x)
     got_a, got_b = shift(part_a, "z", -1), shift(part_b, "z", 1)
     (d_feat,) = call(
         text_out_kernel,
         [BLOCK],
-        [ANY, VM, VM, ANY, ANY],
-        [
-            pltpu.VMEM((320, 1152), F32),
-            pltpu.VMEM((4, 2, 72, 1152), BF),
-            pltpu.VMEM((4, 2, 72, 1152), BF),
-            pltpu.VMEM((1152, 1152), BF),
-            pltpu.SemaphoreType.DMA((3,)),
-        ],
-        vmem=50,
+        [ANY, VM, VM, VM],
+        [pltpu.VMEM((320, 1152), F32), pltpu.SemaphoreType.DMA((1,))],
         flops=1 << 31,
-    )(z, g_own, g_got, near, far)
+    )(z, g_own, g_got, head)
     (one,) = call(pair_sum_kernel, [stack_of()], [VM] * 2)(keep, swap_far(send))
     (pair,) = call(pair_sum_kernel, [stack_of()], [VM] * 2)(one, shift(one, "ylo", 1))
     pair, d_feat = hold((pair, d_feat))
@@ -276,12 +289,13 @@
 
 def on_device(img_emb, txt_feat, w_txt, t_log, bias):
     img, txt = img_emb[0], txt_feat[0]
+    t_log, bias = t_log.reshape(1, 1), bias.reshape(1, 1)
 
     txt_far = shift(txt, "ylo", 1)
-    (w_h,) = call(half_kernel, [stack_of()], [VM])(w_txt)
+    (w_h,) = call(half_kernel, [stack_of()], [VM], vmem=60)(w_txt)
     w_y = swap_far(w_h)
-    (n_img,) = call(unit_kernel, [BLOCK], [VM, ANY])(img, w_h)
-    n_c, n_b, n_a = (shift(n_img, "z", s) for s in (2, -1, 1))
+    w_h, img = hold((w_h, img))
+    img_c, img_b, img_a = (shift(img, "z", s) for s in (2, -1, 1))
     near, far = apart(gather_head, w_h, w_y)
     near, far, txt_far = hold((near, far, txt_far))
 
@@ -294,24 +308,25 @@
             pltpu.VMEM((4, 2, 72, 1152), BF),
             pltpu.VMEM((640, 1152), BF),
             pltpu.VMEM((1152, 1152), BF),
-            pltpu.SemaphoreType.DMA((4,)),
+            pltpu.SemaphoreType.DMA((10,)),
         ],
         vmem=TEXT_MIB,
         flops=1 << 34,
     )(near, far, txt, txt_far)
-    n_txt, n_a, n_b, n_c = hold((n_txt, n_a, n_b, n_c))
+    n_txt, img_a, img_b, img_c = hold((n_txt, img_a, img_b, img_c))
     grad, g_own, g_far, mine, other = call(
         main_kernel,
         [shaped((640, 1280), BF), BLOCK, BLOCK, stack_of(4, 2), stack_of(4, 2)],
-        [SM, SM, VM] + [ANY] * 4 + [VM, ANY, ANY],
+        [VM] * 3 + [ANY] * 4 + [VM, ANY, ANY],
         [
+            pltpu.VMEM((1280, 1152), BF),
             pltpu.VMEM((1280, 1152), BF),
             pltpu.VMEM((640, 1152), BF),
             pltpu.VMEM((1152, 1152), F32),
             pltpu.SemaphoreType.DMA((6,)),
         ],
         vmem=MAIN_MIB,
-    )(t_log, bias, n_txt, n_img, n_a, n_b, n_c, z, txt, txt_far)
+    )(t_log, bias, n_txt, img, img_a, img_b, img_c, z, txt, txt_far)
 
     got_core, (part_c,) = hold(
         (shift(other, "core", 1), parts_of(3, [BLOCK], t_log, grad, n_txt))

time: 104 us -> 102 us (0.981)
  local copies, waits for them, and re-layouts: 2.11 us -> 0.01 us
    unnamed x10 -> x4, local copies, waits for them, and re-layouts: 2.11 us -> 0.01 us
    ppermute x16, waiting for transfers between devices: 16.2 us -> 17.5 us  [shift(): return lax.ppermute(value, axis, [(i, (i + step) % n) for i in range(n)])]
  transfers between devices with their start and end apart: 19 -> 19, of which waited for: 9 -> 10; matrix products, arithmetic and copies ran while one was open for 0% -> 0% of each run, Pallas kernels for 15% -> 16%
where the time goes in v7:
time: 102 us
  Pallas kernels  28.5 us (28%)
  waiting for transfers between devices  26.2 us (26%)
  starting transfers between devices  24.4 us (24%)
  blocking collectives  21 us (21%)
  between operations  2.06 us (2%)
    all_to_all x1, blocking collectives, along_x(): return lax.all_to_all(value, 'x', split_axis=0, concat_axis=0, tiled=True)  21 us
    ppermute x16, starting transfers between devices, shift(): return lax.ppermute(value, axis, [(i, (i + step) % n) for i in range(n)])  19.9 us
    ppermute x16, waiting for transfers between devices, shift(): return lax.ppermute(value, axis, [(i, (i + step) % n) for i in range(n)])  17.5 us
    pallas_call x1, Pallas kernels, on_device(): call(main_kernel, [shaped((640, 1280), BF), BLOCK, BLOCK, stack_of(4, 2),...  11.4 us
    ppermute x2, waiting for transfers between devices, swap_far(): return lax.ppermute(value, ('ylo', 'yhi'), pairs)  6.56 us
    pallas_call x1, Pallas kernels, on_device(): call(text_kernel, [shaped((640, 1152), F32), shaped((640, 1152), BF)], [A...  4.5 us
    ppermute x2, starting transfers between devices, swap_far(): return lax.ppermute(value, ('ylo', 'yhi'), pairs)  3.39 us
    pallas_call x2, Pallas kernels, parts_of(): return call(kernel, shapes, [VM] * 3, flops=1 << 31)(*args)  3.1 us
  transfers between devices with their start and end apart: 19, of which 10 were waited for; matrix products, arithmetic and copies ran while one was open for 0% of the time, Pallas kernels for 16%

profile of v7, /device:TPU:0, one launch (start us, length us, event | category | flops | bytes accessed | tf_op | source)
XLA Modules:
  0.0 102.2 jit_solution(16103516657679399892)
XLA Ops:
  0.6 1.7 %collective-permute-start.2 = (bf16[320,1152]{1,0:T(8,128)(2,1)}, bf16[320,1152]{1,0:T(8,128)(2,1)S(1)}, u32[]{:S(2)}, u32[]{:S(2)}) collective-permute-start(bf16[320,1152]{1,0:T(8,128)(2,1)} %bitcast.10), channel_id=1, source_target_pairs={{0,64},{64,0},{1,65},{65,1},{2,66},{66,2},{3,67},{67,3},{4,68},{68... | collective-permute-start | bytes 2211848 | tf_op jit(solution)/shard_map/ppermute | solution.py:24
  2.4 1.0 shard_map.76
  3.4 2.3 %collective-permute-start.1 = (bf16[72,1152]{1,0:T(8,128)(2,1)S(1)}, bf16[72,1152]{1,0:T(8,128)(2,1)S(1)}, u32[]{:S(2)}, u32[]{:S(2)}) collective-permute-start(bf16[72,1152]{1,0:T(8,128)(2,1)S(1)} %shard_map.76), channel_id=1, source_target_pairs={{0,72},{8,64},{64,8},{72,0},{1,73},{9,65},{65,9},{73,1},{2,74},{10... | collective-permute-start | bytes 497672 | tf_op jit(solution)/shard_map/ppermute | solution.py:34
  5.6 3.9 %collective-permute-start.5 = (bf16[320,1152]{1,0:T(8,128)(2,1)}, bf16[320,1152]{1,0:T(8,128)(2,1)S(1)}, u32[]{:S(2)}, u32[]{:S(2)}) collective-permute-start(bf16[320,1152]{1,0:T(8,128)(2,1)} %bitcast.13), channel_id=1, source_target_pairs={{0,32},{16,48},{32,0},{48,16},{1,33},{17,49},{33,1},{49,17},{2,34}... | collective-permute-start | bytes 2211848 | tf_op jit(solution)/shard_map/ppermute | solution.py:24
  9.5 0.7 collective-permute-start.4
  10.2 1.3 %collective-permute-start.3 = (bf16[320,1152]{1,0:T(8,128)(2,1)}, bf16[320,1152]{1,0:T(8,128)(2,1)}, u32[]{:S(2)}, u32[]{:S(2)}) collective-permute-start(bf16[320,1152]{1,0:T(8,128)(2,1)} %bitcast.15), channel_id=1, source_target_pairs={{0,16},{16,32},{32,48},{48,0},{1,17},{17,33},{33,49},{49,1},{2,18}... | collective-permute-start | bytes 2211848 | tf_op jit(solution)/shard_map/ppermute | solution.py:24
  12.8 0.0 collective-permute-done.1
  12.8 0.0 copy-start
  12.9 24.5 %conditional.1 = (bf16[4,2,72,1152]{3,2,1,0:T(8,128)(2,1)}, bf16[4,2,72,1152]{3,2,1,0:T(8,128)(2,1)}) conditional(s32[]{:T(128)} %convert_element_type.3, () %tuple.24, (bf16[72,1152]{1,0:T(8,128)(2,1)S(1)}, bf16[72,1152]{1,0:T(8,128)(2,1)S(1)}) %tuple.26), branch_computations={%region_0.0_spmd, %region_1.0_spmd} | conditional | flops 1024 | bytes 7963704 | solution.py:220
  12.9 0.1 branch_1_fun.1
  13.0 21.0 %all_to_all.4 = bf16[4,2,72,1152]{3,2,1,0:T(8,128)(2,1)} all-to-all(bf16[4,2,72,1152]{3,2,1,0:T(8,128)(2,1)S(1)} %branch_1_fun.1), channel_id=1, replica_groups=mesh['ylo'=2,'z'=4,'yhi'=2,'x'=4,'core'=2] {'x'}, dimensions={0} | all-to-all | bytes 2654208 | tf_op jit(solution)/shard_map/cond/branch_1_fun/all_to_all | solution.py:237
  34.0 3.4 %collective-permute-done = bf16[4,2,72,1152]{3,2,1,0:T(8,128)(2,1)} collective-permute-done((bf16[4,2,72,1152]{3,2,1,0:T(8,128)(2,1)}, bf16[4,2,72,1152]{3,2,1,0:T(8,128)(2,1)}, u32[]{:S(2)}, u32[]{:S(2)}) %collective-permute-start) | collective-permute-done | bytes 1327136 | tf_op jit(solution)/shard_map/cond/branch_1_fun/ppermute | solution.py:24
  37.4 0.0 collective-permute-done.2.txt_far
  37.4 4.5 %shard_map.77 = (f32[640,1152]{1,0:T(8,128)S(1)}, bf16[640,1152]{1,0:T(8,128)(2,1)S(1)}) custom-call(bf16[4,2,72,1152]{3,2,1,0:T(8,128)(2,1)} %get-tuple-element.80.near, bf16[4,2,72,1152]{3,2,1,0:T(8,128)(2,1)} %get-tuple-element.81.far, bf16[320,1152]{1,0:T(8,128)(2,1)S(1)} %bitcast.11, bf16[320,1152]{1,0:T(8,128)(2,1)S(1)} %collective-permute-done.2.txt_far), custom_call_target="tpu_custom_call" | custom-call | flops 17179869184 | bytes 1024 | tf_op jit(solution)/shard_map/pallas_call | solution.py:302
  41.9 0.3 collective-permute-done.4.img_b
  42.2 0.0 collective-permute-done.3.img_a
  42.2 11.4 %shard_map.78 = (bf16[640,1280]{1,0:T(8,128)(2,1)S(1)}, bf16[320,1152]{1,0:T(8,128)(2,1)S(1)}, bf16[320,1152]{1,0:T(8,128)(2,1)S(1)}, bf16[4,2,72,1152]{3,2,1,0:T(8,128)(2,1)S(1)}, bf16[4,2,72,1152]{3,2,1,0:T(8,128)(2,1)S(1)}) custom-call(f32[1,1]{1,0:T(1,128)} %bitcast.6.t_log, f32[1,1]{1,0:T(1,128)} %bitcast.9.bias, ...), custom_call_target="tpu_custom_call" | custom-call | flops 1024 | bytes 1024 | tf_op jit(solution)/shard_map/pallas_call | solution.py:317
  53.6 0.3 collective-permute-start.6
  53.9 1.0 %shard_map.79 = bf16[320,1152]{1,0:T(8,128)(2,1)S(1)} custom-call(f32[1,1]{1,0:T(1,128)} %bitcast.7.t_log, bf16[640,1280]{1,0:T(8,128)(2,1)S(1)} %get-tuple-element.69.grad, bf16[640,1152]{1,0:T(8,128)(2,1)S(1)} %get-tuple-element.62.n_txt), custom_call_target="tpu_custom_call" | custom-call | flops 2147483648 | bytes 1024 | tf_op jit(solution)/shard_map/pallas_call | solution.py:248
  54.9 2.0 %collective-permute-done.6.got = bf16[4,2,72,1152]{3,2,1,0:T(8,128)(2,1)S(1)} collective-permute-done((bf16[4,2,72,1152]{3,2,1,0:T(8,128)(2,1)S(1)}, bf16[4,2,72,1152]{3,2,1,0:T(8,128)(2,1)S(1)}, u32[]{:S(2)}, u32[]{:S(2)}) %collective-permute-start.6) | collective-permute-done | bytes 1327136 | tf_op jit(solution)/shard_map/ppermute | solution.py:24
  56.9 1.1 %collective-permute-start.10 = (bf16[320,1152]{1,0:T(8,128)(2,1)S(1)}, bf16[320,1152]{1,0:T(8,128)(2,1)S(1)}, u32[]{:S(2)}, u32[]{:S(2)}) collective-permute-start(bf16[320,1152]{1,0:T(8,128)(2,1)S(1)} %shard_map.79), channel_id=1, source_target_pairs={{0,16},{1,49},{16,32},{17,1},{32,48},{33,17},{48,0},{49,33},{2,18}... | collective-permute-start | bytes 2211848 | tf_op jit(solution)/shard_map/ppermute | solution.py:29
  58.0 0.3 shard_map.80
  58.3 3.1 %collective-permute-start.9 = (bf16[2,72,1152]{2,1,0:T(8,128)(2,1)S(1)}, bf16[2,72,1152]{2,1,0:T(8,128)(2,1)S(1)}, u32[]{:S(2)}, u32[]{:S(2)}) collective-permute-start(bf16[2,72,1152]{2,1,0:T(8,128)(2,1)S(1)} %get-tuple-element.74), channel_id=1, source_target_pairs={{0,4},{2,6},{4,0},{6,2},{1,5},{3,7},{5,1},{7,3},{8,12},{10,14},{12... | collective-permute-start | bytes 995336 | tf_op jit(solution)/shard_map/ppermute | solution.py:24
  61.4 0.7 collective-permute-start.13
  62.1 0.6 collective-permute-start.7
  62.7 2.7 %collective-permute-start.8 = (bf16[2,72,1152]{2,1,0:T(8,128)(2,1)S(1)}, bf16[2,72,1152]{2,1,0:T(8,128)(2,1)S(1)}, u32[]{:S(2)}, u32[]{:S(2)}) collective-permute-start(bf16[2,72,1152]{2,1,0:T(8,128)(2,1)S(1)} %get-tuple-element.73), channel_id=1, source_target_pairs={{0,6},{2,0},{4,2},{6,4},{1,7},{3,1},{5,3},{7,5},{8,14},{10,8},{12,... | collective-permute-start | bytes 995336 | tf_op jit(solution)/shard_map/ppermute | solution.py:24
  65.3 2.1 %shard_map.81 = (bf16[320,1152]{1,0:T(8,128)(2,1)S(1)}, bf16[320,1152]{1,0:T(8,128)(2,1)S(1)}, bf16[320,1152]{1,0:T(8,128)(2,1)S(1)}) custom-call(f32[1,1]{1,0:T(1,128)} %bitcast.8.t_log, bf16[640,1280]{1,0:T(8,128)(2,1)S(1)} %get-tuple-element.69.grad, bf16[640,1152]{1,0:T(8,128)(2,1)S(1)} %get-tuple-element.62.n_txt), custom_call_target="tpu_custom_call" | custom-call | flops 2147483648 | bytes 1024 | tf_op jit(solution)/shard_map/pallas_call | solution.py:248
  67.4 2.2 %collective-permute-done.10.got = bf16[320,1152]{1,0:T(8,128)(2,1)S(1)} collective-permute-done((bf16[320,1152]{1,0:T(8,128)(2,1)S(1)}, bf16[320,1152]{1,0:T(8,128)(2,1)S(1)}, u32[]{:S(2)}, u32[]{:S(2)}) %collective-permute-start.10) | collective-permute-done | bytes 737312 | tf_op jit(solution)/shard_map/ppermute | solution.py:29
  69.6 0.4 shard_map.82
  70.0 0.3 collective-permute-done.9.r
  70.4 2.4 %collective-permute-start.17 = (bf16[320,1152]{1,0:T(8,128)(2,1)S(1)}, bf16[320,1152]{1,0:T(8,128)(2,1)S(1)}, u32[]{:S(2)}, u32[]{:S(2)}) collective-permute-start(bf16[320,1152]{1,0:T(8,128)(2,1)S(1)} %get-tuple-element.92), channel_id=1, source_target_pairs={{0,48},{16,0},{32,16},{48,32},{1,49},{17,1},{33,17},{49,33},{2,50}... | collective-permute-start | bytes 2211848 | tf_op jit(solution)/shard_map/ppermute | solution.py:24
  72.8 0.0 collective-permute-start.18
  72.8 1.9 %shard_map.83.head = bf16[1152,1152]{1,0:T(8,128)(2,1)S(1)} custom-call(bf16[4,2,72,1152]{3,2,1,0:T(8,128)(2,1)} %get-tuple-element.80.near, bf16[4,2,72,1152]{3,2,1,0:T(8,128)(2,1)} %get-tuple-element.81.far), custom_call_target="tpu_custom_call" | custom-call | flops 2147483648 | bytes 1024 | tf_op jit(solution)/shard_map/pallas_call | solution.py:263
  74.7 3.0 %collective-permute-done.7.p = bf16[2,72,1152]{2,1,0:T(8,128)(2,1)S(1)} collective-permute-done((bf16[2,72,1152]{2,1,0:T(8,128)(2,1)S(1)}, bf16[2,72,1152]{2,1,0:T(8,128)(2,1)S(1)}, u32[]{:S(2)}, u32[]{:S(2)}) %collective-permute-start.7) | collective-permute-done | bytes 331808 | tf_op jit(solution)/shard_map/ppermute | solution.py:24
  77.7 0.0 collective-permute-done.8.q
  77.7 0.2 shard_map.84
  77.9 1.1 %collective-permute-start.11 = (bf16[72,1152]{1,0:T(8,128)(2,1)S(1)}, bf16[72,1152]{1,0:T(8,128)(2,1)S(1)}, u32[]{:S(2)}, u32[]{:S(2)}) collective-permute-start(bf16[72,1152]{1,0:T(8,128)(2,1)S(1)} %get-tuple-element.86), channel_id=1, source_target_pairs={{0,72},{8,64},{64,8},{72,0},{1,73},{9,65},{65,9},{73,1},{2,74},{10... | collective-permute-start | bytes 497672 | tf_op jit(solution)/shard_map/ppermute | solution.py:34
  79.0 6.6 %collective-permute-done.11.b = bf16[72,1152]{1,0:T(8,128)(2,1)S(1)} collective-permute-done((bf16[72,1152]{1,0:T(8,128)(2,1)S(1)}, bf16[72,1152]{1,0:T(8,128)(2,1)S(1)}, u32[]{:S(2)}, u32[]{:S(2)}) %collective-permute-start.11) | collective-permute-done | bytes 165920 | tf_op jit(solution)/shard_map/ppermute | solution.py:34
  85.6 0.1 collective-permute-start.12
  85.7 3.1 %shard_map.87 = bf16[320,1152]{1,0:T(8,128)(2,1)} custom-call(f32[640,1152]{1,0:T(8,128)S(1)} %get-tuple-element.66.z, bf16[320,1152]{1,0:T(8,128)(2,1)S(1)} %get-tuple-element.87.a, bf16[320,1152]{1,0:T(8,128)(2,1)S(1)} %collective-permute-done.13.b, bf16[1152,1152]{1,0:T(8,128)(2,1)S(1)} %shard_map.83.head), custom_call_target="tpu_custom_call" | custom-call | flops 2147483648 | bytes 1024 | tf_op jit(solution)/shard_map/pallas_call | solution.py:277
  88.8 2.5 %collective-permute-done.12.b = bf16[72,1152]{1,0:T(8,128)(2,1)S(1)} collective-permute-done((bf16[72,1152]{1,0:T(8,128)(2,1)S(1)}, bf16[72,1152]{1,0:T(8,128)(2,1)S(1)}, u32[]{:S(2)}, u32[]{:S(2)}) %collective-permute-start.12) | collective-permute-done | bytes 165920 | tf_op jit(solution)/shard_map/ppermute | solution.py:24
  91.3 0.6 collective-permute-start.16
  91.9 1.5 %collective-permute-start.15 = (bf16[72,1152]{1,0:T(8,128)(2,1)S(1)}, bf16[72,1152]{1,0:T(8,128)(2,1)S(1)}, u32[]{:S(2)}, u32[]{:S(2)}) collective-permute-start(bf16[72,1152]{1,0:T(8,128)(2,1)S(1)} %shard_map.86.a), channel_id=1, source_target_pairs={{0,16},{16,32},{32,48},{48,0},{1,17},{17,33},{33,49},{49,1},{2,18}... | collective-permute-start | bytes 497672 | tf_op jit(solution)/shard_map/ppermute | solution.py:24
  93.4 0.4 collective-permute-start.14
  93.8 1.7 %shard_map.88 = bf16[320,1152]{1,0:T(8,128)(2,1)} custom-call(bf16[320,1152]{1,0:T(8,128)(2,1)S(1)} %bitcast.17, bf16[320,1152]{1,0:T(8,128)(2,1)S(1)} %get-tuple-element.91.a, bf16[320,1152]{1,0:T(8,128)(2,1)S(1)} %collective-permute-done.17.b, bf16[320,1152]{1,0:T(8,128)(2,1)S(1)} %collective-permute-done.18.c), custom_call_target="tpu_custom_call" | custom-call | flops 1073741824 | bytes 1024 | tf_op jit(solution)/shard_map/pallas_call | solution.py:337
  95.4 2.5 %collective-permute-done.16.d = bf16[72,1152]{1,0:T(8,128)(2,1)S(1)} collective-permute-done((bf16[72,1152]{1,0:T(8,128)(2,1)S(1)}, bf16[72,1152]{1,0:T(8,128)(2,1)S(1)}, u32[]{:S(2)}, u32[]{:S(2)}) %collective-permute-start.16) | collective-permute-done | bytes 165920 | tf_op jit(solution)/shard_map/ppermute | solution.py:24
  97.9 3.5 %collective-permute-done.15.c = bf16[72,1152]{1,0:T(8,128)(2,1)S(1)} collective-permute-done((bf16[72,1152]{1,0:T(8,128)(2,1)S(1)}, bf16[72,1152]{1,0:T(8,128)(2,1)S(1)}, u32[]{:S(2)}, u32[]{:S(2)}) %collective-permute-start.15) | collective-permute-done | bytes 165920 | tf_op jit(solution)/shard_map/ppermute | solution.py:24
  101.4 0.8 shard_map.89
  (11 shorter events, 0.1 us)
Async XLA Ops:
  0.6 36.8 %collective-permute-start.2 = (bf16[320,1152]{1,0:T(8,128)(2,1)}, bf16[320,1152]{1,0:T(8,128)(2,1)S(1)}, u32[]{:S(2)}, u32[]{:S(2)}) collective-permute-start(bf16[320,1152]{1,0:T(8,128)(2,1)} %bitcast.10), channel_id=1, source_target_pairs={{0,64},{64,0},{1,65},{65,1},{2,66},{66,2},{3,67},{67,3},{4,68},{68... | collective-permute-start | bytes 2211848 | tf_op jit(solution)/shard_map/ppermute | solution.py:24
  3.4 9.5 %collective-permute-start.1 = (bf16[72,1152]{1,0:T(8,128)(2,1)S(1)}, bf16[72,1152]{1,0:T(8,128)(2,1)S(1)}, u32[]{:S(2)}, u32[]{:S(2)}) collective-permute-start(bf16[72,1152]{1,0:T(8,128)(2,1)S(1)} %shard_map.76), channel_id=1, source_target_pairs={{0,72},{8,64},{64,8},{72,0},{1,73},{9,65},{65,9},{73,1},{2,74},{10... | collective-permute-start | bytes 497672 | tf_op jit(solution)/shard_map/ppermute | solution.py:34
  5.6 36.3 %collective-permute-start.5 = (bf16[320,1152]{1,0:T(8,128)(2,1)}, bf16[320,1152]{1,0:T(8,128)(2,1)S(1)}, u32[]{:S(2)}, u32[]{:S(2)}) collective-permute-start(bf16[320,1152]{1,0:T(8,128)(2,1)} %bitcast.13), channel_id=1, source_target_pairs={{0,32},{16,48},{32,0},{48,16},{1,33},{17,49},{33,1},{49,17},{2,34}... | collective-permute-start | bytes 2211848 | tf_op jit(solution)/shard_map/ppermute | solution.py:24
  9.5 32.7 %collective-permute-start.4 = (bf16[320,1152]{1,0:T(8,128)(2,1)}, bf16[320,1152]{1,0:T(8,128)(2,1)S(1)}, u32[]{:S(2)}, u32[]{:S(2)}) collective-permute-start(bf16[320,1152]{1,0:T(8,128)(2,1)} %bitcast.14), channel_id=1, source_target_pairs={{0,48},{16,0},{32,16},{48,32},{1,49},{17,1},{33,17},{49,33},{2,50}... | collective-permute-start | bytes 2211848 | tf_op jit(solution)/shard_map/ppermute | solution.py:24
  10.2 32.0 %collective-permute-start.3 = (bf16[320,1152]{1,0:T(8,128)(2,1)}, bf16[320,1152]{1,0:T(8,128)(2,1)}, u32[]{:S(2)}, u32[]{:S(2)}) collective-permute-start(bf16[320,1152]{1,0:T(8,128)(2,1)} %bitcast.15), channel_id=1, source_target_pairs={{0,16},{16,32},{32,48},{48,0},{1,17},{17,33},{33,49},{49,1},{2,18}... | collective-permute-start | bytes 2211848 | tf_op jit(solution)/shard_map/ppermute | solution.py:24
  12.8 24.6 %copy-start = (bf16[1,320,1152]{2,1,0:T(8,128)(2,1)S(1)}, bf16[1,320,1152]{2,1,0:T(8,128)(2,1)}, u32[]{:S(2)}) copy-start(bf16[1,320,1152]{2,1,0:T(8,128)(2,1)} %param.8) | copy-start | bytes 2211844
  34.0 3.4 %collective-permute-start = (bf16[4,2,72,1152]{3,2,1,0:T(8,128)(2,1)}, bf16[4,2,72,1152]{3,2,1,0:T(8,128)(2,1)}, u32[]{:S(2)}, u32[]{:S(2)}) collective-permute-start(bf16[4,2,72,1152]{3,2,1,0:T(8,128)(2,1)} %all_to_all.4), channel_id=1, source_target_pairs={{0,1},{1,0},{2,3},{3,2},{4,5},{5,4},{6,7},{7,6},{8,9},{9,8},{10,11... | collective-permute-start | bytes 3981320 | tf_op jit(solution)/shard_map/cond/branch_1_fun/ppermute | solution.py:24
  37.4 4.8 %copy-start.1 = (bf16[1,320,1152]{2,1,0:T(8,128)(2,1)S(1)}, bf16[1,320,1152]{2,1,0:T(8,128)(2,1)}, u32[]{:S(2)}) copy-start(bf16[1,320,1152]{2,1,0:T(8,128)(2,1)} %param.7) | copy-start | bytes 2211844
  53.6 3.3 %collective-permute-start.6 = (bf16[4,2,72,1152]{3,2,1,0:T(8,128)(2,1)S(1)}, bf16[4,2,72,1152]{3,2,1,0:T(8,128)(2,1)S(1)}, u32[]{:S(2)}, u32[]{:S(2)}) collective-permute-start(bf16[4,2,72,1152]{3,2,1,0:T(8,128)(2,1)S(1)} %get-tuple-element.68), channel_id=1, source_target_pairs={{0,1},{1,0},{2,3},{3,2},{4,5},{5,4},{6,7},{7,6},{8,9},{9,8},{10,11... | collective-permute-start | bytes 3981320 | tf_op jit(solution)/shard_map/ppermute | solution.py:24
  56.9 12.7 %collective-permute-start.10 = (bf16[320,1152]{1,0:T(8,128)(2,1)S(1)}, bf16[320,1152]{1,0:T(8,128)(2,1)S(1)}, u32[]{:S(2)}, u32[]{:S(2)}) collective-permute-start(bf16[320,1152]{1,0:T(8,128)(2,1)S(1)} %shard_map.79), channel_id=1, source_target_pairs={{0,16},{1,49},{16,32},{17,1},{32,48},{33,17},{48,0},{49,33},{2,18}... | collective-permute-start | bytes 2211848 | tf_op jit(solution)/shard_map/ppermute | solution.py:29
  58.3 12.0 %collective-permute-start.9 = (bf16[2,72,1152]{2,1,0:T(8,128)(2,1)S(1)}, bf16[2,72,1152]{2,1,0:T(8,128)(2,1)S(1)}, u32[]{:S(2)}, u32[]{:S(2)}) collective-permute-start(bf16[2,72,1152]{2,1,0:T(8,128)(2,1)S(1)} %get-tuple-element.74), channel_id=1, source_target_pairs={{0,4},{2,6},{4,0},{6,2},{1,5},{3,7},{5,1},{7,3},{8,12},{10,14},{12... | collective-permute-start | bytes 995336 | tf_op jit(solution)/shard_map/ppermute | solution.py:24
  61.4 24.3 %collective-permute-start.13 = (bf16[320,1152]{1,0:T(8,128)(2,1)S(1)}, bf16[320,1152]{1,0:T(8,128)(2,1)S(1)}, u32[]{:S(2)}, u32[]{:S(2)}) collective-permute-start(bf16[320,1152]{1,0:T(8,128)(2,1)S(1)} %get-tuple-element.88), channel_id=1, source_target_pairs={{0,64},{64,0},{1,65},{65,1},{2,66},{66,2},{3,67},{67,3},{4,68},{68... | collective-permute-start | bytes 2211848 | tf_op jit(solution)/shard_map/ppermute | solution.py:24
  62.1 15.6 %collective-permute-start.7 = (bf16[2,72,1152]{2,1,0:T(8,128)(2,1)S(1)}, bf16[2,72,1152]{2,1,0:T(8,128)(2,1)S(1)}, u32[]{:S(2)}, u32[]{:S(2)}) collective-permute-start(bf16[2,72,1152]{2,1,0:T(8,128)(2,1)S(1)} %get-tuple-element.72), channel_id=1, source_target_pairs={{0,2},{2,4},{4,6},{6,0},{1,3},{3,5},{5,7},{7,1},{8,10},{10,12},{12... | collective-permute-start | bytes 995336 | tf_op jit(solution)/shard_map/ppermute | solution.py:24
  62.7 15.0 %collective-permute-start.8 = (bf16[2,72,1152]{2,1,0:T(8,128)(2,1)S(1)}, bf16[2,72,1152]{2,1,0:T(8,128)(2,1)S(1)}, u32[]{:S(2)}, u32[]{:S(2)}) collective-permute-start(bf16[2,72,1152]{2,1,0:T(8,128)(2,1)S(1)} %get-tuple-element.73), channel_id=1, source_target_pairs={{0,6},{2,0},{4,2},{6,4},{1,7},{3,1},{5,3},{7,5},{8,14},{10,8},{12,... | collective-permute-start | bytes 995336 | tf_op jit(solution)/shard_map/ppermute | solution.py:24
  70.4 23.4 %collective-permute-start.17 = (bf16[320,1152]{1,0:T(8,128)(2,1)S(1)}, bf16[320,1152]{1,0:T(8,128)(2,1)S(1)}, u32[]{:S(2)}, u32[]{:S(2)}) collective-permute-start(bf16[320,1152]{1,0:T(8,128)(2,1)S(1)} %get-tuple-element.92), channel_id=1, source_target_pairs={{0,48},{16,0},{32,16},{48,32},{1,49},{17,1},{33,17},{49,33},{2,50}... | collective-permute-start | bytes 2211848 | tf_op jit(solution)/shard_map/ppermute | solution.py:24
  72.8 21.0 %collective-permute-start.18 = (bf16[320,1152]{1,0:T(8,128)(2,1)S(1)}, bf16[320,1152]{1,0:T(8,128)(2,1)S(1)}, u32[]{:S(2)}, u32[]{:S(2)}) collective-permute-start(bf16[320,1152]{1,0:T(8,128)(2,1)S(1)} %get-tuple-element.93), channel_id=1, source_target_pairs={{0,16},{16,32},{32,48},{48,0},{1,17},{17,33},{33,49},{49,1},{2,18}... | collective-permute-start | bytes 2211848 | tf_op jit(solution)/shard_map/ppermute | solution.py:24
  77.9 7.7 %collective-permute-start.11 = (bf16[72,1152]{1,0:T(8,128)(2,1)S(1)}, bf16[72,1152]{1,0:T(8,128)(2,1)S(1)}, u32[]{:S(2)}, u32[]{:S(2)}) collective-permute-start(bf16[72,1152]{1,0:T(8,128)(2,1)S(1)} %get-tuple-element.86), channel_id=1, source_target_pairs={{0,72},{8,64},{64,8},{72,0},{1,73},{9,65},{65,9},{73,1},{2,74},{10... | collective-permute-start | bytes 497672 | tf_op jit(solution)/shard_map/ppermute | solution.py:34
  85.6 5.7 %collective-permute-start.12 = (bf16[72,1152]{1,0:T(8,128)(2,1)S(1)}, bf16[72,1152]{1,0:T(8,128)(2,1)S(1)}, u32[]{:S(2)}, u32[]{:S(2)}) collective-permute-start(bf16[72,1152]{1,0:T(8,128)(2,1)S(1)} %shard_map.85.a), channel_id=1, source_target_pairs={{0,64},{64,0},{1,65},{65,1},{2,66},{66,2},{3,67},{67,3},{4,68},{68... | collective-permute-start | bytes 497672 | tf_op jit(solution)/shard_map/ppermute | solution.py:24
  91.3 6.6 %collective-permute-start.16 = (bf16[72,1152]{1,0:T(8,128)(2,1)S(1)}, bf16[72,1152]{1,0:T(8,128)(2,1)S(1)}, u32[]{:S(2)}, u32[]{:S(2)}) collective-permute-start(bf16[72,1152]{1,0:T(8,128)(2,1)S(1)} %shard_map.86.a), channel_id=1, source_target_pairs={{0,48},{16,0},{32,16},{48,32},{1,49},{17,1},{33,17},{49,33},{2,50}... | collective-permute-start | bytes 497672 | tf_op jit(solution)/shard_map/ppermute | solution.py:24
  91.9 9.5 %collective-permute-start.15 = (bf16[72,1152]{1,0:T(8,128)(2,1)S(1)}, bf16[72,1152]{1,0:T(8,128)(2,1)S(1)}, u32[]{:S(2)}, u32[]{:S(2)}) collective-permute-start(bf16[72,1152]{1,0:T(8,128)(2,1)S(1)} %shard_map.86.a), channel_id=1, source_target_pairs={{0,16},{16,32},{32,48},{48,0},{1,17},{17,33},{33,49},{49,1},{2,18}... | collective-permute-start | bytes 497672 | tf_op jit(solution)/shard_map/ppermute | solution.py:24
  93.4 8.0 %collective-permute-start.14 = (bf16[72,1152]{1,0:T(8,128)(2,1)S(1)}, bf16[72,1152]{1,0:T(8,128)(2,1)S(1)}, u32[]{:S(2)}, u32[]{:S(2)}) collective-permute-start(bf16[72,1152]{1,0:T(8,128)(2,1)S(1)} %shard_map.86.a), channel_id=1, source_target_pairs={{0,32},{16,48},{32,0},{48,16},{1,33},{17,49},{33,1},{49,17},{2,34}... | collective-permute-start | bytes 497672 | tf_op jit(solution)/shard_map/ppermute | solution.py:24

commit v8 on v7

--- a/solution.py
+++ b/solution.py
@@ -54,15 +54,19 @@
     return 1.0 / jnp.sqrt(jnp.sum(rows * rows, axis=-1, keepdims=True) + 1e-06)
 
 
-def project(grad, rows):
-    inv = inverse_length(rows)
-    unit = rows * inv
-    inner = jnp.sum(unit * grad, axis=-1, keepdims=True)
-    return (grad - unit * inner) * inv
+def project(grad, rows, inv=None, scale=1.0):
+    inv = inverse_length(rows) if inv is None else inv
+    inner = jnp.sum(rows * grad, axis=-1, keepdims=True)
+    return (grad - rows * (inv * inv * inner)) * (inv * scale)
 
 
 def half_kernel(w, w_half):
     w_half[...] = w[...].astype(BF)
+
+
+def scalar_kernel(t_log, bias, out):
+    row_ids = lax.broadcasted_iota(jnp.int32, out.shape, 0)
+    out[...] = jnp.where(row_ids == 0, jnp.exp(t_log[...]), bias[...])
 
 
 def repeat_kernel(w_h, w_y, out):
@@ -95,7 +99,7 @@
             head[pl.ds((h * 4 + x) * 144, 144), :] = jnp.concatenate([first, second], axis=0).astype(BF)
 
 
-def text_kernel(near, far, txt, txt_far, z, n_txt, mine, other, rows, w_full, sems):
+def text_kernel(near, far, txt, txt_far, z, n_txt, inv, mine, other, rows, w_full, sems):
     copies = load_head(near, far, mine, other, sems)
     late = [
         pltpu.make_async_copy(txt, rows.at[pl.ds(0, 320)], sems.at[8]),
@@ -108,7 +112,8 @@
         c.wait()
     out = jnp.dot(rows[...], w_full[...], preferred_element_type=F32)
     z[...] = out
-    n_txt[...] = (out * inverse_length(out)).astype(BF)
+    inv[...] = inverse_length(out)
+    n_txt[...] = (out * inv[...]).astype(BF)
 
 
 def logit_gradient(scale, bias, left, right):
@@ -118,31 +123,35 @@
     return 1.0 / (1.0 + jnp.exp(-logits))
 
 
-def main_kernel(t_log, bias, n_txt, img, img_a, img_b, img_c, z, txt, txt_far, grad, g_own, g_far, mine, other, raw, rows, feat, wide, sems):
+def main_kernel(scalars, n_txt, img, img_a, img_b, img_c, z, inv, txt, txt_far, grad, g_own, g_far, mine, other, raw, rows, feat, wide, sems):
     moves = [(block, raw.at[pl.ds(k * 320, 320)]) for k, block in enumerate((img, img_a, img_b, img_c))]
     moves += [(txt, feat.at[pl.ds(0, 320)]), (txt_far, feat.at[pl.ds(320, 320)])]
     copies = [pltpu.make_async_copy(a, b, sems.at[k]) for k, (a, b) in enumerate(moves)]
     for c in copies:
         c.start()
-    scale = jnp.exp(t_log[...])
+    scale, bias = scalars[0:1, 0:1], scalars[1:2, 0:1]
     for first, last, ready in ((0, 512, copies[:2]), (512, 1280, copies[2:4])):
         for c in ready:
             c.wait()
         fresh = pl.ds(0 if first == 0 else 640, 640)
         wide_rows = raw[fresh, :].astype(F32)
         rows[fresh, :] = (wide_rows * inverse_length(wide_rows)).astype(BF)
-        g = logit_gradient(scale, bias[...], n_txt[...], rows[pl.ds(first, last - first), :])
-        row_ids = lax.broadcasted_iota(jnp.int32, g.shape, 0)
-        col_ids = lax.broadcasted_iota(jnp.int32, g.shape, 1)
+        g = logit_gradient(scale, bias, n_txt[...], rows[pl.ds(first, last - first), :])
+        grad[:, first:last] = g.astype(BF)
         if first == 0:
-            g = g - jnp.where((row_ids == col_ids) & (row_ids < 320), 1.0, 0.0)
-        grad[:, first:last] = g.astype(BF)
-    total = scale * jnp.dot(grad[...], rows[...], preferred_element_type=F32)
-    g_own[...] = total[:320].astype(BF)
-    g_far[...] = total[320:].astype(BF)
+            own = g[:320, :384]
+            row_ids = lax.broadcasted_iota(jnp.int32, own.shape, 0)
+            col_ids = lax.broadcasted_iota(jnp.int32, own.shape, 1)
+            grad[:320, :384] = (own - jnp.where(row_ids == col_ids, 1.0, 0.0)).astype(BF)
+    parts = []
+    for half, out in enumerate((g_own, g_far)):
+        here = pl.ds(half * 320, 320)
+        total = jnp.dot(grad[here, :], rows[...], preferred_element_type=F32)
+        out[...] = (scale * total).astype(BF)
+        parts.append(project(total, z[here, :], inv[here, :], scale).astype(BF))
+    dz = jnp.concatenate(parts, axis=0)
     for c in copies[4:]:
         c.wait()
-    dz = project(total, z[...]).astype(BF)
     wide[...] = lax.dot_general(
         feat[...], dz, (((0,), (0,)), ((), ())), preferred_element_type=F32
     )
@@ -154,10 +163,10 @@
         other[j % 4, j // 4] = wide[pl.ds(b, 72), :].astype(BF)
 
 
-def part_kernel(first, t_log, grad, n_txt, *outs):
+def part_kernel(first, scalars, grad, n_txt, *outs):
     start = first * 320
     rows = sum(ref.shape[0] for ref in outs)
-    out = jnp.exp(t_log[...]) * lax.dot_general(
+    out = scalars[0:1, 0:1] * lax.dot_general(
         grad[:, start : start + rows], n_txt[...], (((0,), (0,)), ((), ())), preferred_element_type=F32
     )
     at = 0
@@ -237,10 +246,14 @@
     return lax.all_to_all(value, "x", split_axis=0, concat_axis=0, tiled=True)
 
 
-def gather_head(w_h, w_y):
+def gather_head(w_h, w_y, t_log, bias):
     (pieces,) = call(repeat_kernel, [stack_of(4, 2)], [VM, VM])(w_h, w_y)
     near = along_x(pieces)
-    return near, shift(near, "core", 1)
+    near, t_log, bias = hold((near, t_log, bias))
+    (scalars,) = call(scalar_kernel, [shaped((8, 128), F32)], [VM] * 2, flops=1 << 31)(
+        t_log.reshape(1, 1), bias.reshape(1, 1)
+    )
+    return near, shift(near, "core", 1), scalars
 
 
 def parts_of(first, shapes, *args):
@@ -248,17 +261,17 @@
     return call(kernel, shapes, [VM] * 3, flops=1 << 31)(*args)
 
 
-def beside_x(part_c, t_log, grad, n_txt):
+def beside_x(part_c, scalars, grad, n_txt):
     got_c = apart_by_core(part_c)
-    part_own, part_a, part_b = parts_of(0, [BLOCK] * 3, t_log, grad, n_txt)
+    part_own, part_a, part_b = parts_of(0, [BLOCK] * 3, scalars, grad, n_txt)
     return part_own, *call(pass_on_kernel, [BLOCK] * 2, [VM] * 3)(part_a, part_b, got_c)
 
 
-def sum_plane(t_log, mine, got_core, part_c, grad, n_txt, z, g_own, g_far, near, far):
+def sum_plane(scalars, mine, got_core, part_c, grad, n_txt, z, g_own, g_far, near, far):
     rel = call(core_sum_kernel, [stack_of(2)] * 4, [VM] * 2)(mine, got_core)
     got_x = [shift(rel[s], "x", s) for s in (1, 3, 2)]
     g_got = shift(g_far, "ylo", 1)
-    part_own, part_a, part_b = beside_x(part_c, t_log, grad, n_txt)
+    part_own, part_a, part_b = beside_x(part_c, scalars, grad, n_txt)
     got_x[2], part_a, part_b, near, far = hold((got_x[2], part_a, part_b, near, far))
     (head,) = call(
         head_kernel,
@@ -289,19 +302,18 @@
 
 def on_device(img_emb, txt_feat, w_txt, t_log, bias):
     img, txt = img_emb[0], txt_feat[0]
-    t_log, bias = t_log.reshape(1, 1), bias.reshape(1, 1)
 
     txt_far = shift(txt, "ylo", 1)
     (w_h,) = call(half_kernel, [stack_of()], [VM], vmem=60)(w_txt)
     w_y = swap_far(w_h)
     w_h, img = hold((w_h, img))
     img_c, img_b, img_a = (shift(img, "z", s) for s in (2, -1, 1))
-    near, far = apart(gather_head, w_h, w_y)
+    near, far, scalars = apart(gather_head, w_h, w_y, t_log, bias)
     near, far, txt_far = hold((near, far, txt_far))
 
-    z, n_txt = call(
+    z, n_txt, inv = call(
         text_kernel,
-        [shaped((640, 1152), F32), shaped((640, 1152), BF)],
+        [shaped((640, 1152), F32), shaped((640, 1152), BF), shaped((640, 1), F32)],
         [ANY] * 4,
         [
             pltpu.VMEM((4, 2, 72, 1152), BF),
@@ -317,7 +329,7 @@
     grad, g_own, g_far, mine, other = call(
         main_kernel,
         [shaped((640, 1280), BF), BLOCK, BLOCK, stack_of(4, 2), stack_of(4, 2)],
-        [VM] * 3 + [ANY] * 4 + [VM, ANY, ANY],
+        [VM] * 2 + [ANY] * 4 + [VM, VM, ANY, ANY],
         [
             pltpu.VMEM((1280, 1152), BF),
             pltpu.VMEM((1280, 1152), BF),
@@ -326,13 +338,13 @@
             pltpu.SemaphoreType.DMA((6,)),
         ],
         vmem=MAIN_MIB,
-    )(t_log, bias, n_txt, img, img_a, img_b, img_c, z, txt, txt_far)
+    )(scalars, n_txt, img, img_a, img_b, img_c, z, inv, txt, txt_far)
 
     got_core, (part_c,) = hold(
-        (shift(other, "core", 1), parts_of(3, [BLOCK], t_log, grad, n_txt))
+        (shift(other, "core", 1), parts_of(3, [BLOCK], scalars, grad, n_txt))
     )
     quad, d_feat, part_own, got_a, got_b = sum_plane(
-        t_log, mine, got_core, part_c, grad, n_txt, z, g_own, g_far, near, far
+        scalars, mine, got_core, part_c, grad, n_txt, z, g_own, g_far, near, far
     )
     (d_img,) = call(image_out_kernel, [BLOCK], [VM] * 4, flops=1 << 30)(img, part_own, got_a, got_b)
     got_z = [shift(quad, "z", k) for k in (2, 1, -1)]

time: 102 us -> 102 us (level)
  between operations: 2.06 us -> 0.75 us
  Pallas kernels: 28.5 us -> 29.7 us
    pallas_call x1 -> x2, Pallas kernels: 4.5 us -> 5.89 us  [the longest x1 4.53 us: on_device(): call(text_kernel, [shaped((640, 1152), F32), shaped((640, 1152), BF), sha...]
  transfers between devices with their start and end apart: 19 -> 19, of which waited for: 10 -> 10; matrix products, arithmetic and copies ran while one was open for 0% -> 0% of each run, Pallas kernels for 16% -> 17%
where the time goes in v8:
time: 102 us
  Pallas kernels  29.7 us (29%)
  waiting for transfers between devices  26.2 us (26%)
  starting transfers between devices  24.4 us (24%)
  blocking collectives  21 us (21%)
    all_to_all x1, blocking collectives, along_x(): return lax.all_to_all(value, 'x', split_axis=0, concat_axis=0, tiled=True)  21 us
    ppermute x16, starting transfers between devices, shift(): return lax.ppermute(value, axis, [(i, (i + step) % n) for i in range(n)])  19.9 us
    ppermute x16, waiting for transfers between devices, shift(): return lax.ppermute(value, axis, [(i, (i + step) % n) for i in range(n)])  17.5 us
    pallas_call x1, Pallas kernels, on_device(): call(main_kernel, [shaped((640, 1280), BF), BLOCK, BLOCK, stack_of(4, 2),...  11.3 us
    ppermute x2, waiting for transfers between devices, swap_far(): return lax.ppermute(value, ('ylo', 'yhi'), pairs)  6.55 us
    pallas_call x1, Pallas kernels, on_device(): call(text_kernel, [shaped((640, 1152), F32), shaped((640, 1152), BF), sha...  4.53 us
    ppermute x2, starting transfers between devices, swap_far(): return lax.ppermute(value, ('ylo', 'yhi'), pairs)  3.39 us
    pallas_call x2, Pallas kernels, parts_of(): return call(kernel, shapes, [VM] * 3, flops=1 << 31)(*args)  3.1 us
  transfers between devices with their start and end apart: 19, of which 10 were waited for; matrix products, arithmetic and copies ran while one was open for 0% of the time, Pallas kernels for 17%

profile of v8, /device:TPU:0, one launch (start us, length us, event | category | flops | bytes accessed | tf_op | source)
XLA Modules:
  0.0 102.1 jit_solution(10972108695670421074)
XLA Ops:
  0.6 1.7 %collective-permute-start.2 = (bf16[320,1152]{1,0:T(8,128)(2,1)}, bf16[320,1152]{1,0:T(8,128)(2,1)S(1)}, u32[]{:S(2)}, u32[]{:S(2)}) collective-permute-start(bf16[320,1152]{1,0:T(8,128)(2,1)} %bitcast.6), channel_id=1, source_target_pairs={{0,64},{64,0},{1,65},{65,1},{2,66},{66,2},{3,67},{67,3},{4,68},{68... | collective-permute-start | bytes 2211848 | tf_op jit(solution)/shard_map/ppermute | solution.py:24
  2.4 1.0 shard_map.78
  3.4 2.3 %collective-permute-start.1 = (bf16[72,1152]{1,0:T(8,128)(2,1)S(1)}, bf16[72,1152]{1,0:T(8,128)(2,1)S(1)}, u32[]{:S(2)}, u32[]{:S(2)}) collective-permute-start(bf16[72,1152]{1,0:T(8,128)(2,1)S(1)} %shard_map.78), channel_id=1, source_target_pairs={{0,72},{8,64},{64,8},{72,0},{1,73},{9,65},{65,9},{73,1},{2,74},{10... | collective-permute-start | bytes 497672 | tf_op jit(solution)/shard_map/ppermute | solution.py:34
  5.6 3.9 %collective-permute-start.5 = (bf16[320,1152]{1,0:T(8,128)(2,1)}, bf16[320,1152]{1,0:T(8,128)(2,1)S(1)}, u32[]{:S(2)}, u32[]{:S(2)}) collective-permute-start(bf16[320,1152]{1,0:T(8,128)(2,1)} %bitcast.9), channel_id=1, source_target_pairs={{0,32},{16,48},{32,0},{48,16},{1,33},{17,49},{33,1},{49,17},{2,34}... | collective-permute-start | bytes 2211848 | tf_op jit(solution)/shard_map/ppermute | solution.py:24
  9.5 0.7 collective-permute-start.4
  10.2 1.3 %collective-permute-start.3 = (bf16[320,1152]{1,0:T(8,128)(2,1)}, bf16[320,1152]{1,0:T(8,128)(2,1)}, u32[]{:S(2)}, u32[]{:S(2)}) collective-permute-start(bf16[320,1152]{1,0:T(8,128)(2,1)} %bitcast.11), channel_id=1, source_target_pairs={{0,16},{16,32},{32,48},{48,0},{1,17},{17,33},{33,49},{49,1},{2,18}... | collective-permute-start | bytes 2211848 | tf_op jit(solution)/shard_map/ppermute | solution.py:24
  11.5 0.0 collective-permute-done.1
  11.5 24.5 %conditional.1 = (bf16[4,2,72,1152]{3,2,1,0:T(8,128)(2,1)}, bf16[4,2,72,1152]{3,2,1,0:T(8,128)(2,1)}, f32[8,128]{1,0:T(8,128)S(1)}) conditional(s32[]{:T(128)} %convert_element_type.3, () %tuple.25, (bf16[72,1152]{1,0:T(8,128)(2,1)S(1)}, bf16[72,1152]{1,0:T(8,128)(2,1)S(1)}, f32[1]{0:T(128)}, f32[1]{0:T(128)}) %tuple.27), branch_computations={%region_0.0_spmd, %region_1.0_spmd} | conditional | flops 2147484672 | bytes 7964736 | solution.py:229
  11.5 0.1 branch_1_fun.2
  11.7 21.0 %all_to_all.4 = bf16[4,2,72,1152]{3,2,1,0:T(8,128)(2,1)} all-to-all(bf16[4,2,72,1152]{3,2,1,0:T(8,128)(2,1)S(1)} %branch_1_fun.2), channel_id=1, replica_groups=mesh['ylo'=2,'z'=4,'yhi'=2,'x'=4,'core'=2] {'x'}, dimensions={0} | all-to-all | bytes 2654208 | tf_op jit(solution)/shard_map/cond/branch_1_fun/all_to_all | solution.py:246
  32.7 0.0 collective-permute-start
  32.7 1.4 %branch_1_fun.3 = f32[8,128]{1,0:T(8,128)S(1)} custom-call(f32[1,1]{1,0:T(1,128)} %bitcast.t_log, f32[1,1]{1,0:T(1,128)} %bitcast.1.bias), custom_call_target="tpu_custom_call" | custom-call | flops 2147483648 | bytes 1024 | tf_op jit(solution)/shard_map/cond/branch_1_fun/pallas_call | solution.py:253
  34.0 2.0 %collective-permute-done = bf16[4,2,72,1152]{3,2,1,0:T(8,128)(2,1)} collective-permute-done((bf16[4,2,72,1152]{3,2,1,0:T(8,128)(2,1)}, bf16[4,2,72,1152]{3,2,1,0:T(8,128)(2,1)}, u32[]{:S(2)}, u32[]{:S(2)}) %collective-permute-start) | collective-permute-done | bytes 1327136 | tf_op jit(solution)/shard_map/cond/branch_1_fun/ppermute | solution.py:24
  36.1 0.0 collective-permute-done.2.txt_far
  36.1 4.5 %shard_map.79 = (f32[640,1152]{1,0:T(8,128)S(1)}, bf16[640,1152]{1,0:T(8,128)(2,1)S(1)}, f32[640,1]{1,0:T(8,128)S(1)}) custom-call(bf16[4,2,72,1152]{3,2,1,0:T(8,128)(2,1)} %get-tuple-element.93.near, bf16[4,2,72,1152]{3,2,1,0:T(8,128)(2,1)} %get-tuple-element.94.far, bf16[320,1152]{1,0:T(8,128)(2,1)S(1)} %bitcast.7, ...), custom_call_target="tpu_custom_call" | custom-call | flops 17179869184 | bytes 1024 | tf_op jit(solution)/shard_map/pallas_call | solution.py:314
  40.6 0.0 collective-permute-done.5.img_c
  40.6 1.6 %collective-permute-done.4.img_b = bf16[320,1152]{1,0:T(8,128)(2,1)S(1)} collective-permute-done((bf16[320,1152]{1,0:T(8,128)(2,1)}, bf16[320,1152]{1,0:T(8,128)(2,1)S(1)}, u32[]{:S(2)}, u32[]{:S(2)}) %collective-permute-start.4) | collective-permute-done | bytes 737312 | tf_op jit(solution)/shard_map/ppermute | solution.py:24
  42.2 11.3 %shard_map.80 = (bf16[640,1280]{1,0:T(8,128)(2,1)S(1)}, bf16[320,1152]{1,0:T(8,128)(2,1)S(1)}, bf16[320,1152]{1,0:T(8,128)(2,1)S(1)}, bf16[4,2,72,1152]{3,2,1,0:T(8,128)(2,1)S(1)}, bf16[4,2,72,1152]{3,2,1,0:T(8,128)(2,1)S(1)}) custom-call(f32[8,128]{1,0:T(8,128)S(1)} %get-tuple-element.66.scalars, bf16[640,1152]{1,0:T(8,128)(2,1)S(1)} %get-tuple-element.74.n_txt, ...), custom_call_target="tpu_custom_call" | custom-call | flops 1024 | bytes 1024 | tf_op jit(solution)/shard_map/pallas_call | solution.py:329
  53.5 0.3 collective-permute-start.6
  53.8 1.0 %shard_map.81 = bf16[320,1152]{1,0:T(8,128)(2,1)S(1)} custom-call(f32[8,128]{1,0:T(8,128)S(1)} %get-tuple-element.66.scalars, bf16[640,1280]{1,0:T(8,128)(2,1)S(1)} %get-tuple-element.82.grad, bf16[640,1152]{1,0:T(8,128)(2,1)S(1)} %get-tuple-element.74.n_txt), custom_call_target="tpu_custom_call" | custom-call | flops 2147483648 | bytes 1024 | tf_op jit(solution)/shard_map/pallas_call | solution.py:261
  54.9 2.0 %collective-permute-done.6.got = bf16[4,2,72,1152]{3,2,1,0:T(8,128)(2,1)S(1)} collective-permute-done((bf16[4,2,72,1152]{3,2,1,0:T(8,128)(2,1)S(1)}, bf16[4,2,72,1152]{3,2,1,0:T(8,128)(2,1)S(1)}, u32[]{:S(2)}, u32[]{:S(2)}) %collective-permute-start.6) | collective-permute-done | bytes 1327136 | tf_op jit(solution)/shard_map/ppermute | solution.py:24
  56.9 1.1 %collective-permute-start.10 = (bf16[320,1152]{1,0:T(8,128)(2,1)S(1)}, bf16[320,1152]{1,0:T(8,128)(2,1)S(1)}, u32[]{:S(2)}, u32[]{:S(2)}) collective-permute-start(bf16[320,1152]{1,0:T(8,128)(2,1)S(1)} %shard_map.81), channel_id=1, source_target_pairs={{0,16},{1,49},{16,32},{17,1},{32,48},{33,17},{48,0},{49,33},{2,18}... | collective-permute-start | bytes 2211848 | tf_op jit(solution)/shard_map/ppermute | solution.py:29
  58.0 0.3 shard_map.82
  58.3 3.1 %collective-permute-start.9 = (bf16[2,72,1152]{2,1,0:T(8,128)(2,1)S(1)}, bf16[2,72,1152]{2,1,0:T(8,128)(2,1)S(1)}, u32[]{:S(2)}, u32[]{:S(2)}) collective-permute-start(bf16[2,72,1152]{2,1,0:T(8,128)(2,1)S(1)} %get-tuple-element.87), channel_id=1, source_target_pairs={{0,4},{2,6},{4,0},{6,2},{1,5},{3,7},{5,1},{7,3},{8,12},{10,14},{12... | collective-permute-start | bytes 995336 | tf_op jit(solution)/shard_map/ppermute | solution.py:24
  61.4 0.7 collective-permute-start.13
  62.1 0.6 collective-permute-start.7
  62.7 2.6 %collective-permute-start.8 = (bf16[2,72,1152]{2,1,0:T(8,128)(2,1)S(1)}, bf16[2,72,1152]{2,1,0:T(8,128)(2,1)S(1)}, u32[]{:S(2)}, u32[]{:S(2)}) collective-permute-start(bf16[2,72,1152]{2,1,0:T(8,128)(2,1)S(1)} %get-tuple-element.86), channel_id=1, source_target_pairs={{0,6},{2,0},{4,2},{6,4},{1,7},{3,1},{5,3},{7,5},{8,14},{10,8},{12,... | collective-permute-start | bytes 995336 | tf_op jit(solution)/shard_map/ppermute | solution.py:24
  65.3 2.1 %shard_map.83 = (bf16[320,1152]{1,0:T(8,128)(2,1)S(1)}, bf16[320,1152]{1,0:T(8,128)(2,1)S(1)}, bf16[320,1152]{1,0:T(8,128)(2,1)S(1)}) custom-call(f32[8,128]{1,0:T(8,128)S(1)} %get-tuple-element.66.scalars, bf16[640,1280]{1,0:T(8,128)(2,1)S(1)} %get-tuple-element.82.grad, bf16[640,1152]{1,0:T(8,128)(2,1)S(1)} %get-tuple-element.74.n_txt), custom_call_target="tpu_custom_call" | custom-call | flops 2147483648 | bytes 1024 | tf_op jit(solution)/shard_map/pallas_call | solution.py:261
  67.4 2.2 %collective-permute-done.10.got = bf16[320,1152]{1,0:T(8,128)(2,1)S(1)} collective-permute-done((bf16[320,1152]{1,0:T(8,128)(2,1)S(1)}, bf16[320,1152]{1,0:T(8,128)(2,1)S(1)}, u32[]{:S(2)}, u32[]{:S(2)}) %collective-permute-start.10) | collective-permute-done | bytes 737312 | tf_op jit(solution)/shard_map/ppermute | solution.py:29
  69.5 0.4 shard_map.84
  70.0 0.3 collective-permute-done.9.r
  70.3 2.4 %collective-permute-start.17 = (bf16[320,1152]{1,0:T(8,128)(2,1)S(1)}, bf16[320,1152]{1,0:T(8,128)(2,1)S(1)}, u32[]{:S(2)}, u32[]{:S(2)}) collective-permute-start(bf16[320,1152]{1,0:T(8,128)(2,1)S(1)} %get-tuple-element.105), channel_id=1, source_target_pairs={{0,48},{16,0},{32,16},{48,32},{1,49},{17,1},{33,17},{49,33},{2,50}... | collective-permute-start | bytes 2211848 | tf_op jit(solution)/shard_map/ppermute | solution.py:24
  72.7 0.0 collective-permute-start.18
  72.7 1.9 %shard_map.85.head = bf16[1152,1152]{1,0:T(8,128)(2,1)S(1)} custom-call(bf16[4,2,72,1152]{3,2,1,0:T(8,128)(2,1)} %get-tuple-element.93.near, bf16[4,2,72,1152]{3,2,1,0:T(8,128)(2,1)} %get-tuple-element.94.far), custom_call_target="tpu_custom_call" | custom-call | flops 2147483648 | bytes 1024 | tf_op jit(solution)/shard_map/pallas_call | solution.py:276
  74.6 3.0 %collective-permute-done.7.p = bf16[2,72,1152]{2,1,0:T(8,128)(2,1)S(1)} collective-permute-done((bf16[2,72,1152]{2,1,0:T(8,128)(2,1)S(1)}, bf16[2,72,1152]{2,1,0:T(8,128)(2,1)S(1)}, u32[]{:S(2)}, u32[]{:S(2)}) %collective-permute-start.7) | collective-permute-done | bytes 331808 | tf_op jit(solution)/shard_map/ppermute | solution.py:24
  77.6 0.2 shard_map.86
  77.8 1.1 %collective-permute-start.11 = (bf16[72,1152]{1,0:T(8,128)(2,1)S(1)}, bf16[72,1152]{1,0:T(8,128)(2,1)S(1)}, u32[]{:S(2)}, u32[]{:S(2)}) collective-permute-start(bf16[72,1152]{1,0:T(8,128)(2,1)S(1)} %get-tuple-element.99), channel_id=1, source_target_pairs={{0,72},{8,64},{64,8},{72,0},{1,73},{9,65},{65,9},{73,1},{2,74},{10... | collective-permute-start | bytes 497672 | tf_op jit(solution)/shard_map/ppermute | solution.py:34
  79.0 6.5 %collective-permute-done.11.b = bf16[72,1152]{1,0:T(8,128)(2,1)S(1)} collective-permute-done((bf16[72,1152]{1,0:T(8,128)(2,1)S(1)}, bf16[72,1152]{1,0:T(8,128)(2,1)S(1)}, u32[]{:S(2)}, u32[]{:S(2)}) %collective-permute-start.11) | collective-permute-done | bytes 165920 | tf_op jit(solution)/shard_map/ppermute | solution.py:34
  85.5 0.1 collective-permute-start.12
  85.7 3.0 %shard_map.89 = bf16[320,1152]{1,0:T(8,128)(2,1)} custom-call(f32[640,1152]{1,0:T(8,128)S(1)} %get-tuple-element.78.z, bf16[320,1152]{1,0:T(8,128)(2,1)S(1)} %get-tuple-element.100.a, bf16[320,1152]{1,0:T(8,128)(2,1)S(1)} %collective-permute-done.13.b, bf16[1152,1152]{1,0:T(8,128)(2,1)S(1)} %shard_map.85.head), custom_call_target="tpu_custom_call" | custom-call | flops 2147483648 | bytes 1024 | tf_op jit(solution)/shard_map/pallas_call | solution.py:290
  88.6 2.6 %collective-permute-done.12.b = bf16[72,1152]{1,0:T(8,128)(2,1)S(1)} collective-permute-done((bf16[72,1152]{1,0:T(8,128)(2,1)S(1)}, bf16[72,1152]{1,0:T(8,128)(2,1)S(1)}, u32[]{:S(2)}, u32[]{:S(2)}) %collective-permute-start.12) | collective-permute-done | bytes 165920 | tf_op jit(solution)/shard_map/ppermute | solution.py:24
  91.2 0.6 collective-permute-start.16
  91.8 1.5 %collective-permute-start.15 = (bf16[72,1152]{1,0:T(8,128)(2,1)S(1)}, bf16[72,1152]{1,0:T(8,128)(2,1)S(1)}, u32[]{:S(2)}, u32[]{:S(2)}) collective-permute-start(bf16[72,1152]{1,0:T(8,128)(2,1)S(1)} %shard_map.88.a), channel_id=1, source_target_pairs={{0,16},{16,32},{32,48},{48,0},{1,17},{17,33},{33,49},{49,1},{2,18}... | collective-permute-start | bytes 497672 | tf_op jit(solution)/shard_map/ppermute | solution.py:24
  93.3 0.4 collective-permute-start.14
  93.7 1.6 %shard_map.90 = bf16[320,1152]{1,0:T(8,128)(2,1)} custom-call(bf16[320,1152]{1,0:T(8,128)(2,1)S(1)} %bitcast.13, bf16[320,1152]{1,0:T(8,128)(2,1)S(1)} %get-tuple-element.104.a, bf16[320,1152]{1,0:T(8,128)(2,1)S(1)} %collective-permute-done.17.b, bf16[320,1152]{1,0:T(8,128)(2,1)S(1)} %collective-permute-done.18.c), custom_call_target="tpu_custom_call" | custom-call | flops 1073741824 | bytes 1024 | tf_op jit(solution)/shard_map/pallas_call | solution.py:349
  95.3 2.5 %collective-permute-done.16.d = bf16[72,1152]{1,0:T(8,128)(2,1)S(1)} collective-permute-done((bf16[72,1152]{1,0:T(8,128)(2,1)S(1)}, bf16[72,1152]{1,0:T(8,128)(2,1)S(1)}, u32[]{:S(2)}, u32[]{:S(2)}) %collective-permute-start.16) | collective-permute-done | bytes 165920 | tf_op jit(solution)/shard_map/ppermute | solution.py:24
  97.8 3.5 %collective-permute-done.15.c = bf16[72,1152]{1,0:T(8,128)(2,1)S(1)} collective-permute-done((bf16[72,1152]{1,0:T(8,128)(2,1)S(1)}, bf16[72,1152]{1,0:T(8,128)(2,1)S(1)}, u32[]{:S(2)}, u32[]{:S(2)}) %collective-permute-start.15) | collective-permute-done | bytes 165920 | tf_op jit(solution)/shard_map/ppermute | solution.py:24
  101.3 0.8 shard_map.91
  (12 shorter events, 0.1 us)
Async XLA Ops:
  0.6 35.4 %collective-permute-start.2 = (bf16[320,1152]{1,0:T(8,128)(2,1)}, bf16[320,1152]{1,0:T(8,128)(2,1)S(1)}, u32[]{:S(2)}, u32[]{:S(2)}) collective-permute-start(bf16[320,1152]{1,0:T(8,128)(2,1)} %bitcast.6), channel_id=1, source_target_pairs={{0,64},{64,0},{1,65},{65,1},{2,66},{66,2},{3,67},{67,3},{4,68},{68... | collective-permute-start | bytes 2211848 | tf_op jit(solution)/shard_map/ppermute | solution.py:24
  3.4 8.2 %collective-permute-start.1 = (bf16[72,1152]{1,0:T(8,128)(2,1)S(1)}, bf16[72,1152]{1,0:T(8,128)(2,1)S(1)}, u32[]{:S(2)}, u32[]{:S(2)}) collective-permute-start(bf16[72,1152]{1,0:T(8,128)(2,1)S(1)} %shard_map.78), channel_id=1, source_target_pairs={{0,72},{8,64},{64,8},{72,0},{1,73},{9,65},{65,9},{73,1},{2,74},{10... | collective-permute-start | bytes 497672 | tf_op jit(solution)/shard_map/ppermute | solution.py:34
  5.6 35.0 %collective-permute-start.5 = (bf16[320,1152]{1,0:T(8,128)(2,1)}, bf16[320,1152]{1,0:T(8,128)(2,1)S(1)}, u32[]{:S(2)}, u32[]{:S(2)}) collective-permute-start(bf16[320,1152]{1,0:T(8,128)(2,1)} %bitcast.9), channel_id=1, source_target_pairs={{0,32},{16,48},{32,0},{48,16},{1,33},{17,49},{33,1},{49,17},{2,34}... | collective-permute-start | bytes 2211848 | tf_op jit(solution)/shard_map/ppermute | solution.py:24
  9.5 32.7 %collective-permute-start.4 = (bf16[320,1152]{1,0:T(8,128)(2,1)}, bf16[320,1152]{1,0:T(8,128)(2,1)S(1)}, u32[]{:S(2)}, u32[]{:S(2)}) collective-permute-start(bf16[320,1152]{1,0:T(8,128)(2,1)} %bitcast.10), channel_id=1, source_target_pairs={{0,48},{16,0},{32,16},{48,32},{1,49},{17,1},{33,17},{49,33},{2,50}... | collective-permute-start | bytes 2211848 | tf_op jit(solution)/shard_map/ppermute | solution.py:24
  10.2 32.0 %collective-permute-start.3 = (bf16[320,1152]{1,0:T(8,128)(2,1)}, bf16[320,1152]{1,0:T(8,128)(2,1)}, u32[]{:S(2)}, u32[]{:S(2)}) collective-permute-start(bf16[320,1152]{1,0:T(8,128)(2,1)} %bitcast.11), channel_id=1, source_target_pairs={{0,16},{16,32},{32,48},{48,0},{1,17},{17,33},{33,49},{49,1},{2,18}... | collective-permute-start | bytes 2211848 | tf_op jit(solution)/shard_map/ppermute | solution.py:24
  11.5 24.5 %copy-start = (bf16[1,320,1152]{2,1,0:T(8,128)(2,1)S(1)}, bf16[1,320,1152]{2,1,0:T(8,128)(2,1)}, u32[]{:S(2)}) copy-start(bf16[1,320,1152]{2,1,0:T(8,128)(2,1)} %param.8) | copy-start | bytes 2211844
  32.7 3.4 %collective-permute-start = (bf16[4,2,72,1152]{3,2,1,0:T(8,128)(2,1)}, bf16[4,2,72,1152]{3,2,1,0:T(8,128)(2,1)}, u32[]{:S(2)}, u32[]{:S(2)}) collective-permute-start(bf16[4,2,72,1152]{3,2,1,0:T(8,128)(2,1)} %all_to_all.4), channel_id=1, source_target_pairs={{0,1},{1,0},{2,3},{3,2},{4,5},{5,4},{6,7},{7,6},{8,9},{9,8},{10,11... | collective-permute-start | bytes 3981320 | tf_op jit(solution)/shard_map/cond/branch_1_fun/ppermute | solution.py:24
  36.1 6.1 %copy-start.1 = (bf16[1,320,1152]{2,1,0:T(8,128)(2,1)S(1)}, bf16[1,320,1152]{2,1,0:T(8,128)(2,1)}, u32[]{:S(2)}) copy-start(bf16[1,320,1152]{2,1,0:T(8,128)(2,1)} %param.7) | copy-start | bytes 2211844
  53.5 3.3 %collective-permute-start.6 = (bf16[4,2,72,1152]{3,2,1,0:T(8,128)(2,1)S(1)}, bf16[4,2,72,1152]{3,2,1,0:T(8,128)(2,1)S(1)}, u32[]{:S(2)}, u32[]{:S(2)}) collective-permute-start(bf16[4,2,72,1152]{3,2,1,0:T(8,128)(2,1)S(1)} %get-tuple-element.81), channel_id=1, source_target_pairs={{0,1},{1,0},{2,3},{3,2},{4,5},{5,4},{6,7},{7,6},{8,9},{9,8},{10,11... | collective-permute-start | bytes 3981320 | tf_op jit(solution)/shard_map/ppermute | solution.py:24
  56.9 12.7 %collective-permute-start.10 = (bf16[320,1152]{1,0:T(8,128)(2,1)S(1)}, bf16[320,1152]{1,0:T(8,128)(2,1)S(1)}, u32[]{:S(2)}, u32[]{:S(2)}) collective-permute-start(bf16[320,1152]{1,0:T(8,128)(2,1)S(1)} %shard_map.81), channel_id=1, source_target_pairs={{0,16},{1,49},{16,32},{17,1},{32,48},{33,17},{48,0},{49,33},{2,18}... | collective-permute-start | bytes 2211848 | tf_op jit(solution)/shard_map/ppermute | solution.py:29
  58.3 12.0 %collective-permute-start.9 = (bf16[2,72,1152]{2,1,0:T(8,128)(2,1)S(1)}, bf16[2,72,1152]{2,1,0:T(8,128)(2,1)S(1)}, u32[]{:S(2)}, u32[]{:S(2)}) collective-permute-start(bf16[2,72,1152]{2,1,0:T(8,128)(2,1)S(1)} %get-tuple-element.87), channel_id=1, source_target_pairs={{0,4},{2,6},{4,0},{6,2},{1,5},{3,7},{5,1},{7,3},{8,12},{10,14},{12... | collective-permute-start | bytes 995336 | tf_op jit(solution)/shard_map/ppermute | solution.py:24
  61.4 24.3 %collective-permute-start.13 = (bf16[320,1152]{1,0:T(8,128)(2,1)S(1)}, bf16[320,1152]{1,0:T(8,128)(2,1)S(1)}, u32[]{:S(2)}, u32[]{:S(2)}) collective-permute-start(bf16[320,1152]{1,0:T(8,128)(2,1)S(1)} %get-tuple-element.101), channel_id=1, source_target_pairs={{0,64},{64,0},{1,65},{65,1},{2,66},{66,2},{3,67},{67,3},{4,68},{68... | collective-permute-start | bytes 2211848 | tf_op jit(solution)/shard_map/ppermute | solution.py:24
  62.1 15.6 %collective-permute-start.7 = (bf16[2,72,1152]{2,1,0:T(8,128)(2,1)S(1)}, bf16[2,72,1152]{2,1,0:T(8,128)(2,1)S(1)}, u32[]{:S(2)}, u32[]{:S(2)}) collective-permute-start(bf16[2,72,1152]{2,1,0:T(8,128)(2,1)S(1)} %get-tuple-element.85), channel_id=1, source_target_pairs={{0,2},{2,4},{4,6},{6,0},{1,3},{3,5},{5,7},{7,1},{8,10},{10,12},{12... | collective-permute-start | bytes 995336 | tf_op jit(solution)/shard_map/ppermute | solution.py:24
  62.7 15.0 %collective-permute-start.8 = (bf16[2,72,1152]{2,1,0:T(8,128)(2,1)S(1)}, bf16[2,72,1152]{2,1,0:T(8,128)(2,1)S(1)}, u32[]{:S(2)}, u32[]{:S(2)}) collective-permute-start(bf16[2,72,1152]{2,1,0:T(8,128)(2,1)S(1)} %get-tuple-element.86), channel_id=1, source_target_pairs={{0,6},{2,0},{4,2},{6,4},{1,7},{3,1},{5,3},{7,5},{8,14},{10,8},{12,... | collective-permute-start | bytes 995336 | tf_op jit(solution)/shard_map/ppermute | solution.py:24
  70.3 23.4 %collective-permute-start.17 = (bf16[320,1152]{1,0:T(8,128)(2,1)S(1)}, bf16[320,1152]{1,0:T(8,128)(2,1)S(1)}, u32[]{:S(2)}, u32[]{:S(2)}) collective-permute-start(bf16[320,1152]{1,0:T(8,128)(2,1)S(1)} %get-tuple-element.105), channel_id=1, source_target_pairs={{0,48},{16,0},{32,16},{48,32},{1,49},{17,1},{33,17},{49,33},{2,50}... | collective-permute-start | bytes 2211848 | tf_op jit(solution)/shard_map/ppermute | solution.py:24
  72.7 21.0 %collective-permute-start.18 = (bf16[320,1152]{1,0:T(8,128)(2,1)S(1)}, bf16[320,1152]{1,0:T(8,128)(2,1)S(1)}, u32[]{:S(2)}, u32[]{:S(2)}) collective-permute-start(bf16[320,1152]{1,0:T(8,128)(2,1)S(1)} %get-tuple-element.106), channel_id=1, source_target_pairs={{0,16},{16,32},{32,48},{48,0},{1,17},{17,33},{33,49},{49,1},{2,18}... | collective-permute-start | bytes 2211848 | tf_op jit(solution)/shard_map/ppermute | solution.py:24
  77.8 7.7 %collective-permute-start.11 = (bf16[72,1152]{1,0:T(8,128)(2,1)S(1)}, bf16[72,1152]{1,0:T(8,128)(2,1)S(1)}, u32[]{:S(2)}, u32[]{:S(2)}) collective-permute-start(bf16[72,1152]{1,0:T(8,128)(2,1)S(1)} %get-tuple-element.99), channel_id=1, source_target_pairs={{0,72},{8,64},{64,8},{72,0},{1,73},{9,65},{65,9},{73,1},{2,74},{10... | collective-permute-start | bytes 497672 | tf_op jit(solution)/shard_map/ppermute | solution.py:34
  85.5 5.7 %collective-permute-start.12 = (bf16[72,1152]{1,0:T(8,128)(2,1)S(1)}, bf16[72,1152]{1,0:T(8,128)(2,1)S(1)}, u32[]{:S(2)}, u32[]{:S(2)}) collective-permute-start(bf16[72,1152]{1,0:T(8,128)(2,1)S(1)} %shard_map.87.a), channel_id=1, source_target_pairs={{0,64},{64,0},{1,65},{65,1},{2,66},{66,2},{3,67},{67,3},{4,68},{68... | collective-permute-start | bytes 497672 | tf_op jit(solution)/shard_map/ppermute | solution.py:24
  91.2 6.6 %collective-permute-start.16 = (bf16[72,1152]{1,0:T(8,128)(2,1)S(1)}, bf16[72,1152]{1,0:T(8,128)(2,1)S(1)}, u32[]{:S(2)}, u32[]{:S(2)}) collective-permute-start(bf16[72,1152]{1,0:T(8,128)(2,1)S(1)} %shard_map.88.a), channel_id=1, source_target_pairs={{0,48},{16,0},{32,16},{48,32},{1,49},{17,1},{33,17},{49,33},{2,50}... | collective-permute-start | bytes 497672 | tf_op jit(solution)/shard_map/ppermute | solution.py:24
  91.8 9.5 %collective-permute-start.15 = (bf16[72,1152]{1,0:T(8,128)(2,1)S(1)}, bf16[72,1152]{1,0:T(8,128)(2,1)S(1)}, u32[]{:S(2)}, u32[]{:S(2)}) collective-permute-start(bf16[72,1152]{1,0:T(8,128)(2,1)S(1)} %shard_map.88.a), channel_id=1, source_target_pairs={{0,16},{16,32},{32,48},{48,0},{1,17},{17,33},{33,49},{49,1},{2,18}... | collective-permute-start | bytes 497672 | tf_op jit(solution)/shard_map/ppermute | solution.py:24
  93.3 8.0 %collective-permute-start.14 = (bf16[72,1152]{1,0:T(8,128)(2,1)S(1)}, bf16[72,1152]{1,0:T(8,128)(2,1)S(1)}, u32[]{:S(2)}, u32[]{:S(2)}) collective-permute-start(bf16[72,1152]{1,0:T(8,128)(2,1)S(1)} %shard_map.88.a), channel_id=1, source_target_pairs={{0,32},{16,48},{32,0},{48,16},{1,33},{17,49},{33,1},{49,17},{2,34}... | collective-permute-start | bytes 497672 | tf_op jit(solution)/shard_map/ppermute | solution.py:24

commit v9 on v8

--- a/solution.py
+++ b/solution.py
@@ -123,7 +123,7 @@
     return 1.0 / (1.0 + jnp.exp(-logits))
 
 
-def main_kernel(scalars, n_txt, img, img_a, img_b, img_c, z, inv, txt, txt_far, grad, g_own, g_far, mine, other, raw, rows, feat, wide, sems):
+def main_kernel(scalars, n_txt, img, img_a, img_b, img_c, z, inv, txt, txt_far, grad, g_own, g_far, mine_c, other_c, mine, other, raw, rows, feat, wide, sems):
     moves = [(block, raw.at[pl.ds(k * 320, 320)]) for k, block in enumerate((img, img_a, img_b, img_c))]
     moves += [(txt, feat.at[pl.ds(0, 320)]), (txt_far, feat.at[pl.ds(320, 320)])]
     copies = [pltpu.make_async_copy(a, b, sems.at[k]) for k, (a, b) in enumerate(moves)]
@@ -155,12 +155,18 @@
     wide[...] = lax.dot_general(
         feat[...], dz, (((0,), (0,)), ((), ())), preferred_element_type=F32
     )
-    core = lax.axis_index("core")
-    for j in range(8):
-        a = pl.multiple_of((2 * j + core) * 72, 8)
-        b = pl.multiple_of((2 * j + 1 - core) * 72, 8)
-        mine[j % 4, j // 4] = wide[pl.ds(a, 72), :].astype(BF)
-        other[j % 4, j // 4] = wide[pl.ds(b, 72), :].astype(BF)
+    core, x = lax.axis_index("core"), lax.axis_index("x")
+    for step in range(4):
+        for h in range(2):
+            chunk = h * 4 + (x + step) % 4
+            own = pl.multiple_of((2 * chunk + core) * 72, 8)
+            far = pl.multiple_of((2 * chunk + 1 - core) * 72, 8)
+            if step == 2:
+                mine_c[h] = wide[pl.ds(own, 72), :].astype(BF)
+                other_c[h] = wide[pl.ds(far, 72), :].astype(BF)
+            else:
+                mine[min(step, 2), h] = wide[pl.ds(own, 72), :].astype(BF)
+                other[min(step, 2), h] = wide[pl.ds(far, 72), :].astype(BF)
 
 
 def part_kernel(first, scalars, grad, n_txt, *outs):
@@ -182,9 +188,7 @@
 
 
 def core_sum_kernel(mine, got, *outs):
-    x = lax.axis_index("x")
-    for r, out in enumerate(outs):
-        k = (x + r) % 4
+    for k, out in enumerate(outs):
         out[...] = (mine[k].astype(F32) + got[k].astype(F32)).astype(BF)
 
 
@@ -267,12 +271,14 @@
     return part_own, *call(pass_on_kernel, [BLOCK] * 2, [VM] * 3)(part_a, part_b, got_c)
 
 
-def sum_plane(scalars, mine, got_core, part_c, grad, n_txt, z, g_own, g_far, near, far):
-    rel = call(core_sum_kernel, [stack_of(2)] * 4, [VM] * 2)(mine, got_core)
-    got_x = [shift(rel[s], "x", s) for s in (1, 3, 2)]
+def sum_plane(scalars, mine_c, got_c, mine, got, part_c, grad, n_txt, z, g_own, g_far, near, far_core):
+    (far,) = call(pair_sum_kernel, [stack_of(2)], [VM] * 2)(mine_c, got_c)
+    got_x = [shift(far, "x", 2)]
+    own, up, down = call(core_sum_kernel, [stack_of(2)] * 3, [VM] * 2)(mine, got)
+    got_x = [shift(up, "x", 1), shift(down, "x", 3)] + got_x
     g_got = shift(g_far, "ylo", 1)
     part_own, part_a, part_b = beside_x(part_c, scalars, grad, n_txt)
-    got_x[2], part_a, part_b, near, far = hold((got_x[2], part_a, part_b, near, far))
+    got_x[2], part_a, part_b, near, far_core = hold((got_x[2], part_a, part_b, near, far_core))
     (head,) = call(
         head_kernel,
         [shaped((1152, 1152), BF)],
@@ -283,9 +289,9 @@
             pltpu.SemaphoreType.DMA((8,)),
         ],
         flops=1 << 31,
-    )(near, far)
+    )(near, far_core)
     got_x[:2], head = hold((got_x[:2], head))
-    keep, send = call(x_sum_kernel, [stack_of()] * 2, [VM] * 4)(rel[0], *got_x)
+    keep, send = call(x_sum_kernel, [stack_of()] * 2, [VM] * 4)(own, *got_x)
     got_a, got_b = shift(part_a, "z", -1), shift(part_b, "z", 1)
     (d_feat,) = call(
         text_out_kernel,
@@ -326,9 +332,9 @@
         flops=1 << 34,
     )(near, far, txt, txt_far)
     n_txt, img_a, img_b, img_c = hold((n_txt, img_a, img_b, img_c))
-    grad, g_own, g_far, mine, other = call(
+    grad, g_own, g_far, mine_c, other_c, mine, other = call(
         main_kernel,
-        [shaped((640, 1280), BF), BLOCK, BLOCK, stack_of(4, 2), stack_of(4, 2)],
+        [shaped((640, 1280), BF), BLOCK, BLOCK, stack_of(2), stack_of(2), stack_of(3, 2), stack_of(3, 2)],
         [VM] * 2 + [ANY] * 4 + [VM, VM, ANY, ANY],
         [
             pltpu.VMEM((1280, 1152), BF),
@@ -340,11 +346,12 @@
         vmem=MAIN_MIB,
     )(scalars, n_txt, img, img_a, img_b, img_c, z, inv, txt, txt_far)
 
-    got_core, (part_c,) = hold(
-        (shift(other, "core", 1), parts_of(3, [BLOCK], scalars, grad, n_txt))
+    got = shift(other, "core", 1)
+    got_c, (part_c,) = hold(
+        (shift(other_c, "core", 1), parts_of(3, [BLOCK], scalars, grad, n_txt))
     )
     quad, d_feat, part_own, got_a, got_b = sum_plane(
-        scalars, mine, got_core, part_c, grad, n_txt, z, g_own, g_far, near, far
+        scalars, mine_c, got_c, mine, got, part_c, grad, n_txt, z, g_own, g_far, near, far
     )
     (d_img,) = call(image_out_kernel, [BLOCK], [VM] * 4, flops=1 << 30)(img, part_own, got_a, got_b)
     got_z = [shift(quad, "z", k) for k in (2, 1, -1)]

time: 102 us -> 101 us (level)
    pallas_call x3 -> x4, Pallas kernels: 11.8 us -> 11.2 us  [the longest x1 10.7 us: on_device(): call(main_kernel, [shaped((640, 1280), BF), BLOCK, BLOCK, stack_of(2), st...]
    ppermute x16 -> x17, waiting for transfers between devices: 17.5 us -> 17 us  [shift(): return lax.ppermute(value, axis, [(i, (i + step) % n) for i in range(n)])]
    ppermute x16 -> x17, starting transfers between devices: 19.9 us -> 20.1 us  [shift(): return lax.ppermute(value, axis, [(i, (i + step) % n) for i in range(n)])]
  transfers between devices with their start and end apart: 19 -> 20, of which waited for: 10 -> 10; matrix products, arithmetic and copies ran while one was open for 0% -> 0% of each run, Pallas kernels for 17% -> 17%
where the time goes in v9:
time: 101 us
  Pallas kernels  29.2 us (29%)
  waiting for transfers between devices  25.6 us (25%)
  starting transfers between devices  24.6 us (24%)
  blocking collectives  21 us (21%)
    all_to_all x1, blocking collectives, along_x(): return lax.all_to_all(value, 'x', split_axis=0, concat_axis=0, tiled=True)  21 us
    ppermute x17, starting transfers between devices, shift(): return lax.ppermute(value, axis, [(i, (i + step) % n) for i in range(n)])  20.1 us
    ppermute x17, waiting for transfers between devices, shift(): return lax.ppermute(value, axis, [(i, (i + step) % n) for i in range(n)])  17 us
    pallas_call x1, Pallas kernels, on_device(): call(main_kernel, [shaped((640, 1280), BF), BLOCK, BLOCK, stack_of(2), st...  10.7 us
    ppermute x2, waiting for transfers between devices, swap_far(): return lax.ppermute(value, ('ylo', 'yhi'), pairs)  6.55 us
    pallas_call x1, Pallas kernels, on_device(): call(text_kernel, [shaped((640, 1152), F32), shaped((640, 1152), BF), sha...  4.53 us
    ppermute x2, starting transfers between devices, swap_far(): return lax.ppermute(value, ('ylo', 'yhi'), pairs)  3.4 us
    pallas_call x2, Pallas kernels, parts_of(): return call(kernel, shapes, [VM] * 3, flops=1 << 31)(*args)  3.12 us
  transfers between devices with their start and end apart: 20, of which 10 were waited for; matrix products, arithmetic and copies ran while one was open for 0% of the time, Pallas kernels for 17%

profile of v9, /device:TPU:0, one launch (start us, length us, event | category | flops | bytes accessed | tf_op | source)
XLA Modules:
  0.0 101.1 jit_solution(8268037398020153597)
XLA Ops:
  0.6 1.7 %collective-permute-start.2 = (bf16[320,1152]{1,0:T(8,128)(2,1)}, bf16[320,1152]{1,0:T(8,128)(2,1)S(1)}, u32[]{:S(2)}, u32[]{:S(2)}) collective-permute-start(bf16[320,1152]{1,0:T(8,128)(2,1)} %bitcast.6), channel_id=1, source_target_pairs={{0,64},{64,0},{1,65},{65,1},{2,66},{66,2},{3,67},{67,3},{4,68},{68... | collective-permute-start | bytes 2211848 | tf_op jit(solution)/shard_map/ppermute | solution.py:24
  2.4 1.0 shard_map.78
  3.4 2.3 %collective-permute-start.1 = (bf16[72,1152]{1,0:T(8,128)(2,1)S(1)}, bf16[72,1152]{1,0:T(8,128)(2,1)S(1)}, u32[]{:S(2)}, u32[]{:S(2)}) collective-permute-start(bf16[72,1152]{1,0:T(8,128)(2,1)S(1)} %shard_map.78), channel_id=1, source_target_pairs={{0,72},{8,64},{64,8},{72,0},{1,73},{9,65},{65,9},{73,1},{2,74},{10... | collective-permute-start | bytes 497672 | tf_op jit(solution)/shard_map/ppermute | solution.py:34
  5.6 3.9 %collective-permute-start.5 = (bf16[320,1152]{1,0:T(8,128)(2,1)}, bf16[320,1152]{1,0:T(8,128)(2,1)S(1)}, u32[]{:S(2)}, u32[]{:S(2)}) collective-permute-start(bf16[320,1152]{1,0:T(8,128)(2,1)} %bitcast.9), channel_id=1, source_target_pairs={{0,32},{16,48},{32,0},{48,16},{1,33},{17,49},{33,1},{49,17},{2,34}... | collective-permute-start | bytes 2211848 | tf_op jit(solution)/shard_map/ppermute | solution.py:24
  9.5 0.7 collective-permute-start.4
  10.2 1.3 %collective-permute-start.3 = (bf16[320,1152]{1,0:T(8,128)(2,1)}, bf16[320,1152]{1,0:T(8,128)(2,1)}, u32[]{:S(2)}, u32[]{:S(2)}) collective-permute-start(bf16[320,1152]{1,0:T(8,128)(2,1)} %bitcast.11), channel_id=1, source_target_pairs={{0,16},{16,32},{32,48},{48,0},{1,17},{17,33},{33,49},{49,1},{2,18}... | collective-permute-start | bytes 2211848 | tf_op jit(solution)/shard_map/ppermute | solution.py:24
  11.5 0.0 collective-permute-done.1
  11.5 24.5 %conditional.1 = (bf16[4,2,72,1152]{3,2,1,0:T(8,128)(2,1)}, bf16[4,2,72,1152]{3,2,1,0:T(8,128)(2,1)}, f32[8,128]{1,0:T(8,128)S(1)}) conditional(s32[]{:T(128)} %convert_element_type.3, () %tuple.25, (bf16[72,1152]{1,0:T(8,128)(2,1)S(1)}, bf16[72,1152]{1,0:T(8,128)(2,1)S(1)}, f32[1]{0:T(128)}, f32[1]{0:T(128)}) %tuple.27), branch_computations={%region_0.0_spmd, %region_1.0_spmd} | conditional | flops 2147484672 | bytes 7964736 | solution.py:233
  11.5 0.1 branch_1_fun.2
  11.7 21.0 %all_to_all.4 = bf16[4,2,72,1152]{3,2,1,0:T(8,128)(2,1)} all-to-all(bf16[4,2,72,1152]{3,2,1,0:T(8,128)(2,1)S(1)} %branch_1_fun.2), channel_id=1, replica_groups=mesh['ylo'=2,'z'=4,'yhi'=2,'x'=4,'core'=2] {'x'}, dimensions={0} | all-to-all | bytes 2654208 | tf_op jit(solution)/shard_map/cond/branch_1_fun/all_to_all | solution.py:250
  32.7 1.4 %branch_1_fun.3 = f32[8,128]{1,0:T(8,128)S(1)} custom-call(f32[1,1]{1,0:T(1,128)} %bitcast.t_log, f32[1,1]{1,0:T(1,128)} %bitcast.1.bias), custom_call_target="tpu_custom_call" | custom-call | flops 2147483648 | bytes 1024 | tf_op jit(solution)/shard_map/cond/branch_1_fun/pallas_call | solution.py:257
  34.0 2.0 %collective-permute-done = bf16[4,2,72,1152]{3,2,1,0:T(8,128)(2,1)} collective-permute-done((bf16[4,2,72,1152]{3,2,1,0:T(8,128)(2,1)}, bf16[4,2,72,1152]{3,2,1,0:T(8,128)(2,1)}, u32[]{:S(2)}, u32[]{:S(2)}) %collective-permute-start) | collective-permute-done | bytes 1327136 | tf_op jit(solution)/shard_map/cond/branch_1_fun/ppermute | solution.py:24
  36.1 0.0 collective-permute-done.2.txt_far
  36.1 4.5 %shard_map.79 = (f32[640,1152]{1,0:T(8,128)S(1)}, bf16[640,1152]{1,0:T(8,128)(2,1)S(1)}, f32[640,1]{1,0:T(8,128)S(1)}) custom-call(bf16[4,2,72,1152]{3,2,1,0:T(8,128)(2,1)} %get-tuple-element.95.near, bf16[4,2,72,1152]{3,2,1,0:T(8,128)(2,1)} %get-tuple-element.96.far, bf16[320,1152]{1,0:T(8,128)(2,1)S(1)} %bitcast.7, ...), custom_call_target="tpu_custom_call" | custom-call | flops 17179869184 | bytes 1024 | tf_op jit(solution)/shard_map/pallas_call | solution.py:320
  40.6 1.6 %collective-permute-done.4.img_b = bf16[320,1152]{1,0:T(8,128)(2,1)S(1)} collective-permute-done((bf16[320,1152]{1,0:T(8,128)(2,1)}, bf16[320,1152]{1,0:T(8,128)(2,1)S(1)}, u32[]{:S(2)}, u32[]{:S(2)}) %collective-permute-start.4) | collective-permute-done | bytes 737312 | tf_op jit(solution)/shard_map/ppermute | solution.py:24
  42.2 0.0 collective-permute-done.3.img_a
  42.2 10.7 %shard_map.80 = (bf16[640,1280]{1,0:T(8,128)(2,1)S(1)}, bf16[320,1152]{1,0:T(8,128)(2,1)S(1)}, bf16[320,1152]{1,0:T(8,128)(2,1)S(1)}, bf16[2,72,1152]{2,1,0:T(8,...) custom-call(f32[8,128]{1,0:T(8,128)S(1)} %get-tuple-element.67.scala, ...), custom_call_target="tpu_custom_call" | custom-call | flops 1024 | bytes 1024 | tf_op jit(solution)/shard_map/pallas_call | solution.py:335
  53.0 0.1 collective-permute-start.6
  53.1 0.5 collective-permute-start.9
  53.6 1.0 %shard_map.82 = bf16[320,1152]{1,0:T(8,128)(2,1)S(1)} custom-call(f32[8,128]{1,0:T(8,128)S(1)} %get-tuple-element.67.scalars, bf16[640,1280]{1,0:T(8,128)(2,1)S(1)} %get-tuple-element.88.grad, bf16[640,1152]{1,0:T(8,128)(2,1)S(1)} %get-tuple-element.75.n_txt), custom_call_target="tpu_custom_call" | custom-call | flops 2147483648 | bytes 1024 | tf_op jit(solution)/shard_map/pallas_call | solution.py:265
  54.6 1.5 %collective-permute-done.9.b = bf16[2,72,1152]{2,1,0:T(8,128)(2,1)S(1)} collective-permute-done((bf16[2,72,1152]{2,1,0:T(8,128)(2,1)S(1)}, bf16[2,72,1152]{2,1,0:T(8,128)(2,1)S(1)}, u32[]{:S(2)}, u32[]{:S(2)}) %collective-permute-start.9) | collective-permute-done | bytes 331808 | tf_op jit(solution)/shard_map/ppermute | solution.py:24
  56.1 1.1 %collective-permute-start.11 = (bf16[320,1152]{1,0:T(8,128)(2,1)S(1)}, bf16[320,1152]{1,0:T(8,128)(2,1)S(1)}, u32[]{:S(2)}, u32[]{:S(2)}) collective-permute-start(bf16[320,1152]{1,0:T(8,128)(2,1)S(1)} %shard_map.82), channel_id=1, source_target_pairs={{0,16},{1,49},{16,32},{17,1},{32,48},{33,17},{48,0},{49,33},{2,18}... | collective-permute-start | bytes 2211848 | tf_op jit(solution)/shard_map/ppermute | solution.py:29
  57.2 0.1 shard_map.83
  57.3 3.1 %collective-permute-start.10 = (bf16[2,72,1152]{2,1,0:T(8,128)(2,1)S(1)}, bf16[2,72,1152]{2,1,0:T(8,128)(2,1)S(1)}, u32[]{:S(2)}, u32[]{:S(2)}) collective-permute-start(bf16[2,72,1152]{2,1,0:T(8,128)(2,1)S(1)} %shard_map.83), channel_id=1, source_target_pairs={{0,4},{2,6},{4,0},{6,2},{1,5},{3,7},{5,1},{7,3},{8,12},{10,14},{12... | collective-permute-start | bytes 995336 | tf_op jit(solution)/shard_map/ppermute | solution.py:24
  60.4 0.7 collective-permute-start.14
  61.1 0.2 shard_map.81
  61.3 0.7 collective-permute-start.7
  62.0 2.6 %collective-permute-start.8 = (bf16[2,72,1152]{2,1,0:T(8,128)(2,1)S(1)}, bf16[2,72,1152]{2,1,0:T(8,128)(2,1)S(1)}, u32[]{:S(2)}, u32[]{:S(2)}) collective-permute-start(bf16[2,72,1152]{2,1,0:T(8,128)(2,1)S(1)} %get-tuple-element.85), channel_id=1, source_target_pairs={{0,6},{2,0},{4,2},{6,4},{1,7},{3,1},{5,3},{7,5},{8,14},{10,8},{12,... | collective-permute-start | bytes 995336 | tf_op jit(solution)/shard_map/ppermute | solution.py:24
  64.6 2.1 %shard_map.84 = (bf16[320,1152]{1,0:T(8,128)(2,1)S(1)}, bf16[320,1152]{1,0:T(8,128)(2,1)S(1)}, bf16[320,1152]{1,0:T(8,128)(2,1)S(1)}) custom-call(f32[8,128]{1,0:T(8,128)S(1)} %get-tuple-element.67.scalars, bf16[640,1280]{1,0:T(8,128)(2,1)S(1)} %get-tuple-element.88.grad, bf16[640,1152]{1,0:T(8,128)(2,1)S(1)} %get-tuple-element.75.n_txt), custom_call_target="tpu_custom_call" | custom-call | flops 2147483648 | bytes 1024 | tf_op jit(solution)/shard_map/pallas_call | solution.py:265
  66.7 2.1 %collective-permute-done.11.got = bf16[320,1152]{1,0:T(8,128)(2,1)S(1)} collective-permute-done((bf16[320,1152]{1,0:T(8,128)(2,1)S(1)}, bf16[320,1152]{1,0:T(8,128)(2,1)S(1)}, u32[]{:S(2)}, u32[]{:S(2)}) %collective-permute-start.11) | collective-permute-done | bytes 737312 | tf_op jit(solution)/shard_map/ppermute | solution.py:29
  68.8 0.4 shard_map.85
  69.2 0.1 collective-permute-done.10.r
  69.4 2.4 %collective-permute-start.18 = (bf16[320,1152]{1,0:T(8,128)(2,1)S(1)}, bf16[320,1152]{1,0:T(8,128)(2,1)S(1)}, u32[]{:S(2)}, u32[]{:S(2)}) collective-permute-start(bf16[320,1152]{1,0:T(8,128)(2,1)S(1)} %get-tuple-element.107), channel_id=1, source_target_pairs={{0,48},{16,0},{32,16},{48,32},{1,49},{17,1},{33,17},{49,33},{2,50}... | collective-permute-start | bytes 2211848 | tf_op jit(solution)/shard_map/ppermute | solution.py:24
  71.8 1.9 %shard_map.86.head = bf16[1152,1152]{1,0:T(8,128)(2,1)S(1)} custom-call(bf16[4,2,72,1152]{3,2,1,0:T(8,128)(2,1)} %get-tuple-element.95.near, bf16[4,2,72,1152]{3,2,1,0:T(8,128)(2,1)} %get-tuple-element.96.far), custom_call_target="tpu_custom_call" | custom-call | flops 2147483648 | bytes 1024 | tf_op jit(solution)/shard_map/pallas_call | solution.py:282
  73.7 3.0 %collective-permute-done.7.p = bf16[2,72,1152]{2,1,0:T(8,128)(2,1)S(1)} collective-permute-done((bf16[2,72,1152]{2,1,0:T(8,128)(2,1)S(1)}, bf16[2,72,1152]{2,1,0:T(8,128)(2,1)S(1)}, u32[]{:S(2)}, u32[]{:S(2)}) %collective-permute-start.7) | collective-permute-done | bytes 331808 | tf_op jit(solution)/shard_map/ppermute | solution.py:24
  76.7 0.2 shard_map.87
  76.9 1.1 %collective-permute-start.12 = (bf16[72,1152]{1,0:T(8,128)(2,1)S(1)}, bf16[72,1152]{1,0:T(8,128)(2,1)S(1)}, u32[]{:S(2)}, u32[]{:S(2)}) collective-permute-start(bf16[72,1152]{1,0:T(8,128)(2,1)S(1)} %get-tuple-element.101), channel_id=1, source_target_pairs={{0,72},{8,64},{64,8},{72,0},{1,73},{9,65},{65,9},{73,1},{2,74},{10... | collective-permute-start | bytes 497672 | tf_op jit(solution)/shard_map/ppermute | solution.py:34
  78.0 6.5 %collective-permute-done.12.b = bf16[72,1152]{1,0:T(8,128)(2,1)S(1)} collective-permute-done((bf16[72,1152]{1,0:T(8,128)(2,1)S(1)}, bf16[72,1152]{1,0:T(8,128)(2,1)S(1)}, u32[]{:S(2)}, u32[]{:S(2)}) %collective-permute-start.12) | collective-permute-done | bytes 165920 | tf_op jit(solution)/shard_map/ppermute | solution.py:34
  84.6 0.1 collective-permute-start.13
  84.7 3.0 %shard_map.90 = bf16[320,1152]{1,0:T(8,128)(2,1)} custom-call(f32[640,1152]{1,0:T(8,128)S(1)} %get-tuple-element.79.z, bf16[320,1152]{1,0:T(8,128)(2,1)S(1)} %get-tuple-element.102.a, bf16[320,1152]{1,0:T(8,128)(2,1)S(1)} %collective-permute-done.14.b, bf16[1152,1152]{1,0:T(8,128)(2,1)S(1)} %shard_map.86.head), custom_call_target="tpu_custom_call" | custom-call | flops 2147483648 | bytes 1024 | tf_op jit(solution)/shard_map/pallas_call | solution.py:296
  87.7 2.6 %collective-permute-done.13.b = bf16[72,1152]{1,0:T(8,128)(2,1)S(1)} collective-permute-done((bf16[72,1152]{1,0:T(8,128)(2,1)S(1)}, bf16[72,1152]{1,0:T(8,128)(2,1)S(1)}, u32[]{:S(2)}, u32[]{:S(2)}) %collective-permute-start.13) | collective-permute-done | bytes 165920 | tf_op jit(solution)/shard_map/ppermute | solution.py:24
  90.3 0.5 collective-permute-start.17
  90.8 1.6 %collective-permute-start.16 = (bf16[72,1152]{1,0:T(8,128)(2,1)S(1)}, bf16[72,1152]{1,0:T(8,128)(2,1)S(1)}, u32[]{:S(2)}, u32[]{:S(2)}) collective-permute-start(bf16[72,1152]{1,0:T(8,128)(2,1)S(1)} %shard_map.89.a), channel_id=1, source_target_pairs={{0,16},{16,32},{32,48},{48,0},{1,17},{17,33},{33,49},{49,1},{2,18}... | collective-permute-start | bytes 497672 | tf_op jit(solution)/shard_map/ppermute | solution.py:24
  92.4 0.2 collective-permute-start.15
  92.5 1.6 %shard_map.91 = bf16[320,1152]{1,0:T(8,128)(2,1)} custom-call(bf16[320,1152]{1,0:T(8,128)(2,1)S(1)} %bitcast.13, bf16[320,1152]{1,0:T(8,128)(2,1)S(1)} %get-tuple-element.106.a, bf16[320,1152]{1,0:T(8,128)(2,1)S(1)} %collective-permute-done.18.b, bf16[320,1152]{1,0:T(8,128)(2,1)S(1)} %collective-permute-done.19.c), custom_call_target="tpu_custom_call" | custom-call | flops 1073741824 | bytes 1024 | tf_op jit(solution)/shard_map/pallas_call | solution.py:356
  94.2 2.7 %collective-permute-done.17.d = bf16[72,1152]{1,0:T(8,128)(2,1)S(1)} collective-permute-done((bf16[72,1152]{1,0:T(8,128)(2,1)S(1)}, bf16[72,1152]{1,0:T(8,128)(2,1)S(1)}, u32[]{:S(2)}, u32[]{:S(2)}) %collective-permute-start.17) | collective-permute-done | bytes 165920 | tf_op jit(solution)/shard_map/ppermute | solution.py:24
  96.9 3.5 %collective-permute-done.16.c = bf16[72,1152]{1,0:T(8,128)(2,1)S(1)} collective-permute-done((bf16[72,1152]{1,0:T(8,128)(2,1)S(1)}, bf16[72,1152]{1,0:T(8,128)(2,1)S(1)}, u32[]{:S(2)}, u32[]{:S(2)}) %collective-permute-start.16) | collective-permute-done | bytes 165920 | tf_op jit(solution)/shard_map/ppermute | solution.py:24
  100.3 0.8 shard_map.92
  (15 shorter events, 0.1 us)
Async XLA Ops:
  0.6 35.4 %collective-permute-start.2 = (bf16[320,1152]{1,0:T(8,128)(2,1)}, bf16[320,1152]{1,0:T(8,128)(2,1)S(1)}, u32[]{:S(2)}, u32[]{:S(2)}) collective-permute-start(bf16[320,1152]{1,0:T(8,128)(2,1)} %bitcast.6), channel_id=1, source_target_pairs={{0,64},{64,0},{1,65},{65,1},{2,66},{66,2},{3,67},{67,3},{4,68},{68... | collective-permute-start | bytes 2211848 | tf_op jit(solution)/shard_map/ppermute | solution.py:24
  3.4 8.2 %collective-permute-start.1 = (bf16[72,1152]{1,0:T(8,128)(2,1)S(1)}, bf16[72,1152]{1,0:T(8,128)(2,1)S(1)}, u32[]{:S(2)}, u32[]{:S(2)}) collective-permute-start(bf16[72,1152]{1,0:T(8,128)(2,1)S(1)} %shard_map.78), channel_id=1, source_target_pairs={{0,72},{8,64},{64,8},{72,0},{1,73},{9,65},{65,9},{73,1},{2,74},{10... | collective-permute-start | bytes 497672 | tf_op jit(solution)/shard_map/ppermute | solution.py:34
  5.6 35.0 %collective-permute-start.5 = (bf16[320,1152]{1,0:T(8,128)(2,1)}, bf16[320,1152]{1,0:T(8,128)(2,1)S(1)}, u32[]{:S(2)}, u32[]{:S(2)}) collective-permute-start(bf16[320,1152]{1,0:T(8,128)(2,1)} %bitcast.9), channel_id=1, source_target_pairs={{0,32},{16,48},{32,0},{48,16},{1,33},{17,49},{33,1},{49,17},{2,34}... | collective-permute-start | bytes 2211848 | tf_op jit(solution)/shard_map/ppermute | solution.py:24
  9.5 32.7 %collective-permute-start.4 = (bf16[320,1152]{1,0:T(8,128)(2,1)}, bf16[320,1152]{1,0:T(8,128)(2,1)S(1)}, u32[]{:S(2)}, u32[]{:S(2)}) collective-permute-start(bf16[320,1152]{1,0:T(8,128)(2,1)} %bitcast.10), channel_id=1, source_target_pairs={{0,48},{16,0},{32,16},{48,32},{1,49},{17,1},{33,17},{49,33},{2,50}... | collective-permute-start | bytes 2211848 | tf_op jit(solution)/shard_map/ppermute | solution.py:24
  10.2 32.0 %collective-permute-start.3 = (bf16[320,1152]{1,0:T(8,128)(2,1)}, bf16[320,1152]{1,0:T(8,128)(2,1)}, u32[]{:S(2)}, u32[]{:S(2)}) collective-permute-start(bf16[320,1152]{1,0:T(8,128)(2,1)} %bitcast.11), channel_id=1, source_target_pairs={{0,16},{16,32},{32,48},{48,0},{1,17},{17,33},{33,49},{49,1},{2,18}... | collective-permute-start | bytes 2211848 | tf_op jit(solution)/shard_map/ppermute | solution.py:24
  11.5 24.5 %copy-start = (bf16[1,320,1152]{2,1,0:T(8,128)(2,1)S(1)}, bf16[1,320,1152]{2,1,0:T(8,128)(2,1)}, u32[]{:S(2)}) copy-start(bf16[1,320,1152]{2,1,0:T(8,128)(2,1)} %param.8) | copy-start | bytes 2211844
  32.7 3.4 %collective-permute-start = (bf16[4,2,72,1152]{3,2,1,0:T(8,128)(2,1)}, bf16[4,2,72,1152]{3,2,1,0:T(8,128)(2,1)}, u32[]{:S(2)}, u32[]{:S(2)}) collective-permute-start(bf16[4,2,72,1152]{3,2,1,0:T(8,128)(2,1)} %all_to_all.4), channel_id=1, source_target_pairs={{0,1},{1,0},{2,3},{3,2},{4,5},{5,4},{6,7},{7,6},{8,9},{9,8},{10,11... | collective-permute-start | bytes 3981320 | tf_op jit(solution)/shard_map/cond/branch_1_fun/ppermute | solution.py:24
  36.1 6.1 %copy-start.1 = (bf16[1,320,1152]{2,1,0:T(8,128)(2,1)S(1)}, bf16[1,320,1152]{2,1,0:T(8,128)(2,1)}, u32[]{:S(2)}) copy-start(bf16[1,320,1152]{2,1,0:T(8,128)(2,1)} %param.7) | copy-start | bytes 2211844
  53.0 8.1 %collective-permute-start.6 = (bf16[3,2,72,1152]{3,2,1,0:T(8,128)(2,1)S(1)}, bf16[3,2,72,1152]{3,2,1,0:T(8,128)(2,1)S(1)}, u32[]{:S(2)}, u32[]{:S(2)}) collective-permute-start(bf16[3,2,72,1152]{3,2,1,0:T(8,128)(2,1)S(1)} %get-tuple-element.82), channel_id=1, source_target_pairs={{0,1},{1,0},{2,3},{3,2},{4,5},{5,4},{6,7},{7,6},{8,9},{9,8},{10,11... | collective-permute-start | bytes 2985992 | tf_op jit(solution)/shard_map/ppermute | solution.py:24
  53.1 3.0 %collective-permute-start.9 = (bf16[2,72,1152]{2,1,0:T(8,128)(2,1)S(1)}, bf16[2,72,1152]{2,1,0:T(8,128)(2,1)S(1)}, u32[]{:S(2)}, u32[]{:S(2)}) collective-permute-start(bf16[2,72,1152]{2,1,0:T(8,128)(2,1)S(1)} %get-tuple-element.87), channel_id=1, source_target_pairs={{0,1},{1,0},{2,3},{3,2},{4,5},{5,4},{6,7},{7,6},{8,9},{9,8},{10,11... | collective-permute-start | bytes 995336 | tf_op jit(solution)/shard_map/ppermute | solution.py:24
  56.1 12.7 %collective-permute-start.11 = (bf16[320,1152]{1,0:T(8,128)(2,1)S(1)}, bf16[320,1152]{1,0:T(8,128)(2,1)S(1)}, u32[]{:S(2)}, u32[]{:S(2)}) collective-permute-start(bf16[320,1152]{1,0:T(8,128)(2,1)S(1)} %shard_map.82), channel_id=1, source_target_pairs={{0,16},{1,49},{16,32},{17,1},{32,48},{33,17},{48,0},{49,33},{2,18}... | collective-permute-start | bytes 2211848 | tf_op jit(solution)/shard_map/ppermute | solution.py:29
  57.3 12.1 %collective-permute-start.10 = (bf16[2,72,1152]{2,1,0:T(8,128)(2,1)S(1)}, bf16[2,72,1152]{2,1,0:T(8,128)(2,1)S(1)}, u32[]{:S(2)}, u32[]{:S(2)}) collective-permute-start(bf16[2,72,1152]{2,1,0:T(8,128)(2,1)S(1)} %shard_map.83), channel_id=1, source_target_pairs={{0,4},{2,6},{4,0},{6,2},{1,5},{3,7},{5,1},{7,3},{8,12},{10,14},{12... | collective-permute-start | bytes 995336 | tf_op jit(solution)/shard_map/ppermute | solution.py:24
  60.4 24.3 %collective-permute-start.14 = (bf16[320,1152]{1,0:T(8,128)(2,1)S(1)}, bf16[320,1152]{1,0:T(8,128)(2,1)S(1)}, u32[]{:S(2)}, u32[]{:S(2)}) collective-permute-start(bf16[320,1152]{1,0:T(8,128)(2,1)S(1)} %get-tuple-element.103), channel_id=1, source_target_pairs={{0,64},{64,0},{1,65},{65,1},{2,66},{66,2},{3,67},{67,3},{4,68},{68... | collective-permute-start | bytes 2211848 | tf_op jit(solution)/shard_map/ppermute | solution.py:24
  61.3 15.3 %collective-permute-start.7 = (bf16[2,72,1152]{2,1,0:T(8,128)(2,1)S(1)}, bf16[2,72,1152]{2,1,0:T(8,128)(2,1)S(1)}, u32[]{:S(2)}, u32[]{:S(2)}) collective-permute-start(bf16[2,72,1152]{2,1,0:T(8,128)(2,1)S(1)} %get-tuple-element.84), channel_id=1, source_target_pairs={{0,2},{2,4},{4,6},{6,0},{1,3},{3,5},{5,7},{7,1},{8,10},{10,12},{12... | collective-permute-start | bytes 995336 | tf_op jit(solution)/shard_map/ppermute | solution.py:24
  62.0 14.7 %collective-permute-start.8 = (bf16[2,72,1152]{2,1,0:T(8,128)(2,1)S(1)}, bf16[2,72,1152]{2,1,0:T(8,128)(2,1)S(1)}, u32[]{:S(2)}, u32[]{:S(2)}) collective-permute-start(bf16[2,72,1152]{2,1,0:T(8,128)(2,1)S(1)} %get-tuple-element.85), channel_id=1, source_target_pairs={{0,6},{2,0},{4,2},{6,4},{1,7},{3,1},{5,3},{7,5},{8,14},{10,8},{12,... | collective-permute-start | bytes 995336 | tf_op jit(solution)/shard_map/ppermute | solution.py:24
  69.4 23.2 %collective-permute-start.18 = (bf16[320,1152]{1,0:T(8,128)(2,1)S(1)}, bf16[320,1152]{1,0:T(8,128)(2,1)S(1)}, u32[]{:S(2)}, u32[]{:S(2)}) collective-permute-start(bf16[320,1152]{1,0:T(8,128)(2,1)S(1)} %get-tuple-element.107), channel_id=1, source_target_pairs={{0,48},{16,0},{32,16},{48,32},{1,49},{17,1},{33,17},{49,33},{2,50}... | collective-permute-start | bytes 2211848 | tf_op jit(solution)/shard_map/ppermute | solution.py:24
  71.8 20.8 %collective-permute-start.19 = (bf16[320,1152]{1,0:T(8,128)(2,1)S(1)}, bf16[320,1152]{1,0:T(8,128)(2,1)S(1)}, u32[]{:S(2)}, u32[]{:S(2)}) collective-permute-start(bf16[320,1152]{1,0:T(8,128)(2,1)S(1)} %get-tuple-element.108), channel_id=1, source_target_pairs={{0,16},{16,32},{32,48},{48,0},{1,17},{17,33},{33,49},{49,1},{2,18}... | collective-permute-start | bytes 2211848 | tf_op jit(solution)/shard_map/ppermute | solution.py:24
  76.9 7.7 %collective-permute-start.12 = (bf16[72,1152]{1,0:T(8,128)(2,1)S(1)}, bf16[72,1152]{1,0:T(8,128)(2,1)S(1)}, u32[]{:S(2)}, u32[]{:S(2)}) collective-permute-start(bf16[72,1152]{1,0:T(8,128)(2,1)S(1)} %get-tuple-element.101), channel_id=1, source_target_pairs={{0,72},{8,64},{64,8},{72,0},{1,73},{9,65},{65,9},{73,1},{2,74},{10... | collective-permute-start | bytes 497672 | tf_op jit(solution)/shard_map/ppermute | solution.py:34
  84.6 5.7 %collective-permute-start.13 = (bf16[72,1152]{1,0:T(8,128)(2,1)S(1)}, bf16[72,1152]{1,0:T(8,128)(2,1)S(1)}, u32[]{:S(2)}, u32[]{:S(2)}) collective-permute-start(bf16[72,1152]{1,0:T(8,128)(2,1)S(1)} %shard_map.88.a), channel_id=1, source_target_pairs={{0,64},{64,0},{1,65},{65,1},{2,66},{66,2},{3,67},{67,3},{4,68},{68... | collective-permute-start | bytes 497672 | tf_op jit(solution)/shard_map/ppermute | solution.py:24
  90.3 6.6 %collective-permute-start.17 = (bf16[72,1152]{1,0:T(8,128)(2,1)S(1)}, bf16[72,1152]{1,0:T(8,128)(2,1)S(1)}, u32[]{:S(2)}, u32[]{:S(2)}) collective-permute-start(bf16[72,1152]{1,0:T(8,128)(2,1)S(1)} %shard_map.89.a), channel_id=1, source_target_pairs={{0,48},{16,0},{32,16},{48,32},{1,49},{17,1},{33,17},{49,33},{2,50}... | collective-permute-start | bytes 497672 | tf_op jit(solution)/shard_map/ppermute | solution.py:24
  90.8 9.5 %collective-permute-start.16 = (bf16[72,1152]{1,0:T(8,128)(2,1)S(1)}, bf16[72,1152]{1,0:T(8,128)(2,1)S(1)}, u32[]{:S(2)}, u32[]{:S(2)}) collective-permute-start(bf16[72,1152]{1,0:T(8,128)(2,1)S(1)} %shard_map.89.a), channel_id=1, source_target_pairs={{0,16},{16,32},{32,48},{48,0},{1,17},{17,33},{33,49},{49,1},{2,18}... | collective-permute-start | bytes 497672 | tf_op jit(solution)/shard_map/ppermute | solution.py:24
  92.4 8.0 %collective-permute-start.15 = (bf16[72,1152]{1,0:T(8,128)(2,1)S(1)}, bf16[72,1152]{1,0:T(8,128)(2,1)S(1)}, u32[]{:S(2)}, u32[]{:S(2)}) collective-permute-start(bf16[72,1152]{1,0:T(8,128)(2,1)S(1)} %shard_map.89.a), channel_id=1, source_target_pairs={{0,32},{16,48},{32,0},{48,16},{1,33},{17,49},{33,1},{49,17},{2,34}... | collective-permute-start | bytes 497672 | tf_op jit(solution)/shard_map/ppermute | solution.py:24

commit v10 on v9

--- a/solution.py
+++ b/solution.py
@@ -99,11 +99,12 @@
             head[pl.ds((h * 4 + x) * 144, 144), :] = jnp.concatenate([first, second], axis=0).astype(BF)
 
 
-def text_kernel(near, far, txt, txt_far, z, n_txt, inv, mine, other, rows, w_full, sems):
+def text_kernel(near, far, txt, txt_far, img, z, n_txt, inv, rows, n_img, mine, other, w_full, raw, sems):
     copies = load_head(near, far, mine, other, sems)
     late = [
         pltpu.make_async_copy(txt, rows.at[pl.ds(0, 320)], sems.at[8]),
         pltpu.make_async_copy(txt_far, rows.at[pl.ds(320, 320)], sems.at[9]),
+        pltpu.make_async_copy(img, raw, sems.at[10]),
     ]
     for c in late:
         c.start()
@@ -114,6 +115,8 @@
     z[...] = out
     inv[...] = inverse_length(out)
     n_txt[...] = (out * inv[...]).astype(BF)
+    own = raw[...].astype(F32)
+    n_img[...] = (own * inverse_length(own)).astype(BF)
 
 
 def logit_gradient(scale, bias, left, right):
@@ -123,9 +126,9 @@
     return 1.0 / (1.0 + jnp.exp(-logits))
 
 
-def main_kernel(scalars, n_txt, img, img_a, img_b, img_c, z, inv, txt, txt_far, grad, g_own, g_far, mine_c, other_c, mine, other, raw, rows, feat, wide, sems):
-    moves = [(block, raw.at[pl.ds(k * 320, 320)]) for k, block in enumerate((img, img_a, img_b, img_c))]
-    moves += [(txt, feat.at[pl.ds(0, 320)]), (txt_far, feat.at[pl.ds(320, 320)])]
+def main_kernel(scalars, n_txt, n_img, img_a, img_b, img_c, z, inv, feat, grad, g_own, g_far, mine_c, other_c, mine, other, raw, rows, wide, sems):
+    moves = [(n_img, rows.at[pl.ds(0, 320)])]
+    moves += [(block, raw.at[pl.ds(k * 320, 320)]) for k, block in enumerate((img_a, img_b, img_c))]
     copies = [pltpu.make_async_copy(a, b, sems.at[k]) for k, (a, b) in enumerate(moves)]
     for c in copies:
         c.start()
@@ -133,9 +136,9 @@
     for first, last, ready in ((0, 512, copies[:2]), (512, 1280, copies[2:4])):
         for c in ready:
             c.wait()
-        fresh = pl.ds(0 if first == 0 else 640, 640)
-        wide_rows = raw[fresh, :].astype(F32)
-        rows[fresh, :] = (wide_rows * inverse_length(wide_rows)).astype(BF)
+        begin, end = (0, 320) if first == 0 else (320, 960)
+        wide_rows = raw[begin:end, :].astype(F32)
+        rows[begin + 320 : end + 320, :] = (wide_rows * inverse_length(wide_rows)).astype(BF)
         g = logit_gradient(scale, bias, n_txt[...], rows[pl.ds(first, last - first), :])
         grad[:, first:last] = g.astype(BF)
         if first == 0:
@@ -150,8 +153,6 @@
         out[...] = (scale * total).astype(BF)
         parts.append(project(total, z[here, :], inv[here, :], scale).astype(BF))
     dz = jnp.concatenate(parts, axis=0)
-    for c in copies[4:]:
-        c.wait()
     wide[...] = lax.dot_general(
         feat[...], dz, (((0,), (0,)), ((), ())), preferred_element_type=F32
     )
@@ -317,34 +318,39 @@
     near, far, scalars = apart(gather_head, w_h, w_y, t_log, bias)
     near, far, txt_far = hold((near, far, txt_far))
 
-    z, n_txt, inv = call(
+    z, n_txt, inv, feat, n_img = call(
         text_kernel,
-        [shaped((640, 1152), F32), shaped((640, 1152), BF), shaped((640, 1), F32)],
-        [ANY] * 4,
+        [
+            shaped((640, 1152), F32),
+            shaped((640, 1152), BF),
+            shaped((640, 1), F32),
+            shaped((640, 1152), BF),
+            BLOCK,
+        ],
+        [ANY] * 5,
         [
             pltpu.VMEM((4, 2, 72, 1152), BF),
             pltpu.VMEM((4, 2, 72, 1152), BF),
-            pltpu.VMEM((640, 1152), BF),
             pltpu.VMEM((1152, 1152), BF),
-            pltpu.SemaphoreType.DMA((10,)),
+            pltpu.VMEM((320, 1152), BF),
+            pltpu.SemaphoreType.DMA((11,)),
         ],
         vmem=TEXT_MIB,
         flops=1 << 34,
-    )(near, far, txt, txt_far)
+    )(near, far, txt, txt_far, img)
     n_txt, img_a, img_b, img_c = hold((n_txt, img_a, img_b, img_c))
     grad, g_own, g_far, mine_c, other_c, mine, other = call(
         main_kernel,
         [shaped((640, 1280), BF), BLOCK, BLOCK, stack_of(2), stack_of(2), stack_of(3, 2), stack_of(3, 2)],
-        [VM] * 2 + [ANY] * 4 + [VM, VM, ANY, ANY],
+        [VM] * 2 + [ANY] * 4 + [VM] * 3,
         [
+            pltpu.VMEM((960, 1152), BF),
             pltpu.VMEM((1280, 1152), BF),
-            pltpu.VMEM((1280, 1152), BF),
-            pltpu.VMEM((640, 1152), BF),
             pltpu.VMEM((1152, 1152), F32),
-            pltpu.SemaphoreType.DMA((6,)),
+            pltpu.SemaphoreType.DMA((4,)),
         ],
         vmem=MAIN_MIB,
-    )(scalars, n_txt, img, img_a, img_b, img_c, z, inv, txt, txt_far)
+    )(scalars, n_txt, n_img, img_a, img_b, img_c, z, inv, feat)
 
     got = shift(other, "core", 1)
     got_c, (part_c,) = hold(

time: 101 us -> 101 us (level)
  waiting for transfers between devices: 25.6 us -> 23.3 us
  local copies, waits for them, and re-layouts: 0.01 us -> 1.12 us
    ppermute x17, waiting for transfers between devices: 17 us -> 15.5 us  [shift(): return lax.ppermute(value, axis, [(i, (i + step) % n) for i in range(n)])]
    unnamed x4 -> x6, local copies, waits for them, and re-layouts: 0.01 us -> 1.12 us
  transfers between devices with their start and end apart: 20 -> 20, of which waited for: 10 -> 9; matrix products, arithmetic and copies ran while one was open for 0% -> 0% of each run, Pallas kernels for 17% -> 18%
where the time goes in v10:
time: 101 us; the launch traced here: 100 us
  Pallas kernels  28.5 us (28%)
  starting transfers between devices  25.5 us (25%)
  waiting for transfers between devices  23.3 us (23%)
  blocking collectives  21 us (21%)
  local copies, waits for them, and re-layouts  1.12 us (1%)
    all_to_all x1, blocking collectives, along_x(): return lax.all_to_all(value, 'x', split_axis=0, concat_axis=0, tiled=True)  21 us
    ppermute x17, starting transfers between devices, shift(): return lax.ppermute(value, axis, [(i, (i + step) % n) for i in range(n)])  20.2 us
    ppermute x17, waiting for transfers between devices, shift(): return lax.ppermute(value, axis, [(i, (i + step) % n) for i in range(n)])  15.5 us
    pallas_call x1, Pallas kernels, on_device(): call(main_kernel, [shaped((640, 1280), BF), BLOCK, BLOCK, stack_of(2), st...  9.83 us
    ppermute x2, waiting for transfers between devices, swap_far(): return lax.ppermute(value, ('ylo', 'yhi'), pairs)  5.66 us
    pallas_call x1, Pallas kernels, on_device(): call(text_kernel, [shaped((640, 1152), F32), shaped((640, 1152), BF), sha...  4.78 us
    ppermute x2, starting transfers between devices, swap_far(): return lax.ppermute(value, ('ylo', 'yhi'), pairs)  4.28 us
    pallas_call x2, Pallas kernels, parts_of(): return call(kernel, shapes, [VM] * 3, flops=1 << 31)(*args)  3.12 us
  transfers between devices with their start and end apart: 20, of which 9 were waited for; matrix products, arithmetic and copies ran while one was open for 0% of the time, Pallas kernels for 18%

profile of v10, /device:TPU:0, one launch (start us, length us, event | category | flops | bytes accessed | tf_op | source)
XLA Modules:
  0.0 100.2 jit_solution(16381205188960489260)
XLA Ops:
  0.6 1.7 %collective-permute-start.2 = (bf16[320,1152]{1,0:T(8,128)(2,1)}, bf16[320,1152]{1,0:T(8,128)(2,1)}, u32[]{:S(2)}, u32[]{:S(2)}) collective-permute-start(bf16[320,1152]{1,0:T(8,128)(2,1)} %bitcast.6), channel_id=1, source_target_pairs={{0,64},{64,0},{1,65},{65,1},{2,66},{66,2},{3,67},{67,3},{4,68},{68... | collective-permute-start | bytes 2211848 | tf_op jit(solution)/shard_map/ppermute | solution.py:24
  2.4 1.0 shard_map.78
  3.4 2.3 %collective-permute-start.1 = (bf16[72,1152]{1,0:T(8,128)(2,1)S(1)}, bf16[72,1152]{1,0:T(8,128)(2,1)S(1)}, u32[]{:S(2)}, u32[]{:S(2)}) collective-permute-start(bf16[72,1152]{1,0:T(8,128)(2,1)S(1)} %shard_map.78), channel_id=1, source_target_pairs={{0,72},{8,64},{64,8},{72,0},{1,73},{9,65},{65,9},{73,1},{2,74},{10... | collective-permute-start | bytes 497672 | tf_op jit(solution)/shard_map/ppermute | solution.py:34
  5.6 3.9 %collective-permute-start.5 = (bf16[320,1152]{1,0:T(8,128)(2,1)}, bf16[320,1152]{1,0:T(8,128)(2,1)S(1)}, u32[]{:S(2)}, u32[]{:S(2)}) collective-permute-start(bf16[320,1152]{1,0:T(8,128)(2,1)} %bitcast.8), channel_id=1, source_target_pairs={{0,32},{16,48},{32,0},{48,16},{1,33},{17,49},{33,1},{49,17},{2,34}... | collective-permute-start | bytes 2211848 | tf_op jit(solution)/shard_map/ppermute | solution.py:24
  9.5 0.7 collective-permute-start.4
  10.2 1.3 %collective-permute-start.3 = (bf16[320,1152]{1,0:T(8,128)(2,1)}, bf16[320,1152]{1,0:T(8,128)(2,1)S(1)}, u32[]{:S(2)}, u32[]{:S(2)}) collective-permute-start(bf16[320,1152]{1,0:T(8,128)(2,1)} %bitcast.10), channel_id=1, source_target_pairs={{0,16},{16,32},{32,48},{48,0},{1,17},{17,33},{33,49},{49,1},{2,18}... | collective-permute-start | bytes 2211848 | tf_op jit(solution)/shard_map/ppermute | solution.py:24
  11.5 24.5 %conditional.1 = (bf16[4,2,72,1152]{3,2,1,0:T(8,128)(2,1)}, bf16[4,2,72,1152]{3,2,1,0:T(8,128)(2,1)}, f32[8,128]{1,0:T(8,128)S(1)}) conditional(s32[]{:T(128)} %convert_element_type.3, () %tuple.25, (bf16[72,1152]{1,0:T(8,128)(2,1)S(1)}, bf16[72,1152]{1,0:T(8,128)(2,1)S(1)}, f32[1]{0:T(128)}, f32[1]{0:T(128)}) %tuple.27), branch_computations={%region_0.0_spmd, %region_1.0_spmd} | conditional | flops 2147484672 | bytes 7964736 | solution.py:234
  11.5 0.1 branch_1_fun.2
  11.7 21.0 %all_to_all.4 = bf16[4,2,72,1152]{3,2,1,0:T(8,128)(2,1)} all-to-all(bf16[4,2,72,1152]{3,2,1,0:T(8,128)(2,1)S(1)} %branch_1_fun.2), channel_id=1, replica_groups=mesh['ylo'=2,'z'=4,'yhi'=2,'x'=4,'core'=2] {'x'}, dimensions={0} | all-to-all | bytes 2654208 | tf_op jit(solution)/shard_map/cond/branch_1_fun/all_to_all | solution.py:251
  32.7 0.0 collective-permute-start
  32.7 1.4 %branch_1_fun.3 = f32[8,128]{1,0:T(8,128)S(1)} custom-call(f32[1,1]{1,0:T(1,128)} %bitcast.t_log, f32[1,1]{1,0:T(1,128)} %bitcast.1.bias), custom_call_target="tpu_custom_call" | custom-call | flops 2147483648 | bytes 1024 | tf_op jit(solution)/shard_map/cond/branch_1_fun/pallas_call | solution.py:258
  34.0 2.0 %collective-permute-done = bf16[4,2,72,1152]{3,2,1,0:T(8,128)(2,1)} collective-permute-done((bf16[4,2,72,1152]{3,2,1,0:T(8,128)(2,1)}, bf16[4,2,72,1152]{3,2,1,0:T(8,128)(2,1)}, u32[]{:S(2)}, u32[]{:S(2)}) %collective-permute-start) | collective-permute-done | bytes 1327136 | tf_op jit(solution)/shard_map/cond/branch_1_fun/ppermute | solution.py:24
  36.1 1.1 %copy-done.1 = bf16[1,320,1152]{2,1,0:T(8,128)(2,1)S(1)} copy-done((bf16[1,320,1152]{2,1,0:T(8,128)(2,1)S(1)}, bf16[1,320,1152]{2,1,0:T(8,128)(2,1)}, u32[]{:S(2)}) %copy-start.1) | copy-done | bytes 737304
  37.2 4.8 %shard_map.79 = (f32[640,1152]{1,0:T(8,128)S(1)}, bf16[640,1152]{1,0:T(8,128)(2,1)S(1)}, f32[640,1]{1,0:T(8,128)S(1)}, bf16[640,1152]{1,0:T(8,128)(2,1)S(1)}, bf16[320,1152]{1,0:T(8,128)(2,1)S(1)}) custom-call(bf16[4,2,72,1152]{3,2,1,0:T(8,128)(2,1)} %get-tuple-element.99.near, bf16[4,2,72,1152]{3,2,1,0:T(8,128)(2,1)} %get-tuple-element.100.far, ...), custom_call_target="tpu_custom_call" | custom-call | flops 17179869184 | bytes 1024 | tf_op jit(solution)/shard_map/pallas_call | solution.py:321
  42.0 0.0 collective-permute-done.5.img_c
  42.0 0.2 collective-permute-done.4.img_b
  42.2 9.8 %shard_map.80 = (bf16[640,1280]{1,0:T(8,128)(2,1)S(1)}, bf16[320,1152]{1,0:T(8,128)(2,1)S(1)}, bf16[320,1152]{1,0:T(8,128)(2,1)S(1)}, bf16[2,72,1152]{2,1,0:T(8,...) custom-call(f32[8,128]{1,0:T(8,128)S(1)} %get-tuple-element.69.scala, ...), custom_call_target="tpu_custom_call" | custom-call | flops 1024 | bytes 1024 | tf_op jit(solution)/shard_map/pallas_call | solution.py:342
  52.1 0.1 collective-permute-start.6
  52.2 0.5 collective-permute-start.9
  52.7 1.0 %shard_map.82 = bf16[320,1152]{1,0:T(8,128)(2,1)S(1)} custom-call(f32[8,128]{1,0:T(8,128)S(1)} %get-tuple-element.69.scalars, bf16[640,1280]{1,0:T(8,128)(2,1)S(1)} %get-tuple-element.92.grad, bf16[640,1152]{1,0:T(8,128)(2,1)S(1)} %get-tuple-element.77.n_txt), custom_call_target="tpu_custom_call" | custom-call | flops 2147483648 | bytes 1024 | tf_op jit(solution)/shard_map/pallas_call | solution.py:266
  53.7 1.5 %collective-permute-done.9.b = bf16[2,72,1152]{2,1,0:T(8,128)(2,1)S(1)} collective-permute-done((bf16[2,72,1152]{2,1,0:T(8,128)(2,1)S(1)}, bf16[2,72,1152]{2,1,0:T(8,128)(2,1)S(1)}, u32[]{:S(2)}, u32[]{:S(2)}) %collective-permute-start.9) | collective-permute-done | bytes 331808 | tf_op jit(solution)/shard_map/ppermute | solution.py:24
  55.2 1.0 collective-permute-start.11
  56.2 0.1 shard_map.83
  56.3 3.1 %collective-permute-start.10 = (bf16[2,72,1152]{2,1,0:T(8,128)(2,1)S(1)}, bf16[2,72,1152]{2,1,0:T(8,128)(2,1)S(1)}, u32[]{:S(2)}, u32[]{:S(2)}) collective-permute-start(bf16[2,72,1152]{2,1,0:T(8,128)(2,1)S(1)} %shard_map.83), channel_id=1, source_target_pairs={{0,4},{2,6},{4,0},{6,2},{1,5},{3,7},{5,1},{7,3},{8,12},{10,14},{12... | collective-permute-start | bytes 995336 | tf_op jit(solution)/shard_map/ppermute | solution.py:24
  59.4 0.7 collective-permute-start.14
  60.1 0.2 shard_map.81
  60.3 0.7 collective-permute-start.7
  61.0 2.6 %collective-permute-start.8 = (bf16[2,72,1152]{2,1,0:T(8,128)(2,1)S(1)}, bf16[2,72,1152]{2,1,0:T(8,128)(2,1)S(1)}, u32[]{:S(2)}, u32[]{:S(2)}) collective-permute-start(bf16[2,72,1152]{2,1,0:T(8,128)(2,1)S(1)} %get-tuple-element.89), channel_id=1, source_target_pairs={{0,6},{2,0},{4,2},{6,4},{1,7},{3,1},{5,3},{7,5},{8,14},{10,8},{12,... | collective-permute-start | bytes 995336 | tf_op jit(solution)/shard_map/ppermute | solution.py:24
  63.6 2.1 %shard_map.84 = (bf16[320,1152]{1,0:T(8,128)(2,1)S(1)}, bf16[320,1152]{1,0:T(8,128)(2,1)S(1)}, bf16[320,1152]{1,0:T(8,128)(2,1)S(1)}) custom-call(f32[8,128]{1,0:T(8,128)S(1)} %get-tuple-element.69.scalars, bf16[640,1280]{1,0:T(8,128)(2,1)S(1)} %get-tuple-element.92.grad, bf16[640,1152]{1,0:T(8,128)(2,1)S(1)} %get-tuple-element.77.n_txt), custom_call_target="tpu_custom_call" | custom-call | flops 2147483648 | bytes 1024 | tf_op jit(solution)/shard_map/pallas_call | solution.py:266
  65.7 2.2 %collective-permute-done.11.got = bf16[320,1152]{1,0:T(8,128)(2,1)S(1)} collective-permute-done((bf16[320,1152]{1,0:T(8,128)(2,1)S(1)}, bf16[320,1152]{1,0:T(8,128)(2,1)S(1)}, u32[]{:S(2)}, u32[]{:S(2)}) %collective-permute-start.11) | collective-permute-done | bytes 737312 | tf_op jit(solution)/shard_map/ppermute | solution.py:29
  67.9 0.4 shard_map.85
  68.3 2.5 %collective-permute-start.18 = (bf16[320,1152]{1,0:T(8,128)(2,1)S(1)}, bf16[320,1152]{1,0:T(8,128)(2,1)S(1)}, u32[]{:S(2)}, u32[]{:S(2)}) collective-permute-start(bf16[320,1152]{1,0:T(8,128)(2,1)S(1)} %get-tuple-element.111), channel_id=1, source_target_pairs={{0,48},{16,0},{32,16},{48,32},{1,49},{17,1},{33,17},{49,33},{2,50}... | collective-permute-start | bytes 2211848 | tf_op jit(solution)/shard_map/ppermute | solution.py:24
  70.8 1.9 %shard_map.86.head = bf16[1152,1152]{1,0:T(8,128)(2,1)S(1)} custom-call(bf16[4,2,72,1152]{3,2,1,0:T(8,128)(2,1)} %get-tuple-element.99.near, bf16[4,2,72,1152]{3,2,1,0:T(8,128)(2,1)} %get-tuple-element.100.far), custom_call_target="tpu_custom_call" | custom-call | flops 2147483648 | bytes 1024 | tf_op jit(solution)/shard_map/pallas_call | solution.py:283
  72.7 2.9 %collective-permute-done.7.p = bf16[2,72,1152]{2,1,0:T(8,128)(2,1)S(1)} collective-permute-done((bf16[2,72,1152]{2,1,0:T(8,128)(2,1)S(1)}, bf16[2,72,1152]{2,1,0:T(8,128)(2,1)S(1)}, u32[]{:S(2)}, u32[]{:S(2)}) %collective-permute-start.7) | collective-permute-done | bytes 331808 | tf_op jit(solution)/shard_map/ppermute | solution.py:24
  75.7 0.2 shard_map.87
  75.8 2.0 %collective-permute-start.12 = (bf16[72,1152]{1,0:T(8,128)(2,1)S(1)}, bf16[72,1152]{1,0:T(8,128)(2,1)S(1)}, u32[]{:S(2)}, u32[]{:S(2)}) collective-permute-start(bf16[72,1152]{1,0:T(8,128)(2,1)S(1)} %get-tuple-element.105), channel_id=1, source_target_pairs={{0,72},{8,64},{64,8},{72,0},{1,73},{9,65},{65,9},{73,1},{2,74},{10... | collective-permute-start | bytes 497672 | tf_op jit(solution)/shard_map/ppermute | solution.py:34
  77.8 5.7 %collective-permute-done.12.b = bf16[72,1152]{1,0:T(8,128)(2,1)S(1)} collective-permute-done((bf16[72,1152]{1,0:T(8,128)(2,1)S(1)}, bf16[72,1152]{1,0:T(8,128)(2,1)S(1)}, u32[]{:S(2)}, u32[]{:S(2)}) %collective-permute-start.12) | collective-permute-done | bytes 165920 | tf_op jit(solution)/shard_map/ppermute | solution.py:34
  83.6 0.1 collective-permute-start.13
  83.7 0.0 copy-start.2
  83.7 3.0 %shard_map.90 = bf16[320,1152]{1,0:T(8,128)(2,1)} custom-call(f32[640,1152]{1,0:T(8,128)S(1)} %get-tuple-element.82.z, bf16[320,1152]{1,0:T(8,128)(2,1)S(1)} %get-tuple-element.106.a, bf16[320,1152]{1,0:T(8,128)(2,1)S(1)} %collective-permute-done.14.b, bf16[1152,1152]{1,0:T(8,128)(2,1)S(1)} %shard_map.86.head), custom_call_target="tpu_custom_call" | custom-call | flops 2147483648 | bytes 1024 | tf_op jit(solution)/shard_map/pallas_call | solution.py:297
  86.6 2.6 %collective-permute-done.13.b = bf16[72,1152]{1,0:T(8,128)(2,1)S(1)} collective-permute-done((bf16[72,1152]{1,0:T(8,128)(2,1)S(1)}, bf16[72,1152]{1,0:T(8,128)(2,1)S(1)}, u32[]{:S(2)}, u32[]{:S(2)}) %collective-permute-start.13) | collective-permute-done | bytes 165920 | tf_op jit(solution)/shard_map/ppermute | solution.py:24
  89.3 0.8 collective-permute-start.17
  90.0 1.3 %collective-permute-start.16 = (bf16[72,1152]{1,0:T(8,128)(2,1)S(1)}, bf16[72,1152]{1,0:T(8,128)(2,1)S(1)}, u32[]{:S(2)}, u32[]{:S(2)}) collective-permute-start(bf16[72,1152]{1,0:T(8,128)(2,1)S(1)} %shard_map.89.a), channel_id=1, source_target_pairs={{0,16},{16,32},{32,48},{48,0},{1,17},{17,33},{33,49},{49,1},{2,18}... | collective-permute-start | bytes 497672 | tf_op jit(solution)/shard_map/ppermute | solution.py:24
  91.3 0.2 collective-permute-start.15
  91.6 1.6 %shard_map.91 = bf16[320,1152]{1,0:T(8,128)(2,1)} custom-call(bf16[320,1152]{1,0:T(8,128)(2,1)S(1)} %bitcast.12, bf16[320,1152]{1,0:T(8,128)(2,1)S(1)} %get-tuple-element.110.a, bf16[320,1152]{1,0:T(8,128)(2,1)S(1)} %collective-permute-done.18.b, bf16[320,1152]{1,0:T(8,128)(2,1)S(1)} %collective-permute-done.19.c), custom_call_target="tpu_custom_call" | custom-call | flops 1073741824 | bytes 1024 | tf_op jit(solution)/shard_map/pallas_call | solution.py:362
  93.2 2.8 %collective-permute-done.17.d = bf16[72,1152]{1,0:T(8,128)(2,1)S(1)} collective-permute-done((bf16[72,1152]{1,0:T(8,128)(2,1)S(1)}, bf16[72,1152]{1,0:T(8,128)(2,1)S(1)}, u32[]{:S(2)}, u32[]{:S(2)}) %collective-permute-start.17) | collective-permute-done | bytes 165920 | tf_op jit(solution)/shard_map/ppermute | solution.py:24
  96.0 3.4 %collective-permute-done.16.c = bf16[72,1152]{1,0:T(8,128)(2,1)S(1)} collective-permute-done((bf16[72,1152]{1,0:T(8,128)(2,1)S(1)}, bf16[72,1152]{1,0:T(8,128)(2,1)S(1)}, u32[]{:S(2)}, u32[]{:S(2)}) %collective-permute-start.16) | collective-permute-done | bytes 165920 | tf_op jit(solution)/shard_map/ppermute | solution.py:24
  99.4 0.8 shard_map.92
  (17 shorter events, 0.1 us)
Async XLA Ops:
  0.6 35.4 %collective-permute-start.2 = (bf16[320,1152]{1,0:T(8,128)(2,1)}, bf16[320,1152]{1,0:T(8,128)(2,1)}, u32[]{:S(2)}, u32[]{:S(2)}) collective-permute-start(bf16[320,1152]{1,0:T(8,128)(2,1)} %bitcast.6), channel_id=1, source_target_pairs={{0,64},{64,0},{1,65},{65,1},{2,66},{66,2},{3,67},{67,3},{4,68},{68... | collective-permute-start | bytes 2211848 | tf_op jit(solution)/shard_map/ppermute | solution.py:24
  3.4 8.2 %collective-permute-start.1 = (bf16[72,1152]{1,0:T(8,128)(2,1)S(1)}, bf16[72,1152]{1,0:T(8,128)(2,1)S(1)}, u32[]{:S(2)}, u32[]{:S(2)}) collective-permute-start(bf16[72,1152]{1,0:T(8,128)(2,1)S(1)} %shard_map.78), channel_id=1, source_target_pairs={{0,72},{8,64},{64,8},{72,0},{1,73},{9,65},{65,9},{73,1},{2,74},{10... | collective-permute-start | bytes 497672 | tf_op jit(solution)/shard_map/ppermute | solution.py:34
  5.6 36.4 %collective-permute-start.5 = (bf16[320,1152]{1,0:T(8,128)(2,1)}, bf16[320,1152]{1,0:T(8,128)(2,1)S(1)}, u32[]{:S(2)}, u32[]{:S(2)}) collective-permute-start(bf16[320,1152]{1,0:T(8,128)(2,1)} %bitcast.8), channel_id=1, source_target_pairs={{0,32},{16,48},{32,0},{48,16},{1,33},{17,49},{33,1},{49,17},{2,34}... | collective-permute-start | bytes 2211848 | tf_op jit(solution)/shard_map/ppermute | solution.py:24
  9.5 32.7 %collective-permute-start.4 = (bf16[320,1152]{1,0:T(8,128)(2,1)}, bf16[320,1152]{1,0:T(8,128)(2,1)S(1)}, u32[]{:S(2)}, u32[]{:S(2)}) collective-permute-start(bf16[320,1152]{1,0:T(8,128)(2,1)} %bitcast.9), channel_id=1, source_target_pairs={{0,48},{16,0},{32,16},{48,32},{1,49},{17,1},{33,17},{49,33},{2,50}... | collective-permute-start | bytes 2211848 | tf_op jit(solution)/shard_map/ppermute | solution.py:24
  10.2 32.0 %collective-permute-start.3 = (bf16[320,1152]{1,0:T(8,128)(2,1)}, bf16[320,1152]{1,0:T(8,128)(2,1)S(1)}, u32[]{:S(2)}, u32[]{:S(2)}) collective-permute-start(bf16[320,1152]{1,0:T(8,128)(2,1)} %bitcast.10), channel_id=1, source_target_pairs={{0,16},{16,32},{32,48},{48,0},{1,17},{17,33},{33,49},{49,1},{2,18}... | collective-permute-start | bytes 2211848 | tf_op jit(solution)/shard_map/ppermute | solution.py:24
  11.5 24.5 %copy-start = (bf16[1,320,1152]{2,1,0:T(8,128)(2,1)S(1)}, bf16[1,320,1152]{2,1,0:T(8,128)(2,1)}, u32[]{:S(2)}) copy-start(bf16[1,320,1152]{2,1,0:T(8,128)(2,1)} %param.8) | copy-start | bytes 2211844
  32.7 3.4 %collective-permute-start = (bf16[4,2,72,1152]{3,2,1,0:T(8,128)(2,1)}, bf16[4,2,72,1152]{3,2,1,0:T(8,128)(2,1)}, u32[]{:S(2)}, u32[]{:S(2)}) collective-permute-start(bf16[4,2,72,1152]{3,2,1,0:T(8,128)(2,1)} %all_to_all.4), channel_id=1, source_target_pairs={{0,1},{1,0},{2,3},{3,2},{4,5},{5,4},{6,7},{7,6},{8,9},{9,8},{10,11... | collective-permute-start | bytes 3981320 | tf_op jit(solution)/shard_map/cond/branch_1_fun/ppermute | solution.py:24
  36.1 1.1 %copy-start.1 = (bf16[1,320,1152]{2,1,0:T(8,128)(2,1)S(1)}, bf16[1,320,1152]{2,1,0:T(8,128)(2,1)}, u32[]{:S(2)}) copy-start(bf16[1,320,1152]{2,1,0:T(8,128)(2,1)} %param.7) | copy-start | bytes 2211844
  52.1 8.0 %collective-permute-start.6 = (bf16[3,2,72,1152]{3,2,1,0:T(8,128)(2,1)S(1)}, bf16[3,2,72,1152]{3,2,1,0:T(8,128)(2,1)S(1)}, u32[]{:S(2)}, u32[]{:S(2)}) collective-permute-start(bf16[3,2,72,1152]{3,2,1,0:T(8,128)(2,1)S(1)} %get-tuple-element.86), channel_id=1, source_target_pairs={{0,1},{1,0},{2,3},{3,2},{4,5},{5,4},{6,7},{7,6},{8,9},{9,8},{10,11... | collective-permute-start | bytes 2985992 | tf_op jit(solution)/shard_map/ppermute | solution.py:24
  52.2 3.0 %collective-permute-start.9 = (bf16[2,72,1152]{2,1,0:T(8,128)(2,1)S(1)}, bf16[2,72,1152]{2,1,0:T(8,128)(2,1)S(1)}, u32[]{:S(2)}, u32[]{:S(2)}) collective-permute-start(bf16[2,72,1152]{2,1,0:T(8,128)(2,1)S(1)} %get-tuple-element.91), channel_id=1, source_target_pairs={{0,1},{1,0},{2,3},{3,2},{4,5},{5,4},{6,7},{7,6},{8,9},{9,8},{10,11... | collective-permute-start | bytes 995336 | tf_op jit(solution)/shard_map/ppermute | solution.py:24
  55.2 12.7 %collective-permute-start.11 = (bf16[320,1152]{1,0:T(8,128)(2,1)S(1)}, bf16[320,1152]{1,0:T(8,128)(2,1)S(1)}, u32[]{:S(2)}, u32[]{:S(2)}) collective-permute-start(bf16[320,1152]{1,0:T(8,128)(2,1)S(1)} %shard_map.82), channel_id=1, source_target_pairs={{0,16},{1,49},{16,32},{17,1},{32,48},{33,17},{48,0},{49,33},{2,18}... | collective-permute-start | bytes 2211848 | tf_op jit(solution)/shard_map/ppermute | solution.py:29
  56.3 12.0 %collective-permute-start.10 = (bf16[2,72,1152]{2,1,0:T(8,128)(2,1)S(1)}, bf16[2,72,1152]{2,1,0:T(8,128)(2,1)S(1)}, u32[]{:S(2)}, u32[]{:S(2)}) collective-permute-start(bf16[2,72,1152]{2,1,0:T(8,128)(2,1)S(1)} %shard_map.83), channel_id=1, source_target_pairs={{0,4},{2,6},{4,0},{6,2},{1,5},{3,7},{5,1},{7,3},{8,12},{10,14},{12... | collective-permute-start | bytes 995336 | tf_op jit(solution)/shard_map/ppermute | solution.py:24
  59.4 24.3 %collective-permute-start.14 = (bf16[320,1152]{1,0:T(8,128)(2,1)S(1)}, bf16[320,1152]{1,0:T(8,128)(2,1)S(1)}, u32[]{:S(2)}, u32[]{:S(2)}) collective-permute-start(bf16[320,1152]{1,0:T(8,128)(2,1)S(1)} %get-tuple-element.107), channel_id=1, source_target_pairs={{0,64},{64,0},{1,65},{65,1},{2,66},{66,2},{3,67},{67,3},{4,68},{68... | collective-permute-start | bytes 2211848 | tf_op jit(solution)/shard_map/ppermute | solution.py:24
  60.3 15.3 %collective-permute-start.7 = (bf16[2,72,1152]{2,1,0:T(8,128)(2,1)S(1)}, bf16[2,72,1152]{2,1,0:T(8,128)(2,1)S(1)}, u32[]{:S(2)}, u32[]{:S(2)}) collective-permute-start(bf16[2,72,1152]{2,1,0:T(8,128)(2,1)S(1)} %get-tuple-element.88), channel_id=1, source_target_pairs={{0,2},{2,4},{4,6},{6,0},{1,3},{3,5},{5,7},{7,1},{8,10},{10,12},{12... | collective-permute-start | bytes 995336 | tf_op jit(solution)/shard_map/ppermute | solution.py:24
  61.0 14.7 %collective-permute-start.8 = (bf16[2,72,1152]{2,1,0:T(8,128)(2,1)S(1)}, bf16[2,72,1152]{2,1,0:T(8,128)(2,1)S(1)}, u32[]{:S(2)}, u32[]{:S(2)}) collective-permute-start(bf16[2,72,1152]{2,1,0:T(8,128)(2,1)S(1)} %get-tuple-element.89), channel_id=1, source_target_pairs={{0,6},{2,0},{4,2},{6,4},{1,7},{3,1},{5,3},{7,5},{8,14},{10,8},{12,... | collective-permute-start | bytes 995336 | tf_op jit(solution)/shard_map/ppermute | solution.py:24
  68.3 23.3 %collective-permute-start.18 = (bf16[320,1152]{1,0:T(8,128)(2,1)S(1)}, bf16[320,1152]{1,0:T(8,128)(2,1)S(1)}, u32[]{:S(2)}, u32[]{:S(2)}) collective-permute-start(bf16[320,1152]{1,0:T(8,128)(2,1)S(1)} %get-tuple-element.111), channel_id=1, source_target_pairs={{0,48},{16,0},{32,16},{48,32},{1,49},{17,1},{33,17},{49,33},{2,50}... | collective-permute-start | bytes 2211848 | tf_op jit(solution)/shard_map/ppermute | solution.py:24
  70.8 20.8 %collective-permute-start.19 = (bf16[320,1152]{1,0:T(8,128)(2,1)S(1)}, bf16[320,1152]{1,0:T(8,128)(2,1)S(1)}, u32[]{:S(2)}, u32[]{:S(2)}) collective-permute-start(bf16[320,1152]{1,0:T(8,128)(2,1)S(1)} %get-tuple-element.112), channel_id=1, source_target_pairs={{0,16},{16,32},{32,48},{48,0},{1,17},{17,33},{33,49},{49,1},{2,18}... | collective-permute-start | bytes 2211848 | tf_op jit(solution)/shard_map/ppermute | solution.py:24
  75.8 7.7 %collective-permute-start.12 = (bf16[72,1152]{1,0:T(8,128)(2,1)S(1)}, bf16[72,1152]{1,0:T(8,128)(2,1)S(1)}, u32[]{:S(2)}, u32[]{:S(2)}) collective-permute-start(bf16[72,1152]{1,0:T(8,128)(2,1)S(1)} %get-tuple-element.105), channel_id=1, source_target_pairs={{0,72},{8,64},{64,8},{72,0},{1,73},{9,65},{65,9},{73,1},{2,74},{10... | collective-permute-start | bytes 497672 | tf_op jit(solution)/shard_map/ppermute | solution.py:34
  83.6 5.7 %collective-permute-start.13 = (bf16[72,1152]{1,0:T(8,128)(2,1)S(1)}, bf16[72,1152]{1,0:T(8,128)(2,1)S(1)}, u32[]{:S(2)}, u32[]{:S(2)}) collective-permute-start(bf16[72,1152]{1,0:T(8,128)(2,1)S(1)} %shard_map.88.a), channel_id=1, source_target_pairs={{0,64},{64,0},{1,65},{65,1},{2,66},{66,2},{3,67},{67,3},{4,68},{68... | collective-permute-start | bytes 497672 | tf_op jit(solution)/shard_map/ppermute | solution.py:24
  83.7 7.9 %copy-start.2 = (bf16[1,320,1152]{2,1,0:T(8,128)(2,1)S(1)}, bf16[1,320,1152]{2,1,0:T(8,128)(2,1)}, u32[]{:S(2)}) copy-start(bf16[1,320,1152]{2,1,0:T(8,128)(2,1)} %param.7) | copy-start | bytes 2211844
  89.3 6.8 %collective-permute-start.17 = (bf16[72,1152]{1,0:T(8,128)(2,1)S(1)}, bf16[72,1152]{1,0:T(8,128)(2,1)S(1)}, u32[]{:S(2)}, u32[]{:S(2)}) collective-permute-start(bf16[72,1152]{1,0:T(8,128)(2,1)S(1)} %shard_map.89.a), channel_id=1, source_target_pairs={{0,48},{16,0},{32,16},{48,32},{1,49},{17,1},{33,17},{49,33},{2,50}... | collective-permute-start | bytes 497672 | tf_op jit(solution)/shard_map/ppermute | solution.py:24
  90.0 9.4 %collective-permute-start.16 = (bf16[72,1152]{1,0:T(8,128)(2,1)S(1)}, bf16[72,1152]{1,0:T(8,128)(2,1)S(1)}, u32[]{:S(2)}, u32[]{:S(2)}) collective-permute-start(bf16[72,1152]{1,0:T(8,128)(2,1)S(1)} %shard_map.89.a), channel_id=1, source_target_pairs={{0,16},{16,32},{32,48},{48,0},{1,17},{17,33},{33,49},{49,1},{2,18}... | collective-permute-start | bytes 497672 | tf_op jit(solution)/shard_map/ppermute | solution.py:24
  91.3 8.1 %collective-permute-start.15 = (bf16[72,1152]{1,0:T(8,128)(2,1)S(1)}, bf16[72,1152]{1,0:T(8,128)(2,1)S(1)}, u32[]{:S(2)}, u32[]{:S(2)}) collective-permute-start(bf16[72,1152]{1,0:T(8,128)(2,1)S(1)} %shard_map.89.a), channel_id=1, source_target_pairs={{0,32},{16,48},{32,0},{48,16},{1,33},{17,49},{33,1},{49,17},{2,34}... | collective-permute-start | bytes 497672 | tf_op jit(solution)/shard_map/ppermute | solution.py:24

commit v11 on v10

--- a/solution.py
+++ b/solution.py
@@ -202,11 +202,6 @@
 
 def pair_sum_kernel(a, b, out):
     out[...] = (a[...].astype(F32) + b[...].astype(F32)).astype(BF)
-
-
-def quad_sum_kernel(a, b, c, d, out):
-    total = (a[...].astype(F32) + b[...].astype(F32)) + (c[...].astype(F32) + d[...].astype(F32))
-    out[...] = total.astype(out.dtype)
 
 
 def image_out_kernel(img, a, b, c, out):
@@ -362,7 +357,8 @@
     (d_img,) = call(image_out_kernel, [BLOCK], [VM] * 4, flops=1 << 30)(img, part_own, got_a, got_b)
     got_z = [shift(quad, "z", k) for k in (2, 1, -1)]
     got_z, d_img = hold((got_z, d_img))
-    (d_weight,) = call(quad_sum_kernel, [shaped((72, 1152), F32)], [VM] * 4)(quad, *got_z)
+    a, b, c, d = (v.astype(F32) for v in (quad, *got_z))
+    d_weight = (a + b) + (c + d)
     return (d_img[None], d_feat[None], d_weight)
 
 

time: 101 us -> 101 us (level)
  no operation moved by 1% of the time
where the time goes in v11:
time: 101 us; the launch traced here: 100 us
  Pallas kernels  27.7 us (27%)
  starting transfers between devices  25.5 us (25%)
  waiting for transfers between devices  23.3 us (23%)
  blocking collectives  21 us (21%)
  local copies, waits for them, and re-layouts  1.12 us (1%)
    all_to_all x1, blocking collectives, along_x(): return lax.all_to_all(value, 'x', split_axis=0, concat_axis=0, tiled=True)  21 us
    ppermute x17, starting transfers between devices, shift(): return lax.ppermute(value, axis, [(i, (i + step) % n) for i in range(n)])  20.2 us
    ppermute x17, waiting for transfers between devices, shift(): return lax.ppermute(value, axis, [(i, (i + step) % n) for i in range(n)])  15.5 us
    pallas_call x1, Pallas kernels, on_device(): call(main_kernel, [shaped((640, 1280), BF), BLOCK, BLOCK, stack_of(2), st...  9.83 us
    ppermute x2, waiting for transfers between devices, swap_far(): return lax.ppermute(value, ('ylo', 'yhi'), pairs)  5.66 us
    pallas_call x1, Pallas kernels, on_device(): call(text_kernel, [shaped((640, 1152), F32), shaped((640, 1152), BF), sha...  4.78 us
    ppermute x2, starting transfers between devices, swap_far(): return lax.ppermute(value, ('ylo', 'yhi'), pairs)  4.28 us
    pallas_call x2, Pallas kernels, parts_of(): return call(kernel, shapes, [VM] * 3, flops=1 << 31)(*args)  3.12 us
  transfers between devices with their start and end apart: 20, of which 9 were waited for; matrix products, arithmetic and copies ran while one was open for 0% of the time, Pallas kernels for 18%

profile of v11, /device:TPU:0, one launch (start us, length us, event | category | flops | bytes accessed | tf_op | source)
XLA Modules:
  0.0 100.2 jit_solution(1921647503612642395)
XLA Ops:
  0.6 1.7 %collective-permute-start.2 = (bf16[320,1152]{1,0:T(8,128)(2,1)}, bf16[320,1152]{1,0:T(8,128)(2,1)}, u32[]{:S(2)}, u32[]{:S(2)}) collective-permute-start(bf16[320,1152]{1,0:T(8,128)(2,1)} %bitcast.6), channel_id=1, source_target_pairs={{0,64},{64,0},{1,65},{65,1},{2,66},{66,2},{3,67},{67,3},{4,68},{68... | collective-permute-start | bytes 2211848 | tf_op jit(solution)/shard_map/ppermute | solution.py:24
  2.4 1.0 shard_map.78
  3.4 2.3 %collective-permute-start.1 = (bf16[72,1152]{1,0:T(8,128)(2,1)S(1)}, bf16[72,1152]{1,0:T(8,128)(2,1)S(1)}, u32[]{:S(2)}, u32[]{:S(2)}) collective-permute-start(bf16[72,1152]{1,0:T(8,128)(2,1)S(1)} %shard_map.78), channel_id=1, source_target_pairs={{0,72},{8,64},{64,8},{72,0},{1,73},{9,65},{65,9},{73,1},{2,74},{10... | collective-permute-start | bytes 497672 | tf_op jit(solution)/shard_map/ppermute | solution.py:34
  5.6 3.9 %collective-permute-start.5 = (bf16[320,1152]{1,0:T(8,128)(2,1)}, bf16[320,1152]{1,0:T(8,128)(2,1)S(1)}, u32[]{:S(2)}, u32[]{:S(2)}) collective-permute-start(bf16[320,1152]{1,0:T(8,128)(2,1)} %bitcast.8), channel_id=1, source_target_pairs={{0,32},{16,48},{32,0},{48,16},{1,33},{17,49},{33,1},{49,17},{2,34}... | collective-permute-start | bytes 2211848 | tf_op jit(solution)/shard_map/ppermute | solution.py:24
  9.5 0.7 collective-permute-start.4
  10.2 1.3 %collective-permute-start.3 = (bf16[320,1152]{1,0:T(8,128)(2,1)}, bf16[320,1152]{1,0:T(8,128)(2,1)S(1)}, u32[]{:S(2)}, u32[]{:S(2)}) collective-permute-start(bf16[320,1152]{1,0:T(8,128)(2,1)} %bitcast.10), channel_id=1, source_target_pairs={{0,16},{16,32},{32,48},{48,0},{1,17},{17,33},{33,49},{49,1},{2,18}... | collective-permute-start | bytes 2211848 | tf_op jit(solution)/shard_map/ppermute | solution.py:24
  11.5 24.5 %conditional.1 = (bf16[4,2,72,1152]{3,2,1,0:T(8,128)(2,1)}, bf16[4,2,72,1152]{3,2,1,0:T(8,128)(2,1)}, f32[8,128]{1,0:T(8,128)S(1)}) conditional(s32[]{:T(128)} %convert_element_type.15, () %tuple.25, (bf16[72,1152]{1,0:T(8,128)(2,1)S(1)}, bf16[72,1152]{1,0:T(8,128)(2,1)S(1)}, f32[1]{0:T(128)}, f32[1]{0:T(128)}) %tuple.27), branch_computations={%region_0.0_spmd, %region_1.0_spmd} | conditional | flops 2147484672 | bytes 7964736 | solution.py:229
  11.5 0.1 branch_1_fun.2
  11.7 21.0 %all_to_all.4 = bf16[4,2,72,1152]{3,2,1,0:T(8,128)(2,1)} all-to-all(bf16[4,2,72,1152]{3,2,1,0:T(8,128)(2,1)S(1)} %branch_1_fun.2), channel_id=1, replica_groups=mesh['ylo'=2,'z'=4,'yhi'=2,'x'=4,'core'=2] {'x'}, dimensions={0} | all-to-all | bytes 2654208 | tf_op jit(solution)/shard_map/cond/branch_1_fun/all_to_all | solution.py:246
  32.7 0.0 collective-permute-start
  32.7 1.4 %branch_1_fun.3 = f32[8,128]{1,0:T(8,128)S(1)} custom-call(f32[1,1]{1,0:T(1,128)} %bitcast.t_log, f32[1,1]{1,0:T(1,128)} %bitcast.1.bias), custom_call_target="tpu_custom_call" | custom-call | flops 2147483648 | bytes 1024 | tf_op jit(solution)/shard_map/cond/branch_1_fun/pallas_call | solution.py:253
  34.0 2.0 %collective-permute-done = bf16[4,2,72,1152]{3,2,1,0:T(8,128)(2,1)} collective-permute-done((bf16[4,2,72,1152]{3,2,1,0:T(8,128)(2,1)}, bf16[4,2,72,1152]{3,2,1,0:T(8,128)(2,1)}, u32[]{:S(2)}, u32[]{:S(2)}) %collective-permute-start) | collective-permute-done | bytes 1327136 | tf_op jit(solution)/shard_map/cond/branch_1_fun/ppermute | solution.py:24
  36.1 1.1 %copy-done.1 = bf16[1,320,1152]{2,1,0:T(8,128)(2,1)S(1)} copy-done((bf16[1,320,1152]{2,1,0:T(8,128)(2,1)S(1)}, bf16[1,320,1152]{2,1,0:T(8,128)(2,1)}, u32[]{:S(2)}) %copy-start.1) | copy-done | bytes 737304
  37.2 4.8 %shard_map.79 = (f32[640,1152]{1,0:T(8,128)S(1)}, bf16[640,1152]{1,0:T(8,128)(2,1)S(1)}, f32[640,1]{1,0:T(8,128)S(1)}, bf16[640,1152]{1,0:T(8,128)(2,1)S(1)}, bf16[320,1152]{1,0:T(8,128)(2,1)S(1)}) custom-call(bf16[4,2,72,1152]{3,2,1,0:T(8,128)(2,1)} %get-tuple-element.99.near, bf16[4,2,72,1152]{3,2,1,0:T(8,128)(2,1)} %get-tuple-element.100.far, ...), custom_call_target="tpu_custom_call" | custom-call | flops 17179869184 | bytes 1024 | tf_op jit(solution)/shard_map/pallas_call | solution.py:316
  42.0 0.0 collective-permute-done.5.img_c
  42.0 0.2 collective-permute-done.4.img_b
  42.2 9.8 %shard_map.80 = (bf16[640,1280]{1,0:T(8,128)(2,1)S(1)}, bf16[320,1152]{1,0:T(8,128)(2,1)S(1)}, bf16[320,1152]{1,0:T(8,128)(2,1)S(1)}, bf16[2,72,1152]{2,1,0:T(8,...) custom-call(f32[8,128]{1,0:T(8,128)S(1)} %get-tuple-element.69.scala, ...), custom_call_target="tpu_custom_call" | custom-call | flops 1024 | bytes 1024 | tf_op jit(solution)/shard_map/pallas_call | solution.py:337
  52.1 0.1 collective-permute-start.6
  52.2 0.5 collective-permute-start.9
  52.7 1.0 %shard_map.82 = bf16[320,1152]{1,0:T(8,128)(2,1)S(1)} custom-call(f32[8,128]{1,0:T(8,128)S(1)} %get-tuple-element.69.scalars, bf16[640,1280]{1,0:T(8,128)(2,1)S(1)} %get-tuple-element.92.grad, bf16[640,1152]{1,0:T(8,128)(2,1)S(1)} %get-tuple-element.77.n_txt), custom_call_target="tpu_custom_call" | custom-call | flops 2147483648 | bytes 1024 | tf_op jit(solution)/shard_map/pallas_call | solution.py:261
  53.7 1.5 %collective-permute-done.9.b = bf16[2,72,1152]{2,1,0:T(8,128)(2,1)S(1)} collective-permute-done((bf16[2,72,1152]{2,1,0:T(8,128)(2,1)S(1)}, bf16[2,72,1152]{2,1,0:T(8,128)(2,1)S(1)}, u32[]{:S(2)}, u32[]{:S(2)}) %collective-permute-start.9) | collective-permute-done | bytes 331808 | tf_op jit(solution)/shard_map/ppermute | solution.py:24
  55.2 1.0 collective-permute-start.11
  56.2 0.1 shard_map.83
  56.3 3.1 %collective-permute-start.10 = (bf16[2,72,1152]{2,1,0:T(8,128)(2,1)S(1)}, bf16[2,72,1152]{2,1,0:T(8,128)(2,1)S(1)}, u32[]{:S(2)}, u32[]{:S(2)}) collective-permute-start(bf16[2,72,1152]{2,1,0:T(8,128)(2,1)S(1)} %shard_map.83), channel_id=1, source_target_pairs={{0,4},{2,6},{4,0},{6,2},{1,5},{3,7},{5,1},{7,3},{8,12},{10,14},{12... | collective-permute-start | bytes 995336 | tf_op jit(solution)/shard_map/ppermute | solution.py:24
  59.4 0.7 collective-permute-start.14
  60.1 0.2 shard_map.81
  60.3 0.7 collective-permute-start.7
  61.0 2.6 %collective-permute-start.8 = (bf16[2,72,1152]{2,1,0:T(8,128)(2,1)S(1)}, bf16[2,72,1152]{2,1,0:T(8,128)(2,1)S(1)}, u32[]{:S(2)}, u32[]{:S(2)}) collective-permute-start(bf16[2,72,1152]{2,1,0:T(8,128)(2,1)S(1)} %get-tuple-element.89), channel_id=1, source_target_pairs={{0,6},{2,0},{4,2},{6,4},{1,7},{3,1},{5,3},{7,5},{8,14},{10,8},{12,... | collective-permute-start | bytes 995336 | tf_op jit(solution)/shard_map/ppermute | solution.py:24
  63.6 2.1 %shard_map.84 = (bf16[320,1152]{1,0:T(8,128)(2,1)S(1)}, bf16[320,1152]{1,0:T(8,128)(2,1)S(1)}, bf16[320,1152]{1,0:T(8,128)(2,1)S(1)}) custom-call(f32[8,128]{1,0:T(8,128)S(1)} %get-tuple-element.69.scalars, bf16[640,1280]{1,0:T(8,128)(2,1)S(1)} %get-tuple-element.92.grad, bf16[640,1152]{1,0:T(8,128)(2,1)S(1)} %get-tuple-element.77.n_txt), custom_call_target="tpu_custom_call" | custom-call | flops 2147483648 | bytes 1024 | tf_op jit(solution)/shard_map/pallas_call | solution.py:261
  65.7 2.2 %collective-permute-done.11.got = bf16[320,1152]{1,0:T(8,128)(2,1)S(1)} collective-permute-done((bf16[320,1152]{1,0:T(8,128)(2,1)S(1)}, bf16[320,1152]{1,0:T(8,128)(2,1)S(1)}, u32[]{:S(2)}, u32[]{:S(2)}) %collective-permute-start.11) | collective-permute-done | bytes 737312 | tf_op jit(solution)/shard_map/ppermute | solution.py:29
  67.9 0.4 shard_map.85
  68.3 2.5 %collective-permute-start.18 = (bf16[320,1152]{1,0:T(8,128)(2,1)S(1)}, bf16[320,1152]{1,0:T(8,128)(2,1)S(1)}, u32[]{:S(2)}, u32[]{:S(2)}) collective-permute-start(bf16[320,1152]{1,0:T(8,128)(2,1)S(1)} %get-tuple-element.111), channel_id=1, source_target_pairs={{0,48},{16,0},{32,16},{48,32},{1,49},{17,1},{33,17},{49,33},{2,50}... | collective-permute-start | bytes 2211848 | tf_op jit(solution)/shard_map/ppermute | solution.py:24
  70.8 1.9 %shard_map.86.head = bf16[1152,1152]{1,0:T(8,128)(2,1)S(1)} custom-call(bf16[4,2,72,1152]{3,2,1,0:T(8,128)(2,1)} %get-tuple-element.99.near, bf16[4,2,72,1152]{3,2,1,0:T(8,128)(2,1)} %get-tuple-element.100.far), custom_call_target="tpu_custom_call" | custom-call | flops 2147483648 | bytes 1024 | tf_op jit(solution)/shard_map/pallas_call | solution.py:278
  72.7 2.9 %collective-permute-done.7.p = bf16[2,72,1152]{2,1,0:T(8,128)(2,1)S(1)} collective-permute-done((bf16[2,72,1152]{2,1,0:T(8,128)(2,1)S(1)}, bf16[2,72,1152]{2,1,0:T(8,128)(2,1)S(1)}, u32[]{:S(2)}, u32[]{:S(2)}) %collective-permute-start.7) | collective-permute-done | bytes 331808 | tf_op jit(solution)/shard_map/ppermute | solution.py:24
  75.7 0.2 shard_map.87
  75.8 2.0 %collective-permute-start.12 = (bf16[72,1152]{1,0:T(8,128)(2,1)S(1)}, bf16[72,1152]{1,0:T(8,128)(2,1)S(1)}, u32[]{:S(2)}, u32[]{:S(2)}) collective-permute-start(bf16[72,1152]{1,0:T(8,128)(2,1)S(1)} %get-tuple-element.105), channel_id=1, source_target_pairs={{0,72},{8,64},{64,8},{72,0},{1,73},{9,65},{65,9},{73,1},{2,74},{10... | collective-permute-start | bytes 497672 | tf_op jit(solution)/shard_map/ppermute | solution.py:34
  77.8 5.7 %collective-permute-done.12.b = bf16[72,1152]{1,0:T(8,128)(2,1)S(1)} collective-permute-done((bf16[72,1152]{1,0:T(8,128)(2,1)S(1)}, bf16[72,1152]{1,0:T(8,128)(2,1)S(1)}, u32[]{:S(2)}, u32[]{:S(2)}) %collective-permute-start.12) | collective-permute-done | bytes 165920 | tf_op jit(solution)/shard_map/ppermute | solution.py:34
  83.6 0.1 collective-permute-start.13
  83.7 0.0 copy-start.2
  83.7 3.0 %shard_map.90 = bf16[320,1152]{1,0:T(8,128)(2,1)} custom-call(f32[640,1152]{1,0:T(8,128)S(1)} %get-tuple-element.82.z, bf16[320,1152]{1,0:T(8,128)(2,1)S(1)} %get-tuple-element.106.a, bf16[320,1152]{1,0:T(8,128)(2,1)S(1)} %collective-permute-done.14.b, bf16[1152,1152]{1,0:T(8,128)(2,1)S(1)} %shard_map.86.head), custom_call_target="tpu_custom_call" | custom-call | flops 2147483648 | bytes 1024 | tf_op jit(solution)/shard_map/pallas_call | solution.py:292
  86.6 2.6 %collective-permute-done.13.b = bf16[72,1152]{1,0:T(8,128)(2,1)S(1)} collective-permute-done((bf16[72,1152]{1,0:T(8,128)(2,1)S(1)}, bf16[72,1152]{1,0:T(8,128)(2,1)S(1)}, u32[]{:S(2)}, u32[]{:S(2)}) %collective-permute-start.13) | collective-permute-done | bytes 165920 | tf_op jit(solution)/shard_map/ppermute | solution.py:24
  89.3 0.8 collective-permute-start.17
  90.0 1.3 %collective-permute-start.16 = (bf16[72,1152]{1,0:T(8,128)(2,1)S(1)}, bf16[72,1152]{1,0:T(8,128)(2,1)S(1)}, u32[]{:S(2)}, u32[]{:S(2)}) collective-permute-start(bf16[72,1152]{1,0:T(8,128)(2,1)S(1)} %shard_map.89), channel_id=1, source_target_pairs={{0,16},{16,32},{32,48},{48,0},{1,17},{17,33},{33,49},{49,1},{2,18}... | collective-permute-start | bytes 497672 | tf_op jit(solution)/shard_map/ppermute | solution.py:24
  91.3 0.2 collective-permute-start.15
  91.6 1.6 %shard_map.91 = bf16[320,1152]{1,0:T(8,128)(2,1)} custom-call(bf16[320,1152]{1,0:T(8,128)(2,1)S(1)} %bitcast.12, bf16[320,1152]{1,0:T(8,128)(2,1)S(1)} %get-tuple-element.110.a, bf16[320,1152]{1,0:T(8,128)(2,1)S(1)} %collective-permute-done.18.b, bf16[320,1152]{1,0:T(8,128)(2,1)S(1)} %collective-permute-done.19.c), custom_call_target="tpu_custom_call" | custom-call | flops 1073741824 | bytes 1024 | tf_op jit(solution)/shard_map/pallas_call | solution.py:357
  93.2 2.8 %collective-permute-done.17 = bf16[72,1152]{1,0:T(8,128)(2,1)S(1)} collective-permute-done((bf16[72,1152]{1,0:T(8,128)(2,1)S(1)}, bf16[72,1152]{1,0:T(8,128)(2,1)S(1)}, u32[]{:S(2)}, u32[]{:S(2)}) %collective-permute-start.17) | collective-permute-done | bytes 165920 | tf_op jit(solution)/shard_map/ppermute | solution.py:24
  96.0 3.4 %collective-permute-done.16 = bf16[72,1152]{1,0:T(8,128)(2,1)S(1)} collective-permute-done((bf16[72,1152]{1,0:T(8,128)(2,1)S(1)}, bf16[72,1152]{1,0:T(8,128)(2,1)S(1)}, u32[]{:S(2)}, u32[]{:S(2)}) %collective-permute-start.16) | collective-permute-done | bytes 165920 | tf_op jit(solution)/shard_map/ppermute | solution.py:24
  99.4 0.8 add_add_fusion
  (17 shorter events, 0.1 us)
Async XLA Ops:
  0.6 35.4 %collective-permute-start.2 = (bf16[320,1152]{1,0:T(8,128)(2,1)}, bf16[320,1152]{1,0:T(8,128)(2,1)}, u32[]{:S(2)}, u32[]{:S(2)}) collective-permute-start(bf16[320,1152]{1,0:T(8,128)(2,1)} %bitcast.6), channel_id=1, source_target_pairs={{0,64},{64,0},{1,65},{65,1},{2,66},{66,2},{3,67},{67,3},{4,68},{68... | collective-permute-start | bytes 2211848 | tf_op jit(solution)/shard_map/ppermute | solution.py:24
  3.4 8.2 %collective-permute-start.1 = (bf16[72,1152]{1,0:T(8,128)(2,1)S(1)}, bf16[72,1152]{1,0:T(8,128)(2,1)S(1)}, u32[]{:S(2)}, u32[]{:S(2)}) collective-permute-start(bf16[72,1152]{1,0:T(8,128)(2,1)S(1)} %shard_map.78), channel_id=1, source_target_pairs={{0,72},{8,64},{64,8},{72,0},{1,73},{9,65},{65,9},{73,1},{2,74},{10... | collective-permute-start | bytes 497672 | tf_op jit(solution)/shard_map/ppermute | solution.py:34
  5.6 36.4 %collective-permute-start.5 = (bf16[320,1152]{1,0:T(8,128)(2,1)}, bf16[320,1152]{1,0:T(8,128)(2,1)S(1)}, u32[]{:S(2)}, u32[]{:S(2)}) collective-permute-start(bf16[320,1152]{1,0:T(8,128)(2,1)} %bitcast.8), channel_id=1, source_target_pairs={{0,32},{16,48},{32,0},{48,16},{1,33},{17,49},{33,1},{49,17},{2,34}... | collective-permute-start | bytes 2211848 | tf_op jit(solution)/shard_map/ppermute | solution.py:24
  9.5 32.7 %collective-permute-start.4 = (bf16[320,1152]{1,0:T(8,128)(2,1)}, bf16[320,1152]{1,0:T(8,128)(2,1)S(1)}, u32[]{:S(2)}, u32[]{:S(2)}) collective-permute-start(bf16[320,1152]{1,0:T(8,128)(2,1)} %bitcast.9), channel_id=1, source_target_pairs={{0,48},{16,0},{32,16},{48,32},{1,49},{17,1},{33,17},{49,33},{2,50}... | collective-permute-start | bytes 2211848 | tf_op jit(solution)/shard_map/ppermute | solution.py:24
  10.2 32.0 %collective-permute-start.3 = (bf16[320,1152]{1,0:T(8,128)(2,1)}, bf16[320,1152]{1,0:T(8,128)(2,1)S(1)}, u32[]{:S(2)}, u32[]{:S(2)}) collective-permute-start(bf16[320,1152]{1,0:T(8,128)(2,1)} %bitcast.10), channel_id=1, source_target_pairs={{0,16},{16,32},{32,48},{48,0},{1,17},{17,33},{33,49},{49,1},{2,18}... | collective-permute-start | bytes 2211848 | tf_op jit(solution)/shard_map/ppermute | solution.py:24
  11.5 24.5 %copy-start = (bf16[1,320,1152]{2,1,0:T(8,128)(2,1)S(1)}, bf16[1,320,1152]{2,1,0:T(8,128)(2,1)}, u32[]{:S(2)}) copy-start(bf16[1,320,1152]{2,1,0:T(8,128)(2,1)} %param.8) | copy-start | bytes 2211844
  32.7 3.4 %collective-permute-start = (bf16[4,2,72,1152]{3,2,1,0:T(8,128)(2,1)}, bf16[4,2,72,1152]{3,2,1,0:T(8,128)(2,1)}, u32[]{:S(2)}, u32[]{:S(2)}) collective-permute-start(bf16[4,2,72,1152]{3,2,1,0:T(8,128)(2,1)} %all_to_all.4), channel_id=1, source_target_pairs={{0,1},{1,0},{2,3},{3,2},{4,5},{5,4},{6,7},{7,6},{8,9},{9,8},{10,11... | collective-permute-start | bytes 3981320 | tf_op jit(solution)/shard_map/cond/branch_1_fun/ppermute | solution.py:24
  36.1 1.1 %copy-start.1 = (bf16[1,320,1152]{2,1,0:T(8,128)(2,1)S(1)}, bf16[1,320,1152]{2,1,0:T(8,128)(2,1)}, u32[]{:S(2)}) copy-start(bf16[1,320,1152]{2,1,0:T(8,128)(2,1)} %param.7) | copy-start | bytes 2211844
  52.1 8.0 %collective-permute-start.6 = (bf16[3,2,72,1152]{3,2,1,0:T(8,128)(2,1)S(1)}, bf16[3,2,72,1152]{3,2,1,0:T(8,128)(2,1)S(1)}, u32[]{:S(2)}, u32[]{:S(2)}) collective-permute-start(bf16[3,2,72,1152]{3,2,1,0:T(8,128)(2,1)S(1)} %get-tuple-element.86), channel_id=1, source_target_pairs={{0,1},{1,0},{2,3},{3,2},{4,5},{5,4},{6,7},{7,6},{8,9},{9,8},{10,11... | collective-permute-start | bytes 2985992 | tf_op jit(solution)/shard_map/ppermute | solution.py:24
  52.2 3.0 %collective-permute-start.9 = (bf16[2,72,1152]{2,1,0:T(8,128)(2,1)S(1)}, bf16[2,72,1152]{2,1,0:T(8,128)(2,1)S(1)}, u32[]{:S(2)}, u32[]{:S(2)}) collective-permute-start(bf16[2,72,1152]{2,1,0:T(8,128)(2,1)S(1)} %get-tuple-element.91), channel_id=1, source_target_pairs={{0,1},{1,0},{2,3},{3,2},{4,5},{5,4},{6,7},{7,6},{8,9},{9,8},{10,11... | collective-permute-start | bytes 995336 | tf_op jit(solution)/shard_map/ppermute | solution.py:24
  55.2 12.7 %collective-permute-start.11 = (bf16[320,1152]{1,0:T(8,128)(2,1)S(1)}, bf16[320,1152]{1,0:T(8,128)(2,1)S(1)}, u32[]{:S(2)}, u32[]{:S(2)}) collective-permute-start(bf16[320,1152]{1,0:T(8,128)(2,1)S(1)} %shard_map.82), channel_id=1, source_target_pairs={{0,16},{1,49},{16,32},{17,1},{32,48},{33,17},{48,0},{49,33},{2,18}... | collective-permute-start | bytes 2211848 | tf_op jit(solution)/shard_map/ppermute | solution.py:29
  56.3 12.0 %collective-permute-start.10 = (bf16[2,72,1152]{2,1,0:T(8,128)(2,1)S(1)}, bf16[2,72,1152]{2,1,0:T(8,128)(2,1)S(1)}, u32[]{:S(2)}, u32[]{:S(2)}) collective-permute-start(bf16[2,72,1152]{2,1,0:T(8,128)(2,1)S(1)} %shard_map.83), channel_id=1, source_target_pairs={{0,4},{2,6},{4,0},{6,2},{1,5},{3,7},{5,1},{7,3},{8,12},{10,14},{12... | collective-permute-start | bytes 995336 | tf_op jit(solution)/shard_map/ppermute | solution.py:24
  59.4 24.3 %collective-permute-start.14 = (bf16[320,1152]{1,0:T(8,128)(2,1)S(1)}, bf16[320,1152]{1,0:T(8,128)(2,1)S(1)}, u32[]{:S(2)}, u32[]{:S(2)}) collective-permute-start(bf16[320,1152]{1,0:T(8,128)(2,1)S(1)} %get-tuple-element.107), channel_id=1, source_target_pairs={{0,64},{64,0},{1,65},{65,1},{2,66},{66,2},{3,67},{67,3},{4,68},{68... | collective-permute-start | bytes 2211848 | tf_op jit(solution)/shard_map/ppermute | solution.py:24
  60.3 15.3 %collective-permute-start.7 = (bf16[2,72,1152]{2,1,0:T(8,128)(2,1)S(1)}, bf16[2,72,1152]{2,1,0:T(8,128)(2,1)S(1)}, u32[]{:S(2)}, u32[]{:S(2)}) collective-permute-start(bf16[2,72,1152]{2,1,0:T(8,128)(2,1)S(1)} %get-tuple-element.88), channel_id=1, source_target_pairs={{0,2},{2,4},{4,6},{6,0},{1,3},{3,5},{5,7},{7,1},{8,10},{10,12},{12... | collective-permute-start | bytes 995336 | tf_op jit(solution)/shard_map/ppermute | solution.py:24
  61.0 14.7 %collective-permute-start.8 = (bf16[2,72,1152]{2,1,0:T(8,128)(2,1)S(1)}, bf16[2,72,1152]{2,1,0:T(8,128)(2,1)S(1)}, u32[]{:S(2)}, u32[]{:S(2)}) collective-permute-start(bf16[2,72,1152]{2,1,0:T(8,128)(2,1)S(1)} %get-tuple-element.89), channel_id=1, source_target_pairs={{0,6},{2,0},{4,2},{6,4},{1,7},{3,1},{5,3},{7,5},{8,14},{10,8},{12,... | collective-permute-start | bytes 995336 | tf_op jit(solution)/shard_map/ppermute | solution.py:24
  68.3 23.3 %collective-permute-start.18 = (bf16[320,1152]{1,0:T(8,128)(2,1)S(1)}, bf16[320,1152]{1,0:T(8,128)(2,1)S(1)}, u32[]{:S(2)}, u32[]{:S(2)}) collective-permute-start(bf16[320,1152]{1,0:T(8,128)(2,1)S(1)} %get-tuple-element.111), channel_id=1, source_target_pairs={{0,48},{16,0},{32,16},{48,32},{1,49},{17,1},{33,17},{49,33},{2,50}... | collective-permute-start | bytes 2211848 | tf_op jit(solution)/shard_map/ppermute | solution.py:24
  70.8 20.8 %collective-permute-start.19 = (bf16[320,1152]{1,0:T(8,128)(2,1)S(1)}, bf16[320,1152]{1,0:T(8,128)(2,1)S(1)}, u32[]{:S(2)}, u32[]{:S(2)}) collective-permute-start(bf16[320,1152]{1,0:T(8,128)(2,1)S(1)} %get-tuple-element.112), channel_id=1, source_target_pairs={{0,16},{16,32},{32,48},{48,0},{1,17},{17,33},{33,49},{49,1},{2,18}... | collective-permute-start | bytes 2211848 | tf_op jit(solution)/shard_map/ppermute | solution.py:24
  75.8 7.7 %collective-permute-start.12 = (bf16[72,1152]{1,0:T(8,128)(2,1)S(1)}, bf16[72,1152]{1,0:T(8,128)(2,1)S(1)}, u32[]{:S(2)}, u32[]{:S(2)}) collective-permute-start(bf16[72,1152]{1,0:T(8,128)(2,1)S(1)} %get-tuple-element.105), channel_id=1, source_target_pairs={{0,72},{8,64},{64,8},{72,0},{1,73},{9,65},{65,9},{73,1},{2,74},{10... | collective-permute-start | bytes 497672 | tf_op jit(solution)/shard_map/ppermute | solution.py:34
  83.6 5.7 %collective-permute-start.13 = (bf16[72,1152]{1,0:T(8,128)(2,1)S(1)}, bf16[72,1152]{1,0:T(8,128)(2,1)S(1)}, u32[]{:S(2)}, u32[]{:S(2)}) collective-permute-start(bf16[72,1152]{1,0:T(8,128)(2,1)S(1)} %shard_map.88.a), channel_id=1, source_target_pairs={{0,64},{64,0},{1,65},{65,1},{2,66},{66,2},{3,67},{67,3},{4,68},{68... | collective-permute-start | bytes 497672 | tf_op jit(solution)/shard_map/ppermute | solution.py:24
  83.7 7.9 %copy-start.2 = (bf16[1,320,1152]{2,1,0:T(8,128)(2,1)S(1)}, bf16[1,320,1152]{2,1,0:T(8,128)(2,1)}, u32[]{:S(2)}) copy-start(bf16[1,320,1152]{2,1,0:T(8,128)(2,1)} %param.7) | copy-start | bytes 2211844
  89.3 6.8 %collective-permute-start.17 = (bf16[72,1152]{1,0:T(8,128)(2,1)S(1)}, bf16[72,1152]{1,0:T(8,128)(2,1)S(1)}, u32[]{:S(2)}, u32[]{:S(2)}) collective-permute-start(bf16[72,1152]{1,0:T(8,128)(2,1)S(1)} %shard_map.89), channel_id=1, source_target_pairs={{0,48},{16,0},{32,16},{48,32},{1,49},{17,1},{33,17},{49,33},{2,50}... | collective-permute-start | bytes 497672 | tf_op jit(solution)/shard_map/ppermute | solution.py:24
  90.0 9.4 %collective-permute-start.16 = (bf16[72,1152]{1,0:T(8,128)(2,1)S(1)}, bf16[72,1152]{1,0:T(8,128)(2,1)S(1)}, u32[]{:S(2)}, u32[]{:S(2)}) collective-permute-start(bf16[72,1152]{1,0:T(8,128)(2,1)S(1)} %shard_map.89), channel_id=1, source_target_pairs={{0,16},{16,32},{32,48},{48,0},{1,17},{17,33},{33,49},{49,1},{2,18}... | collective-permute-start | bytes 497672 | tf_op jit(solution)/shard_map/ppermute | solution.py:24
  91.3 8.1 %collective-permute-start.15 = (bf16[72,1152]{1,0:T(8,128)(2,1)S(1)}, bf16[72,1152]{1,0:T(8,128)(2,1)S(1)}, u32[]{:S(2)}, u32[]{:S(2)}) collective-permute-start(bf16[72,1152]{1,0:T(8,128)(2,1)S(1)} %shard_map.89), channel_id=1, source_target_pairs={{0,32},{16,48},{32,0},{48,16},{1,33},{17,49},{33,1},{49,17},{2,34}... | collective-permute-start | bytes 497672 | tf_op jit(solution)/shard_map/ppermute | solution.py:24
